TPU v7x, 32 devices: a whole 2x2x4 slice. The times are simulated.
32 devices in a mesh: seq: 8 (over z, x), exp: 4 (over y, core).
Axes of the slice: x: 2, y: 2, z: 4, core: 2. Of those that a mesh axis runs over, the one named last changes fastest.
Arguments:
- queries: bfloat16 [4, 32, 1536], P(None, 'exp'), may hold values from -200 to 200
- new_key_value: bfloat16 [4, 32, 2, 512], P(None, 'exp'), may hold values from -8 to 8
- key_value_cache: bfloat16 [32, 64, 64, 2, 512], P('exp', 'seq'), may hold values from -8 to 8
- page_table: int32 [32, 64], P('exp', 'seq'), may hold values from 0 to 63, as said below
- cache_len: int32 [32], P('exp'), may hold values from 1 to 4096
- routes: int32 [4, 32, 8], P(None, 'exp'), may hold values from 0 to 39, all different within a row; in each aligned block of 8 rows (0 to 7, 8 to 15, ..., all dimensions but the last counted through in order) at most 4 rows name the same one
- residual: bfloat16 [4, 32, 1536], P(None, 'exp', 'seq'), may hold values from -8 to 8
- w_out: bfloat16 [1536, 1536], P(None, 'seq'), may hold values from -0.15625 to 0.15625
- norm_gain: float32 [1536], P('seq'), may hold values from 0.1 to 1.9
- w_router: bfloat16 [1536, 40], P('seq'), may hold values from -0.15625 to 0.15625
- w_gate_up: bfloat16 [40, 1536, 2, 512], P('exp', 'seq'), may hold values from -0.15625 to 0.15625
- w_down: bfloat16 [40, 1536, 512], P('exp', 'seq'), may hold values from -0.25 to 0.25
Outputs:
- layer_out: bfloat16 [4, 32, 1536], P(None, 'exp', 'seq')
Inputs may be any that keep to these rules, and one draw needn't show every extreme that they name: `page_table`: within the block of one index of exp and one index of seq (8 rows, 8 columns) the entries are each page slot once. `routes`: in each step the 8 tokens of one index of exp name one expert at most 4 times; a row's 8 experts differ.
All inputs are finite; a program needn't handle non-finite values.
Results may differ from a plain program's by a relative error of at most 0.0053.
Values may be sent and summed in bfloat16 or wider, within the bound.
No kernel may reach another device: no remote copies, remote signals or barrier semaphores. Data moves between devices by JAX's collectives and lax.ppermute only.
A program may use at most 128 MiB of HBM per device.

v0:
```python
import functools

import jax
import jax.numpy as jnp
from jax import lax
from jax.experimental import pallas as pl
from jax.experimental.pallas import tpu as pltpu
from jax.sharding import PartitionSpec as P

D = 1536
QUERY_HEADS = 24
KEY_VALUE_HEADS = 8
HEAD_SIZE = 64
GROUP = QUERY_HEADS // KEY_VALUE_HEADS
KV_WIDTH = KEY_VALUE_HEADS * HEAD_SIZE
EXPERTS = 40
FF = 512
CAP = 4
LANES = 128
SIDE_KEYS = 2
ROUND_ROWS = 384

NEG_FILL = -1e30
F32 = jnp.float32
BF16 = jnp.bfloat16
VMEM_LIMIT = 48 * 1024 * 1024


def iota(shape, dimension):
    return lax.broadcasted_iota(jnp.int32, shape, dimension)


def dot_nt(a, b):
    return lax.dot_general(a, b, (((1,), (1,)), ((), ())), preferred_element_type=F32)


def dot_tn(a, b):
    return lax.dot_general(a, b, (((0,), (0,)), ((), ())), preferred_element_type=F32)


def dot_nn(a, b):
    return lax.dot_general(a, b, (((1,), (0,)), ((), ())), preferred_element_type=F32)


def round16(x):
    return x.astype(BF16).astype(F32)


def swap_halves(x):
    return pltpu.roll(x, HEAD_SIZE, 1)


def tile_of(x, index):
    return x[:, index * LANES : (index + 1) * LANES]


def padded(width):
    return -(-width // LANES) * LANES


def params():
    return pltpu.CompilerParams(vmem_limit_bytes=VMEM_LIMIT)


def attend_kernel(steps, pages, page_rows, table_ref, len_ref, seq_ref, q_ref, fresh_ref, *refs):
    page_refs, out_ref = refs[:pages], refs[pages]
    request = pl.program_id(0)
    q = q_ref[0].astype(F32)
    low = iota((steps, LANES), 1) < HEAD_SIZE
    by_group = []
    for g in range(GROUP):
        tiles = []
        for j in range(KV_WIDTH // LANES):
            first = tile_of(q, (6 * j + g) // 2)
            second = tile_of(q, (6 * j + 3 + g) // 2)
            if g % 2 == 0:
                tiles.append(jnp.where(low, first, second))
            else:
                tiles.append(swap_halves(jnp.where(low, second, first)))
        by_group.append(jnp.concatenate(tiles, axis=1))
    rows = steps * GROUP * KEY_VALUE_HEADS
    stacked = jnp.concatenate(
        [
            jnp.broadcast_to(by_group[g][t : t + 1], (KEY_VALUE_HEADS, KV_WIDTH))
            for t in range(steps)
            for g in range(GROUP)
        ],
        axis=0,
    )
    own = iota((rows, KV_WIDTH), 1) // HEAD_SIZE == iota((rows, KV_WIDTH), 0) % KEY_VALUE_HEADS
    spread = jnp.where(own, stacked, 0.0).astype(BF16)
    keys = jnp.concatenate([ref[0, 0] for ref in page_refs], axis=0)
    values = jnp.concatenate([ref[0, 1] for ref in page_refs], axis=0)
    span = pages * page_rows
    scores = dot_nt(spread, keys) * 0.125
    live = seq_ref[0] * span + iota((rows, span), 1) < len_ref[request]
    scores = jnp.where(live, scores, NEG_FILL)
    fresh_keys, fresh_values = fresh_ref[0, 0], fresh_ref[0, 1]
    fresh_rows = fresh_keys.shape[0]
    fresh_scores = dot_nt(spread, fresh_keys) * 0.125
    row_step = iota((rows, fresh_rows), 0) // (GROUP * KEY_VALUE_HEADS)
    kept = jnp.logical_and(iota((rows, fresh_rows), 1) <= row_step, seq_ref[0] == 0)
    fresh_scores = jnp.where(kept, fresh_scores, NEG_FILL)
    largest = jnp.maximum(
        jnp.max(scores, axis=1, keepdims=True), jnp.max(fresh_scores, axis=1, keepdims=True)
    )
    weights = jnp.where(live, jnp.exp(scores - largest), 0.0)
    fresh_weights = jnp.where(kept, jnp.exp(fresh_scores - largest), 0.0)
    total = jnp.sum(weights, axis=1, keepdims=True) + jnp.sum(fresh_weights, axis=1, keepdims=True)
    acc = dot_nn(weights.astype(BF16), values) + dot_nn(fresh_weights.astype(BF16), fresh_values)
    some = total > 0.0
    safe = jnp.where(some, total, 1.0)
    acc = jnp.where(own, acc * (1.0 / safe), 0.0)
    acc = jnp.sum(acc.reshape(steps * GROUP, KEY_VALUE_HEADS, KV_WIDTH), axis=1)
    level = jnp.where(some, largest + jnp.log(safe), NEG_FILL)
    high = round16(level)
    middle = round16(level - high)
    rest = level - high - middle
    lane = iota((rows, LANES), 1)
    head = iota((rows, LANES), 0) % KEY_VALUE_HEADS
    side = jnp.where(lane == head, high, 0.0)
    side = jnp.where(lane == head + 8, middle, side)
    side = jnp.where(lane == head + 16, rest, side)
    side = jnp.sum(side.reshape(steps * GROUP, KEY_VALUE_HEADS, LANES), axis=1)
    out_ref[0, :, 0:KV_WIDTH] = acc.astype(BF16)
    out_ref[0, :, KV_WIDTH : KV_WIDTH + LANES] = side.astype(BF16)


def attend(queries, new_key_value, pool, page_table, cache_len, seq_index):
    steps, requests, width = queries.shape
    pages = page_table.shape[1]
    page_rows = pool.shape[2]
    by_request = queries.transpose(1, 0, 2)
    fresh = new_key_value.transpose(1, 2, 0, 3)
    fresh = jnp.pad(fresh, ((0, 0), (0, 0), (0, 16 - steps), (0, 0)))

    def page_map(page):
        return lambda r, table, lens, seq: (table[r * pages + page], 0, 0, 0)

    return pl.pallas_call(
        functools.partial(attend_kernel, steps, pages, page_rows),
        grid_spec=pltpu.PrefetchScalarGridSpec(
            num_scalar_prefetch=3,
            grid=(requests,),
            in_specs=[
                pl.BlockSpec((1, steps, width), lambda r, *_: (r, 0, 0)),
                pl.BlockSpec((1, 2, 16, KV_WIDTH), lambda r, *_: (r, 0, 0, 0)),
            ]
            + [pl.BlockSpec((1, 2, page_rows, KV_WIDTH), page_map(page)) for page in range(pages)],
            out_specs=pl.BlockSpec(
                (1, steps * GROUP, KV_WIDTH + LANES), lambda r, *_: (r, 0, 0)
            ),
        ),
        out_shape=jax.ShapeDtypeStruct((requests, steps * GROUP, KV_WIDTH + LANES), BF16),
        compiler_params=params(),
        name="attend",
    )(page_table.reshape(-1), cache_len, seq_index, by_request, fresh, *([pool] * pages))


def join_kernel(x_ref, out_ref):
    blocks, rows, _ = x_ref.shape
    tokens = rows // GROUP
    levels = []
    for b in range(blocks):
        side = x_ref[b, :, KV_WIDTH : KV_WIDTH + LANES].astype(F32)
        levels.append(side + pltpu.roll(side, LANES - 8, 1) + pltpu.roll(side, LANES - 16, 1))
    largest = functools.reduce(jnp.maximum, levels)
    weights = [jnp.exp(level - largest) for level in levels]
    inverse = 1.0 / functools.reduce(jnp.add, weights)
    low = iota((rows, LANES), 1) < HEAD_SIZE
    acc = [jnp.zeros((rows, LANES), F32) for _ in range(KV_WIDTH // LANES)]
    for b in range(blocks):
        share = weights[b] * inverse
        for j in range(KV_WIDTH // LANES):
            factor = jnp.where(low, share[:, 2 * j : 2 * j + 1], share[:, 2 * j + 1 : 2 * j + 2])
            acc[j] = acc[j] + factor * x_ref[b, :, j * LANES : (j + 1) * LANES].astype(F32)

    def piece(head, half):
        k, g = head // GROUP, head % GROUP
        tile = jnp.concatenate(
            [acc[k // 2][t * GROUP + g : t * GROUP + g + 1] for t in range(tokens)], axis=0
        )
        return tile if k % 2 == half else swap_halves(tile)

    low_tokens = iota((tokens, LANES), 1) < HEAD_SIZE
    for m in range(QUERY_HEADS // 2):
        tile = jnp.where(low_tokens, piece(2 * m, 0), piece(2 * m + 1, 1)).astype(BF16)
        for b in range(blocks):
            out_ref[b, :, m * LANES : (m + 1) * LANES] = tile


def join(parts):
    blocks, rows, _ = parts.shape
    return pl.pallas_call(
        join_kernel,
        out_shape=jax.ShapeDtypeStruct((blocks, rows // GROUP, QUERY_HEADS * HEAD_SIZE), BF16),
        compiler_params=params(),
        name="join",
    )(parts)


def side_place(features, count):
    tile, offset = features // LANES * LANES, features % LANES
    return (tile, offset) if offset and offset + count <= LANES else (padded(features), 0)


def hidden_kernel(attn_ref, residual_ref, w_ref, gain_ref, routes_ref, hidden_ref, out_ref, wide_ref):
    steps, requests, features = residual_ref.shape
    tokens = steps * requests
    blocks = [attn_ref[b].astype(F32) for b in range(attn_ref.shape[0])]
    attn = jnp.concatenate(blocks, axis=0).astype(BF16)
    row, column = iota((tokens, tokens), 0), iota((tokens, tokens), 1)
    reorder = jnp.logical_and(row % requests == column // steps, row // requests == column % steps)
    attn = dot_nn(reorder.astype(F32).astype(BF16), attn).astype(BF16)
    residual = residual_ref[...].astype(F32).reshape(tokens, features)
    hidden = residual + dot_nt(attn, w_ref[...])
    hidden_ref[...] = hidden
    squares = jnp.sum(hidden * hidden, axis=1, keepdims=True)
    tile, offset = side_place(features, SIDE_KEYS + EXPERTS)
    wide_ref[...] = jnp.zeros_like(wide_ref)
    wide_ref[:, 0:features] = hidden * gain_ref[...]
    routes = routes_ref[...].reshape(tokens, routes_ref.shape[2])
    lane = iota((tokens, LANES), 1) - offset
    side = wide_ref[:, tile : tile + LANES]
    for k in range(routes.shape[1]):
        side = jnp.where(lane == routes[:, k : k + 1] + SIDE_KEYS, 1.0, side)
    high = round16(squares)
    side = jnp.where(lane == 0, high, side)
    wide_ref[:, tile : tile + LANES] = jnp.where(lane == 1, squares - high, side)
    made = wide_ref[...].astype(BF16)
    for e in range(out_ref.shape[0]):
        out_ref[e] = made


def hidden_state(attn, residual, w_out, gain, routes, exp_count):
    steps, requests, features = residual.shape
    tokens = steps * requests
    wide = side_place(features, SIDE_KEYS + EXPERTS)[0] + LANES
    return pl.pallas_call(
        hidden_kernel,
        out_shape=(
            jax.ShapeDtypeStruct((tokens, features), F32),
            jax.ShapeDtypeStruct((exp_count, tokens, wide), BF16),
        ),
        scratch_shapes=[pltpu.VMEM((tokens, wide), F32)],
        compiler_params=params(),
        name="hidden",
    )(attn, residual, w_out.T, gain.reshape(1, features), routes)


def window_start(first, rows, window):
    return pl.multiple_of(jnp.clip(first // 16 * 16, 0, rows - window), 16)


def gate_up_kernel(
    features, local, turn, where_ref, x_ref, w_ref, router_ref,
    out_ref, pick_ref, range_ref, first_ref, most_ref, row_ref, acc_ref,
):
    total = x_ref.shape[0]
    rows = pick_ref.shape[1]
    blocks = out_ref.shape[0]
    share = rows // blocks
    width = w_ref.shape[3]
    window = total // 2 + 16
    tile, offset = side_place(features, SIDE_KEYS + EXPERTS)
    me = where_ref[0]
    own_side = x_ref[:, tile : tile + LANES].astype(F32)
    lane = iota((total, LANES), 1)
    flags = pltpu.roll(own_side, LANES - offset - SIDE_KEYS, 1)
    flags = jnp.where(lane < EXPERTS, flags, 0.0)
    owners = EXPERTS // local
    counts = jnp.sum(flags, axis=0, keepdims=True)
    most = jnp.int32(0)
    for o in range(owners):
        held = jnp.logical_and(lane[0:1] >= o * local, lane[0:1] < (o + 1) * local)
        most = jnp.maximum(most, jnp.sum(jnp.where(held, counts, 0.0)).astype(jnp.int32))
    most_ref[0] = most
    mine = pltpu.roll(flags, lax.rem(LANES - me * local, LANES), 1)
    mine = jnp.where(lane < local, mine, 0.0)
    mine16 = mine.astype(BF16)
    row, column = iota((total, total), 0), iota((total, total), 1)
    earlier = (column < row).astype(F32).astype(BF16)
    ranks = dot_nn(earlier, mine16)
    counts = jnp.sum(mine, axis=0, keepdims=True)
    before = (iota((LANES, LANES), 0) < iota((LANES, LANES), 1)).astype(F32).astype(BF16)
    first = dot_nn(jnp.broadcast_to(counts, (8, LANES)).astype(BF16), before)[0:1] - turn * rows
    place = jnp.where(mine > 0.0, first + ranks, -1.0).astype(jnp.int32)
    at = iota((total, rows), 1)
    pick = jnp.zeros((total, rows), F32)
    for j in range(local):
        pick = jnp.where(at == place[:, j : j + 1], 1.0, pick)
    pick = pick.astype(BF16)
    pick_ref[...] = pick
    ranges = jnp.where(iota((16, LANES), 0) < 8, first, first + counts)
    ranges = jnp.concatenate([ranges[0:8], ranges[8:16]] + [jnp.zeros((LANES - 16, LANES), F32)], axis=0)
    ranges = ranges.T
    range_ref[...] = ranges[0:16]
    row_ref[...] = dot_tn(pick, x_ref[...]).astype(BF16)
    acc_ref[...] = jnp.zeros_like(acc_ref)
    for j in range(local):
        start_row = jnp.sum(first[:, j : j + 1]).astype(jnp.int32)
        first_ref[j] = start_row
        start = window_start(start_row, rows, window)
        part = row_ref[pl.ds(start, window), 0:features]
        fresh = start + iota((window, width), 0) >= start_row
        for half in range(2):
            into = (pl.ds(start, window), slice(half * width, (half + 1) * width))
            made = dot_nn(part, w_ref[j, half])
            acc_ref[into] = jnp.where(fresh, made, acc_ref[into])
    for b in range(blocks):
        for piece in range(2 * width // LANES):
            out_ref[b, piece * share : (piece + 1) * share, :] = acc_ref[
                b * share : (b + 1) * share, piece * LANES : (piece + 1) * LANES
            ].astype(BF16)
    logits = dot_nt(router_ref[...], x_ref[:, 0:features])
    high = round16(logits)
    both = jnp.concatenate([high, logits - high], axis=0).astype(BF16)
    both = dot_nn(both, pick)
    turned = jnp.zeros((EXPERTS, rows), jnp.bool_)
    expert = iota((EXPERTS, rows), 0) - me * local
    where_row = iota((EXPERTS, rows), 1).astype(F32)
    for j in range(local):
        inside = jnp.logical_and(
            where_row >= first[:, j : j + 1], where_row < (first + counts)[:, j : j + 1]
        )
        turned = jnp.logical_or(turned, jnp.logical_and(inside, expert == j))
    squares = dot_tn(own_side.astype(BF16), pick)
    side = jnp.concatenate(
        [
            jnp.sum(jnp.where(turned, both[0:EXPERTS], 0.0), axis=0, keepdims=True),
            jnp.sum(jnp.where(turned, both[EXPERTS : 2 * EXPERTS], 0.0), axis=0, keepdims=True),
            squares[offset : offset + 2],
            jnp.zeros((12, rows), F32),
        ],
        axis=0,
    )
    for b in range(blocks):
        end = 2 * width // LANES * share
        out_ref[b, end : end + 16, :] = jnp.zeros((16, LANES), BF16)
        out_ref[b, end : end + 16, 0:share] = side[:, b * share : (b + 1) * share].astype(BF16)


def gate_up(exp_index, tokens, weights, w_router, rows, blocks, turn):
    local, _, features, width = weights.shape
    total, wide = tokens.shape
    smem, vmem = pl.BlockSpec(memory_space=pltpu.SMEM), pl.BlockSpec(memory_space=pltpu.VMEM)
    return pl.pallas_call(
        functools.partial(gate_up_kernel, features, local, turn),
        in_specs=[smem, vmem, vmem, vmem],
        out_specs=(vmem, vmem, vmem, smem, smem),
        out_shape=(
            jax.ShapeDtypeStruct((blocks, 2 * width // LANES * (rows // blocks) + 16, LANES), BF16),
            jax.ShapeDtypeStruct((total, rows), BF16),
            jax.ShapeDtypeStruct((16, LANES), F32),
            jax.ShapeDtypeStruct((16,), jnp.int32),
            jax.ShapeDtypeStruct((1,), jnp.int32),
        ),
        scratch_shapes=[pltpu.VMEM((rows, wide), BF16), pltpu.VMEM((rows, 2 * width), F32)],
        compiler_params=params(),
        name="gate_up",
    )(exp_index, tokens, weights, w_router.T)


def inner_kernel(x_ref, out_ref):
    blocks, height, _ = x_ref.shape
    pieces = 2 * FF // LANES
    share = (height - 16) // pieces
    half = pieces // 2

    def total(start, size):
        added = x_ref[0, start : start + size].astype(F32)
        for b in range(1, blocks):
            added = added + x_ref[b, start : start + size].astype(F32)
        return added

    side = total(pieces * share, 16)
    logit = side[0:1] + side[1:2]
    squares = side[2:3] + side[3:4]
    inverse = lax.rsqrt(squares * (1.0 / D) + 1e-6)
    down_column = jnp.broadcast_to(inverse, (LANES, LANES)).T[0:share, 0:1]
    for piece in range(half):
        gate = total(piece * share, share) * down_column
        up = total((half + piece) * share, share) * down_column
        made = (gate / (1.0 + jnp.exp(-gate)) * up).astype(BF16)
        for b in range(blocks):
            out_ref[b, piece * share : (piece + 1) * share, :] = made
    logit = logit * inverse
    high = round16(logit)
    middle = round16(logit - high)
    own = jnp.concatenate(
        [high, middle, logit - high - middle, jnp.zeros((13, LANES), F32)], axis=0
    ).astype(BF16)
    for b in range(blocks):
        out_ref[b, half * share : half * share + 16, :] = own


def inner(parts):
    blocks, height, _ = parts.shape
    return pl.pallas_call(
        inner_kernel,
        out_shape=jax.ShapeDtypeStruct((blocks, (height - 16) // 2 + 16, LANES), BF16),
        compiler_params=params(),
        name="inner",
    )(parts)


def down_kernel(features, local, first_ref, range_ref, pick_ref, x_ref, w_ref, out_ref, row_ref, made_ref):
    blocks, height, _ = x_ref.shape
    total, rows = pick_ref.shape
    width = w_ref.shape[2]
    pieces = width // LANES
    share = (height - 16) // pieces
    window = total // 2 + 16
    for b in range(blocks):
        for piece in range(pieces):
            row_ref[b * share : (b + 1) * share, piece * LANES : (piece + 1) * LANES] = x_ref[
                b, piece * share : (piece + 1) * share, :
            ]
    made_ref[...] = jnp.zeros_like(made_ref)
    for j in range(local):
        start_row = first_ref[j]
        start = window_start(start_row, rows, window)
        made = dot_nt(row_ref[pl.ds(start, window), :], w_ref[j])
        fresh = start + iota((window, features), 0) >= start_row
        into = (pl.ds(start, window), slice(0, features))
        made_ref[into] = jnp.where(fresh, made, made_ref[into])
    logit = jnp.concatenate(
        [x_ref[b, pieces * share :, 0:share].astype(F32) for b in range(blocks)], axis=1
    )
    pick = pick_ref[...]
    where_row = iota((16, rows), 1).astype(F32)
    inside = jnp.logical_and(where_row >= range_ref[:, 0:1], where_row < range_ref[:, 8:9])
    inside = jnp.logical_and(inside, iota((16, rows), 0) < local)
    spread = [jnp.where(inside, logit[k : k + 1], 0.0) for k in range(3)]
    spread.append(inside.astype(F32))
    found = dot_nt(jnp.concatenate(spread, axis=0).astype(BF16), pick)
    valid = found[48:64] > 0.5
    logits = jnp.where(valid, found[0:16] + found[16:32] + found[32:48], NEG_FILL)
    top = jnp.max(logits, axis=0, keepdims=True)
    weights = jnp.where(valid, jnp.exp(logits - top), 0.0)
    summed = jnp.sum(weights, axis=0, keepdims=True)
    high = round16(weights)
    both = dot_nn(jnp.concatenate([high, weights - high], axis=0).astype(BF16), pick)
    weight = jnp.sum(jnp.where(inside, both[0:16] + both[16:32], 0.0), axis=0, keepdims=True)
    column = jnp.broadcast_to(weight, (LANES, rows)).T[:, 0:1]
    acc = dot_nn(pick, (made_ref[...] * column).astype(BF16))
    tile, offset = side_place(features, 2)
    pair = jnp.where(iota((LANES, total), 0) == 0, top, summed).T
    count, tokens, _ = out_ref.shape
    for e in range(count):
        at = slice(e * tokens, (e + 1) * tokens)
        out_ref[e] = acc[at]
        lane = iota((tokens, LANES), 1) - offset
        side = jnp.where(lane == 0, pair[at, 0:1], acc[at, tile : tile + LANES])
        out_ref[e, :, tile : tile + LANES] = jnp.where(lane == 1, pair[at, 1:2], side)


def down(first, ranges, pick, parts, weights, exp_count):
    local, features, width = weights.shape
    total, rows = pick.shape
    wide = side_place(features, 2)[0] + LANES
    smem, vmem = pl.BlockSpec(memory_space=pltpu.SMEM), pl.BlockSpec(memory_space=pltpu.VMEM)
    return pl.pallas_call(
        functools.partial(down_kernel, features, local),
        in_specs=[smem] + [vmem] * 4,
        out_shape=jax.ShapeDtypeStruct((exp_count, total // exp_count, wide), F32),
        scratch_shapes=[pltpu.VMEM((rows, width), BF16), pltpu.VMEM((rows, wide), F32)],
        compiler_params=params(),
        name="down",
    )(first, ranges, pick, parts, weights)


def finish_kernel(x_ref, hidden_ref, out_ref):
    owners = x_ref.shape[0]
    features = hidden_ref.shape[1]
    tile, offset = side_place(features, 2)
    sides = [x_ref[e, :, tile : tile + LANES] for e in range(owners)]
    tops = [side[:, offset : offset + 1] for side in sides]
    top = functools.reduce(jnp.maximum, tops)
    scales = [jnp.exp(one - top) for one in tops]
    total = functools.reduce(
        jnp.add, [s * side[:, offset + 1 : offset + 2] for s, side in zip(scales, sides)]
    )
    acc = functools.reduce(
        jnp.add, [s * x_ref[e, :, 0:features] for e, s in enumerate(scales)]
    )
    out = hidden_ref[...] + acc * (1.0 / total)
    out_ref[...] = out.reshape(out_ref.shape).astype(BF16)


def finish(parts, hidden, shape):
    return pl.pallas_call(
        finish_kernel,
        out_shape=jax.ShapeDtypeStruct(shape, BF16),
        compiler_params=params(),
        name="finish",
    )(parts, hidden)


def join_rounds(features, one, other):
    tile, offset = side_place(features, 2)
    at = tile + offset
    top = jnp.maximum(one[..., at : at + 1], other[..., at : at + 1])
    scales = [jnp.exp(part[..., at : at + 1] - top) for part in (one, other)]
    joined = one * scales[0] + other * scales[1]
    return jnp.where(jnp.arange(one.shape[-1]) == at, top, joined)


def swap(x, axis):
    return lax.all_to_all(x, axis, split_axis=0, concat_axis=0, tiled=True)


def local(
    queries,
    new_key_value,
    key_value_cache,
    page_table,
    cache_len,
    routes,
    residual,
    w_out,
    norm_gain,
    w_router,
    w_gate_up,
    w_down,
):
    exp_count = lax.axis_size("exp")
    seq_count = lax.axis_size("seq")
    exp_index = lax.axis_index("exp").astype(jnp.int32).reshape(1)
    seq_index = lax.axis_index("seq").astype(jnp.int32).reshape(1)
    steps, requests, width = queries.shape
    tokens = steps * requests
    features = w_out.shape[1]
    page_rows = key_value_cache.shape[2]
    pool = key_value_cache.reshape(-1, page_rows, 2, KV_WIDTH).transpose(0, 2, 1, 3)

    shares = attend(queries, new_key_value, pool, page_table, cache_len, seq_index)
    shares = swap(shares.reshape(seq_count, -1, KV_WIDTH + LANES), "seq")
    attn = join(shares)
    w_gate_up, attn = lax.optimization_barrier((w_gate_up, attn))
    attn = swap(attn, "seq")
    gate_up_weights = w_gate_up.transpose(0, 2, 1, 3)
    gate_up_weights, attn = lax.optimization_barrier((gate_up_weights, attn))
    hidden, outgoing = hidden_state(attn, residual, w_out, norm_gain, routes, exp_count)
    incoming = swap(outgoing, "exp").reshape(exp_count * tokens, -1)
    rows = -(-ROUND_ROWS // (16 * seq_count)) * 16 * seq_count

    def one_round(turn):
        parts, pick, ranges, first, most = gate_up(
            exp_index, incoming, gate_up_weights, w_router, rows, seq_count, turn
        )
        made = swap(inner(swap(parts, "seq")), "seq")
        return down(first, ranges, pick, made, w_down, exp_count), most

    made, most = one_round(0)
    pairs = w_gate_up.shape[0] * exp_count * steps * CAP
    for turn in range(1, -(-pairs // rows)):
        made = lax.cond(
            most[0] > turn * rows,
            lambda made: join_rounds(features, made, one_round(turn)[0]),
            lambda made: made,
            made,
        )
    return finish(swap(made, "exp"), hidden, (steps, requests, features))


def solution(mesh):
    in_specs = (
        P(None, "exp", None),
        P(None, "exp", None, None),
        P("exp", "seq", None, None, None),
        P("exp", "seq"),
        P("exp"),
        P(None, "exp", None),
        P(None, "exp", "seq"),
        P(None, "seq"),
        P("seq"),
        P("seq", None),
        P("exp", "seq", None, None),
        P("exp", "seq", None),
    )
    out_specs = P(None, "exp", "seq")
    return jax.shard_map(local, mesh=mesh, in_specs=in_specs, out_specs=out_specs, check_vma=False)
```

profile of v0, /device:TPU:0, one launch (start us, length us, event | category | flops | bytes accessed | tf_op | source)
XLA Modules:
  0.0 111.3 jit_solution(13167918788863814689)
XLA Ops:
  0.0 0.8 reshape.23.table_ref
  0.8 0.9 copy.26
  1.7 0.9 copy.25
  2.6 0.0 copy-start.4
  2.6 8.8 %copy.19 = bf16[8,8,64,2,512]{4,2,3,1,0:T(8,128)(2,1)} copy(bf16[8,8,64,2,512]{4,3,2,1,0:T(2,128)(2,1)} %param.16) | data formatting | bytes 16777216 | tf_op args[2]
  11.5 0.0 copy-done.4
  11.5 10.0 %attend.1 = bf16[8,12,640]{2,1,0:T(8,128)(2,1)S(1)} custom-call(s32[64]{0:T(128)S(1)} %reshape.23.table_ref, s32[8]{0:T(128)S(1)} %copy-done.4, s32[1]{0:T(128)} %bitcast.2.seq_ref, bf16[8,4,1536]{2,1,0:T(4,128)(2,1)S(1)} %bitcast.21, bf16[8,2,16,512]{3,2,1,0:T(8,128)(2,1)S(1)} %pad.4.fresh_ref, bf16[64,2,64,512]{3,2,1,0:T(8,128)(2,1)} %bitcast.23, ...), custom_call_target="tpu_custom_call" | custom-call | tf_op jit(solution)/shard_map/attend/pallas_call | solution.py:140
  21.5 14.6 %all_to_all.39.x_ref = bf16[8,12,640]{2,1,0:T(8,128)(2,1)S(1)} all-to-all(bf16[8,12,640]{2,1,0:T(8,128)(2,1)S(1)} %attend.1), channel_id=1, replica_groups=mesh['seq'=8,'exp'=4] {'seq'}, dimensions={0} | all-to-all | bytes 245760 | tf_op jit(solution)/shard_map/all_to_all | solution.py:510
  36.2 1.1 %join.1 = bf16[8,4,1536]{2,1,0:T(4,128)(2,1)} custom-call(bf16[8,12,640]{2,1,0:T(8,128)(2,1)S(1)} %all_to_all.39.x_ref), custom_call_target="tpu_custom_call" | custom-call | tf_op jit(solution)/shard_map/join/pallas_call | solution.py:194
  37.3 3.4 %all-to-all-start.3 = ((bf16[8,4,1536]{2,1,0:T(4,128)(2,1)}), bf16[8,4,1536]{2,1,0:T(4,128)(2,1)S(1)}, u32[]{:S(2)}, u32[]{:S(2)}) async-start(bf16[8,4,1536]{2,1,0:T(4,128)(2,1)} %join.1), calls=%async_computation.3 | async-start | bytes 196608 | tf_op jit(solution)/shard_map/all_to_all | solution.py:510
  40.7 0.0 copy-start
  40.7 0.0 copy-start.1
  40.7 0.0 copy-start.2
  40.7 0.0 copy-start.3
  40.7 0.0 copy-start.6
  40.7 4.8 %copy.24 = bf16[10,192,2,512]{3,1,2,0:T(8,128)(2,1)} copy(bf16[10,192,2,512]{3,2,1,0:T(2,128)(2,1)} %param.24) | data formatting | bytes 7864320 | tf_op jit(solution)/shard_map/optimization_barrier | solution.py:540
  45.6 2.2 %all-to-all-done.3.attn_ref = bf16[8,4,1536]{2,1,0:T(4,128)(2,1)S(1)} async-done(((bf16[8,4,1536]{2,1,0:T(4,128)(2,1)}), bf16[8,4,1536]{2,1,0:T(4,128)(2,1)S(1)}, u32[]{:S(2)}, u32[]{:S(2)}) %all-to-all-start.3) | async-done | bytes 98336 | tf_op jit(solution)/shard_map/all_to_all | solution.py:510
  47.7 0.0 copy-done
  47.7 0.0 copy-done.1
  47.7 0.0 copy-done.2
  47.7 0.0 copy-done.3
  47.7 1.1 hidden.1
  48.8 3.4 %all-to-all-start.4 = ((bf16[4,32,256]{2,1,0:T(8,128)(2,1)}), bf16[4,32,256]{2,1,0:T(8,128)(2,1)S(1)}, u32[]{:S(2)}, u32[]{:S(2)}) async-start(bf16[4,32,256]{2,1,0:T(8,128)(2,1)} %get-tuple-element.45), calls=%async_computation.4 | async-start | bytes 131072 | tf_op jit(solution)/shard_map/all_to_all | solution.py:510
  52.3 4.1 %all-to-all-done.4 = bf16[4,32,256]{2,1,0:T(8,128)(2,1)S(1)} async-done(((bf16[4,32,256]{2,1,0:T(8,128)(2,1)}), bf16[4,32,256]{2,1,0:T(8,128)(2,1)S(1)}, u32[]{:S(2)}, u32[]{:S(2)}) %all-to-all-start.4) | async-done | bytes 65568 | tf_op jit(solution)/shard_map/all_to_all | solution.py:510
  56.3 4.3 %gate_up.3 = (bf16[8,400,128]{2,1,0:T(8,128)(2,1)S(1)}, bf16[128,384]{1,0:T(8,128)(2,1)S(1)}, f32[16,128]{1,0:T(8,128)S(1)}, s32[16]{0:T(128)S(1)}, s32[1]{0:T(128)}) custom-call(s32[1]{0:T(128)} %bitcast.1.where_ref, bf16[128,256]{1,0:T(8,128)(2,1)S(1)} %bitcast.33, bf16[10,2,192,512]{3,2,1,0:T(8,128)(2,1)} %bitcast.31, bf16[40,192]{1,0:T(8,128)(2,1)S(1)} %bitcast.36), custom_call_target="tpu_custom_call" | custom-call | tf_op jit(solution)/shard_map/gate_up/pallas_call | solution.py:347
  60.7 25.0 %all_to_all.40.x_ref = bf16[8,400,128]{2,1,0:T(8,128)(2,1)S(1)} all-to-all(bf16[8,400,128]{2,1,0:T(8,128)(2,1)S(1)} %get-tuple-element.51), channel_id=1, replica_groups=mesh['seq'=8,'exp'=4] {'seq'}, dimensions={0} | all-to-all | bytes 1638400 | tf_op jit(solution)/shard_map/all_to_all | solution.py:510
  85.6 1.0 inner.3
  86.6 3.5 %all-to-all-start.6 = ((bf16[8,208,128]{2,1,0:T(8,128)(2,1)}), bf16[8,208,128]{2,1,0:T(8,128)(2,1)S(1)}, u32[]{:S(2)}, u32[]{:S(2)}) async-start(bf16[8,208,128]{2,1,0:T(8,128)(2,1)} %inner.3), calls=%async_computation.6 | async-start | bytes 851968 | tf_op jit(solution)/shard_map/all_to_all | solution.py:510
  90.8 10.7 %all-to-all-done.6.x_ref = bf16[8,208,128]{2,1,0:T(8,128)(2,1)S(1)} async-done(((bf16[8,208,128]{2,1,0:T(8,128)(2,1)}), bf16[8,208,128]{2,1,0:T(8,128)(2,1)S(1)}, u32[]{:S(2)}, u32[]{:S(2)}) %all-to-all-start.6) | async-done | bytes 426016 | tf_op jit(solution)/shard_map/all_to_all | solution.py:510
  101.5 2.0 %down.3 = f32[4,32,256]{2,1,0:T(8,128)S(1)} custom-call(s32[16]{0:T(128)S(1)} %get-tuple-element.48.first_ref, f32[16,128]{1,0:T(8,128)S(1)} %get-tuple-element.49.range_ref, bf16[128,384]{1,0:T(8,128)(2,1)S(1)} %get-tuple-element.50.pick_ref, bf16[8,208,128]{2,1,0:T(8,128)(2,1)S(1)} %all-to-all-done.6.x_ref, bf16[10,192,512]{2,1,0:T(8,128)(2,1)S(1)} %copy-done.5), custom_call_target="tpu_custom_call" | custom-call | tf_op jit(solution)/shard_map/down/pallas_call | solution.py:463
  103.5 7.0 %all_to_all.41.x_ref = f32[4,32,256]{2,1,0:T(8,128)S(1)} all-to-all(f32[4,32,256]{2,1,0:T(8,128)S(1)} %get-tuple-element.56), channel_id=1, replica_groups=mesh['seq'=8,'exp'=4] {'exp'}, dimensions={0} | all-to-all | bytes 262144 | tf_op jit(solution)/shard_map/all_to_all | solution.py:510
  110.5 0.8 finish.1
  (5 shorter events, 0.0 us)
Async XLA Ops:
  2.6 8.9 %copy-start.4 = (s32[8]{0:T(128)S(1)}, s32[8]{0:T(128)}, u32[]{:S(2)}) copy-start(s32[8]{0:T(128)} %len_ref.1) | copy-start | bytes 100
  37.3 10.4 %all-to-all-start.3 = ((bf16[8,4,1536]{2,1,0:T(4,128)(2,1)}), bf16[8,4,1536]{2,1,0:T(4,128)(2,1)S(1)}, u32[]{:S(2)}, u32[]{:S(2)}) async-start(bf16[8,4,1536]{2,1,0:T(4,128)(2,1)} %join.1), calls=%async_computation.3 | async-start | bytes 196608 | tf_op jit(solution)/shard_map/all_to_all | solution.py:510
  40.7 7.1 %copy-start = (bf16[1536,192]{0,1:T(8,128)(2,1)S(1)}, bf16[1536,192]{0,1:T(8,128)(2,1)}, u32[]{:S(2)}) copy-start(bf16[1536,192]{0,1:T(8,128)(2,1)} %param.21) | copy-start | bytes 1769476
  40.7 7.1 %copy-start.1 = (bf16[4,8,192]{2,1,0:T(8,128)(2,1)S(1)}, bf16[4,8,192]{2,1,0:T(8,128)(2,1)}, u32[]{:S(2)}) copy-start(bf16[4,8,192]{2,1,0:T(8,128)(2,1)} %residual_ref.1) | copy-start | bytes 36868
  40.7 7.0 %copy-start.2 = (s32[4,8,8]{2,1,0:T(8,128)S(1)}, s32[4,8,8]{2,1,0:T(8,128)}, u32[]{:S(2)}) copy-start(s32[4,8,8]{2,1,0:T(8,128)} %routes_ref.1) | copy-start | bytes 3076
  40.7 7.0 %copy-start.3 = (f32[192]{0:T(256)S(1)}, f32[192]{0:T(256)}, u32[]{:S(2)}) copy-start(f32[192]{0:T(256)} %param.22) | copy-start | bytes 2308
  40.7 15.6 %copy-start.6 = (bf16[192,40]{0,1:T(8,128)(2,1)S(1)}, bf16[192,40]{0,1:T(8,128)(2,1)}, u32[]{:S(2)}) copy-start(bf16[192,40]{0,1:T(8,128)(2,1)} %param.23) | copy-start | bytes 46084
  48.8 52.7 %copy-start.5 = (bf16[10,192,512]{2,1,0:T(8,128)(2,1)S(1)}, bf16[10,192,512]{2,1,0:T(8,128)(2,1)}, u32[]{:S(2)}) copy-start(bf16[10,192,512]{2,1,0:T(8,128)(2,1)} %w_ref.1) | copy-start | bytes 5898244
  48.8 7.5 %all-to-all-start.4 = ((bf16[4,32,256]{2,1,0:T(8,128)(2,1)}), bf16[4,32,256]{2,1,0:T(8,128)(2,1)S(1)}, u32[]{:S(2)}, u32[]{:S(2)}) async-start(bf16[4,32,256]{2,1,0:T(8,128)(2,1)} %get-tuple-element.45), calls=%async_computation.4 | async-start | bytes 131072 | tf_op jit(solution)/shard_map/all_to_all | solution.py:510
  86.6 14.9 %all-to-all-start.6 = ((bf16[8,208,128]{2,1,0:T(8,128)(2,1)}), bf16[8,208,128]{2,1,0:T(8,128)(2,1)S(1)}, u32[]{:S(2)}, u32[]{:S(2)}) async-start(bf16[8,208,128]{2,1,0:T(8,128)(2,1)} %inner.3), calls=%async_computation.6 | async-start | bytes 851968 | tf_op jit(solution)/shard_map/all_to_all | solution.py:510
where the time goes:
time: 112 us; the launch traced here: 111 us
  blocking collectives  46.6 us (42%)
  Pallas kernels  20.3 us (18%)
  waiting for transfers between devices  17 us (15%)
  local copies, waits for them, and re-layouts  16.4 us (15%)
  starting transfers between devices  10.2 us (9%)
    all_to_all x3, blocking collectives, swap(): return lax.all_to_all(x, axis, split_axis=0, concat_axis=0, tiled=True)  46.6 us
    all_to_all x3, waiting for transfers between devices, swap(): return lax.all_to_all(x, axis, split_axis=0, concat_axis=0, tiled=True)  17 us
    unnamed x17, local copies, waits for them, and re-layouts  10.7 us
    all_to_all x3, starting transfers between devices, swap(): return lax.all_to_all(x, axis, split_axis=0, concat_axis=0, tiled=True)  10.2 us
    pallas_call x1, Pallas kernels, attend(): pl.pallas_call(functools.partial(attend_kernel, steps, pages, page_rows),...  10 us
    optimization_barrier x1, local copies, waits for them, and re-layouts, local(): w_gate_up, attn = lax.optimization_barrier((w_gate_up, attn))  4.84 us
    pallas_call x1, Pallas kernels, gate_up(): pl.pallas_call(functools.partial(gate_up_kernel, features, local, turn),...  4.3 us
  transfers between devices with their start and end apart: 3, of which 3 were waited for; matrix products, arithmetic and copies ran while one was open for 4% of the time, Pallas kernels for 0%

commit v1 on v0

--- a/solution.py
+++ b/solution.py
@@ -62,99 +62,150 @@
     return pltpu.CompilerParams(vmem_limit_bytes=VMEM_LIMIT)
 
 
-def attend_kernel(steps, pages, page_rows, table_ref, len_ref, seq_ref, q_ref, fresh_ref, *refs):
-    page_refs, out_ref = refs[:pages], refs[pages]
-    request = pl.program_id(0)
-    q = q_ref[0].astype(F32)
-    low = iota((steps, LANES), 1) < HEAD_SIZE
-    by_group = []
-    for g in range(GROUP):
-        tiles = []
-        for j in range(KV_WIDTH // LANES):
-            first = tile_of(q, (6 * j + g) // 2)
-            second = tile_of(q, (6 * j + 3 + g) // 2)
-            if g % 2 == 0:
-                tiles.append(jnp.where(low, first, second))
-            else:
-                tiles.append(swap_halves(jnp.where(low, second, first)))
-        by_group.append(jnp.concatenate(tiles, axis=1))
+def attend_kernel(
+    classes, table_ref, len_ref, seq_ref, q_ref, fresh_ref, cache_ref, out_ref,
+    page_ref, split_ref, query_ref, new_ref, sems,
+):
+    steps, requests, _ = q_ref.shape
+    page_rows = cache_ref.shape[1]
+    pages = table_ref.shape[1]
+    span = pages * page_rows
+    first = seq_ref[0] * span
+
+    def copy(r, page):
+        at = r * pages + page
+        return pltpu.make_async_copy(cache_ref.at[table_ref[r, page]], page_ref.at[at], sems.at[at])
+
+    def needed(r, low):
+        return len_ref[r] - first > low * page_rows
+
+    bounds = list(zip((0,) + classes[:-1], classes))
+
+    def start(r, carry):
+        for low, high in bounds:
+
+            @pl.when(needed(r, low))
+            def _():
+                for page in range(low, high):
+                    copy(r, page).start()
+
+        return carry
+
+    lax.fori_loop(0, requests, start, 0)
+
+    low = iota((requests, LANES), 1) < HEAD_SIZE
+    for t in range(steps):
+        q = q_ref[t].astype(F32)
+        for g in range(GROUP):
+            for j in range(KV_WIDTH // LANES):
+                one = tile_of(q, (6 * j + g) // 2)
+                two = tile_of(q, (6 * j + 3 + g) // 2)
+                if g % 2 == 0:
+                    tile = jnp.where(low, one, two)
+                else:
+                    tile = swap_halves(jnp.where(low, two, one))
+                query_ref[t * GROUP + g, :, j * LANES : (j + 1) * LANES] = tile
+        new_ref[t] = fresh_ref[t].reshape(2 * requests, KV_WIDTH).astype(F32)
+
     rows = steps * GROUP * KEY_VALUE_HEADS
-    stacked = jnp.concatenate(
-        [
-            jnp.broadcast_to(by_group[g][t : t + 1], (KEY_VALUE_HEADS, KV_WIDTH))
-            for t in range(steps)
-            for g in range(GROUP)
-        ],
-        axis=0,
-    )
     own = iota((rows, KV_WIDTH), 1) // HEAD_SIZE == iota((rows, KV_WIDTH), 0) % KEY_VALUE_HEADS
-    spread = jnp.where(own, stacked, 0.0).astype(BF16)
-    keys = jnp.concatenate([ref[0, 0] for ref in page_refs], axis=0)
-    values = jnp.concatenate([ref[0, 1] for ref in page_refs], axis=0)
-    span = pages * page_rows
-    scores = dot_nt(spread, keys) * 0.125
-    live = seq_ref[0] * span + iota((rows, span), 1) < len_ref[request]
-    scores = jnp.where(live, scores, NEG_FILL)
-    fresh_keys, fresh_values = fresh_ref[0, 0], fresh_ref[0, 1]
-    fresh_rows = fresh_keys.shape[0]
-    fresh_scores = dot_nt(spread, fresh_keys) * 0.125
-    row_step = iota((rows, fresh_rows), 0) // (GROUP * KEY_VALUE_HEADS)
-    kept = jnp.logical_and(iota((rows, fresh_rows), 1) <= row_step, seq_ref[0] == 0)
-    fresh_scores = jnp.where(kept, fresh_scores, NEG_FILL)
-    largest = jnp.maximum(
-        jnp.max(scores, axis=1, keepdims=True), jnp.max(fresh_scores, axis=1, keepdims=True)
-    )
-    weights = jnp.where(live, jnp.exp(scores - largest), 0.0)
-    fresh_weights = jnp.where(kept, jnp.exp(fresh_scores - largest), 0.0)
-    total = jnp.sum(weights, axis=1, keepdims=True) + jnp.sum(fresh_weights, axis=1, keepdims=True)
-    acc = dot_nn(weights.astype(BF16), values) + dot_nn(fresh_weights.astype(BF16), fresh_values)
-    some = total > 0.0
-    safe = jnp.where(some, total, 1.0)
-    acc = jnp.where(own, acc * (1.0 / safe), 0.0)
-    acc = jnp.sum(acc.reshape(steps * GROUP, KEY_VALUE_HEADS, KV_WIDTH), axis=1)
-    level = jnp.where(some, largest + jnp.log(safe), NEG_FILL)
-    high = round16(level)
-    middle = round16(level - high)
-    rest = level - high - middle
     lane = iota((rows, LANES), 1)
     head = iota((rows, LANES), 0) % KEY_VALUE_HEADS
-    side = jnp.where(lane == head, high, 0.0)
-    side = jnp.where(lane == head + 8, middle, side)
-    side = jnp.where(lane == head + 16, rest, side)
-    side = jnp.sum(side.reshape(steps * GROUP, KEY_VALUE_HEADS, LANES), axis=1)
-    out_ref[0, :, 0:KV_WIDTH] = acc.astype(BF16)
-    out_ref[0, :, KV_WIDTH : KV_WIDTH + LANES] = side.astype(BF16)
-
-
-def attend(queries, new_key_value, pool, page_table, cache_len, seq_index):
-    steps, requests, width = queries.shape
+
+    def fresh_rows(r, which):
+        found = [new_ref[u, pl.ds(2 * r + which, 1), :] for u in range(steps)]
+        return jnp.concatenate(found + [jnp.zeros((16 - steps, KV_WIDTH), F32)], axis=0).astype(BF16)
+
+    def attend_pages(r, count):
+        spread = jnp.concatenate(
+            [
+                jnp.broadcast_to(query_ref[i, pl.ds(r, 1), :], (KEY_VALUE_HEADS, KV_WIDTH))
+                for i in range(steps * GROUP)
+            ],
+            axis=0,
+        )
+        spread = jnp.where(own, spread, 0.0).astype(BF16)
+        halves = ([], [])
+        for page in range(count):
+            copy(r, page).wait()
+            block = page_ref[r * pages + page].reshape(2 * page_rows, KV_WIDTH).astype(F32)
+            for j in range(KV_WIDTH // LANES):
+                split_ref[page, j] = tile_of(block, j)
+            for which in range(2):
+                tiles = [
+                    split_ref[page, j, pl.ds(which, page_rows, 2), :] for j in range(KV_WIDTH // LANES)
+                ]
+                halves[which].append(jnp.concatenate(tiles, axis=1).astype(BF16))
+        keys, values = jnp.concatenate(halves[0], axis=0), jnp.concatenate(halves[1], axis=0)
+        scores = dot_nt(spread, keys) * 0.125
+        live = first + iota((rows, count * page_rows), 1) < len_ref[r]
+        scores = jnp.where(live, scores, NEG_FILL)
+        fresh_scores = dot_nt(spread, fresh_rows(r, 0)) * 0.125
+        row_step = iota((rows, 16), 0) // (GROUP * KEY_VALUE_HEADS)
+        kept = jnp.logical_and(iota((rows, 16), 1) <= row_step, seq_ref[0] == 0)
+        fresh_scores = jnp.where(kept, fresh_scores, NEG_FILL)
+        largest = jnp.maximum(
+            jnp.max(scores, axis=1, keepdims=True), jnp.max(fresh_scores, axis=1, keepdims=True)
+        )
+        weights = jnp.where(live, jnp.exp(scores - largest), 0.0)
+        fresh_weights = jnp.where(kept, jnp.exp(fresh_scores - largest), 0.0)
+        total = jnp.sum(weights, axis=1, keepdims=True)
+        total = total + jnp.sum(fresh_weights, axis=1, keepdims=True)
+        acc = dot_nn(weights.astype(BF16), values)
+        acc = acc + dot_nn(fresh_weights.astype(BF16), fresh_rows(r, 1))
+        acc = jnp.where(own, acc * (1.0 / total), 0.0)
+        acc = jnp.sum(acc.reshape(steps * GROUP, KEY_VALUE_HEADS, KV_WIDTH), axis=1)
+        level = largest + jnp.log(total)
+        high = round16(level)
+        middle = round16(level - high)
+        side = jnp.where(lane == head, high, 0.0)
+        side = jnp.where(lane == head + 8, middle, side)
+        side = jnp.where(lane == head + 16, level - high - middle, side)
+        side = jnp.sum(side.reshape(steps * GROUP, KEY_VALUE_HEADS, LANES), axis=1)
+        out_ref[r, :, 0:KV_WIDTH] = acc.astype(BF16)
+        out_ref[r, :, KV_WIDTH : KV_WIDTH + LANES] = side.astype(BF16)
+
+    def one_request(r, carry):
+        for low, high in bounds:
+            enough = needed(r, low)
+            if high < pages:
+                enough = jnp.logical_and(enough, jnp.logical_not(needed(r, high)))
+
+            @pl.when(enough)
+            def _():
+                attend_pages(r, high)
+
+        @pl.when(jnp.logical_not(needed(r, 0)))
+        def _():
+            out_ref[r, :, 0:KV_WIDTH] = jnp.zeros((steps * GROUP, KV_WIDTH), BF16)
+            empty = jnp.where(iota((steps * GROUP, LANES), 1) < KEY_VALUE_HEADS, NEG_FILL, 0.0)
+            out_ref[r, :, KV_WIDTH : KV_WIDTH + LANES] = empty.astype(BF16)
+
+        return carry
+
+    lax.fori_loop(0, requests, one_request, 0)
+
+
+def attend(queries, new_key_value, cache, page_table, cache_len, seq_index):
+    steps, requests, _ = queries.shape
     pages = page_table.shape[1]
-    page_rows = pool.shape[2]
-    by_request = queries.transpose(1, 0, 2)
-    fresh = new_key_value.transpose(1, 2, 0, 3)
-    fresh = jnp.pad(fresh, ((0, 0), (0, 0), (0, 16 - steps), (0, 0)))
-
-    def page_map(page):
-        return lambda r, table, lens, seq: (table[r * pages + page], 0, 0, 0)
-
+    page_rows = cache.shape[1]
+    classes = tuple(c for c in (2, 4) if c < pages) + (pages,)
+    smem, vmem = pl.BlockSpec(memory_space=pltpu.SMEM), pl.BlockSpec(memory_space=pltpu.VMEM)
     return pl.pallas_call(
-        functools.partial(attend_kernel, steps, pages, page_rows),
-        grid_spec=pltpu.PrefetchScalarGridSpec(
-            num_scalar_prefetch=3,
-            grid=(requests,),
-            in_specs=[
-                pl.BlockSpec((1, steps, width), lambda r, *_: (r, 0, 0)),
-                pl.BlockSpec((1, 2, 16, KV_WIDTH), lambda r, *_: (r, 0, 0, 0)),
-            ]
-            + [pl.BlockSpec((1, 2, page_rows, KV_WIDTH), page_map(page)) for page in range(pages)],
-            out_specs=pl.BlockSpec(
-                (1, steps * GROUP, KV_WIDTH + LANES), lambda r, *_: (r, 0, 0)
-            ),
-        ),
+        functools.partial(attend_kernel, classes),
+        in_specs=[smem, smem, smem, vmem, vmem, pl.BlockSpec(memory_space=pl.ANY)],
         out_shape=jax.ShapeDtypeStruct((requests, steps * GROUP, KV_WIDTH + LANES), BF16),
+        scratch_shapes=[
+            pltpu.VMEM((requests * pages, page_rows, 2, KV_WIDTH), BF16),
+            pltpu.VMEM((pages, KV_WIDTH // LANES, 2 * page_rows, LANES), F32),
+            pltpu.VMEM((steps * GROUP, requests, KV_WIDTH), F32),
+            pltpu.VMEM((steps, 2 * requests, KV_WIDTH), F32),
+            pltpu.SemaphoreType.DMA((requests * pages,)),
+        ],
         compiler_params=params(),
         name="attend",
-    )(page_table.reshape(-1), cache_len, seq_index, by_request, fresh, *([pool] * pages))
+    )(page_table, cache_len, seq_index, queries, new_key_value, cache)
 
 
 def join_kernel(x_ref, out_ref):
@@ -227,12 +278,10 @@
     high = round16(squares)
     side = jnp.where(lane == 0, high, side)
     wide_ref[:, tile : tile + LANES] = jnp.where(lane == 1, squares - high, side)
-    made = wide_ref[...].astype(BF16)
-    for e in range(out_ref.shape[0]):
-        out_ref[e] = made
-
-
-def hidden_state(attn, residual, w_out, gain, routes, exp_count):
+    out_ref[...] = wide_ref[...].astype(BF16)
+
+
+def hidden_state(attn, residual, w_out, gain, routes):
     steps, requests, features = residual.shape
     tokens = steps * requests
     wide = side_place(features, SIDE_KEYS + EXPERTS)[0] + LANES
@@ -240,7 +289,7 @@
         hidden_kernel,
         out_shape=(
             jax.ShapeDtypeStruct((tokens, features), F32),
-            jax.ShapeDtypeStruct((exp_count, tokens, wide), BF16),
+            jax.ShapeDtypeStruct((tokens, wide), BF16),
         ),
         scratch_shapes=[pltpu.VMEM((tokens, wide), F32)],
         compiler_params=params(),
@@ -253,10 +302,13 @@
 
 
 def gate_up_kernel(
-    features, local, turn, where_ref, x_ref, w_ref, router_ref,
-    out_ref, pick_ref, range_ref, first_ref, most_ref, row_ref, acc_ref,
+    features, local, turn, sources, where_ref, w_ref, router_ref, *refs,
 ):
+    part_refs, refs = refs[:sources], refs[sources:]
+    out_ref, pick_ref, range_ref, first_ref, most_ref, x_ref, row_ref, acc_ref = refs
     total = x_ref.shape[0]
+    for e, part_ref in enumerate(part_refs):
+        x_ref[e * (total // sources) : (e + 1) * (total // sources)] = part_ref[...]
     rows = pick_ref.shape[1]
     blocks = out_ref.shape[0]
     share = rows // blocks
@@ -342,11 +394,12 @@
 
 def gate_up(exp_index, tokens, weights, w_router, rows, blocks, turn):
     local, _, features, width = weights.shape
-    total, wide = tokens.shape
+    sources, wide = len(tokens), tokens[0].shape[1]
+    total = sources * tokens[0].shape[0]
     smem, vmem = pl.BlockSpec(memory_space=pltpu.SMEM), pl.BlockSpec(memory_space=pltpu.VMEM)
     return pl.pallas_call(
-        functools.partial(gate_up_kernel, features, local, turn),
-        in_specs=[smem, vmem, vmem, vmem],
+        functools.partial(gate_up_kernel, features, local, turn, sources),
+        in_specs=[smem] + [vmem] * (2 + sources),
         out_specs=(vmem, vmem, vmem, smem, smem),
         out_shape=(
             jax.ShapeDtypeStruct((blocks, 2 * width // LANES * (rows // blocks) + 16, LANES), BF16),
@@ -355,10 +408,14 @@
             jax.ShapeDtypeStruct((16,), jnp.int32),
             jax.ShapeDtypeStruct((1,), jnp.int32),
         ),
-        scratch_shapes=[pltpu.VMEM((rows, wide), BF16), pltpu.VMEM((rows, 2 * width), F32)],
+        scratch_shapes=[
+            pltpu.VMEM((total, wide), BF16),
+            pltpu.VMEM((rows, wide), BF16),
+            pltpu.VMEM((rows, 2 * width), F32),
+        ],
         compiler_params=params(),
         name="gate_up",
-    )(exp_index, tokens, weights, w_router.T)
+    )(exp_index, weights, w_router.T, *tokens)
 
 
 def inner_kernel(x_ref, out_ref):
@@ -404,7 +461,8 @@
     )(parts)
 
 
-def down_kernel(features, local, first_ref, range_ref, pick_ref, x_ref, w_ref, out_ref, row_ref, made_ref):
+def down_kernel(features, local, first_ref, range_ref, pick_ref, x_ref, w_ref, *refs):
+    out_refs, (row_ref, made_ref) = refs[:-2], refs[-2:]
     blocks, height, _ = x_ref.shape
     total, rows = pick_ref.shape
     width = w_ref.shape[2]
@@ -446,13 +504,13 @@
     acc = dot_nn(pick, (made_ref[...] * column).astype(BF16))
     tile, offset = side_place(features, 2)
     pair = jnp.where(iota((LANES, total), 0) == 0, top, summed).T
-    count, tokens, _ = out_ref.shape
-    for e in range(count):
+    tokens = total // len(out_refs)
+    for e, out_ref in enumerate(out_refs):
         at = slice(e * tokens, (e + 1) * tokens)
-        out_ref[e] = acc[at]
+        out_ref[...] = acc[at]
         lane = iota((tokens, LANES), 1) - offset
         side = jnp.where(lane == 0, pair[at, 0:1], acc[at, tile : tile + LANES])
-        out_ref[e, :, tile : tile + LANES] = jnp.where(lane == 1, pair[at, 1:2], side)
+        out_ref[:, tile : tile + LANES] = jnp.where(lane == 1, pair[at, 1:2], side)
 
 
 def down(first, ranges, pick, parts, weights, exp_count):
@@ -463,18 +521,18 @@
     return pl.pallas_call(
         functools.partial(down_kernel, features, local),
         in_specs=[smem] + [vmem] * 4,
-        out_shape=jax.ShapeDtypeStruct((exp_count, total // exp_count, wide), F32),
+        out_shape=(jax.ShapeDtypeStruct((total // exp_count, wide), F32),) * exp_count,
         scratch_shapes=[pltpu.VMEM((rows, width), BF16), pltpu.VMEM((rows, wide), F32)],
         compiler_params=params(),
         name="down",
     )(first, ranges, pick, parts, weights)
 
 
-def finish_kernel(x_ref, hidden_ref, out_ref):
-    owners = x_ref.shape[0]
+def finish_kernel(hidden_ref, *refs):
+    part_refs, out_ref = refs[:-1], refs[-1]
     features = hidden_ref.shape[1]
     tile, offset = side_place(features, 2)
-    sides = [x_ref[e, :, tile : tile + LANES] for e in range(owners)]
+    sides = [x_ref[:, tile : tile + LANES] for x_ref in part_refs]
     tops = [side[:, offset : offset + 1] for side in sides]
     top = functools.reduce(jnp.maximum, tops)
     scales = [jnp.exp(one - top) for one in tops]
@@ -482,7 +540,7 @@
         jnp.add, [s * side[:, offset + 1 : offset + 2] for s, side in zip(scales, sides)]
     )
     acc = functools.reduce(
-        jnp.add, [s * x_ref[e, :, 0:features] for e, s in enumerate(scales)]
+        jnp.add, [s * x_ref[:, 0:features] for x_ref, s in zip(part_refs, scales)]
     )
     out = hidden_ref[...] + acc * (1.0 / total)
     out_ref[...] = out.reshape(out_ref.shape).astype(BF16)
@@ -494,7 +552,7 @@
         out_shape=jax.ShapeDtypeStruct(shape, BF16),
         compiler_params=params(),
         name="finish",
-    )(parts, hidden)
+    )(hidden, *parts)
 
 
 def join_rounds(features, one, other):
@@ -504,6 +562,11 @@
     scales = [jnp.exp(part[..., at : at + 1] - top) for part in (one, other)]
     joined = one * scales[0] + other * scales[1]
     return jnp.where(jnp.arange(one.shape[-1]) == at, top, joined)
+
+
+def send(x, axis, distance):
+    count = lax.axis_size(axis)
+    return lax.ppermute(x, axis, [(i, (i + distance) % count) for i in range(count)])
 
 
 def swap(x, axis):
@@ -532,7 +595,7 @@
     tokens = steps * requests
     features = w_out.shape[1]
     page_rows = key_value_cache.shape[2]
-    pool = key_value_cache.reshape(-1, page_rows, 2, KV_WIDTH).transpose(0, 2, 1, 3)
+    pool = key_value_cache.reshape(-1, page_rows, 2, KV_WIDTH)
 
     shares = attend(queries, new_key_value, pool, page_table, cache_len, seq_index)
     shares = swap(shares.reshape(seq_count, -1, KV_WIDTH + LANES), "seq")
@@ -541,8 +604,8 @@
     attn = swap(attn, "seq")
     gate_up_weights = w_gate_up.transpose(0, 2, 1, 3)
     gate_up_weights, attn = lax.optimization_barrier((gate_up_weights, attn))
-    hidden, outgoing = hidden_state(attn, residual, w_out, norm_gain, routes, exp_count)
-    incoming = swap(outgoing, "exp").reshape(exp_count * tokens, -1)
+    hidden, outgoing = hidden_state(attn, residual, w_out, norm_gain, routes)
+    incoming = [outgoing] + [send(outgoing, "exp", k) for k in range(1, exp_count)]
     rows = -(-ROUND_ROWS // (16 * seq_count)) * 16 * seq_count
 
     def one_round(turn):
@@ -557,11 +620,14 @@
     for turn in range(1, -(-pairs // rows)):
         made = lax.cond(
             most[0] > turn * rows,
-            lambda made: join_rounds(features, made, one_round(turn)[0]),
+            lambda made: tuple(
+                join_rounds(features, *both) for both in zip(made, one_round(turn)[0])
+            ),
             lambda made: made,
             made,
         )
-    return finish(swap(made, "exp"), hidden, (steps, requests, features))
+    made = [made[0]] + [send(made[k], "exp", -k) for k in range(1, exp_count)]
+    return finish(made, hidden, (steps, requests, features))
 
 
 def solution(mesh):

time: 112 us -> 98.1 us (0.88)
  blocking collectives: 46.6 us -> 36.5 us
  local copies, waits for them, and re-layouts: 16.4 us -> 7.97 us
  starting transfers between devices: 10.2 us -> 14.9 us
    all_to_all x3 -> x2, blocking collectives: 46.6 us -> 36.5 us  [swap(): return lax.all_to_all(x, axis, split_axis=0, concat_axis=0, tiled=True)]
    ppermute x0 -> x6, starting transfers between devices: none -> 8.07 us  [send(): lax.ppermute(x, axis, [(i, (i + distance) % count) for i in range(count)])]
    unnamed x17 -> x20, local copies, waits for them, and re-layouts: 10.7 us -> 3.11 us
    ppermute x0 -> x6, waiting for transfers between devices: none -> 4.62 us  [send(): lax.ppermute(x, axis, [(i, (i + distance) % count) for i in range(count)])]
    all_to_all x3 -> x2, waiting for transfers between devices: 17 us -> 13.5 us  [swap(): return lax.all_to_all(x, axis, split_axis=0, concat_axis=0, tiled=True)]
    all_to_all x3 -> x2, starting transfers between devices: 10.2 us -> 6.82 us  [swap(): return lax.all_to_all(x, axis, split_axis=0, concat_axis=0, tiled=True)]
  transfers between devices with their start and end apart: 3 -> 8, of which waited for: 3 -> 6; matrix products, arithmetic and copies ran while one was open for 4% -> 5% of each run, Pallas kernels for 0% -> 0%
where the time goes in v1:
time: 98.1 us; the launch traced here: 97.8 us
  blocking collectives  36.5 us (37%)
  Pallas kernels  19.6 us (20%)
  waiting for transfers between devices  18.1 us (18%)
  starting transfers between devices  14.9 us (15%)
  local copies, waits for them, and re-layouts  7.97 us (8%)
    all_to_all x2, blocking collectives, swap(): return lax.all_to_all(x, axis, split_axis=0, concat_axis=0, tiled=True)  36.5 us
    all_to_all x2, waiting for transfers between devices, swap(): return lax.all_to_all(x, axis, split_axis=0, concat_axis=0, tiled=True)  13.5 us
    pallas_call x1, Pallas kernels, attend(): pl.pallas_call(functools.partial(attend_kernel, classes), in_specs=[smem,...  9.87 us
    ppermute x6, starting transfers between devices, send(): lax.ppermute(x, axis, [(i, (i + distance) % count) for i in range(count)])  8.07 us
    all_to_all x2, starting transfers between devices, swap(): return lax.all_to_all(x, axis, split_axis=0, concat_axis=0, tiled=True)  6.82 us
    optimization_barrier x1, local copies, waits for them, and re-layouts, local(): w_gate_up, attn = lax.optimization_barrier((w_gate_up, attn))  4.86 us
    ppermute x6, waiting for transfers between devices, send(): lax.ppermute(x, axis, [(i, (i + distance) % count) for i in range(count)])  4.62 us
    pallas_call x1, Pallas kernels, gate_up(): pl.pallas_call(functools.partial(gate_up_kernel, features, local, turn, s...  4.47 us
  transfers between devices with their start and end apart: 8, of which 6 were waited for; matrix products, arithmetic and copies ran while one was open for 5% of the time, Pallas kernels for 0%

profile of v1, /device:TPU:0, one launch (start us, length us, event | category | flops | bytes accessed | tf_op | source)
XLA Modules:
  0.0 97.8 jit_solution(3140868287430512485)
XLA Ops:
  0.0 0.9 copy-done.1
  0.9 0.8 copy-done.2
  1.7 0.7 copy-done.5
  2.4 0.7 copy-done.7
  3.1 9.9 %attend.1 = bf16[8,12,640]{2,1,0:T(8,128)(2,1)S(1)} custom-call(s32[8,8]{1,0:T(8,128)S(1)} %copy-done.5, s32[8]{0:T(128)S(1)} %copy-done.7, s32[1]{0:T(128)} %bitcast.1.seq_ref, bf16[4,8,1536]{2,1,0:T(8,128)(2,1)S(1)} %copy-done.1, bf16[4,8,2,512]{3,2,1,0:T(2,128)(2,1)S(1)} %copy-done.2, bf16[64,64,2,512]{3,2,1,0:T(2,128)(2,1)} %bitcast.15), custom_call_target="tpu_custom_call" | custom-call | tf_op jit(solution)/shard_map/attend/pallas_call | solution.py:195
  13.0 10.8 %all_to_all.29.x_ref = bf16[8,12,640]{2,1,0:T(8,128)(2,1)S(1)} all-to-all(bf16[8,12,640]{2,1,0:T(8,128)(2,1)S(1)} %attend.1), channel_id=1, replica_groups=mesh['seq'=8,'exp'=4] {'seq'}, dimensions={0} | all-to-all | bytes 245760 | tf_op jit(solution)/shard_map/all_to_all | solution.py:573
  23.7 1.1 %join.1 = bf16[8,4,1536]{2,1,0:T(4,128)(2,1)} custom-call(bf16[8,12,640]{2,1,0:T(8,128)(2,1)S(1)} %all_to_all.29.x_ref), custom_call_target="tpu_custom_call" | custom-call | tf_op jit(solution)/shard_map/join/pallas_call | solution.py:245
  24.8 3.4 %all-to-all-start.3 = ((bf16[8,4,1536]{2,1,0:T(4,128)(2,1)}), bf16[8,4,1536]{2,1,0:T(4,128)(2,1)S(1)}, u32[]{:S(2)}, u32[]{:S(2)}) async-start(bf16[8,4,1536]{2,1,0:T(4,128)(2,1)} %join.1), calls=%async_computation.3 | async-start | bytes 196608 | tf_op jit(solution)/shard_map/all_to_all | solution.py:573
  28.2 0.0 copy-start
  28.2 0.0 copy-start.3
  28.2 0.0 copy-start.4
  28.3 4.9 %copy.16 = bf16[10,192,2,512]{3,1,2,0:T(8,128)(2,1)} copy(bf16[10,192,2,512]{3,2,1,0:T(2,128)(2,1)} %param.24) | data formatting | bytes 7864320 | tf_op jit(solution)/shard_map/optimization_barrier | solution.py:603
  33.1 2.1 %all-to-all-done.3.attn_ref = bf16[8,4,1536]{2,1,0:T(4,128)(2,1)S(1)} async-done(((bf16[8,4,1536]{2,1,0:T(4,128)(2,1)}), bf16[8,4,1536]{2,1,0:T(4,128)(2,1)S(1)}, u32[]{:S(2)}, u32[]{:S(2)}) %all-to-all-start.3) | async-done | bytes 98336 | tf_op jit(solution)/shard_map/all_to_all | solution.py:573
  35.3 0.5 hidden.1
  35.7 0.0 copy-start.8
  35.8 0.1 collective-permute-start
  35.8 4.1 %collective-permute-start.1 = (bf16[32,256]{1,0:T(8,128)(2,1)S(1)}, bf16[32,256]{1,0:T(8,128)(2,1)S(1)}, u32[]{:S(2)}, u32[]{:S(2)}) collective-permute-start(bf16[32,256]{1,0:T(8,128)(2,1)S(1)} %get-tuple-element.81.refs_0_), channel_id=1, source_target_pairs={{0,2},{1,3},{2,0},{3,1},{4,6},{5,7},{6,4},{7,5},{8,10},{9,11},{10,... | collective-permute-start | bytes 49160 | tf_op jit(solution)/shard_map/ppermute | solution.py:569
  40.0 1.4 %collective-permute-start.2 = (bf16[32,256]{1,0:T(8,128)(2,1)S(1)}, bf16[32,256]{1,0:T(8,128)(2,1)S(1)}, u32[]{:S(2)}, u32[]{:S(2)}) collective-permute-start(bf16[32,256]{1,0:T(8,128)(2,1)S(1)} %get-tuple-element.81.refs_0_), channel_id=1, source_target_pairs={{0,3},{1,0},{2,1},{3,2},{4,7},{5,4},{6,5},{7,6},{8,11},{9,8},{10,9... | collective-permute-start | bytes 49160 | tf_op jit(solution)/shard_map/ppermute | solution.py:569
  41.3 0.3 collective-permute-done.1.refs_2_
  41.7 1.1 %collective-permute-done.2.refs_3_ = bf16[32,256]{1,0:T(8,128)(2,1)S(1)} collective-permute-done((bf16[32,256]{1,0:T(8,128)(2,1)S(1)}, bf16[32,256]{1,0:T(8,128)(2,1)S(1)}, u32[]{:S(2)}, u32[]{:S(2)}) %collective-permute-start.2) | collective-permute-done | bytes 16416 | tf_op jit(solution)/shard_map/ppermute | solution.py:569
  42.8 4.5 %gate_up.3 = (bf16[8,400,128]{2,1,0:T(8,128)(2,1)S(1)}, bf16[128,384]{1,0:T(8,128)(2,1)S(1)}, f32[16,128]{1,0:T(8,128)S(1)}, s32[16]{0:T(128)S(1)}, s32[1]{0:T(128)}) custom-call(s32[1]{0:T(128)} %bitcast.6.where_ref, bf16[10,2,192,512]{3,2,1,0:T(8,128)(2,1)} %bitcast.13, bf16[40,192]{1,0:T(8,128)(2,1)S(1)} %bitcast.16, ...), custom_call_target="tpu_custom_call" | custom-call | tf_op jit(solution)/shard_map/gate_up/pallas_call | solution.py:400
  47.3 25.7 %all_to_all.30.x_ref = bf16[8,400,128]{2,1,0:T(8,128)(2,1)S(1)} all-to-all(bf16[8,400,128]{2,1,0:T(8,128)(2,1)S(1)} %get-tuple-element.86), channel_id=1, replica_groups=mesh['seq'=8,'exp'=4] {'seq'}, dimensions={0} | all-to-all | bytes 1638400 | tf_op jit(solution)/shard_map/all_to_all | solution.py:573
  73.0 1.0 inner.3
  74.0 3.5 %all-to-all-start.5 = ((bf16[8,208,128]{2,1,0:T(8,128)(2,1)}), bf16[8,208,128]{2,1,0:T(8,128)(2,1)S(1)}, u32[]{:S(2)}, u32[]{:S(2)}) async-start(bf16[8,208,128]{2,1,0:T(8,128)(2,1)} %inner.3), calls=%async_computation.5 | async-start | bytes 851968 | tf_op jit(solution)/shard_map/all_to_all | solution.py:573
  78.0 11.3 %all-to-all-done.5.x_ref = bf16[8,208,128]{2,1,0:T(8,128)(2,1)S(1)} async-done(((bf16[8,208,128]{2,1,0:T(8,128)(2,1)}), bf16[8,208,128]{2,1,0:T(8,128)(2,1)S(1)}, u32[]{:S(2)}, u32[]{:S(2)}) %all-to-all-start.5) | async-done | bytes 426016 | tf_op jit(solution)/shard_map/all_to_all | solution.py:573
  89.3 2.0 %down.3 = (f32[32,256]{1,0:T(8,128)S(1)}, f32[32,256]{1,0:T(8,128)S(1)}, f32[32,256]{1,0:T(8,128)S(1)}, f32[32,256]{1,0:T(8,128)S(1)}) custom-call(s32[16]{0:T(128)S(1)} %get-tuple-element.83.first_ref, f32[16,128]{1,0:T(8,128)S(1)} %get-tuple-element.84.range_ref, bf16[128,384]{1,0:T(8,128)(2,1)S(1)} %get-tuple-element.85.pick_ref, ...), custom_call_target="tpu_custom_call" | custom-call | tf_op jit(solution)/shard_map/down/pallas_call | solution.py:521
  91.4 0.7 collective-permute-start.3
  92.0 1.6 %collective-permute-start.4 = (f32[32,256]{1,0:T(8,128)S(1)}, f32[32,256]{1,0:T(8,128)S(1)}, u32[]{:S(2)}, u32[]{:S(2)}) collective-permute-start(f32[32,256]{1,0:T(8,128)S(1)} %get-tuple-element.93), channel_id=1, source_target_pairs={{0,2},{1,3},{2,0},{3,1},{4,6},{5,7},{6,4},{7,5},{8,10},{9,11},{10,... | collective-permute-start | bytes 98312 | tf_op jit(solution)/shard_map/ppermute | solution.py:569
  93.7 0.2 collective-permute-start.5
  93.8 2.2 %collective-permute-done.4.refs_2_ = f32[32,256]{1,0:T(8,128)S(1)} collective-permute-done((f32[32,256]{1,0:T(8,128)S(1)}, f32[32,256]{1,0:T(8,128)S(1)}, u32[]{:S(2)}, u32[]{:S(2)}) %collective-permute-start.4) | collective-permute-done | bytes 32800 | tf_op jit(solution)/shard_map/ppermute | solution.py:569
  96.0 1.0 %collective-permute-done.5.refs_3_ = f32[32,256]{1,0:T(8,128)S(1)} collective-permute-done((f32[32,256]{1,0:T(8,128)S(1)}, f32[32,256]{1,0:T(8,128)S(1)}, u32[]{:S(2)}, u32[]{:S(2)}) %collective-permute-start.5) | collective-permute-done | bytes 32800 | tf_op jit(solution)/shard_map/ppermute | solution.py:569
  97.0 0.8 finish.1
  (15 shorter events, 0.0 us)
Async XLA Ops:
  0.0 0.9 copy-start.1
  0.9 0.8 copy-start.2
  1.7 0.7 copy-start.5
  2.4 0.7 copy-start.7
  24.8 10.4 %all-to-all-start.3 = ((bf16[8,4,1536]{2,1,0:T(4,128)(2,1)}), bf16[8,4,1536]{2,1,0:T(4,128)(2,1)S(1)}, u32[]{:S(2)}, u32[]{:S(2)}) async-start(bf16[8,4,1536]{2,1,0:T(4,128)(2,1)} %join.1), calls=%async_computation.3 | async-start | bytes 196608 | tf_op jit(solution)/shard_map/all_to_all | solution.py:573
  28.2 7.1 %copy-start = (bf16[1536,192]{0,1:T(8,128)(2,1)S(1)}, bf16[1536,192]{0,1:T(8,128)(2,1)}, u32[]{:S(2)}) copy-start(bf16[1536,192]{0,1:T(8,128)(2,1)} %param.21) | copy-start | bytes 1769476
  28.2 7.1 %copy-start.3 = (bf16[4,8,192]{2,1,0:T(8,128)(2,1)S(1)}, bf16[4,8,192]{2,1,0:T(8,128)(2,1)}, u32[]{:S(2)}) copy-start(bf16[4,8,192]{2,1,0:T(8,128)(2,1)} %residual_ref.1) | copy-start | bytes 36868
  28.2 7.0 %copy-start.4 = (s32[4,8,8]{2,1,0:T(8,128)S(1)}, s32[4,8,8]{2,1,0:T(8,128)}, u32[]{:S(2)}) copy-start(s32[4,8,8]{2,1,0:T(8,128)} %routes_ref.1) | copy-start | bytes 3076
  28.2 7.0 %copy-start.6 = (f32[192]{0:T(256)S(1)}, f32[192]{0:T(256)}, u32[]{:S(2)}) copy-start(f32[192]{0:T(256)} %param.22) | copy-start | bytes 2308
  28.2 14.5 %copy-start.9 = (bf16[192,40]{0,1:T(8,128)(2,1)S(1)}, bf16[192,40]{0,1:T(8,128)(2,1)}, u32[]{:S(2)}) copy-start(bf16[192,40]{0,1:T(8,128)(2,1)} %param.23) | copy-start | bytes 46084
  35.7 53.6 %copy-start.8 = (bf16[10,192,512]{2,1,0:T(8,128)(2,1)S(1)}, bf16[10,192,512]{2,1,0:T(8,128)(2,1)}, u32[]{:S(2)}) copy-start(bf16[10,192,512]{2,1,0:T(8,128)(2,1)} %w_ref.1) | copy-start | bytes 5898244
  35.8 5.6 %collective-permute-start = (bf16[32,256]{1,0:T(8,128)(2,1)S(1)}, bf16[32,256]{1,0:T(8,128)(2,1)S(1)}, u32[]{:S(2)}, u32[]{:S(2)}) collective-permute-start(bf16[32,256]{1,0:T(8,128)(2,1)S(1)} %get-tuple-element.81.refs_0_), channel_id=1, source_target_pairs={{0,1},{1,2},{2,3},{3,0},{4,5},{5,6},{6,7},{7,4},{8,9},{9,10},{10,1... | collective-permute-start | bytes 49160 | tf_op jit(solution)/shard_map/ppermute | solution.py:569
  35.8 5.9 %collective-permute-start.1 = (bf16[32,256]{1,0:T(8,128)(2,1)S(1)}, bf16[32,256]{1,0:T(8,128)(2,1)S(1)}, u32[]{:S(2)}, u32[]{:S(2)}) collective-permute-start(bf16[32,256]{1,0:T(8,128)(2,1)S(1)} %get-tuple-element.81.refs_0_), channel_id=1, source_target_pairs={{0,2},{1,3},{2,0},{3,1},{4,6},{5,7},{6,4},{7,5},{8,10},{9,11},{10,... | collective-permute-start | bytes 49160 | tf_op jit(solution)/shard_map/ppermute | solution.py:569
  40.0 2.8 %collective-permute-start.2 = (bf16[32,256]{1,0:T(8,128)(2,1)S(1)}, bf16[32,256]{1,0:T(8,128)(2,1)S(1)}, u32[]{:S(2)}, u32[]{:S(2)}) collective-permute-start(bf16[32,256]{1,0:T(8,128)(2,1)S(1)} %get-tuple-element.81.refs_0_), channel_id=1, source_target_pairs={{0,3},{1,0},{2,1},{3,2},{4,7},{5,4},{6,5},{7,6},{8,11},{9,8},{10,9... | collective-permute-start | bytes 49160 | tf_op jit(solution)/shard_map/ppermute | solution.py:569
  74.0 15.3 %all-to-all-start.5 = ((bf16[8,208,128]{2,1,0:T(8,128)(2,1)}), bf16[8,208,128]{2,1,0:T(8,128)(2,1)S(1)}, u32[]{:S(2)}, u32[]{:S(2)}) async-start(bf16[8,208,128]{2,1,0:T(8,128)(2,1)} %inner.3), calls=%async_computation.5 | async-start | bytes 851968 | tf_op jit(solution)/shard_map/all_to_all | solution.py:573
  91.4 2.5 %collective-permute-start.3 = (f32[32,256]{1,0:T(8,128)S(1)}, f32[32,256]{1,0:T(8,128)S(1)}, u32[]{:S(2)}, u32[]{:S(2)}) collective-permute-start(f32[32,256]{1,0:T(8,128)S(1)} %get-tuple-element.92), channel_id=1, source_target_pairs={{0,3},{1,0},{2,1},{3,2},{4,7},{5,4},{6,5},{7,6},{8,11},{9,8},{10,9... | collective-permute-start | bytes 98312 | tf_op jit(solution)/shard_map/ppermute | solution.py:569
  92.0 4.0 %collective-permute-start.4 = (f32[32,256]{1,0:T(8,128)S(1)}, f32[32,256]{1,0:T(8,128)S(1)}, u32[]{:S(2)}, u32[]{:S(2)}) collective-permute-start(f32[32,256]{1,0:T(8,128)S(1)} %get-tuple-element.93), channel_id=1, source_target_pairs={{0,2},{1,3},{2,0},{3,1},{4,6},{5,7},{6,4},{7,5},{8,10},{9,11},{10,... | collective-permute-start | bytes 98312 | tf_op jit(solution)/shard_map/ppermute | solution.py:569
  93.7 3.3 %collective-permute-start.5 = (f32[32,256]{1,0:T(8,128)S(1)}, f32[32,256]{1,0:T(8,128)S(1)}, u32[]{:S(2)}, u32[]{:S(2)}) collective-permute-start(f32[32,256]{1,0:T(8,128)S(1)} %get-tuple-element.94), channel_id=1, source_target_pairs={{0,1},{1,2},{2,3},{3,0},{4,5},{5,6},{6,7},{7,4},{8,9},{9,10},{10,1... | collective-permute-start | bytes 98312 | tf_op jit(solution)/shard_map/ppermute | solution.py:569

commit v2 on v1

--- a/solution.py
+++ b/solution.py
@@ -24,6 +24,7 @@
 F32 = jnp.float32
 BF16 = jnp.bfloat16
 VMEM_LIMIT = 48 * 1024 * 1024
+ATTEND_VMEM = 60 * 1024 * 1024
 
 
 def iota(shape, dimension):
@@ -63,14 +64,29 @@
 
 
 def attend_kernel(
-    classes, table_ref, len_ref, seq_ref, q_ref, fresh_ref, cache_ref, out_ref,
-    page_ref, split_ref, query_ref, new_ref, sems,
+    classes, table_ref, len_ref, seq_ref, q_hbm, fresh_hbm, cache_ref, out_ref,
+    page_ref, split_ref, q_ref, fresh_ref, query_ref, new_ref, order_ref, sems, small_sems,
 ):
     steps, requests, _ = q_ref.shape
     page_rows = cache_ref.shape[1]
     pages = table_ref.shape[1]
     span = pages * page_rows
     first = seq_ref[0] * span
+    small = [
+        pltpu.make_async_copy(q_hbm, q_ref, small_sems.at[0]),
+        pltpu.make_async_copy(fresh_hbm, fresh_ref, small_sems.at[1]),
+    ]
+    for one in small:
+        one.start()
+
+    held = [jnp.clip(len_ref[r] - first, 0, span) for r in range(requests)]
+    for r in range(requests):
+        ahead = jnp.int32(0)
+        for other in range(requests):
+            if other != r:
+                longer = held[other] >= held[r] if other < r else held[other] > held[r]
+                ahead = ahead + longer.astype(jnp.int32)
+        order_ref[ahead] = r
 
     def copy(r, page):
         at = r * pages + page
@@ -81,21 +97,25 @@
 
     bounds = list(zip((0,) + classes[:-1], classes))
 
-    def start(r, carry):
+    def start(pair, carry):
+        both = order_ref[2 * pair], order_ref[2 * pair + 1]
         for low, high in bounds:
 
-            @pl.when(needed(r, low))
+            @pl.when(needed(both[0], low))
             def _():
                 for page in range(low, high):
-                    copy(r, page).start()
+                    for r in both:
+                        copy(r, page).start()
 
         return carry
 
-    lax.fori_loop(0, requests, start, 0)
+    lax.fori_loop(0, requests // 2, start, 0)
+    for one in small:
+        one.wait()
 
     low = iota((requests, LANES), 1) < HEAD_SIZE
     for t in range(steps):
-        q = q_ref[t].astype(F32)
+        q = q_ref[t].astype(F32) * 0.125
         for g in range(GROUP):
             for j in range(KV_WIDTH // LANES):
                 one = tile_of(q, (6 * j + g) // 2)
@@ -111,12 +131,15 @@
     own = iota((rows, KV_WIDTH), 1) // HEAD_SIZE == iota((rows, KV_WIDTH), 0) % KEY_VALUE_HEADS
     lane = iota((rows, LANES), 1)
     head = iota((rows, LANES), 0) % KEY_VALUE_HEADS
+    row_step = iota((rows, 16), 0) // (GROUP * KEY_VALUE_HEADS)
+    kept = jnp.logical_and(iota((rows, 16), 1) <= row_step, seq_ref[0] == 0)
+    fresh_bias = jnp.where(kept, 0.0, NEG_FILL)
 
     def fresh_rows(r, which):
         found = [new_ref[u, pl.ds(2 * r + which, 1), :] for u in range(steps)]
         return jnp.concatenate(found + [jnp.zeros((16 - steps, KV_WIDTH), F32)], axis=0).astype(BF16)
 
-    def attend_pages(r, count):
+    def attend_pages(r, slot, count):
         spread = jnp.concatenate(
             [
                 jnp.broadcast_to(query_ref[i, pl.ds(r, 1), :], (KEY_VALUE_HEADS, KV_WIDTH))
@@ -127,63 +150,67 @@
         spread = jnp.where(own, spread, 0.0).astype(BF16)
         halves = ([], [])
         for page in range(count):
-            copy(r, page).wait()
             block = page_ref[r * pages + page].reshape(2 * page_rows, KV_WIDTH).astype(F32)
             for j in range(KV_WIDTH // LANES):
-                split_ref[page, j] = tile_of(block, j)
+                split_ref[slot, page, j] = tile_of(block, j)
             for which in range(2):
                 tiles = [
-                    split_ref[page, j, pl.ds(which, page_rows, 2), :] for j in range(KV_WIDTH // LANES)
+                    split_ref[slot, page, j, pl.ds(which, page_rows, 2), :]
+                    for j in range(KV_WIDTH // LANES)
                 ]
                 halves[which].append(jnp.concatenate(tiles, axis=1).astype(BF16))
         keys, values = jnp.concatenate(halves[0], axis=0), jnp.concatenate(halves[1], axis=0)
-        scores = dot_nt(spread, keys) * 0.125
-        live = first + iota((rows, count * page_rows), 1) < len_ref[r]
-        scores = jnp.where(live, scores, NEG_FILL)
-        fresh_scores = dot_nt(spread, fresh_rows(r, 0)) * 0.125
-        row_step = iota((rows, 16), 0) // (GROUP * KEY_VALUE_HEADS)
-        kept = jnp.logical_and(iota((rows, 16), 1) <= row_step, seq_ref[0] == 0)
-        fresh_scores = jnp.where(kept, fresh_scores, NEG_FILL)
+        size = count * page_rows
+        live = first + iota((1, size), 1) < len_ref[r]
+        scores = dot_nt(spread, keys) + jnp.where(live, 0.0, NEG_FILL)
+        fresh_scores = dot_nt(spread, fresh_rows(r, 0)) + fresh_bias
         largest = jnp.maximum(
             jnp.max(scores, axis=1, keepdims=True), jnp.max(fresh_scores, axis=1, keepdims=True)
         )
-        weights = jnp.where(live, jnp.exp(scores - largest), 0.0)
-        fresh_weights = jnp.where(kept, jnp.exp(fresh_scores - largest), 0.0)
+        weights = jnp.exp(scores - largest)
+        fresh_weights = jnp.exp(fresh_scores - largest)
         total = jnp.sum(weights, axis=1, keepdims=True)
         total = total + jnp.sum(fresh_weights, axis=1, keepdims=True)
         acc = dot_nn(weights.astype(BF16), values)
         acc = acc + dot_nn(fresh_weights.astype(BF16), fresh_rows(r, 1))
         acc = jnp.where(own, acc * (1.0 / total), 0.0)
         acc = jnp.sum(acc.reshape(steps * GROUP, KEY_VALUE_HEADS, KV_WIDTH), axis=1)
-        level = largest + jnp.log(total)
+        level = jnp.where(needed(r, 0), largest + jnp.log(total), NEG_FILL)
         high = round16(level)
         middle = round16(level - high)
         side = jnp.where(lane == head, high, 0.0)
         side = jnp.where(lane == head + 8, middle, side)
         side = jnp.where(lane == head + 16, level - high - middle, side)
         side = jnp.sum(side.reshape(steps * GROUP, KEY_VALUE_HEADS, LANES), axis=1)
-        out_ref[r, :, 0:KV_WIDTH] = acc.astype(BF16)
-        out_ref[r, :, KV_WIDTH : KV_WIDTH + LANES] = side.astype(BF16)
-
-    def one_request(r, carry):
+        return acc.astype(BF16), side.astype(BF16)
+
+    def one_pair(pair, carry):
+        both = order_ref[2 * pair], order_ref[2 * pair + 1]
         for low, high in bounds:
-            enough = needed(r, low)
+            enough = needed(both[0], low)
             if high < pages:
-                enough = jnp.logical_and(enough, jnp.logical_not(needed(r, high)))
+                enough = jnp.logical_and(enough, jnp.logical_not(needed(both[0], high)))
 
             @pl.when(enough)
             def _():
-                attend_pages(r, high)
-
-        @pl.when(jnp.logical_not(needed(r, 0)))
+                for page in range(high):
+                    for r in both:
+                        copy(r, page).wait()
+                made = [attend_pages(r, slot, high) for slot, r in enumerate(both)]
+                for r, (acc, side) in zip(both, made):
+                    out_ref[r, :, 0:KV_WIDTH] = acc
+                    out_ref[r, :, KV_WIDTH : KV_WIDTH + LANES] = side
+
+        @pl.when(jnp.logical_not(needed(both[0], 0)))
         def _():
-            out_ref[r, :, 0:KV_WIDTH] = jnp.zeros((steps * GROUP, KV_WIDTH), BF16)
             empty = jnp.where(iota((steps * GROUP, LANES), 1) < KEY_VALUE_HEADS, NEG_FILL, 0.0)
-            out_ref[r, :, KV_WIDTH : KV_WIDTH + LANES] = empty.astype(BF16)
+            for r in both:
+                out_ref[r, :, 0:KV_WIDTH] = jnp.zeros((steps * GROUP, KV_WIDTH), BF16)
+                out_ref[r, :, KV_WIDTH : KV_WIDTH + LANES] = empty.astype(BF16)
 
         return carry
 
-    lax.fori_loop(0, requests, one_request, 0)
+    lax.fori_loop(0, requests // 2, one_pair, 0)
 
 
 def attend(queries, new_key_value, cache, page_table, cache_len, seq_index):
@@ -191,19 +218,23 @@
     pages = page_table.shape[1]
     page_rows = cache.shape[1]
     classes = tuple(c for c in (2, 4) if c < pages) + (pages,)
-    smem, vmem = pl.BlockSpec(memory_space=pltpu.SMEM), pl.BlockSpec(memory_space=pltpu.VMEM)
+    smem, hbm = pl.BlockSpec(memory_space=pltpu.SMEM), pl.BlockSpec(memory_space=pl.ANY)
     return pl.pallas_call(
         functools.partial(attend_kernel, classes),
-        in_specs=[smem, smem, smem, vmem, vmem, pl.BlockSpec(memory_space=pl.ANY)],
+        in_specs=[smem] * 3 + [hbm] * 3,
         out_shape=jax.ShapeDtypeStruct((requests, steps * GROUP, KV_WIDTH + LANES), BF16),
         scratch_shapes=[
             pltpu.VMEM((requests * pages, page_rows, 2, KV_WIDTH), BF16),
-            pltpu.VMEM((pages, KV_WIDTH // LANES, 2 * page_rows, LANES), F32),
+            pltpu.VMEM((2, pages, KV_WIDTH // LANES, 2 * page_rows, LANES), F32),
+            pltpu.VMEM(queries.shape, BF16),
+            pltpu.VMEM(new_key_value.shape, BF16),
             pltpu.VMEM((steps * GROUP, requests, KV_WIDTH), F32),
             pltpu.VMEM((steps, 2 * requests, KV_WIDTH), F32),
+            pltpu.SMEM((requests,), jnp.int32),
             pltpu.SemaphoreType.DMA((requests * pages,)),
+            pltpu.SemaphoreType.DMA((2,)),
         ],
-        compiler_params=params(),
+        compiler_params=pltpu.CompilerParams(vmem_limit_bytes=ATTEND_VMEM),
         name="attend",
     )(page_table, cache_len, seq_index, queries, new_key_value, cache)
 

time: 98.1 us -> 96.5 us (0.984)
  local copies, waits for them, and re-layouts: 7.97 us -> 4.89 us
  Pallas kernels: 19.6 us -> 21 us
  starting transfers between devices: 14.9 us -> 13.6 us
    unnamed x20 -> x12, local copies, waits for them, and re-layouts: 3.11 us -> 0.04 us
    ppermute x6, starting transfers between devices: 8.07 us -> 6.42 us  [send(): lax.ppermute(x, axis, [(i, (i + distance) % count) for i in range(count)])]
    pallas_call x1, Pallas kernels: 9.87 us -> 11.2 us  [attend(): pl.pallas_call(functools.partial(attend_kernel, classes), in_specs=[smem]...]
where the time goes in v2:
time: 96.5 us; the launch traced here: 95.5 us
  blocking collectives  36.8 us (38%)
  Pallas kernels  21 us (22%)
  waiting for transfers between devices  18.5 us (19%)
  starting transfers between devices  13.6 us (14%)
  local copies, waits for them, and re-layouts  4.89 us (5%)
    all_to_all x2, blocking collectives, swap(): return lax.all_to_all(x, axis, split_axis=0, concat_axis=0, tiled=True)  36.8 us
    all_to_all x2, waiting for transfers between devices, swap(): return lax.all_to_all(x, axis, split_axis=0, concat_axis=0, tiled=True)  13.8 us
    pallas_call x1, Pallas kernels, attend(): pl.pallas_call(functools.partial(attend_kernel, classes), in_specs=[smem]...  11.2 us
    all_to_all x2, starting transfers between devices, swap(): return lax.all_to_all(x, axis, split_axis=0, concat_axis=0, tiled=True)  7.21 us
    ppermute x6, starting transfers between devices, send(): lax.ppermute(x, axis, [(i, (i + distance) % count) for i in range(count)])  6.42 us
    optimization_barrier x1, local copies, waits for them, and re-layouts, local(): w_gate_up, attn = lax.optimization_barrier((w_gate_up, attn))  4.86 us
    ppermute x6, waiting for transfers between devices, send(): lax.ppermute(x, axis, [(i, (i + distance) % count) for i in range(count)])  4.62 us
    pallas_call x1, Pallas kernels, gate_up(): pl.pallas_call(functools.partial(gate_up_kernel, features, local, turn, s...  4.5 us
  transfers between devices with their start and end apart: 8, of which 6 were waited for; matrix products, arithmetic and copies ran while one was open for 5% of the time, Pallas kernels for 0%

profile of v2, /device:TPU:0, one launch (start us, length us, event | category | flops | bytes accessed | tf_op | source)
XLA Modules:
  0.0 95.5 jit_solution(15600749416606463832)
XLA Ops:
  0.0 11.2 %attend.1 = bf16[8,12,640]{2,1,0:T(8,128)(2,1)} custom-call(s32[8,8]{1,0:T(8,128)} %table_ref.1, s32[8]{0:T(128)} %len_ref.1, s32[1]{0:T(128)} %bitcast.1.seq_ref, bf16[4,8,1536]{2,1,0:T(8,128)(2,1)} %q_hbm.1, bf16[4,8,2,512]{3,2,1,0:T(2,128)(2,1)} %fresh_hbm.1, bf16[64,64,2,512]{3,2,1,0:T(2,128)(2,1)} %bitcast.15), custom_call_target="tpu_custom_call" | custom-call | tf_op jit(solution)/shard_map/attend/pallas_call | solution.py:222
  11.2 11.1 %all_to_all.29.x_ref = bf16[8,12,640]{2,1,0:T(8,128)(2,1)S(1)} all-to-all(bf16[8,12,640]{2,1,0:T(8,128)(2,1)} %attend.1), channel_id=1, replica_groups=mesh['seq'=8,'exp'=4] {'seq'}, dimensions={0} | all-to-all | bytes 245760 | tf_op jit(solution)/shard_map/all_to_all | solution.py:604
  22.3 1.1 %join.1 = bf16[8,4,1536]{2,1,0:T(4,128)(2,1)} custom-call(bf16[8,12,640]{2,1,0:T(8,128)(2,1)S(1)} %all_to_all.29.x_ref), custom_call_target="tpu_custom_call" | custom-call | tf_op jit(solution)/shard_map/join/pallas_call | solution.py:276
  23.4 3.7 %all-to-all-start.3 = ((bf16[8,4,1536]{2,1,0:T(4,128)(2,1)}), bf16[8,4,1536]{2,1,0:T(4,128)(2,1)S(1)}, u32[]{:S(2)}, u32[]{:S(2)}) async-start(bf16[8,4,1536]{2,1,0:T(4,128)(2,1)} %join.1), calls=%async_computation.3 | async-start | bytes 196608 | tf_op jit(solution)/shard_map/all_to_all | solution.py:604
  27.2 0.0 copy-start.1
  27.2 0.0 copy-start.2
  27.2 0.0 copy-start.3
  27.2 0.0 copy-start.5
  27.2 4.9 %copy.16 = bf16[10,192,2,512]{3,1,2,0:T(8,128)(2,1)} copy(bf16[10,192,2,512]{3,2,1,0:T(2,128)(2,1)} %param.24) | data formatting | bytes 7864320 | tf_op jit(solution)/shard_map/optimization_barrier | solution.py:634
  32.1 2.5 %all-to-all-done.3.attn_ref = bf16[8,4,1536]{2,1,0:T(4,128)(2,1)S(1)} async-done(((bf16[8,4,1536]{2,1,0:T(4,128)(2,1)}), bf16[8,4,1536]{2,1,0:T(4,128)(2,1)S(1)}, u32[]{:S(2)}, u32[]{:S(2)}) %all-to-all-start.3) | async-done | bytes 98336 | tf_op jit(solution)/shard_map/all_to_all | solution.py:604
  34.6 0.0 copy-done
  34.6 0.5 hidden.1
  35.0 0.0 copy-start.4
  35.1 0.1 collective-permute-start
  35.1 2.5 %collective-permute-start.1 = (bf16[32,256]{1,0:T(8,128)(2,1)S(1)}, bf16[32,256]{1,0:T(8,128)(2,1)S(1)}, u32[]{:S(2)}, u32[]{:S(2)}) collective-permute-start(bf16[32,256]{1,0:T(8,128)(2,1)S(1)} %get-tuple-element.81.refs_0_), channel_id=1, source_target_pairs={{0,2},{1,3},{2,0},{3,1},{4,6},{5,7},{6,4},{7,5},{8,10},{9,11},{10,... | collective-permute-start | bytes 49160 | tf_op jit(solution)/shard_map/ppermute | solution.py:600
  37.7 1.4 %collective-permute-start.2 = (bf16[32,256]{1,0:T(8,128)(2,1)S(1)}, bf16[32,256]{1,0:T(8,128)(2,1)S(1)}, u32[]{:S(2)}, u32[]{:S(2)}) collective-permute-start(bf16[32,256]{1,0:T(8,128)(2,1)S(1)} %get-tuple-element.81.refs_0_), channel_id=1, source_target_pairs={{0,3},{1,0},{2,1},{3,2},{4,7},{5,4},{6,5},{7,6},{8,11},{9,8},{10,9... | collective-permute-start | bytes 49160 | tf_op jit(solution)/shard_map/ppermute | solution.py:600
  39.0 0.0 collective-permute-done.refs_1_
  39.0 0.3 collective-permute-done.1.refs_2_
  39.4 1.1 %collective-permute-done.2.refs_3_ = bf16[32,256]{1,0:T(8,128)(2,1)S(1)} collective-permute-done((bf16[32,256]{1,0:T(8,128)(2,1)S(1)}, bf16[32,256]{1,0:T(8,128)(2,1)S(1)}, u32[]{:S(2)}, u32[]{:S(2)}) %collective-permute-start.2) | collective-permute-done | bytes 16416 | tf_op jit(solution)/shard_map/ppermute | solution.py:600
  40.5 4.5 %gate_up.3 = (bf16[8,400,128]{2,1,0:T(8,128)(2,1)S(1)}, bf16[128,384]{1,0:T(8,128)(2,1)S(1)}, f32[16,128]{1,0:T(8,128)S(1)}, s32[16]{0:T(128)S(1)}, s32[1]{0:T(128)}) custom-call(s32[1]{0:T(128)} %bitcast.6.where_ref, bf16[10,2,192,512]{3,2,1,0:T(8,128)(2,1)} %bitcast.13, bf16[40,192]{1,0:T(8,128)(2,1)S(1)} %bitcast.16, ...), custom_call_target="tpu_custom_call" | custom-call | tf_op jit(solution)/shard_map/gate_up/pallas_call | solution.py:431
  45.0 25.7 %all_to_all.30.x_ref = bf16[8,400,128]{2,1,0:T(8,128)(2,1)S(1)} all-to-all(bf16[8,400,128]{2,1,0:T(8,128)(2,1)S(1)} %get-tuple-element.86), channel_id=1, replica_groups=mesh['seq'=8,'exp'=4] {'seq'}, dimensions={0} | all-to-all | bytes 1638400 | tf_op jit(solution)/shard_map/all_to_all | solution.py:604
  70.7 1.0 %inner.3 = bf16[8,208,128]{2,1,0:T(8,128)(2,1)} custom-call(bf16[8,400,128]{2,1,0:T(8,128)(2,1)S(1)} %all_to_all.30.x_ref), custom_call_target="tpu_custom_call" | custom-call | tf_op jit(solution)/shard_map/inner/pallas_call | solution.py:487
  71.7 3.5 %all-to-all-start.5 = ((bf16[8,208,128]{2,1,0:T(8,128)(2,1)}), bf16[8,208,128]{2,1,0:T(8,128)(2,1)S(1)}, u32[]{:S(2)}, u32[]{:S(2)}) async-start(bf16[8,208,128]{2,1,0:T(8,128)(2,1)} %inner.3), calls=%async_computation.5 | async-start | bytes 851968 | tf_op jit(solution)/shard_map/all_to_all | solution.py:604
  75.7 11.4 %all-to-all-done.5.x_ref = bf16[8,208,128]{2,1,0:T(8,128)(2,1)S(1)} async-done(((bf16[8,208,128]{2,1,0:T(8,128)(2,1)}), bf16[8,208,128]{2,1,0:T(8,128)(2,1)S(1)}, u32[]{:S(2)}, u32[]{:S(2)}) %all-to-all-start.5) | async-done | bytes 426016 | tf_op jit(solution)/shard_map/all_to_all | solution.py:604
  87.1 2.0 %down.3 = (f32[32,256]{1,0:T(8,128)S(1)}, f32[32,256]{1,0:T(8,128)S(1)}, f32[32,256]{1,0:T(8,128)S(1)}, f32[32,256]{1,0:T(8,128)S(1)}) custom-call(s32[16]{0:T(128)S(1)} %get-tuple-element.83.first_ref, f32[16,128]{1,0:T(8,128)S(1)} %get-tuple-element.84.range_ref, bf16[128,384]{1,0:T(8,128)(2,1)S(1)} %get-tuple-element.85.pick_ref, ...), custom_call_target="tpu_custom_call" | custom-call | tf_op jit(solution)/shard_map/down/pallas_call | solution.py:552
  89.1 0.6 collective-permute-start.3
  89.7 1.7 %collective-permute-start.4 = (f32[32,256]{1,0:T(8,128)S(1)}, f32[32,256]{1,0:T(8,128)S(1)}, u32[]{:S(2)}, u32[]{:S(2)}) collective-permute-start(f32[32,256]{1,0:T(8,128)S(1)} %get-tuple-element.93), channel_id=1, source_target_pairs={{0,2},{1,3},{2,0},{3,1},{4,6},{5,7},{6,4},{7,5},{8,10},{9,11},{10,... | collective-permute-start | bytes 98312 | tf_op jit(solution)/shard_map/ppermute | solution.py:600
  91.4 0.2 collective-permute-start.5
  91.5 0.0 collective-permute-done.3.refs_1_
  91.5 2.2 %collective-permute-done.4.refs_2_ = f32[32,256]{1,0:T(8,128)S(1)} collective-permute-done((f32[32,256]{1,0:T(8,128)S(1)}, f32[32,256]{1,0:T(8,128)S(1)}, u32[]{:S(2)}, u32[]{:S(2)}) %collective-permute-start.4) | collective-permute-done | bytes 32800 | tf_op jit(solution)/shard_map/ppermute | solution.py:600
  93.7 1.0 %collective-permute-done.5.refs_3_ = f32[32,256]{1,0:T(8,128)S(1)} collective-permute-done((f32[32,256]{1,0:T(8,128)S(1)}, f32[32,256]{1,0:T(8,128)S(1)}, u32[]{:S(2)}, u32[]{:S(2)}) %collective-permute-start.5) | collective-permute-done | bytes 32800 | tf_op jit(solution)/shard_map/ppermute | solution.py:600
  94.7 0.8 finish.1
  (7 shorter events, 0.0 us)
Async XLA Ops:
  23.4 11.1 %all-to-all-start.3 = ((bf16[8,4,1536]{2,1,0:T(4,128)(2,1)}), bf16[8,4,1536]{2,1,0:T(4,128)(2,1)S(1)}, u32[]{:S(2)}, u32[]{:S(2)}) async-start(bf16[8,4,1536]{2,1,0:T(4,128)(2,1)} %join.1), calls=%async_computation.3 | async-start | bytes 196608 | tf_op jit(solution)/shard_map/all_to_all | solution.py:604
  27.2 7.4 %copy-start = (bf16[1536,192]{0,1:T(8,128)(2,1)S(1)}, bf16[1536,192]{0,1:T(8,128)(2,1)}, u32[]{:S(2)}) copy-start(bf16[1536,192]{0,1:T(8,128)(2,1)} %param.21) | copy-start | bytes 1769476
  27.2 7.4 %copy-start.1 = (bf16[4,8,192]{2,1,0:T(8,128)(2,1)S(1)}, bf16[4,8,192]{2,1,0:T(8,128)(2,1)}, u32[]{:S(2)}) copy-start(bf16[4,8,192]{2,1,0:T(8,128)(2,1)} %residual_ref.1) | copy-start | bytes 36868
  27.2 7.4 %copy-start.2 = (s32[4,8,8]{2,1,0:T(8,128)S(1)}, s32[4,8,8]{2,1,0:T(8,128)}, u32[]{:S(2)}) copy-start(s32[4,8,8]{2,1,0:T(8,128)} %routes_ref.1) | copy-start | bytes 3076
  27.2 7.4 %copy-start.3 = (f32[192]{0:T(256)S(1)}, f32[192]{0:T(256)}, u32[]{:S(2)}) copy-start(f32[192]{0:T(256)} %param.22) | copy-start | bytes 2308
  27.2 13.3 %copy-start.5 = (bf16[192,40]{0,1:T(8,128)(2,1)S(1)}, bf16[192,40]{0,1:T(8,128)(2,1)}, u32[]{:S(2)}) copy-start(bf16[192,40]{0,1:T(8,128)(2,1)} %param.23) | copy-start | bytes 46084
  35.0 52.0 %copy-start.4 = (bf16[10,192,512]{2,1,0:T(8,128)(2,1)S(1)}, bf16[10,192,512]{2,1,0:T(8,128)(2,1)}, u32[]{:S(2)}) copy-start(bf16[10,192,512]{2,1,0:T(8,128)(2,1)} %w_ref.1) | copy-start | bytes 5898244
  35.1 4.0 %collective-permute-start = (bf16[32,256]{1,0:T(8,128)(2,1)S(1)}, bf16[32,256]{1,0:T(8,128)(2,1)S(1)}, u32[]{:S(2)}, u32[]{:S(2)}) collective-permute-start(bf16[32,256]{1,0:T(8,128)(2,1)S(1)} %get-tuple-element.81.refs_0_), channel_id=1, source_target_pairs={{0,1},{1,2},{2,3},{3,0},{4,5},{5,6},{6,7},{7,4},{8,9},{9,10},{10,1... | collective-permute-start | bytes 49160 | tf_op jit(solution)/shard_map/ppermute | solution.py:600
  35.1 4.2 %collective-permute-start.1 = (bf16[32,256]{1,0:T(8,128)(2,1)S(1)}, bf16[32,256]{1,0:T(8,128)(2,1)S(1)}, u32[]{:S(2)}, u32[]{:S(2)}) collective-permute-start(bf16[32,256]{1,0:T(8,128)(2,1)S(1)} %get-tuple-element.81.refs_0_), channel_id=1, source_target_pairs={{0,2},{1,3},{2,0},{3,1},{4,6},{5,7},{6,4},{7,5},{8,10},{9,11},{10,... | collective-permute-start | bytes 49160 | tf_op jit(solution)/shard_map/ppermute | solution.py:600
  37.7 2.8 %collective-permute-start.2 = (bf16[32,256]{1,0:T(8,128)(2,1)S(1)}, bf16[32,256]{1,0:T(8,128)(2,1)S(1)}, u32[]{:S(2)}, u32[]{:S(2)}) collective-permute-start(bf16[32,256]{1,0:T(8,128)(2,1)S(1)} %get-tuple-element.81.refs_0_), channel_id=1, source_target_pairs={{0,3},{1,0},{2,1},{3,2},{4,7},{5,4},{6,5},{7,6},{8,11},{9,8},{10,9... | collective-permute-start | bytes 49160 | tf_op jit(solution)/shard_map/ppermute | solution.py:600
  71.7 15.4 %all-to-all-start.5 = ((bf16[8,208,128]{2,1,0:T(8,128)(2,1)}), bf16[8,208,128]{2,1,0:T(8,128)(2,1)S(1)}, u32[]{:S(2)}, u32[]{:S(2)}) async-start(bf16[8,208,128]{2,1,0:T(8,128)(2,1)} %inner.3), calls=%async_computation.5 | async-start | bytes 851968 | tf_op jit(solution)/shard_map/all_to_all | solution.py:604
  89.1 2.5 %collective-permute-start.3 = (f32[32,256]{1,0:T(8,128)S(1)}, f32[32,256]{1,0:T(8,128)S(1)}, u32[]{:S(2)}, u32[]{:S(2)}) collective-permute-start(f32[32,256]{1,0:T(8,128)S(1)} %get-tuple-element.92), channel_id=1, source_target_pairs={{0,3},{1,0},{2,1},{3,2},{4,7},{5,4},{6,5},{7,6},{8,11},{9,8},{10,9... | collective-permute-start | bytes 98312 | tf_op jit(solution)/shard_map/ppermute | solution.py:600
  89.7 4.0 %collective-permute-start.4 = (f32[32,256]{1,0:T(8,128)S(1)}, f32[32,256]{1,0:T(8,128)S(1)}, u32[]{:S(2)}, u32[]{:S(2)}) collective-permute-start(f32[32,256]{1,0:T(8,128)S(1)} %get-tuple-element.93), channel_id=1, source_target_pairs={{0,2},{1,3},{2,0},{3,1},{4,6},{5,7},{6,4},{7,5},{8,10},{9,11},{10,... | collective-permute-start | bytes 98312 | tf_op jit(solution)/shard_map/ppermute | solution.py:600
  91.4 3.3 %collective-permute-start.5 = (f32[32,256]{1,0:T(8,128)S(1)}, f32[32,256]{1,0:T(8,128)S(1)}, u32[]{:S(2)}, u32[]{:S(2)}) collective-permute-start(f32[32,256]{1,0:T(8,128)S(1)} %get-tuple-element.94), channel_id=1, source_target_pairs={{0,1},{1,2},{2,3},{3,0},{4,5},{5,6},{6,7},{7,4},{8,9},{9,10},{10,1... | collective-permute-start | bytes 98312 | tf_op jit(solution)/shard_map/ppermute | solution.py:600

commit v3 on v2

--- a/solution.py
+++ b/solution.py
@@ -18,7 +18,9 @@
 CAP = 4
 LANES = 128
 SIDE_KEYS = 2
-ROUND_ROWS = 384
+ROUND_ROWS = 352
+PIECES = 8
+PIECE_WIDTH = FF // PIECES
 
 NEG_FILL = -1e30
 F32 = jnp.float32
@@ -333,16 +335,15 @@
 
 
 def gate_up_kernel(
-    features, local, turn, sources, where_ref, w_ref, router_ref, *refs,
+    features, local, turn, sources, parts, where_ref, w_ref, router_ref, *refs,
 ):
     part_refs, refs = refs[:sources], refs[sources:]
-    out_ref, pick_ref, range_ref, first_ref, most_ref, x_ref, row_ref, acc_ref = refs
+    out_refs, refs = refs[: len(parts)], refs[len(parts) :]
+    pick_ref, range_ref, first_ref, most_ref, x_ref, row_ref, acc_ref = refs
     total = x_ref.shape[0]
     for e, part_ref in enumerate(part_refs):
         x_ref[e * (total // sources) : (e + 1) * (total // sources)] = part_ref[...]
     rows = pick_ref.shape[1]
-    blocks = out_ref.shape[0]
-    share = rows // blocks
     width = w_ref.shape[3]
     window = total // 2 + 16
     tile, offset = side_place(features, SIDE_KEYS + EXPERTS)
@@ -390,11 +391,6 @@
             into = (pl.ds(start, window), slice(half * width, (half + 1) * width))
             made = dot_nn(part, w_ref[j, half])
             acc_ref[into] = jnp.where(fresh, made, acc_ref[into])
-    for b in range(blocks):
-        for piece in range(2 * width // LANES):
-            out_ref[b, piece * share : (piece + 1) * share, :] = acc_ref[
-                b * share : (b + 1) * share, piece * LANES : (piece + 1) * LANES
-            ].astype(BF16)
     logits = dot_nt(router_ref[...], x_ref[:, 0:features])
     high = round16(logits)
     both = jnp.concatenate([high, logits - high], axis=0).astype(BF16)
@@ -417,23 +413,48 @@
         ],
         axis=0,
     )
-    for b in range(blocks):
-        end = 2 * width // LANES * share
-        out_ref[b, end : end + 16, :] = jnp.zeros((16, LANES), BF16)
-        out_ref[b, end : end + 16, 0:share] = side[:, b * share : (b + 1) * share].astype(BF16)
-
-
-def gate_up(exp_index, tokens, weights, w_router, rows, blocks, turn):
+    begin = 0
+    for part, out_ref in zip(parts, out_refs):
+        blocks = out_ref.shape[0]
+        share = part * PIECES // blocks
+        low = iota((share, LANES), 1) < PIECE_WIDTH
+        for b in range(blocks):
+            piece, start = b % PIECES, begin + b // PIECES * share
+            tile = piece // 2 * LANES
+            gate = acc_ref[start : start + share, tile : tile + LANES]
+            up = acc_ref[start : start + share, width + tile : width + tile + LANES]
+            if piece % 2 == 0:
+                made = jnp.where(low, gate, swap_halves(up))
+            else:
+                made = jnp.where(low, swap_halves(gate), up)
+            out_ref[b, 0:share, :] = made.astype(BF16)
+            if piece == 0:
+                strips = []
+                for at in range(0, share, LANES):
+                    size = min(LANES, share - at)
+                    strip = side[0:4, start + at : start + at + size]
+                    if size < LANES:
+                        strip = jnp.concatenate([strip, jnp.zeros((4, LANES - size), F32)], axis=1)
+                    strips.append(strip)
+                strips.append(jnp.zeros((16 - 4 * len(strips), LANES), F32))
+                strips = jnp.concatenate(strips, axis=0).astype(BF16)
+            out_ref[b, share : share + 16, :] = strips
+        begin += part
+
+
+def gate_up(exp_index, tokens, weights, w_router, parts, blocks, turn):
     local, _, features, width = weights.shape
     sources, wide = len(tokens), tokens[0].shape[1]
-    total = sources * tokens[0].shape[0]
+    total, rows = sources * tokens[0].shape[0], sum(parts)
     smem, vmem = pl.BlockSpec(memory_space=pltpu.SMEM), pl.BlockSpec(memory_space=pltpu.VMEM)
     return pl.pallas_call(
-        functools.partial(gate_up_kernel, features, local, turn, sources),
+        functools.partial(gate_up_kernel, features, local, turn, sources, parts),
         in_specs=[smem] + [vmem] * (2 + sources),
-        out_specs=(vmem, vmem, vmem, smem, smem),
-        out_shape=(
-            jax.ShapeDtypeStruct((blocks, 2 * width // LANES * (rows // blocks) + 16, LANES), BF16),
+        out_specs=(vmem,) * len(parts) + (vmem, vmem, smem, smem),
+        out_shape=tuple(
+            jax.ShapeDtypeStruct((blocks, part * PIECES // blocks + 16, LANES), BF16) for part in parts
+        )
+        + (
             jax.ShapeDtypeStruct((total, rows), BF16),
             jax.ShapeDtypeStruct((16, LANES), F32),
             jax.ShapeDtypeStruct((16,), jnp.int32),
@@ -449,11 +470,10 @@
     )(exp_index, weights, w_router.T, *tokens)
 
 
-def inner_kernel(x_ref, out_ref):
+def inner_kernel(x_ref, out_ref, logit_ref):
     blocks, height, _ = x_ref.shape
-    pieces = 2 * FF // LANES
-    share = (height - 16) // pieces
-    half = pieces // 2
+    share = height - 16
+    half = share // 2
 
     def total(start, size):
         added = x_ref[0, start : start + size].astype(F32)
@@ -461,50 +481,58 @@
             added = added + x_ref[b, start : start + size].astype(F32)
         return added
 
-    side = total(pieces * share, 16)
-    logit = side[0:1] + side[1:2]
-    squares = side[2:3] + side[3:4]
-    inverse = lax.rsqrt(squares * (1.0 / D) + 1e-6)
-    down_column = jnp.broadcast_to(inverse, (LANES, LANES)).T[0:share, 0:1]
-    for piece in range(half):
-        gate = total(piece * share, share) * down_column
-        up = total((half + piece) * share, share) * down_column
-        made = (gate / (1.0 + jnp.exp(-gate)) * up).astype(BF16)
-        for b in range(blocks):
-            out_ref[b, piece * share : (piece + 1) * share, :] = made
-    logit = logit * inverse
-    high = round16(logit)
-    middle = round16(logit - high)
-    own = jnp.concatenate(
-        [high, middle, logit - high - middle, jnp.zeros((13, LANES), F32)], axis=0
-    ).astype(BF16)
+    side = total(share, 16)
+    columns, logits = [], []
+    for strip in range(-(-share // LANES)):
+        values = side[4 * strip : 4 * strip + 4]
+        inverse = lax.rsqrt((values[2:3] + values[3:4]) * (1.0 / D) + 1e-6)
+        logits.append((values[0:1] + values[1:2]) * inverse)
+        columns.append(jnp.broadcast_to(inverse, (LANES, LANES)).T)
+    logit_ref[...] = jnp.concatenate(logits + [jnp.zeros((8 - len(logits), LANES), F32)], axis=0)
+    scaled = total(0, share) * jnp.concatenate(columns, axis=0)[0:share]
+    made = scaled / (1.0 + jnp.exp(-scaled)) * swap_halves(scaled)
+    low = iota((half, LANES), 1) < PIECE_WIDTH
+    made = jnp.where(low, made[0:half], swap_halves(made[half:share])).astype(BF16)
     for b in range(blocks):
-        out_ref[b, half * share : half * share + 16, :] = own
+        out_ref[b] = made
 
 
 def inner(parts):
     blocks, height, _ = parts.shape
     return pl.pallas_call(
         inner_kernel,
-        out_shape=jax.ShapeDtypeStruct((blocks, (height - 16) // 2 + 16, LANES), BF16),
+        out_shape=(
+            jax.ShapeDtypeStruct((blocks, (height - 16) // 2, LANES), BF16),
+            jax.ShapeDtypeStruct((8, LANES), F32),
+        ),
         compiler_params=params(),
         name="inner",
     )(parts)
 
 
-def down_kernel(features, local, first_ref, range_ref, pick_ref, x_ref, w_ref, *refs):
+def down_kernel(features, local, parts, first_ref, range_ref, pick_ref, w_ref, *refs):
+    part_refs, logit_refs, refs = refs[: len(parts)], refs[len(parts) : 2 * len(parts)], refs[2 * len(parts) :]
     out_refs, (row_ref, made_ref) = refs[:-2], refs[-2:]
-    blocks, height, _ = x_ref.shape
     total, rows = pick_ref.shape
     width = w_ref.shape[2]
-    pieces = width // LANES
-    share = (height - 16) // pieces
     window = total // 2 + 16
-    for b in range(blocks):
-        for piece in range(pieces):
-            row_ref[b * share : (b + 1) * share, piece * LANES : (piece + 1) * LANES] = x_ref[
-                b, piece * share : (piece + 1) * share, :
-            ]
+    begin, logit = 0, []
+    for part, x_ref, logit_ref in zip(parts, part_refs, logit_refs):
+        blocks, half, _ = x_ref.shape
+        share = 2 * half
+        low = iota((half, LANES), 1) < PIECE_WIDTH
+        for b in range(0, blocks, 2):
+            start, tile = begin + b // PIECES * share, b % PIECES // 2 * LANES
+            one, two = x_ref[b].astype(F32), x_ref[b + 1].astype(F32)
+            above = jnp.where(low, one, swap_halves(two)).astype(BF16)
+            below = jnp.where(low, swap_halves(one), two).astype(BF16)
+            row_ref[start : start + half, tile : tile + LANES] = above
+            row_ref[start + half : start + share, tile : tile + LANES] = below
+        for piece in range(blocks // PIECES):
+            for strip in range(-(-share // LANES)):
+                size = min(LANES, share - strip * LANES)
+                logit.append(logit_ref[piece, strip : strip + 1, 0:size])
+        begin += part
     made_ref[...] = jnp.zeros_like(made_ref)
     for j in range(local):
         start_row = first_ref[j]
@@ -513,14 +541,14 @@
         fresh = start + iota((window, features), 0) >= start_row
         into = (pl.ds(start, window), slice(0, features))
         made_ref[into] = jnp.where(fresh, made, made_ref[into])
-    logit = jnp.concatenate(
-        [x_ref[b, pieces * share :, 0:share].astype(F32) for b in range(blocks)], axis=1
-    )
+    logit = jnp.concatenate(logit, axis=1)
+    high = round16(logit)
+    middle = round16(logit - high)
     pick = pick_ref[...]
     where_row = iota((16, rows), 1).astype(F32)
     inside = jnp.logical_and(where_row >= range_ref[:, 0:1], where_row < range_ref[:, 8:9])
     inside = jnp.logical_and(inside, iota((16, rows), 0) < local)
-    spread = [jnp.where(inside, logit[k : k + 1], 0.0) for k in range(3)]
+    spread = [jnp.where(inside, part, 0.0) for part in (high, middle, logit - high - middle)]
     spread.append(inside.astype(F32))
     found = dot_nt(jnp.concatenate(spread, axis=0).astype(BF16), pick)
     valid = found[48:64] > 0.5
@@ -544,19 +572,19 @@
         out_ref[:, tile : tile + LANES] = jnp.where(lane == 1, pair[at, 1:2], side)
 
 
-def down(first, ranges, pick, parts, weights, exp_count):
+def down(first, ranges, pick, parts, made, logits, weights, exp_count):
     local, features, width = weights.shape
     total, rows = pick.shape
     wide = side_place(features, 2)[0] + LANES
     smem, vmem = pl.BlockSpec(memory_space=pltpu.SMEM), pl.BlockSpec(memory_space=pltpu.VMEM)
     return pl.pallas_call(
-        functools.partial(down_kernel, features, local),
-        in_specs=[smem] + [vmem] * 4,
+        functools.partial(down_kernel, features, local, parts),
+        in_specs=[smem] + [vmem] * (3 + 2 * len(parts)),
         out_shape=(jax.ShapeDtypeStruct((total // exp_count, wide), F32),) * exp_count,
         scratch_shapes=[pltpu.VMEM((rows, width), BF16), pltpu.VMEM((rows, wide), F32)],
         compiler_params=params(),
         name="down",
-    )(first, ranges, pick, parts, weights)
+    )(first, ranges, pick, weights, *made, *logits)
 
 
 def finish_kernel(hidden_ref, *refs):
@@ -637,14 +665,24 @@
     gate_up_weights, attn = lax.optimization_barrier((gate_up_weights, attn))
     hidden, outgoing = hidden_state(attn, residual, w_out, norm_gain, routes)
     incoming = [outgoing] + [send(outgoing, "exp", k) for k in range(1, exp_count)]
-    rows = -(-ROUND_ROWS // (16 * seq_count)) * 16 * seq_count
+    pieces = seq_count // PIECES
+    units = -(-ROUND_ROWS // (32 * pieces))
+    parts = tuple(32 * pieces * count for count in (-(-units // 2), units // 2))
+    rows = sum(parts)
+
+    def logits_of(row_logits):
+        if pieces == 1:
+            return row_logits[None]
+        return lax.all_gather(row_logits, "seq")[::PIECES]
 
     def one_round(turn):
-        parts, pick, ranges, first, most = gate_up(
-            exp_index, incoming, gate_up_weights, w_router, rows, seq_count, turn
+        *partial, pick, ranges, first, most = gate_up(
+            exp_index, incoming, gate_up_weights, w_router, parts, seq_count, turn
         )
-        made = swap(inner(swap(parts, "seq")), "seq")
-        return down(first, ranges, pick, made, w_down, exp_count), most
+        made, logits = zip(*[inner(swap(part, "seq")) for part in partial])
+        made = [swap(part, "seq") for part in made]
+        logits = [logits_of(part) for part in logits]
+        return down(first, ranges, pick, parts, made, logits, w_down, exp_count), most
 
     made, most = one_round(0)
     pairs = w_gate_up.shape[0] * exp_count * steps * CAP

time: 96.5 us -> 108 us (1.12)
  waiting for transfers between devices: 18.5 us -> 31.5 us
  blocking collectives: 36.8 us -> 26.4 us
  starting transfers between devices: 13.6 us -> 20.9 us
  Pallas kernels: 21 us -> 22.4 us
    all_to_all x2 -> x4, waiting for transfers between devices: 13.8 us -> 26.8 us  [swap(): return lax.all_to_all(x, axis, split_axis=0, concat_axis=0, tiled=True)]
    all_to_all x2, blocking collectives: 36.8 us -> 26.4 us  [swap(): return lax.all_to_all(x, axis, split_axis=0, concat_axis=0, tiled=True)]
    all_to_all x2 -> x4, starting transfers between devices: 7.21 us -> 13.8 us  [swap(): return lax.all_to_all(x, axis, split_axis=0, concat_axis=0, tiled=True)]
    pallas_call x2 -> x3, Pallas kernels: 2.97 us -> 3.98 us  [the longest x1 2.09 us: down(): pl.pallas_call(functools.partial(down_kernel, features, local, parts), in...]
  transfers between devices with their start and end apart: 8 -> 10, of which waited for: 6 -> 8; matrix products, arithmetic and copies ran while one was open for 5% -> 5% of each run, Pallas kernels for 0% -> 2%
where the time goes in v3:
time: 108 us; the launch traced here: 107 us
  waiting for transfers between devices  31.5 us (29%)
  blocking collectives  26.4 us (24%)
  Pallas kernels  22.4 us (21%)
  starting transfers between devices  20.9 us (19%)
  local copies, waits for them, and re-layouts  4.87 us (5%)
    all_to_all x4, waiting for transfers between devices, swap(): return lax.all_to_all(x, axis, split_axis=0, concat_axis=0, tiled=True)  26.8 us
    all_to_all x2, blocking collectives, swap(): return lax.all_to_all(x, axis, split_axis=0, concat_axis=0, tiled=True)  26.4 us
    all_to_all x4, starting transfers between devices, swap(): return lax.all_to_all(x, axis, split_axis=0, concat_axis=0, tiled=True)  13.8 us
    pallas_call x1, Pallas kernels, attend(): pl.pallas_call(functools.partial(attend_kernel, classes), in_specs=[smem]...  11.2 us
    ppermute x6, starting transfers between devices, send(): lax.ppermute(x, axis, [(i, (i + distance) % count) for i in range(count)])  7.03 us
    pallas_call x1, Pallas kernels, gate_up(): pl.pallas_call(functools.partial(gate_up_kernel, features, local, turn, s...  4.88 us
    optimization_barrier x1, local copies, waits for them, and re-layouts, local(): w_gate_up, attn = lax.optimization_barrier((w_gate_up, attn))  4.83 us
    ppermute x6, waiting for transfers between devices, send(): lax.ppermute(x, axis, [(i, (i + distance) % count) for i in range(count)])  4.62 us
  transfers between devices with their start and end apart: 10, of which 8 were waited for; matrix products, arithmetic and copies ran while one was open for 5% of the time, Pallas kernels for 2%

profile of v3, /device:TPU:0, one launch (start us, length us, event | category | flops | bytes accessed | tf_op | source)
XLA Modules:
  0.0 106.9 jit_solution(9827294449193286582)
XLA Ops:
  0.0 11.2 %attend.1 = bf16[8,12,640]{2,1,0:T(8,128)(2,1)} custom-call(s32[8,8]{1,0:T(8,128)} %table_ref.1, s32[8]{0:T(128)} %len_ref.1, s32[1]{0:T(128)} %bitcast.3.seq_ref, bf16[4,8,1536]{2,1,0:T(8,128)(2,1)} %q_hbm.1, bf16[4,8,2,512]{3,2,1,0:T(2,128)(2,1)} %fresh_hbm.1, bf16[64,64,2,512]{3,2,1,0:T(2,128)(2,1)} %bitcast.23), custom_call_target="tpu_custom_call" | custom-call | tf_op jit(solution)/shard_map/attend/pallas_call | solution.py:224
  11.2 10.9 %all_to_all.47.x_ref = bf16[8,12,640]{2,1,0:T(8,128)(2,1)S(1)} all-to-all(bf16[8,12,640]{2,1,0:T(8,128)(2,1)} %attend.1), channel_id=1, replica_groups=mesh['seq'=8,'exp'=4] {'seq'}, dimensions={0} | all-to-all | bytes 245760 | tf_op jit(solution)/shard_map/all_to_all | solution.py:632
  22.1 1.1 %join.1 = bf16[8,4,1536]{2,1,0:T(4,128)(2,1)} custom-call(bf16[8,12,640]{2,1,0:T(8,128)(2,1)S(1)} %all_to_all.47.x_ref), custom_call_target="tpu_custom_call" | custom-call | tf_op jit(solution)/shard_map/join/pallas_call | solution.py:278
  23.2 3.4 %all-to-all-start.5 = ((bf16[8,4,1536]{2,1,0:T(4,128)(2,1)}), bf16[8,4,1536]{2,1,0:T(4,128)(2,1)S(1)}, u32[]{:S(2)}, u32[]{:S(2)}) async-start(bf16[8,4,1536]{2,1,0:T(4,128)(2,1)} %join.1), calls=%async_computation.5 | async-start | bytes 196608 | tf_op jit(solution)/shard_map/all_to_all | solution.py:632
  26.6 0.0 copy-start
  26.6 0.0 copy-start.2
  26.6 0.0 copy-start.3
  26.6 4.8 %copy.16 = bf16[10,192,2,512]{3,1,2,0:T(8,128)(2,1)} copy(bf16[10,192,2,512]{3,2,1,0:T(2,128)(2,1)} %param.24) | data formatting | bytes 7864320 | tf_op jit(solution)/shard_map/optimization_barrier | solution.py:662
  31.5 2.2 %all-to-all-done.5.attn_ref = bf16[8,4,1536]{2,1,0:T(4,128)(2,1)S(1)} async-done(((bf16[8,4,1536]{2,1,0:T(4,128)(2,1)}), bf16[8,4,1536]{2,1,0:T(4,128)(2,1)S(1)}, u32[]{:S(2)}, u32[]{:S(2)}) %all-to-all-start.5) | async-done | bytes 98336 | tf_op jit(solution)/shard_map/all_to_all | solution.py:632
  33.7 0.5 hidden.1
  34.1 0.1 collective-permute-start
  34.2 3.0 %collective-permute-start.1 = (bf16[32,256]{1,0:T(8,128)(2,1)S(1)}, bf16[32,256]{1,0:T(8,128)(2,1)S(1)}, u32[]{:S(2)}, u32[]{:S(2)}) collective-permute-start(bf16[32,256]{1,0:T(8,128)(2,1)S(1)} %get-tuple-element.91.refs_0_), channel_id=1, source_target_pairs={{0,2},{1,3},{2,0},{3,1},{4,6},{5,7},{6,4},{7,5},{8,10},{9,11},{10,... | collective-permute-start | bytes 49160 | tf_op jit(solution)/shard_map/ppermute | solution.py:628
  37.2 1.4 %collective-permute-start.2 = (bf16[32,256]{1,0:T(8,128)(2,1)S(1)}, bf16[32,256]{1,0:T(8,128)(2,1)S(1)}, u32[]{:S(2)}, u32[]{:S(2)}) collective-permute-start(bf16[32,256]{1,0:T(8,128)(2,1)S(1)} %get-tuple-element.91.refs_0_), channel_id=1, source_target_pairs={{0,3},{1,0},{2,1},{3,2},{4,7},{5,4},{6,5},{7,6},{8,11},{9,8},{10,9... | collective-permute-start | bytes 49160 | tf_op jit(solution)/shard_map/ppermute | solution.py:628
  38.6 0.3 collective-permute-done.1.refs_2_
  38.9 1.1 %collective-permute-done.2.refs_3_ = bf16[32,256]{1,0:T(8,128)(2,1)S(1)} collective-permute-done((bf16[32,256]{1,0:T(8,128)(2,1)S(1)}, bf16[32,256]{1,0:T(8,128)(2,1)S(1)}, u32[]{:S(2)}, u32[]{:S(2)}) %collective-permute-start.2) | collective-permute-done | bytes 16416 | tf_op jit(solution)/shard_map/ppermute | solution.py:628
  40.1 4.9 %gate_up.3 = (bf16[8,208,128]{2,1,0:T(8,128)(2,1)}, bf16[8,176,128]{2,1,0:T(8,128)(2,1)S(1)}, bf16[128,352]{1,0:T(8,128)(2,1)S(1)}, f32[16,128]{1,0:T(8,128)S(1)}, s32[16]{0:T(128)S(1)}, /*index=5*/s32[1]{0:T(128)}) custom-call(s32[1]{0:T(128)} %bitcast.8.where_ref, bf16[10,2,192,512]{3,2,1,0:T(8,128)(2,1)} %bitcast.21, bf16[40,192]{1,0:T(8,128)(2,1)S(1)} %bitcast.24, ...), custom_call_target="tpu_custom_call" | custom-call | tf_op jit(solution)/shard_map/gate_up/pallas_call | solution.py:450
  45.0 15.5 %all_to_all.48.x_ref = bf16[8,176,128]{2,1,0:T(8,128)(2,1)S(1)} all-to-all(bf16[8,176,128]{2,1,0:T(8,128)(2,1)S(1)} %get-tuple-element.98), channel_id=1, replica_groups=mesh['seq'=8,'exp'=4] {'seq'}, dimensions={0} | all-to-all | bytes 720896 | tf_op jit(solution)/shard_map/all_to_all | solution.py:632
  60.5 3.5 %all-to-all-start.6 = ((bf16[8,208,128]{2,1,0:T(8,128)(2,1)}), bf16[8,208,128]{2,1,0:T(8,128)(2,1)S(1)}, u32[]{:S(2)}, u32[]{:S(2)}) async-start(bf16[8,208,128]{2,1,0:T(8,128)(2,1)} %get-tuple-element.96), calls=%async_computation.6 | async-start | bytes 851968 | tf_op jit(solution)/shard_map/all_to_all | solution.py:632
  64.0 0.9 inner.7
  64.9 11.0 %all-to-all-done.6.x_ref = bf16[8,208,128]{2,1,0:T(8,128)(2,1)S(1)} async-done(((bf16[8,208,128]{2,1,0:T(8,128)(2,1)}), bf16[8,208,128]{2,1,0:T(8,128)(2,1)S(1)}, u32[]{:S(2)}, u32[]{:S(2)}) %all-to-all-start.6) | async-done | bytes 426016 | tf_op jit(solution)/shard_map/all_to_all | solution.py:632
  75.9 3.6 %all-to-all-start.9 = ((bf16[8,80,128]{2,1,0:T(8,128)(2,1)}), bf16[8,80,128]{2,1,0:T(8,128)(2,1)S(1)}, u32[]{:S(2)}, u32[]{:S(2)}) async-start(bf16[8,80,128]{2,1,0:T(8,128)(2,1)} %get-tuple-element.99), calls=%async_computation.9 | async-start | bytes 327680 | tf_op jit(solution)/shard_map/all_to_all | solution.py:632
  79.6 1.0 inner.6
  80.5 6.6 %all-to-all-done.9.refs_1_ = bf16[8,80,128]{2,1,0:T(8,128)(2,1)S(1)} async-done(((bf16[8,80,128]{2,1,0:T(8,128)(2,1)}), bf16[8,80,128]{2,1,0:T(8,128)(2,1)S(1)}, u32[]{:S(2)}, u32[]{:S(2)}) %all-to-all-start.9) | async-done | bytes 163872 | tf_op jit(solution)/shard_map/all_to_all | solution.py:632
  87.1 3.4 %all-to-all-start.7 = ((bf16[8,96,128]{2,1,0:T(8,128)(2,1)}), bf16[8,96,128]{2,1,0:T(8,128)(2,1)S(1)}, u32[]{:S(2)}, u32[]{:S(2)}) async-start(bf16[8,96,128]{2,1,0:T(8,128)(2,1)} %get-tuple-element.97), calls=%async_computation.7 | async-start | bytes 393216 | tf_op jit(solution)/shard_map/all_to_all | solution.py:632
  91.2 7.0 %all-to-all-done.7.refs_0_ = bf16[8,96,128]{2,1,0:T(8,128)(2,1)S(1)} async-done(((bf16[8,96,128]{2,1,0:T(8,128)(2,1)}), bf16[8,96,128]{2,1,0:T(8,128)(2,1)S(1)}, u32[]{:S(2)}, u32[]{:S(2)}) %all-to-all-start.7) | async-done | bytes 196640 | tf_op jit(solution)/shard_map/all_to_all | solution.py:632
  98.3 2.1 %down.3 = (f32[32,256]{1,0:T(8,128)S(1)}, f32[32,256]{1,0:T(8,128)S(1)}, f32[32,256]{1,0:T(8,128)S(1)}, f32[32,256]{1,0:T(8,128)S(1)}) custom-call(s32[16]{0:T(128)S(1)} %get-tuple-element.93.first_ref, f32[16,128]{1,0:T(8,128)S(1)} %get-tuple-element.94.range_ref, bf16[128,352]{1,0:T(8,128)(2,1)S(1)} %get-tuple-element.95.pick_ref, ...), custom_call_target="tpu_custom_call" | custom-call | tf_op jit(solution)/shard_map/down/pallas_call | solution.py:580
  100.4 0.1 collective-permute-start.3
  100.4 2.3 %collective-permute-start.4 = (f32[32,256]{1,0:T(8,128)S(1)}, f32[32,256]{1,0:T(8,128)S(1)}, u32[]{:S(2)}, u32[]{:S(2)}) collective-permute-start(f32[32,256]{1,0:T(8,128)S(1)} %get-tuple-element.108), channel_id=1, source_target_pairs={{0,2},{1,3},{2,0},{3,1},{4,6},{5,7},{6,4},{7,5},{8,10},{9,11},{10,... | collective-permute-start | bytes 98312 | tf_op jit(solution)/shard_map/ppermute | solution.py:628
  102.7 0.2 collective-permute-start.5
  102.9 2.2 %collective-permute-done.4.refs_2_ = f32[32,256]{1,0:T(8,128)S(1)} collective-permute-done((f32[32,256]{1,0:T(8,128)S(1)}, f32[32,256]{1,0:T(8,128)S(1)}, u32[]{:S(2)}, u32[]{:S(2)}) %collective-permute-start.4) | collective-permute-done | bytes 32800 | tf_op jit(solution)/shard_map/ppermute | solution.py:628
  105.1 1.0 collective-permute-done.5.refs_3_
  106.1 0.8 finish.1
  (12 shorter events, 0.0 us)
Async XLA Ops:
  23.2 10.4 %all-to-all-start.5 = ((bf16[8,4,1536]{2,1,0:T(4,128)(2,1)}), bf16[8,4,1536]{2,1,0:T(4,128)(2,1)S(1)}, u32[]{:S(2)}, u32[]{:S(2)}) async-start(bf16[8,4,1536]{2,1,0:T(4,128)(2,1)} %join.1), calls=%async_computation.5 | async-start | bytes 196608 | tf_op jit(solution)/shard_map/all_to_all | solution.py:632
  26.6 7.1 %copy-start = (bf16[1536,192]{0,1:T(8,128)(2,1)S(1)}, bf16[1536,192]{0,1:T(8,128)(2,1)}, u32[]{:S(2)}) copy-start(bf16[1536,192]{0,1:T(8,128)(2,1)} %param.21) | copy-start | bytes 1769476
  26.6 7.1 %copy-start.1 = (bf16[4,8,192]{2,1,0:T(8,128)(2,1)S(1)}, bf16[4,8,192]{2,1,0:T(8,128)(2,1)}, u32[]{:S(2)}) copy-start(bf16[4,8,192]{2,1,0:T(8,128)(2,1)} %residual_ref.1) | copy-start | bytes 36868
  26.6 7.0 %copy-start.2 = (s32[4,8,8]{2,1,0:T(8,128)S(1)}, s32[4,8,8]{2,1,0:T(8,128)}, u32[]{:S(2)}) copy-start(s32[4,8,8]{2,1,0:T(8,128)} %routes_ref.1) | copy-start | bytes 3076
  26.6 7.0 %copy-start.3 = (f32[192]{0:T(256)S(1)}, f32[192]{0:T(256)}, u32[]{:S(2)}) copy-start(f32[192]{0:T(256)} %param.22) | copy-start | bytes 2308
  26.6 13.4 %copy-start.5 = (bf16[192,40]{0,1:T(8,128)(2,1)S(1)}, bf16[192,40]{0,1:T(8,128)(2,1)}, u32[]{:S(2)}) copy-start(bf16[192,40]{0,1:T(8,128)(2,1)} %param.23) | copy-start | bytes 46084
  31.5 66.8 %copy-start.4 = (bf16[10,192,512]{2,1,0:T(8,128)(2,1)S(1)}, bf16[10,192,512]{2,1,0:T(8,128)(2,1)}, u32[]{:S(2)}) copy-start(bf16[10,192,512]{2,1,0:T(8,128)(2,1)} %w_ref.1) | copy-start | bytes 5898244
  34.1 4.5 %collective-permute-start = (bf16[32,256]{1,0:T(8,128)(2,1)S(1)}, bf16[32,256]{1,0:T(8,128)(2,1)S(1)}, u32[]{:S(2)}, u32[]{:S(2)}) collective-permute-start(bf16[32,256]{1,0:T(8,128)(2,1)S(1)} %get-tuple-element.91.refs_0_), channel_id=1, source_target_pairs={{0,1},{1,2},{2,3},{3,0},{4,5},{5,6},{6,7},{7,4},{8,9},{9,10},{10,1... | collective-permute-start | bytes 49160 | tf_op jit(solution)/shard_map/ppermute | solution.py:628
  34.2 4.8 %collective-permute-start.1 = (bf16[32,256]{1,0:T(8,128)(2,1)S(1)}, bf16[32,256]{1,0:T(8,128)(2,1)S(1)}, u32[]{:S(2)}, u32[]{:S(2)}) collective-permute-start(bf16[32,256]{1,0:T(8,128)(2,1)S(1)} %get-tuple-element.91.refs_0_), channel_id=1, source_target_pairs={{0,2},{1,3},{2,0},{3,1},{4,6},{5,7},{6,4},{7,5},{8,10},{9,11},{10,... | collective-permute-start | bytes 49160 | tf_op jit(solution)/shard_map/ppermute | solution.py:628
  37.2 2.8 %collective-permute-start.2 = (bf16[32,256]{1,0:T(8,128)(2,1)S(1)}, bf16[32,256]{1,0:T(8,128)(2,1)S(1)}, u32[]{:S(2)}, u32[]{:S(2)}) collective-permute-start(bf16[32,256]{1,0:T(8,128)(2,1)S(1)} %get-tuple-element.91.refs_0_), channel_id=1, source_target_pairs={{0,3},{1,0},{2,1},{3,2},{4,7},{5,4},{6,5},{7,6},{8,11},{9,8},{10,9... | collective-permute-start | bytes 49160 | tf_op jit(solution)/shard_map/ppermute | solution.py:628
  60.5 15.4 %all-to-all-start.6 = ((bf16[8,208,128]{2,1,0:T(8,128)(2,1)}), bf16[8,208,128]{2,1,0:T(8,128)(2,1)S(1)}, u32[]{:S(2)}, u32[]{:S(2)}) async-start(bf16[8,208,128]{2,1,0:T(8,128)(2,1)} %get-tuple-element.96), calls=%async_computation.6 | async-start | bytes 851968 | tf_op jit(solution)/shard_map/all_to_all | solution.py:632
  75.9 11.2 %all-to-all-start.9 = ((bf16[8,80,128]{2,1,0:T(8,128)(2,1)}), bf16[8,80,128]{2,1,0:T(8,128)(2,1)S(1)}, u32[]{:S(2)}, u32[]{:S(2)}) async-start(bf16[8,80,128]{2,1,0:T(8,128)(2,1)} %get-tuple-element.99), calls=%async_computation.9 | async-start | bytes 327680 | tf_op jit(solution)/shard_map/all_to_all | solution.py:632
  87.1 11.1 %all-to-all-start.7 = ((bf16[8,96,128]{2,1,0:T(8,128)(2,1)}), bf16[8,96,128]{2,1,0:T(8,128)(2,1)S(1)}, u32[]{:S(2)}, u32[]{:S(2)}) async-start(bf16[8,96,128]{2,1,0:T(8,128)(2,1)} %get-tuple-element.97), calls=%async_computation.7 | async-start | bytes 393216 | tf_op jit(solution)/shard_map/all_to_all | solution.py:632
  100.4 2.6 %collective-permute-start.3 = (f32[32,256]{1,0:T(8,128)S(1)}, f32[32,256]{1,0:T(8,128)S(1)}, u32[]{:S(2)}, u32[]{:S(2)}) collective-permute-start(f32[32,256]{1,0:T(8,128)S(1)} %get-tuple-element.107), channel_id=1, source_target_pairs={{0,3},{1,0},{2,1},{3,2},{4,7},{5,4},{6,5},{7,6},{8,11},{9,8},{10,9... | collective-permute-start | bytes 98312 | tf_op jit(solution)/shard_map/ppermute | solution.py:628
  100.4 4.7 %collective-permute-start.4 = (f32[32,256]{1,0:T(8,128)S(1)}, f32[32,256]{1,0:T(8,128)S(1)}, u32[]{:S(2)}, u32[]{:S(2)}) collective-permute-start(f32[32,256]{1,0:T(8,128)S(1)} %get-tuple-element.108), channel_id=1, source_target_pairs={{0,2},{1,3},{2,0},{3,1},{4,6},{5,7},{6,4},{7,5},{8,10},{9,11},{10,... | collective-permute-start | bytes 98312 | tf_op jit(solution)/shard_map/ppermute | solution.py:628
  102.7 3.3 %collective-permute-start.5 = (f32[32,256]{1,0:T(8,128)S(1)}, f32[32,256]{1,0:T(8,128)S(1)}, u32[]{:S(2)}, u32[]{:S(2)}) collective-permute-start(f32[32,256]{1,0:T(8,128)S(1)} %get-tuple-element.109), channel_id=1, source_target_pairs={{0,1},{1,2},{2,3},{3,0},{4,5},{5,6},{6,7},{7,4},{8,9},{9,10},{10,1... | collective-permute-start | bytes 98312 | tf_op jit(solution)/shard_map/ppermute | solution.py:628

commit v4 on v3

--- a/solution.py
+++ b/solution.py
@@ -66,9 +66,10 @@
 
 
 def attend_kernel(
-    classes, table_ref, len_ref, seq_ref, q_hbm, fresh_hbm, cache_ref, out_ref,
-    page_ref, split_ref, q_ref, fresh_ref, query_ref, new_ref, order_ref, sems, small_sems,
+    classes, devices, table_ref, len_ref, seq_ref, q_hbm, fresh_hbm, cache_ref, *refs,
 ):
+    out_refs, refs = refs[:devices], refs[devices:]
+    share_ref, page_ref, split_ref, q_ref, fresh_ref, query_ref, new_ref, order_ref, sems, small_sems = refs
     steps, requests, _ = q_ref.shape
     page_rows = cache_ref.shape[1]
     pages = table_ref.shape[1]
@@ -89,6 +90,15 @@
                 longer = held[other] >= held[r] if other < r else held[other] > held[r]
                 ahead = ahead + longer.astype(jnp.int32)
         order_ref[ahead] = r
+
+    share = share_ref.shape[1]
+    per_request = steps * GROUP // share
+
+    def put(r, acc, side):
+        for i in range(per_request):
+            at = r * per_request + i
+            share_ref[at, :, 0:KV_WIDTH] = acc[i * share : (i + 1) * share]
+            share_ref[at, :, KV_WIDTH : KV_WIDTH + LANES] = side[i * share : (i + 1) * share]
 
     def copy(r, page):
         at = r * pages + page
@@ -200,32 +210,34 @@
                         copy(r, page).wait()
                 made = [attend_pages(r, slot, high) for slot, r in enumerate(both)]
                 for r, (acc, side) in zip(both, made):
-                    out_ref[r, :, 0:KV_WIDTH] = acc
-                    out_ref[r, :, KV_WIDTH : KV_WIDTH + LANES] = side
+                    put(r, acc, side)
 
         @pl.when(jnp.logical_not(needed(both[0], 0)))
         def _():
             empty = jnp.where(iota((steps * GROUP, LANES), 1) < KEY_VALUE_HEADS, NEG_FILL, 0.0)
             for r in both:
-                out_ref[r, :, 0:KV_WIDTH] = jnp.zeros((steps * GROUP, KV_WIDTH), BF16)
-                out_ref[r, :, KV_WIDTH : KV_WIDTH + LANES] = empty.astype(BF16)
+                put(r, jnp.zeros((steps * GROUP, KV_WIDTH), BF16), empty.astype(BF16))
 
         return carry
 
     lax.fori_loop(0, requests // 2, one_pair, 0)
-
-
-def attend(queries, new_key_value, cache, page_table, cache_len, seq_index):
+    for k, out_ref in enumerate(out_refs):
+        out_ref[...] = share_ref[lax.rem(seq_ref[0] + k, devices)]
+
+
+def attend(queries, new_key_value, cache, page_table, cache_len, seq_index, devices):
     steps, requests, _ = queries.shape
     pages = page_table.shape[1]
     page_rows = cache.shape[1]
     classes = tuple(c for c in (2, 4) if c < pages) + (pages,)
+    share = (requests * steps * GROUP // devices, KV_WIDTH + LANES)
     smem, hbm = pl.BlockSpec(memory_space=pltpu.SMEM), pl.BlockSpec(memory_space=pl.ANY)
     return pl.pallas_call(
-        functools.partial(attend_kernel, classes),
+        functools.partial(attend_kernel, classes, devices),
         in_specs=[smem] * 3 + [hbm] * 3,
-        out_shape=jax.ShapeDtypeStruct((requests, steps * GROUP, KV_WIDTH + LANES), BF16),
+        out_shape=(jax.ShapeDtypeStruct(share, BF16),) * devices,
         scratch_shapes=[
+            pltpu.VMEM((devices,) + share, BF16),
             pltpu.VMEM((requests * pages, page_rows, 2, KV_WIDTH), BF16),
             pltpu.VMEM((2, pages, KV_WIDTH // LANES, 2 * page_rows, LANES), F32),
             pltpu.VMEM(queries.shape, BF16),
@@ -241,23 +253,24 @@
     )(page_table, cache_len, seq_index, queries, new_key_value, cache)
 
 
-def join_kernel(x_ref, out_ref):
-    blocks, rows, _ = x_ref.shape
+def join_kernel(*refs):
+    x_refs, out_ref = refs[:-1], refs[-1]
+    rows = x_refs[0].shape[0]
     tokens = rows // GROUP
     levels = []
-    for b in range(blocks):
-        side = x_ref[b, :, KV_WIDTH : KV_WIDTH + LANES].astype(F32)
+    for x_ref in x_refs:
+        side = x_ref[:, KV_WIDTH : KV_WIDTH + LANES].astype(F32)
         levels.append(side + pltpu.roll(side, LANES - 8, 1) + pltpu.roll(side, LANES - 16, 1))
     largest = functools.reduce(jnp.maximum, levels)
     weights = [jnp.exp(level - largest) for level in levels]
     inverse = 1.0 / functools.reduce(jnp.add, weights)
     low = iota((rows, LANES), 1) < HEAD_SIZE
     acc = [jnp.zeros((rows, LANES), F32) for _ in range(KV_WIDTH // LANES)]
-    for b in range(blocks):
-        share = weights[b] * inverse
+    for x_ref, weight in zip(x_refs, weights):
+        share = weight * inverse
         for j in range(KV_WIDTH // LANES):
             factor = jnp.where(low, share[:, 2 * j : 2 * j + 1], share[:, 2 * j + 1 : 2 * j + 2])
-            acc[j] = acc[j] + factor * x_ref[b, :, j * LANES : (j + 1) * LANES].astype(F32)
+            acc[j] = acc[j] + factor * x_ref[:, j * LANES : (j + 1) * LANES].astype(F32)
 
     def piece(head, half):
         k, g = head // GROUP, head % GROUP
@@ -269,18 +282,17 @@
     low_tokens = iota((tokens, LANES), 1) < HEAD_SIZE
     for m in range(QUERY_HEADS // 2):
         tile = jnp.where(low_tokens, piece(2 * m, 0), piece(2 * m + 1, 1)).astype(BF16)
-        for b in range(blocks):
-            out_ref[b, :, m * LANES : (m + 1) * LANES] = tile
+        out_ref[:, m * LANES : (m + 1) * LANES] = tile
 
 
 def join(parts):
-    blocks, rows, _ = parts.shape
+    rows = parts[0].shape[0]
     return pl.pallas_call(
         join_kernel,
-        out_shape=jax.ShapeDtypeStruct((blocks, rows // GROUP, QUERY_HEADS * HEAD_SIZE), BF16),
+        out_shape=jax.ShapeDtypeStruct((rows // GROUP, QUERY_HEADS * HEAD_SIZE), BF16),
         compiler_params=params(),
         name="join",
-    )(parts)
+    )(*parts)
 
 
 def side_place(features, count):
@@ -288,13 +300,16 @@
     return (tile, offset) if offset and offset + count <= LANES else (padded(features), 0)
 
 
-def hidden_kernel(attn_ref, residual_ref, w_ref, gain_ref, routes_ref, hidden_ref, out_ref, wide_ref):
+def hidden_kernel(seq_ref, residual_ref, w_ref, gain_ref, routes_ref, *refs):
+    attn_refs, (hidden_ref, out_ref, wide_ref) = refs[:-3], refs[-3:]
     steps, requests, features = residual_ref.shape
     tokens = steps * requests
-    blocks = [attn_ref[b].astype(F32) for b in range(attn_ref.shape[0])]
-    attn = jnp.concatenate(blocks, axis=0).astype(BF16)
+    attn = jnp.concatenate([ref[...].astype(F32) for ref in attn_refs], axis=0).astype(BF16)
     row, column = iota((tokens, tokens), 0), iota((tokens, tokens), 1)
-    reorder = jnp.logical_and(row % requests == column // steps, row // requests == column % steps)
+    devices, share = len(attn_refs), attn_refs[0].shape[0]
+    token = seq_ref[0] + devices - column // share
+    token = jnp.where(token >= devices, token - devices, token) * share + column % share
+    reorder = jnp.logical_and(row % requests == token // steps, row // requests == token % steps)
     attn = dot_nn(reorder.astype(F32).astype(BF16), attn).astype(BF16)
     residual = residual_ref[...].astype(F32).reshape(tokens, features)
     hidden = residual + dot_nt(attn, w_ref[...])
@@ -314,12 +329,14 @@
     out_ref[...] = wide_ref[...].astype(BF16)
 
 
-def hidden_state(attn, residual, w_out, gain, routes):
+def hidden_state(seq_index, attn, residual, w_out, gain, routes):
     steps, requests, features = residual.shape
     tokens = steps * requests
     wide = side_place(features, SIDE_KEYS + EXPERTS)[0] + LANES
+    smem, vmem = pl.BlockSpec(memory_space=pltpu.SMEM), pl.BlockSpec(memory_space=pltpu.VMEM)
     return pl.pallas_call(
         hidden_kernel,
+        in_specs=[smem] + [vmem] * (4 + len(attn)),
         out_shape=(
             jax.ShapeDtypeStruct((tokens, features), F32),
             jax.ShapeDtypeStruct((tokens, wide), BF16),
@@ -327,7 +344,7 @@
         scratch_shapes=[pltpu.VMEM((tokens, wide), F32)],
         compiler_params=params(),
         name="hidden",
-    )(attn, residual, w_out.T, gain.reshape(1, features), routes)
+    )(seq_index, residual, w_out.T, gain.reshape(1, features), routes, *attn)
 
 
 def window_start(first, rows, window):
@@ -335,11 +352,11 @@
 
 
 def gate_up_kernel(
-    features, local, turn, sources, parts, where_ref, w_ref, router_ref, *refs,
+    features, local, turn, sources, devices, where_ref, seq_ref, w_ref, router_ref, *refs,
 ):
     part_refs, refs = refs[:sources], refs[sources:]
-    out_refs, refs = refs[: len(parts)], refs[len(parts) :]
-    pick_ref, range_ref, first_ref, most_ref, x_ref, row_ref, acc_ref = refs
+    out_refs, refs = refs[:devices], refs[devices:]
+    pick_ref, range_ref, first_ref, most_ref, x_ref, row_ref, acc_ref, share_ref = refs
     total = x_ref.shape[0]
     for e, part_ref in enumerate(part_refs):
         x_ref[e * (total // sources) : (e + 1) * (total // sources)] = part_ref[...]
@@ -413,47 +430,44 @@
         ],
         axis=0,
     )
-    begin = 0
-    for part, out_ref in zip(parts, out_refs):
-        blocks = out_ref.shape[0]
-        share = part * PIECES // blocks
-        low = iota((share, LANES), 1) < PIECE_WIDTH
-        for b in range(blocks):
-            piece, start = b % PIECES, begin + b // PIECES * share
-            tile = piece // 2 * LANES
-            gate = acc_ref[start : start + share, tile : tile + LANES]
-            up = acc_ref[start : start + share, width + tile : width + tile + LANES]
-            if piece % 2 == 0:
-                made = jnp.where(low, gate, swap_halves(up))
-            else:
-                made = jnp.where(low, swap_halves(gate), up)
-            out_ref[b, 0:share, :] = made.astype(BF16)
-            if piece == 0:
-                strips = []
-                for at in range(0, share, LANES):
-                    size = min(LANES, share - at)
-                    strip = side[0:4, start + at : start + at + size]
-                    if size < LANES:
-                        strip = jnp.concatenate([strip, jnp.zeros((4, LANES - size), F32)], axis=1)
-                    strips.append(strip)
-                strips.append(jnp.zeros((16 - 4 * len(strips), LANES), F32))
-                strips = jnp.concatenate(strips, axis=0).astype(BF16)
-            out_ref[b, share : share + 16, :] = strips
-        begin += part
-
-
-def gate_up(exp_index, tokens, weights, w_router, parts, blocks, turn):
+    share = share_ref.shape[1] - 16
+    low = iota((share, LANES), 1) < PIECE_WIDTH
+    for b in range(devices):
+        piece, start = b % PIECES, b // PIECES * share
+        tile = piece // 2 * LANES
+        gate = acc_ref[start : start + share, tile : tile + LANES]
+        up = acc_ref[start : start + share, width + tile : width + tile + LANES]
+        if piece % 2 == 0:
+            made = jnp.where(low, gate, swap_halves(up))
+        else:
+            made = jnp.where(low, swap_halves(gate), up)
+        share_ref[b, 0:share, :] = made.astype(BF16)
+        if piece == 0:
+            strips = []
+            for at in range(0, share, LANES):
+                size = min(LANES, share - at)
+                strip = side[0:4, start + at : start + at + size]
+                if size < LANES:
+                    strip = jnp.concatenate([strip, jnp.zeros((4, LANES - size), F32)], axis=1)
+                strips.append(strip)
+            strips.append(jnp.zeros((16 - 4 * len(strips), LANES), F32))
+            strips = jnp.concatenate(strips, axis=0).astype(BF16)
+        share_ref[b, share : share + 16, :] = strips
+    for k, out_ref in enumerate(out_refs):
+        out_ref[...] = share_ref[lax.rem(seq_ref[0] + k, devices)]
+
+
+def gate_up(exp_index, seq_index, tokens, weights, w_router, rows, devices, turn):
     local, _, features, width = weights.shape
     sources, wide = len(tokens), tokens[0].shape[1]
-    total, rows = sources * tokens[0].shape[0], sum(parts)
+    total = sources * tokens[0].shape[0]
+    share = (rows * PIECES // devices + 16, LANES)
     smem, vmem = pl.BlockSpec(memory_space=pltpu.SMEM), pl.BlockSpec(memory_space=pltpu.VMEM)
     return pl.pallas_call(
-        functools.partial(gate_up_kernel, features, local, turn, sources, parts),
-        in_specs=[smem] + [vmem] * (2 + sources),
-        out_specs=(vmem,) * len(parts) + (vmem, vmem, smem, smem),
-        out_shape=tuple(
-            jax.ShapeDtypeStruct((blocks, part * PIECES // blocks + 16, LANES), BF16) for part in parts
-        )
+        functools.partial(gate_up_kernel, features, local, turn, sources, devices),
+        in_specs=[smem] * 2 + [vmem] * (2 + sources),
+        out_specs=(vmem,) * devices + (vmem, vmem, smem, smem),
+        out_shape=(jax.ShapeDtypeStruct(share, BF16),) * devices
         + (
             jax.ShapeDtypeStruct((total, rows), BF16),
             jax.ShapeDtypeStruct((16, LANES), F32),
@@ -464,22 +478,22 @@
             pltpu.VMEM((total, wide), BF16),
             pltpu.VMEM((rows, wide), BF16),
             pltpu.VMEM((rows, 2 * width), F32),
+            pltpu.VMEM((devices,) + share, BF16),
         ],
         compiler_params=params(),
         name="gate_up",
-    )(exp_index, weights, w_router.T, *tokens)
-
-
-def inner_kernel(x_ref, out_ref, logit_ref):
-    blocks, height, _ = x_ref.shape
-    share = height - 16
+    )(exp_index, seq_index, weights, w_router.T, *tokens)
+
+
+def inner_kernel(*refs):
+    x_refs, (out_ref, logit_ref) = refs[:-2], refs[-2:]
+    share = x_refs[0].shape[0] - 16
     half = share // 2
 
     def total(start, size):
-        added = x_ref[0, start : start + size].astype(F32)
-        for b in range(1, blocks):
-            added = added + x_ref[b, start : start + size].astype(F32)
-        return added
+        return functools.reduce(
+            jnp.add, [x_ref[start : start + size].astype(F32) for x_ref in x_refs]
+        )
 
     side = total(share, 16)
     columns, logits = [], []
@@ -492,47 +506,43 @@
     scaled = total(0, share) * jnp.concatenate(columns, axis=0)[0:share]
     made = scaled / (1.0 + jnp.exp(-scaled)) * swap_halves(scaled)
     low = iota((half, LANES), 1) < PIECE_WIDTH
-    made = jnp.where(low, made[0:half], swap_halves(made[half:share])).astype(BF16)
-    for b in range(blocks):
-        out_ref[b] = made
+    out_ref[...] = jnp.where(low, made[0:half], swap_halves(made[half:share])).astype(BF16)
 
 
 def inner(parts):
-    blocks, height, _ = parts.shape
     return pl.pallas_call(
         inner_kernel,
         out_shape=(
-            jax.ShapeDtypeStruct((blocks, (height - 16) // 2, LANES), BF16),
+            jax.ShapeDtypeStruct(((parts[0].shape[0] - 16) // 2, LANES), BF16),
             jax.ShapeDtypeStruct((8, LANES), F32),
         ),
         compiler_params=params(),
         name="inner",
-    )(parts)
-
-
-def down_kernel(features, local, parts, first_ref, range_ref, pick_ref, w_ref, *refs):
-    part_refs, logit_refs, refs = refs[: len(parts)], refs[len(parts) : 2 * len(parts)], refs[2 * len(parts) :]
-    out_refs, (row_ref, made_ref) = refs[:-2], refs[-2:]
+    )(*parts)
+
+
+def down_kernel(features, local, devices, first_ref, seq_ref, range_ref, pick_ref, w_ref, logit_ref, *refs):
+    part_refs, out_refs, (x_ref, row_ref, made_ref) = refs[:devices], refs[devices:-3], refs[-3:]
     total, rows = pick_ref.shape
     width = w_ref.shape[2]
     window = total // 2 + 16
-    begin, logit = 0, []
-    for part, x_ref, logit_ref in zip(parts, part_refs, logit_refs):
-        blocks, half, _ = x_ref.shape
-        share = 2 * half
-        low = iota((half, LANES), 1) < PIECE_WIDTH
-        for b in range(0, blocks, 2):
-            start, tile = begin + b // PIECES * share, b % PIECES // 2 * LANES
-            one, two = x_ref[b].astype(F32), x_ref[b + 1].astype(F32)
-            above = jnp.where(low, one, swap_halves(two)).astype(BF16)
-            below = jnp.where(low, swap_halves(one), two).astype(BF16)
-            row_ref[start : start + half, tile : tile + LANES] = above
-            row_ref[start + half : start + share, tile : tile + LANES] = below
-        for piece in range(blocks // PIECES):
-            for strip in range(-(-share // LANES)):
-                size = min(LANES, share - strip * LANES)
-                logit.append(logit_ref[piece, strip : strip + 1, 0:size])
-        begin += part
+    for k, part_ref in enumerate(part_refs):
+        x_ref[lax.rem(seq_ref[0] + devices - k, devices)] = part_ref[...]
+    half = x_ref.shape[1]
+    share = 2 * half
+    low = iota((half, LANES), 1) < PIECE_WIDTH
+    for b in range(0, devices, 2):
+        start, tile = b // PIECES * share, b % PIECES // 2 * LANES
+        one, two = x_ref[b].astype(F32), x_ref[b + 1].astype(F32)
+        above = jnp.where(low, one, swap_halves(two)).astype(BF16)
+        below = jnp.where(low, swap_halves(one), two).astype(BF16)
+        row_ref[start : start + half, tile : tile + LANES] = above
+        row_ref[start + half : start + share, tile : tile + LANES] = below
+    logit = []
+    for piece in range(devices // PIECES):
+        for strip in range(-(-share // LANES)):
+            size = min(LANES, share - strip * LANES)
+            logit.append(logit_ref[piece, strip : strip + 1, 0:size])
     made_ref[...] = jnp.zeros_like(made_ref)
     for j in range(local):
         start_row = first_ref[j]
@@ -572,19 +582,23 @@
         out_ref[:, tile : tile + LANES] = jnp.where(lane == 1, pair[at, 1:2], side)
 
 
-def down(first, ranges, pick, parts, made, logits, weights, exp_count):
+def down(first, seq_index, ranges, pick, made, logits, weights, exp_count):
     local, features, width = weights.shape
     total, rows = pick.shape
     wide = side_place(features, 2)[0] + LANES
     smem, vmem = pl.BlockSpec(memory_space=pltpu.SMEM), pl.BlockSpec(memory_space=pltpu.VMEM)
     return pl.pallas_call(
-        functools.partial(down_kernel, features, local, parts),
-        in_specs=[smem] + [vmem] * (3 + 2 * len(parts)),
+        functools.partial(down_kernel, features, local, len(made)),
+        in_specs=[smem] * 2 + [vmem] * (4 + len(made)),
         out_shape=(jax.ShapeDtypeStruct((total // exp_count, wide), F32),) * exp_count,
-        scratch_shapes=[pltpu.VMEM((rows, width), BF16), pltpu.VMEM((rows, wide), F32)],
+        scratch_shapes=[
+            pltpu.VMEM((len(made),) + made[0].shape, BF16),
+            pltpu.VMEM((rows, width), BF16),
+            pltpu.VMEM((rows, wide), F32),
+        ],
         compiler_params=params(),
         name="down",
-    )(first, ranges, pick, weights, *made, *logits)
+    )(first, seq_index, ranges, pick, weights, logits, *made)
 
 
 def finish_kernel(hidden_ref, *refs):
@@ -628,8 +642,12 @@
     return lax.ppermute(x, axis, [(i, (i + distance) % count) for i in range(count)])
 
 
-def swap(x, axis):
-    return lax.all_to_all(x, axis, split_axis=0, concat_axis=0, tiled=True)
+def exchange(parts, axis, direction):
+    return [parts[0]] + [send(part, axis, direction * k) for k, part in enumerate(parts) if k]
+
+
+def gather(block, axis):
+    return exchange([block] * lax.axis_size(axis), axis, 1)
 
 
 def local(
@@ -656,33 +674,27 @@
     page_rows = key_value_cache.shape[2]
     pool = key_value_cache.reshape(-1, page_rows, 2, KV_WIDTH)
 
-    shares = attend(queries, new_key_value, pool, page_table, cache_len, seq_index)
-    shares = swap(shares.reshape(seq_count, -1, KV_WIDTH + LANES), "seq")
-    attn = join(shares)
+    shares = attend(
+        queries, new_key_value, pool, page_table, cache_len, seq_index, seq_count
+    )
+    attn = join(exchange(shares, "seq", 1))
     w_gate_up, attn = lax.optimization_barrier((w_gate_up, attn))
-    attn = swap(attn, "seq")
+    gathered = gather(attn, "seq")
     gate_up_weights = w_gate_up.transpose(0, 2, 1, 3)
-    gate_up_weights, attn = lax.optimization_barrier((gate_up_weights, attn))
-    hidden, outgoing = hidden_state(attn, residual, w_out, norm_gain, routes)
-    incoming = [outgoing] + [send(outgoing, "exp", k) for k in range(1, exp_count)]
+    gate_up_weights, gathered = lax.optimization_barrier((gate_up_weights, gathered))
+    hidden, outgoing = hidden_state(seq_index, gathered, residual, w_out, norm_gain, routes)
+    incoming = gather(outgoing, "exp")
     pieces = seq_count // PIECES
-    units = -(-ROUND_ROWS // (32 * pieces))
-    parts = tuple(32 * pieces * count for count in (-(-units // 2), units // 2))
-    rows = sum(parts)
-
-    def logits_of(row_logits):
-        if pieces == 1:
-            return row_logits[None]
-        return lax.all_gather(row_logits, "seq")[::PIECES]
+    rows = -(-ROUND_ROWS // (32 * pieces)) * 32 * pieces
 
     def one_round(turn):
         *partial, pick, ranges, first, most = gate_up(
-            exp_index, incoming, gate_up_weights, w_router, parts, seq_count, turn
+            exp_index, seq_index, incoming, gate_up_weights, w_router, rows, seq_count, turn
         )
-        made, logits = zip(*[inner(swap(part, "seq")) for part in partial])
-        made = [swap(part, "seq") for part in made]
-        logits = [logits_of(part) for part in logits]
-        return down(first, ranges, pick, parts, made, logits, w_down, exp_count), most
+        made, logits = inner(exchange(partial, "seq", 1))
+        logits = logits[None] if pieces == 1 else lax.all_gather(logits, "seq")[::PIECES]
+        made = gather(made, "seq")
+        return down(first, seq_index, ranges, pick, made, logits, w_down, exp_count), most
 
     made, most = one_round(0)
     pairs = w_gate_up.shape[0] * exp_count * steps * CAP
@@ -695,8 +707,7 @@
             lambda made: made,
             made,
         )
-    made = [made[0]] + [send(made[k], "exp", -k) for k in range(1, exp_count)]
-    return finish(made, hidden, (steps, requests, features))
+    return finish(exchange(made, "exp", -1), hidden, (steps, requests, features))
 
 
 def solution(mesh):

time: 108 us -> 93.1 us (0.86)
  starting transfers between devices: 20.9 us -> 50 us
  blocking collectives: 26.4 us -> 0 us
  waiting for transfers between devices: 31.5 us -> 18.5 us
  Pallas kernels: 22.4 us -> 20 us
  local copies, waits for them, and re-layouts: 4.87 us -> 3.46 us
    ppermute x6 -> x34, starting transfers between devices: 7.03 us -> 50 us  [send(): lax.ppermute(x, axis, [(i, (i + distance) % count) for i in range(count)])]
    all_to_all x4 -> x0, waiting for transfers between devices: 26.8 us -> none  [swap(): return lax.all_to_all(x, axis, split_axis=0, concat_axis=0, tiled=True)]
    all_to_all x2 -> x0, blocking collectives: 26.4 us -> none  [swap(): return lax.all_to_all(x, axis, split_axis=0, concat_axis=0, tiled=True)]
    ppermute x6 -> x34, waiting for transfers between devices: 4.62 us -> 18.5 us  [send(): lax.ppermute(x, axis, [(i, (i + distance) % count) for i in range(count)])]
    all_to_all x4 -> x0, starting transfers between devices: 13.8 us -> none  [swap(): return lax.all_to_all(x, axis, split_axis=0, concat_axis=0, tiled=True)]
    optimization_barrier x1, local copies, waits for them, and re-layouts: 4.83 us -> 2.7 us  [local(): w_gate_up, attn = lax.optimization_barrier((w_gate_up, attn))]
    pallas_call x6 -> x5, Pallas kernels: 16.8 us -> 15 us  [the longest x1 11.6 us: attend(): pl.pallas_call(functools.partial(attend_kernel, classes, devices), in_spe...]
  transfers between devices with their start and end apart: 10 -> 34, of which waited for: 8 -> 13; matrix products, arithmetic and copies ran while one was open for 5% -> 3% of each run, Pallas kernels for 2% -> 0%
where the time goes in v4:
time: 93.1 us; the launch traced here: 92.8 us
  starting transfers between devices  50 us (54%)
  Pallas kernels  20 us (21%)
  waiting for transfers between devices  18.5 us (20%)
  local copies, waits for them, and re-layouts  3.46 us (4%)
    ppermute x34, starting transfers between devices, send(): lax.ppermute(x, axis, [(i, (i + distance) % count) for i in range(count)])  50 us
    ppermute x34, waiting for transfers between devices, send(): lax.ppermute(x, axis, [(i, (i + distance) % count) for i in range(count)])  18.5 us
    pallas_call x1, Pallas kernels, attend(): pl.pallas_call(functools.partial(attend_kernel, classes, devices), in_spe...  11.6 us
    pallas_call x1, Pallas kernels, gate_up(): pl.pallas_call(functools.partial(gate_up_kernel, features, local, turn, s...  4.25 us
    optimization_barrier x1, local copies, waits for them, and re-layouts, local(): w_gate_up, attn = lax.optimization_barrier((w_gate_up, attn))  2.7 us
    pallas_call x1, Pallas kernels, down(): pl.pallas_call(functools.partial(down_kernel, features, local, len(made))...  2.12 us
  transfers between devices with their start and end apart: 34, of which 13 were waited for; matrix products, arithmetic and copies ran while one was open for 3% of the time, Pallas kernels for 0%

profile of v4, /device:TPU:0, one launch (start us, length us, event | category | flops | bytes accessed | tf_op | source)
XLA Modules:
  0.0 92.8 jit_solution(16202901361433183529)
XLA Ops:
  0.0 11.6 %attend.1 = (bf16[12,640]{1,0:T(8,128)(2,1)}, bf16[12,640]{1,0:T(8,128)(2,1)}, bf16[12,640]{1,0:T(8,128)(2,1)}, bf16[12,640]{1,0:T(8,128)(2,1)}, bf16[12,640]{1,...) custom-call(s32[8,8]{1,0:T(8,128)} %table_ref.1, s32[8]{0:T(128)} %len_ref.1, ...), custom_call_target="tpu_custom_call" | custom-call | tf_op jit(solution)/shard_map/attend/pallas_call | solution.py:235
  12.3 1.6 %collective-permute-start.16 = (bf16[12,640]{1,0:T(8,128)(2,1)}, bf16[12,640]{1,0:T(8,128)(2,1)S(1)}, u32[]{:S(2)}, u32[]{:S(2)}) collective-permute-start(bf16[12,640]{1,0:T(8,128)(2,1)} %get-tuple-element.115), channel_id=1, source_target_pairs={{0,12},{4,16},{8,20},{12,24},{16,28},{20,0},{24,4},{28,8},{1,13},{... | collective-permute-start | bytes 46088 | tf_op jit(solution)/shard_map/ppermute | solution.py:642
  13.9 3.1 %collective-permute-start.17 = (bf16[12,640]{1,0:T(8,128)(2,1)}, bf16[12,640]{1,0:T(8,128)(2,1)S(1)}, u32[]{:S(2)}, u32[]{:S(2)}) collective-permute-start(bf16[12,640]{1,0:T(8,128)(2,1)} %get-tuple-element.116), channel_id=1, source_target_pairs={{0,16},{4,20},{8,24},{12,28},{16,0},{20,4},{24,8},{28,12},{1,17},{... | collective-permute-start | bytes 46088 | tf_op jit(solution)/shard_map/ppermute | solution.py:642
  17.0 1.4 %collective-permute-done.14.refs_1_ = bf16[12,640]{1,0:T(8,128)(2,1)S(1)} collective-permute-done((bf16[12,640]{1,0:T(8,128)(2,1)}, bf16[12,640]{1,0:T(8,128)(2,1)S(1)}, u32[]{:S(2)}, u32[]{:S(2)}) %collective-permute-start.14) | collective-permute-done | bytes 15392 | tf_op jit(solution)/shard_map/ppermute | solution.py:642
  18.4 1.6 %collective-permute-start.19 = (bf16[12,640]{1,0:T(8,128)(2,1)}, bf16[12,640]{1,0:T(8,128)(2,1)S(1)}, u32[]{:S(2)}, u32[]{:S(2)}) collective-permute-start(bf16[12,640]{1,0:T(8,128)(2,1)} %get-tuple-element.118), channel_id=1, source_target_pairs={{0,24},{4,28},{8,0},{12,4},{16,8},{20,12},{24,16},{28,20},{1,25},{... | collective-permute-start | bytes 46088 | tf_op jit(solution)/shard_map/ppermute | solution.py:642
  20.0 1.4 %collective-permute-start.20 = (bf16[12,640]{1,0:T(8,128)(2,1)}, bf16[12,640]{1,0:T(8,128)(2,1)S(1)}, u32[]{:S(2)}, u32[]{:S(2)}) collective-permute-start(bf16[12,640]{1,0:T(8,128)(2,1)} %get-tuple-element.119), channel_id=1, source_target_pairs={{0,28},{4,0},{8,4},{12,8},{16,12},{20,16},{24,20},{28,24},{1,29},{... | collective-permute-start | bytes 46088 | tf_op jit(solution)/shard_map/ppermute | solution.py:642
  22.5 1.5 %collective-permute-done.20.refs_7_ = bf16[12,640]{1,0:T(8,128)(2,1)S(1)} collective-permute-done((bf16[12,640]{1,0:T(8,128)(2,1)}, bf16[12,640]{1,0:T(8,128)(2,1)S(1)}, u32[]{:S(2)}, u32[]{:S(2)}) %collective-permute-start.20) | collective-permute-done | bytes 15392 | tf_op jit(solution)/shard_map/ppermute | solution.py:642
  25.2 2.4 %collective-permute-start.21 = (bf16[4,1536]{1,0:T(4,128)(2,1)S(1)}, bf16[4,1536]{1,0:T(4,128)(2,1)S(1)}, u32[]{:S(2)}, u32[]{:S(2)}) collective-permute-start(bf16[4,1536]{1,0:T(4,128)(2,1)S(1)} %join.1.refs_0_), channel_id=1, source_target_pairs={{0,4},{4,8},{8,12},{12,16},{16,20},{20,24},{24,28},{28,0},{1,5},{5... | collective-permute-start | bytes 36872 | tf_op jit(solution)/shard_map/ppermute | solution.py:642
  27.6 2.0 %collective-permute-start.22 = (bf16[4,1536]{1,0:T(4,128)(2,1)S(1)}, bf16[4,1536]{1,0:T(4,128)(2,1)S(1)}, u32[]{:S(2)}, u32[]{:S(2)}) collective-permute-start(bf16[4,1536]{1,0:T(4,128)(2,1)S(1)} %join.1.refs_0_), channel_id=1, source_target_pairs={{0,8},{4,12},{8,16},{12,20},{16,24},{20,28},{24,0},{28,4},{1,9},{5... | collective-permute-start | bytes 36872 | tf_op jit(solution)/shard_map/ppermute | solution.py:642
  29.9 2.0 %collective-permute-start.24 = (bf16[4,1536]{1,0:T(4,128)(2,1)S(1)}, bf16[4,1536]{1,0:T(4,128)(2,1)S(1)}, u32[]{:S(2)}, u32[]{:S(2)}) collective-permute-start(bf16[4,1536]{1,0:T(4,128)(2,1)S(1)} %join.1.refs_0_), channel_id=1, source_target_pairs={{0,16},{4,20},{8,24},{12,28},{16,0},{20,4},{24,8},{28,12},{1,17},{... | collective-permute-start | bytes 36872 | tf_op jit(solution)/shard_map/ppermute | solution.py:642
  32.0 2.4 %collective-permute-start.25 = (bf16[4,1536]{1,0:T(4,128)(2,1)S(1)}, bf16[4,1536]{1,0:T(4,128)(2,1)S(1)}, u32[]{:S(2)}, u32[]{:S(2)}) collective-permute-start(bf16[4,1536]{1,0:T(4,128)(2,1)S(1)} %join.1.refs_0_), channel_id=1, source_target_pairs={{0,20},{4,24},{8,28},{12,0},{16,4},{20,8},{24,12},{28,16},{1,21},{... | collective-permute-start | bytes 36872 | tf_op jit(solution)/shard_map/ppermute | solution.py:642
  34.3 1.5 %collective-permute-start.26 = (bf16[4,1536]{1,0:T(4,128)(2,1)S(1)}, bf16[4,1536]{1,0:T(4,128)(2,1)S(1)}, u32[]{:S(2)}, u32[]{:S(2)}) collective-permute-start(bf16[4,1536]{1,0:T(4,128)(2,1)S(1)} %join.1.refs_0_), channel_id=1, source_target_pairs={{0,24},{4,28},{8,0},{12,4},{16,8},{20,12},{24,16},{28,20},{1,25},{... | collective-permute-start | bytes 36872 | tf_op jit(solution)/shard_map/ppermute | solution.py:642
  35.8 1.5 %collective-permute-start.27 = (bf16[4,1536]{1,0:T(4,128)(2,1)S(1)}, bf16[4,1536]{1,0:T(4,128)(2,1)S(1)}, u32[]{:S(2)}, u32[]{:S(2)}) collective-permute-start(bf16[4,1536]{1,0:T(4,128)(2,1)S(1)} %join.1.refs_0_), channel_id=1, source_target_pairs={{0,28},{4,0},{8,4},{12,8},{16,12},{20,16},{24,20},{28,24},{1,29},{... | collective-permute-start | bytes 36872 | tf_op jit(solution)/shard_map/ppermute | solution.py:642
  37.3 2.7 %copy.16 = bf16[10,192,2,512]{3,1,2,0:T(8,128)(2,1)} copy(bf16[10,192,2,512]{3,2,1,0:T(2,128)(2,1)S(1)} %copy-done.6) | data formatting | bytes 7864320 | tf_op jit(solution)/shard_map/optimization_barrier | solution.py:681
  40.6 3.0 %collective-permute-start.29 = (bf16[32,256]{1,0:T(8,128)(2,1)S(1)}, bf16[32,256]{1,0:T(8,128)(2,1)S(1)}, u32[]{:S(2)}, u32[]{:S(2)}) collective-permute-start(bf16[32,256]{1,0:T(8,128)(2,1)S(1)} %get-tuple-element.132.refs_0_), channel_id=1, source_target_pairs={{0,2},{1,3},{2,0},{3,1},{4,6},{5,7},{6,4},{7,5},{8,10},{9,11},{10,... | collective-permute-start | bytes 49160 | tf_op jit(solution)/shard_map/ppermute | solution.py:642
  43.7 1.4 %collective-permute-start.30 = (bf16[32,256]{1,0:T(8,128)(2,1)S(1)}, bf16[32,256]{1,0:T(8,128)(2,1)S(1)}, u32[]{:S(2)}, u32[]{:S(2)}) collective-permute-start(bf16[32,256]{1,0:T(8,128)(2,1)S(1)} %get-tuple-element.132.refs_0_), channel_id=1, source_target_pairs={{0,3},{1,0},{2,1},{3,2},{4,7},{5,4},{6,5},{7,6},{8,11},{9,8},{10,9... | collective-permute-start | bytes 49160 | tf_op jit(solution)/shard_map/ppermute | solution.py:642
  46.5 4.3 %gate_up.3 = (bf16[368,128]{1,0:T(8,128)(2,1)S(1)}, bf16[368,128]{1,0:T(8,128)(2,1)S(1)}, bf16[368,128]{1,0:T(8,128)(2,1)S(1)}, bf16[368,128]{1,0:T(8,128)(2,1)S...) custom-call(s32[1]{0:T(128)} %bitcast.7.where_ref, ...), custom_call_target="tpu_custom_call" | custom-call | tf_op jit(solution)/shard_map/gate_up/pallas_call | solution.py:466
  52.3 2.0 %collective-permute-start.33 = (bf16[368,128]{1,0:T(8,128)(2,1)S(1)}, bf16[368,128]{1,0:T(8,128)(2,1)S(1)}, u32[]{:S(2)}, u32[]{:S(2)}) collective-permute-start(bf16[368,128]{1,0:T(8,128)(2,1)S(1)} %get-tuple-element.140), channel_id=1, source_target_pairs={{0,12},{4,16},{8,20},{12,24},{16,28},{20,0},{24,4},{28,8},{1,13},{... | collective-permute-start | bytes 282632 | tf_op jit(solution)/shard_map/ppermute | solution.py:642
  54.3 1.8 %collective-permute-start.34 = (bf16[368,128]{1,0:T(8,128)(2,1)S(1)}, bf16[368,128]{1,0:T(8,128)(2,1)S(1)}, u32[]{:S(2)}, u32[]{:S(2)}) collective-permute-start(bf16[368,128]{1,0:T(8,128)(2,1)S(1)} %get-tuple-element.141), channel_id=1, source_target_pairs={{0,16},{4,20},{8,24},{12,28},{16,0},{20,4},{24,8},{28,12},{1,17},{... | collective-permute-start | bytes 282632 | tf_op jit(solution)/shard_map/ppermute | solution.py:642
  56.1 3.3 %collective-permute-start.35 = (bf16[368,128]{1,0:T(8,128)(2,1)S(1)}, bf16[368,128]{1,0:T(8,128)(2,1)S(1)}, u32[]{:S(2)}, u32[]{:S(2)}) collective-permute-start(bf16[368,128]{1,0:T(8,128)(2,1)S(1)} %get-tuple-element.142), channel_id=1, source_target_pairs={{0,20},{4,24},{8,28},{12,0},{16,4},{20,8},{24,12},{28,16},{1,21},{... | collective-permute-start | bytes 282632 | tf_op jit(solution)/shard_map/ppermute | solution.py:642
  59.6 1.8 %collective-permute-start.37 = (bf16[368,128]{1,0:T(8,128)(2,1)S(1)}, bf16[368,128]{1,0:T(8,128)(2,1)S(1)}, u32[]{:S(2)}, u32[]{:S(2)}) collective-permute-start(bf16[368,128]{1,0:T(8,128)(2,1)S(1)} %get-tuple-element.144), channel_id=1, source_target_pairs={{0,28},{4,0},{8,4},{12,8},{16,12},{20,16},{24,20},{28,24},{1,29},{... | collective-permute-start | bytes 282632 | tf_op jit(solution)/shard_map/ppermute | solution.py:642
  61.4 5.3 %collective-permute-done.33.refs_3_ = bf16[368,128]{1,0:T(8,128)(2,1)S(1)} collective-permute-done((bf16[368,128]{1,0:T(8,128)(2,1)S(1)}, bf16[368,128]{1,0:T(8,128)(2,1)S(1)}, u32[]{:S(2)}, u32[]{:S(2)}) %collective-permute-start.33) | collective-permute-done | bytes 94240 | tf_op jit(solution)/shard_map/ppermute | solution.py:642
  66.7 2.1 %collective-permute-done.36.refs_6_ = bf16[368,128]{1,0:T(8,128)(2,1)S(1)} collective-permute-done((bf16[368,128]{1,0:T(8,128)(2,1)S(1)}, bf16[368,128]{1,0:T(8,128)(2,1)S(1)}, u32[]{:S(2)}, u32[]{:S(2)}) %collective-permute-start.36) | collective-permute-done | bytes 94240 | tf_op jit(solution)/shard_map/ppermute | solution.py:642
  69.2 2.5 %collective-permute-start.38 = (bf16[176,128]{1,0:T(8,128)(2,1)S(1)}, bf16[176,128]{1,0:T(8,128)(2,1)S(1)}, u32[]{:S(2)}, u32[]{:S(2)}) collective-permute-start(bf16[176,128]{1,0:T(8,128)(2,1)S(1)} %get-tuple-element.146.refs_0_), channel_id=1, source_target_pairs={{0,4},{4,8},{8,12},{12,16},{16,20},{20,24},{24,28},{28,0},{1,5},{5... | collective-permute-start | bytes 135176 | tf_op jit(solution)/shard_map/ppermute | solution.py:642
  71.7 2.9 %collective-permute-start.39 = (bf16[176,128]{1,0:T(8,128)(2,1)S(1)}, bf16[176,128]{1,0:T(8,128)(2,1)S(1)}, u32[]{:S(2)}, u32[]{:S(2)}) collective-permute-start(bf16[176,128]{1,0:T(8,128)(2,1)S(1)} %get-tuple-element.146.refs_0_), channel_id=1, source_target_pairs={{0,8},{4,12},{8,16},{12,20},{16,24},{20,28},{24,0},{28,4},{1,9},{5... | collective-permute-start | bytes 135176 | tf_op jit(solution)/shard_map/ppermute | solution.py:642
  75.0 2.0 %collective-permute-start.41 = (bf16[176,128]{1,0:T(8,128)(2,1)S(1)}, bf16[176,128]{1,0:T(8,128)(2,1)S(1)}, u32[]{:S(2)}, u32[]{:S(2)}) collective-permute-start(bf16[176,128]{1,0:T(8,128)(2,1)S(1)} %get-tuple-element.146.refs_0_), channel_id=1, source_target_pairs={{0,16},{4,20},{8,24},{12,28},{16,0},{20,4},{24,8},{28,12},{1,17},{... | collective-permute-start | bytes 135176 | tf_op jit(solution)/shard_map/ppermute | solution.py:642
  77.0 2.9 %collective-permute-start.42 = (bf16[176,128]{1,0:T(8,128)(2,1)S(1)}, bf16[176,128]{1,0:T(8,128)(2,1)S(1)}, u32[]{:S(2)}, u32[]{:S(2)}) collective-permute-start(bf16[176,128]{1,0:T(8,128)(2,1)S(1)} %get-tuple-element.146.refs_0_), channel_id=1, source_target_pairs={{0,20},{4,24},{8,28},{12,0},{16,4},{20,8},{24,12},{28,16},{1,21},{... | collective-permute-start | bytes 135176 | tf_op jit(solution)/shard_map/ppermute | solution.py:642
  79.9 1.6 %collective-permute-start.43 = (bf16[176,128]{1,0:T(8,128)(2,1)S(1)}, bf16[176,128]{1,0:T(8,128)(2,1)S(1)}, u32[]{:S(2)}, u32[]{:S(2)}) collective-permute-start(bf16[176,128]{1,0:T(8,128)(2,1)S(1)} %get-tuple-element.146.refs_0_), channel_id=1, source_target_pairs={{0,24},{4,28},{8,0},{12,4},{16,8},{20,12},{24,16},{28,20},{1,25},{... | collective-permute-start | bytes 135176 | tf_op jit(solution)/shard_map/ppermute | solution.py:642
  83.0 1.2 %collective-permute-done.43.refs_6_ = bf16[176,128]{1,0:T(8,128)(2,1)S(1)} collective-permute-done((bf16[176,128]{1,0:T(8,128)(2,1)S(1)}, bf16[176,128]{1,0:T(8,128)(2,1)S(1)}, u32[]{:S(2)}, u32[]{:S(2)}) %collective-permute-start.43) | collective-permute-done | bytes 45088 | tf_op jit(solution)/shard_map/ppermute | solution.py:642
  84.2 1.2 %collective-permute-done.44.refs_7_ = bf16[176,128]{1,0:T(8,128)(2,1)S(1)} collective-permute-done((bf16[176,128]{1,0:T(8,128)(2,1)S(1)}, bf16[176,128]{1,0:T(8,128)(2,1)S(1)}, u32[]{:S(2)}, u32[]{:S(2)}) %collective-permute-start.44) | collective-permute-done | bytes 45088 | tf_op jit(solution)/shard_map/ppermute | solution.py:642
  85.5 2.1 %down.3 = (f32[32,256]{1,0:T(8,128)S(1)}, f32[32,256]{1,0:T(8,128)S(1)}, f32[32,256]{1,0:T(8,128)S(1)}, f32[32,256]{1,0:T(8,128)S(1)}) custom-call(s32[16]{0:T(128)S(1)} %get-tuple-element.134.first_ref, s32[1]{0:T(128)} %bitcast.2.seq_ref, f32[16,128]{1,0:T(8,128)S(1)} %get-tuple-element.135.range_ref, bf16[128,352]{1,0:T(8,128)(2,1)S(1)} %get-tuple-element.136.pick_ref, ...), custom_call_target="tpu_custom_call" | custom-call | tf_op jit(solution)/shard_map/down/pallas_call | solution.py:590
  89.3 2.4 %collective-permute-done.46.refs_2_ = f32[32,256]{1,0:T(8,128)S(1)} collective-permute-done((f32[32,256]{1,0:T(8,128)S(1)}, f32[32,256]{1,0:T(8,128)S(1)}, u32[]{:S(2)}, u32[]{:S(2)}) %collective-permute-start.46) | collective-permute-done | bytes 32800 | tf_op jit(solution)/shard_map/ppermute | solution.py:642
  (61 shorter events, 11.6 us)
Async XLA Ops:
  11.6 6.7 %collective-permute-start.14 = (bf16[12,640]{1,0:T(8,128)(2,1)}, bf16[12,640]{1,0:T(8,128)(2,1)S(1)}, u32[]{:S(2)}, u32[]{:S(2)}) collective-permute-start(bf16[12,640]{1,0:T(8,128)(2,1)} %get-tuple-element.113), channel_id=1, source_target_pairs={{0,4},{4,8},{8,12},{12,16},{16,20},{20,24},{24,28},{28,0},{1,5},{5... | collective-permute-start | bytes 46088 | tf_op jit(solution)/shard_map/ppermute | solution.py:642
  12.3 7.7 %collective-permute-start.15 = (bf16[12,640]{1,0:T(8,128)(2,1)}, bf16[12,640]{1,0:T(8,128)(2,1)S(1)}, u32[]{:S(2)}, u32[]{:S(2)}) collective-permute-start(bf16[12,640]{1,0:T(8,128)(2,1)} %get-tuple-element.114), channel_id=1, source_target_pairs={{0,8},{4,12},{8,16},{12,20},{16,24},{20,28},{24,0},{28,4},{1,9},{5... | collective-permute-start | bytes 46088 | tf_op jit(solution)/shard_map/ppermute | solution.py:642
  12.3 9.0 %collective-permute-start.16 = (bf16[12,640]{1,0:T(8,128)(2,1)}, bf16[12,640]{1,0:T(8,128)(2,1)S(1)}, u32[]{:S(2)}, u32[]{:S(2)}) collective-permute-start(bf16[12,640]{1,0:T(8,128)(2,1)} %get-tuple-element.115), channel_id=1, source_target_pairs={{0,12},{4,16},{8,20},{12,24},{16,28},{20,0},{24,4},{28,8},{1,13},{... | collective-permute-start | bytes 46088 | tf_op jit(solution)/shard_map/ppermute | solution.py:642
  13.9 7.5 %collective-permute-start.17 = (bf16[12,640]{1,0:T(8,128)(2,1)}, bf16[12,640]{1,0:T(8,128)(2,1)S(1)}, u32[]{:S(2)}, u32[]{:S(2)}) collective-permute-start(bf16[12,640]{1,0:T(8,128)(2,1)} %get-tuple-element.116), channel_id=1, source_target_pairs={{0,16},{4,20},{8,24},{12,28},{16,0},{20,4},{24,8},{28,12},{1,17},{... | collective-permute-start | bytes 46088 | tf_op jit(solution)/shard_map/ppermute | solution.py:642
  17.0 4.9 %collective-permute-start.18 = (bf16[12,640]{1,0:T(8,128)(2,1)}, bf16[12,640]{1,0:T(8,128)(2,1)S(1)}, u32[]{:S(2)}, u32[]{:S(2)}) collective-permute-start(bf16[12,640]{1,0:T(8,128)(2,1)} %get-tuple-element.117), channel_id=1, source_target_pairs={{0,20},{4,24},{8,28},{12,0},{16,4},{20,8},{24,12},{28,16},{1,21},{... | collective-permute-start | bytes 46088 | tf_op jit(solution)/shard_map/ppermute | solution.py:642
  18.4 4.1 %collective-permute-start.19 = (bf16[12,640]{1,0:T(8,128)(2,1)}, bf16[12,640]{1,0:T(8,128)(2,1)S(1)}, u32[]{:S(2)}, u32[]{:S(2)}) collective-permute-start(bf16[12,640]{1,0:T(8,128)(2,1)} %get-tuple-element.118), channel_id=1, source_target_pairs={{0,24},{4,28},{8,0},{12,4},{16,8},{20,12},{24,16},{28,20},{1,25},{... | collective-permute-start | bytes 46088 | tf_op jit(solution)/shard_map/ppermute | solution.py:642
  20.0 4.0 %collective-permute-start.20 = (bf16[12,640]{1,0:T(8,128)(2,1)}, bf16[12,640]{1,0:T(8,128)(2,1)S(1)}, u32[]{:S(2)}, u32[]{:S(2)}) collective-permute-start(bf16[12,640]{1,0:T(8,128)(2,1)} %get-tuple-element.119), channel_id=1, source_target_pairs={{0,28},{4,0},{8,4},{12,8},{16,12},{20,16},{24,20},{28,24},{1,29},{... | collective-permute-start | bytes 46088 | tf_op jit(solution)/shard_map/ppermute | solution.py:642
  25.2 9.1 %collective-permute-start.21 = (bf16[4,1536]{1,0:T(4,128)(2,1)S(1)}, bf16[4,1536]{1,0:T(4,128)(2,1)S(1)}, u32[]{:S(2)}, u32[]{:S(2)}) collective-permute-start(bf16[4,1536]{1,0:T(4,128)(2,1)S(1)} %join.1.refs_0_), channel_id=1, source_target_pairs={{0,4},{4,8},{8,12},{12,16},{16,20},{20,24},{24,28},{28,0},{1,5},{5... | collective-permute-start | bytes 36872 | tf_op jit(solution)/shard_map/ppermute | solution.py:642
  27.6 8.2 %collective-permute-start.22 = (bf16[4,1536]{1,0:T(4,128)(2,1)S(1)}, bf16[4,1536]{1,0:T(4,128)(2,1)S(1)}, u32[]{:S(2)}, u32[]{:S(2)}) collective-permute-start(bf16[4,1536]{1,0:T(4,128)(2,1)S(1)} %join.1.refs_0_), channel_id=1, source_target_pairs={{0,8},{4,12},{8,16},{12,20},{16,24},{20,28},{24,0},{28,4},{1,9},{5... | collective-permute-start | bytes 36872 | tf_op jit(solution)/shard_map/ppermute | solution.py:642
  29.6 10.4 %collective-permute-start.23 = (bf16[4,1536]{1,0:T(4,128)(2,1)S(1)}, bf16[4,1536]{1,0:T(4,128)(2,1)S(1)}, u32[]{:S(2)}, u32[]{:S(2)}) collective-permute-start(bf16[4,1536]{1,0:T(4,128)(2,1)S(1)} %join.1.refs_0_), channel_id=1, source_target_pairs={{0,12},{4,16},{8,20},{12,24},{16,28},{20,0},{24,4},{28,8},{1,13},{... | collective-permute-start | bytes 36872 | tf_op jit(solution)/shard_map/ppermute | solution.py:642
  29.9 10.1 %collective-permute-start.24 = (bf16[4,1536]{1,0:T(4,128)(2,1)S(1)}, bf16[4,1536]{1,0:T(4,128)(2,1)S(1)}, u32[]{:S(2)}, u32[]{:S(2)}) collective-permute-start(bf16[4,1536]{1,0:T(4,128)(2,1)S(1)} %join.1.refs_0_), channel_id=1, source_target_pairs={{0,16},{4,20},{8,24},{12,28},{16,0},{20,4},{24,8},{28,12},{1,17},{... | collective-permute-start | bytes 36872 | tf_op jit(solution)/shard_map/ppermute | solution.py:642
  32.0 8.1 %collective-permute-start.25 = (bf16[4,1536]{1,0:T(4,128)(2,1)S(1)}, bf16[4,1536]{1,0:T(4,128)(2,1)S(1)}, u32[]{:S(2)}, u32[]{:S(2)}) collective-permute-start(bf16[4,1536]{1,0:T(4,128)(2,1)S(1)} %join.1.refs_0_), channel_id=1, source_target_pairs={{0,20},{4,24},{8,28},{12,0},{16,4},{20,8},{24,12},{28,16},{1,21},{... | collective-permute-start | bytes 36872 | tf_op jit(solution)/shard_map/ppermute | solution.py:642
  34.3 5.7 %collective-permute-start.26 = (bf16[4,1536]{1,0:T(4,128)(2,1)S(1)}, bf16[4,1536]{1,0:T(4,128)(2,1)S(1)}, u32[]{:S(2)}, u32[]{:S(2)}) collective-permute-start(bf16[4,1536]{1,0:T(4,128)(2,1)S(1)} %join.1.refs_0_), channel_id=1, source_target_pairs={{0,24},{4,28},{8,0},{12,4},{16,8},{20,12},{24,16},{28,20},{1,25},{... | collective-permute-start | bytes 36872 | tf_op jit(solution)/shard_map/ppermute | solution.py:642
  35.8 4.3 %collective-permute-start.27 = (bf16[4,1536]{1,0:T(4,128)(2,1)S(1)}, bf16[4,1536]{1,0:T(4,128)(2,1)S(1)}, u32[]{:S(2)}, u32[]{:S(2)}) collective-permute-start(bf16[4,1536]{1,0:T(4,128)(2,1)S(1)} %join.1.refs_0_), channel_id=1, source_target_pairs={{0,28},{4,0},{8,4},{12,8},{16,12},{20,16},{24,20},{28,24},{1,29},{... | collective-permute-start | bytes 36872 | tf_op jit(solution)/shard_map/ppermute | solution.py:642
  40.6 4.5 %collective-permute-start.28 = (bf16[32,256]{1,0:T(8,128)(2,1)S(1)}, bf16[32,256]{1,0:T(8,128)(2,1)S(1)}, u32[]{:S(2)}, u32[]{:S(2)}) collective-permute-start(bf16[32,256]{1,0:T(8,128)(2,1)S(1)} %get-tuple-element.132.refs_0_), channel_id=1, source_target_pairs={{0,1},{1,2},{2,3},{3,0},{4,5},{5,6},{6,7},{7,4},{8,9},{9,10},{10,1... | collective-permute-start | bytes 49160 | tf_op jit(solution)/shard_map/ppermute | solution.py:642
  40.6 4.8 %collective-permute-start.29 = (bf16[32,256]{1,0:T(8,128)(2,1)S(1)}, bf16[32,256]{1,0:T(8,128)(2,1)S(1)}, u32[]{:S(2)}, u32[]{:S(2)}) collective-permute-start(bf16[32,256]{1,0:T(8,128)(2,1)S(1)} %get-tuple-element.132.refs_0_), channel_id=1, source_target_pairs={{0,2},{1,3},{2,0},{3,1},{4,6},{5,7},{6,4},{7,5},{8,10},{9,11},{10,... | collective-permute-start | bytes 49160 | tf_op jit(solution)/shard_map/ppermute | solution.py:642
  50.8 8.6 %collective-permute-start.31 = (bf16[368,128]{1,0:T(8,128)(2,1)S(1)}, bf16[368,128]{1,0:T(8,128)(2,1)S(1)}, u32[]{:S(2)}, u32[]{:S(2)}) collective-permute-start(bf16[368,128]{1,0:T(8,128)(2,1)S(1)} %get-tuple-element.138), channel_id=1, source_target_pairs={{0,4},{4,8},{8,12},{12,16},{16,20},{20,24},{24,28},{28,0},{1,5},{5... | collective-permute-start | bytes 282632 | tf_op jit(solution)/shard_map/ppermute | solution.py:642
  51.3 8.3 %collective-permute-start.32 = (bf16[368,128]{1,0:T(8,128)(2,1)S(1)}, bf16[368,128]{1,0:T(8,128)(2,1)S(1)}, u32[]{:S(2)}, u32[]{:S(2)}) collective-permute-start(bf16[368,128]{1,0:T(8,128)(2,1)S(1)} %get-tuple-element.139), channel_id=1, source_target_pairs={{0,8},{4,12},{8,16},{12,20},{16,24},{20,28},{24,0},{28,4},{1,9},{5... | collective-permute-start | bytes 282632 | tf_op jit(solution)/shard_map/ppermute | solution.py:642
  52.3 14.5 %collective-permute-start.33 = (bf16[368,128]{1,0:T(8,128)(2,1)S(1)}, bf16[368,128]{1,0:T(8,128)(2,1)S(1)}, u32[]{:S(2)}, u32[]{:S(2)}) collective-permute-start(bf16[368,128]{1,0:T(8,128)(2,1)S(1)} %get-tuple-element.140), channel_id=1, source_target_pairs={{0,12},{4,16},{8,20},{12,24},{16,28},{20,0},{24,4},{28,8},{1,13},{... | collective-permute-start | bytes 282632 | tf_op jit(solution)/shard_map/ppermute | solution.py:642
  54.3 12.4 %collective-permute-start.34 = (bf16[368,128]{1,0:T(8,128)(2,1)S(1)}, bf16[368,128]{1,0:T(8,128)(2,1)S(1)}, u32[]{:S(2)}, u32[]{:S(2)}) collective-permute-start(bf16[368,128]{1,0:T(8,128)(2,1)S(1)} %get-tuple-element.141), channel_id=1, source_target_pairs={{0,16},{4,20},{8,24},{12,28},{16,0},{20,4},{24,8},{28,12},{1,17},{... | collective-permute-start | bytes 282632 | tf_op jit(solution)/shard_map/ppermute | solution.py:642
  56.1 10.6 %collective-permute-start.35 = (bf16[368,128]{1,0:T(8,128)(2,1)S(1)}, bf16[368,128]{1,0:T(8,128)(2,1)S(1)}, u32[]{:S(2)}, u32[]{:S(2)}) collective-permute-start(bf16[368,128]{1,0:T(8,128)(2,1)S(1)} %get-tuple-element.142), channel_id=1, source_target_pairs={{0,20},{4,24},{8,28},{12,0},{16,4},{20,8},{24,12},{28,16},{1,21},{... | collective-permute-start | bytes 282632 | tf_op jit(solution)/shard_map/ppermute | solution.py:642
  59.4 9.4 %collective-permute-start.36 = (bf16[368,128]{1,0:T(8,128)(2,1)S(1)}, bf16[368,128]{1,0:T(8,128)(2,1)S(1)}, u32[]{:S(2)}, u32[]{:S(2)}) collective-permute-start(bf16[368,128]{1,0:T(8,128)(2,1)S(1)} %get-tuple-element.143), channel_id=1, source_target_pairs={{0,24},{4,28},{8,0},{12,4},{16,8},{20,12},{24,16},{28,20},{1,25},{... | collective-permute-start | bytes 282632 | tf_op jit(solution)/shard_map/ppermute | solution.py:642
  59.6 9.2 %collective-permute-start.37 = (bf16[368,128]{1,0:T(8,128)(2,1)S(1)}, bf16[368,128]{1,0:T(8,128)(2,1)S(1)}, u32[]{:S(2)}, u32[]{:S(2)}) collective-permute-start(bf16[368,128]{1,0:T(8,128)(2,1)S(1)} %get-tuple-element.144), channel_id=1, source_target_pairs={{0,28},{4,0},{8,4},{12,8},{16,12},{20,16},{24,20},{28,24},{1,29},{... | collective-permute-start | bytes 282632 | tf_op jit(solution)/shard_map/ppermute | solution.py:642
  69.2 10.7 %collective-permute-start.38 = (bf16[176,128]{1,0:T(8,128)(2,1)S(1)}, bf16[176,128]{1,0:T(8,128)(2,1)S(1)}, u32[]{:S(2)}, u32[]{:S(2)}) collective-permute-start(bf16[176,128]{1,0:T(8,128)(2,1)S(1)} %get-tuple-element.146.refs_0_), channel_id=1, source_target_pairs={{0,4},{4,8},{8,12},{12,16},{16,20},{20,24},{24,28},{28,0},{1,5},{5... | collective-permute-start | bytes 135176 | tf_op jit(solution)/shard_map/ppermute | solution.py:642
  71.7 9.8 %collective-permute-start.39 = (bf16[176,128]{1,0:T(8,128)(2,1)S(1)}, bf16[176,128]{1,0:T(8,128)(2,1)S(1)}, u32[]{:S(2)}, u32[]{:S(2)}) collective-permute-start(bf16[176,128]{1,0:T(8,128)(2,1)S(1)} %get-tuple-element.146.refs_0_), channel_id=1, source_target_pairs={{0,8},{4,12},{8,16},{12,20},{16,24},{20,28},{24,0},{28,4},{1,9},{5... | collective-permute-start | bytes 135176 | tf_op jit(solution)/shard_map/ppermute | solution.py:642
  74.6 8.4 %collective-permute-start.40 = (bf16[176,128]{1,0:T(8,128)(2,1)S(1)}, bf16[176,128]{1,0:T(8,128)(2,1)S(1)}, u32[]{:S(2)}, u32[]{:S(2)}) collective-permute-start(bf16[176,128]{1,0:T(8,128)(2,1)S(1)} %get-tuple-element.146.refs_0_), channel_id=1, source_target_pairs={{0,12},{4,16},{8,20},{12,24},{16,28},{20,0},{24,4},{28,8},{1,13},{... | collective-permute-start | bytes 135176 | tf_op jit(solution)/shard_map/ppermute | solution.py:642
  75.0 8.0 %collective-permute-start.41 = (bf16[176,128]{1,0:T(8,128)(2,1)S(1)}, bf16[176,128]{1,0:T(8,128)(2,1)S(1)}, u32[]{:S(2)}, u32[]{:S(2)}) collective-permute-start(bf16[176,128]{1,0:T(8,128)(2,1)S(1)} %get-tuple-element.146.refs_0_), channel_id=1, source_target_pairs={{0,16},{4,20},{8,24},{12,28},{16,0},{20,4},{24,8},{28,12},{1,17},{... | collective-permute-start | bytes 135176 | tf_op jit(solution)/shard_map/ppermute | solution.py:642
  77.0 6.0 %collective-permute-start.42 = (bf16[176,128]{1,0:T(8,128)(2,1)S(1)}, bf16[176,128]{1,0:T(8,128)(2,1)S(1)}, u32[]{:S(2)}, u32[]{:S(2)}) collective-permute-start(bf16[176,128]{1,0:T(8,128)(2,1)S(1)} %get-tuple-element.146.refs_0_), channel_id=1, source_target_pairs={{0,20},{4,24},{8,28},{12,0},{16,4},{20,8},{24,12},{28,16},{1,21},{... | collective-permute-start | bytes 135176 | tf_op jit(solution)/shard_map/ppermute | solution.py:642
  79.9 4.4 %collective-permute-start.43 = (bf16[176,128]{1,0:T(8,128)(2,1)S(1)}, bf16[176,128]{1,0:T(8,128)(2,1)S(1)}, u32[]{:S(2)}, u32[]{:S(2)}) collective-permute-start(bf16[176,128]{1,0:T(8,128)(2,1)S(1)} %get-tuple-element.146.refs_0_), channel_id=1, source_target_pairs={{0,24},{4,28},{8,0},{12,4},{16,8},{20,12},{24,16},{28,20},{1,25},{... | collective-permute-start | bytes 135176 | tf_op jit(solution)/shard_map/ppermute | solution.py:642
  81.4 4.0 %collective-permute-start.44 = (bf16[176,128]{1,0:T(8,128)(2,1)S(1)}, bf16[176,128]{1,0:T(8,128)(2,1)S(1)}, u32[]{:S(2)}, u32[]{:S(2)}) collective-permute-start(bf16[176,128]{1,0:T(8,128)(2,1)S(1)} %get-tuple-element.146.refs_0_), channel_id=1, source_target_pairs={{0,28},{4,0},{8,4},{12,8},{16,12},{20,16},{24,20},{28,24},{1,29},{... | collective-permute-start | bytes 135176 | tf_op jit(solution)/shard_map/ppermute | solution.py:642
  87.7 4.0 %collective-permute-start.46 = (f32[32,256]{1,0:T(8,128)S(1)}, f32[32,256]{1,0:T(8,128)S(1)}, u32[]{:S(2)}, u32[]{:S(2)}) collective-permute-start(f32[32,256]{1,0:T(8,128)S(1)} %get-tuple-element.153), channel_id=1, source_target_pairs={{0,2},{1,3},{2,0},{3,1},{4,6},{5,7},{6,4},{7,5},{8,10},{9,11},{10,... | collective-permute-start | bytes 98312 | tf_op jit(solution)/shard_map/ppermute | solution.py:642
  88.7 3.3 %collective-permute-start.47 = (f32[32,256]{1,0:T(8,128)S(1)}, f32[32,256]{1,0:T(8,128)S(1)}, u32[]{:S(2)}, u32[]{:S(2)}) collective-permute-start(f32[32,256]{1,0:T(8,128)S(1)} %get-tuple-element.154), channel_id=1, source_target_pairs={{0,1},{1,2},{2,3},{3,0},{4,5},{5,6},{6,7},{7,4},{8,9},{9,10},{10,1... | collective-permute-start | bytes 98312 | tf_op jit(solution)/shard_map/ppermute | solution.py:642
  (10 other events, 168.8 us)

commit v5 on v4

--- a/solution.py
+++ b/solution.py
@@ -66,21 +66,24 @@
 
 
 def attend_kernel(
-    classes, devices, table_ref, len_ref, seq_ref, q_hbm, fresh_hbm, cache_ref, *refs,
+    classes, seq_ref, table_hbm, len_hbm, q_hbm, fresh_hbm, cache_ref, share_ref,
+    page_ref, table_ref, len_ref, q_ref, fresh_ref, query_ref, new_ref, order_ref, sems, small_sems,
 ):
-    out_refs, refs = refs[:devices], refs[devices:]
-    share_ref, page_ref, split_ref, q_ref, fresh_ref, query_ref, new_ref, order_ref, sems, small_sems = refs
     steps, requests, _ = q_ref.shape
     page_rows = cache_ref.shape[1]
     pages = table_ref.shape[1]
     span = pages * page_rows
     first = seq_ref[0] * span
     small = [
-        pltpu.make_async_copy(q_hbm, q_ref, small_sems.at[0]),
-        pltpu.make_async_copy(fresh_hbm, fresh_ref, small_sems.at[1]),
+        pltpu.make_async_copy(source, target, small_sems.at[i])
+        for i, (source, target) in enumerate(
+            [(table_hbm, table_ref), (len_hbm, len_ref), (q_hbm, q_ref), (fresh_hbm, fresh_ref)]
+        )
     ]
     for one in small:
         one.start()
+    for one in small[:2]:
+        one.wait()
 
     held = [jnp.clip(len_ref[r] - first, 0, span) for r in range(requests)]
     for r in range(requests):
@@ -122,7 +125,7 @@
         return carry
 
     lax.fori_loop(0, requests // 2, start, 0)
-    for one in small:
+    for one in small[2:]:
         one.wait()
 
     low = iota((requests, LANES), 1) < HEAD_SIZE
@@ -151,7 +154,7 @@
         found = [new_ref[u, pl.ds(2 * r + which, 1), :] for u in range(steps)]
         return jnp.concatenate(found + [jnp.zeros((16 - steps, KV_WIDTH), F32)], axis=0).astype(BF16)
 
-    def attend_pages(r, slot, count):
+    def attend_pages(r, count):
         spread = jnp.concatenate(
             [
                 jnp.broadcast_to(query_ref[i, pl.ds(r, 1), :], (KEY_VALUE_HEADS, KV_WIDTH))
@@ -160,21 +163,12 @@
             axis=0,
         )
         spread = jnp.where(own, spread, 0.0).astype(BF16)
-        halves = ([], [])
-        for page in range(count):
-            block = page_ref[r * pages + page].reshape(2 * page_rows, KV_WIDTH).astype(F32)
-            for j in range(KV_WIDTH // LANES):
-                split_ref[slot, page, j] = tile_of(block, j)
-            for which in range(2):
-                tiles = [
-                    split_ref[slot, page, j, pl.ds(which, page_rows, 2), :]
-                    for j in range(KV_WIDTH // LANES)
-                ]
-                halves[which].append(jnp.concatenate(tiles, axis=1).astype(BF16))
-        keys, values = jnp.concatenate(halves[0], axis=0), jnp.concatenate(halves[1], axis=0)
-        size = count * page_rows
-        live = first + iota((1, size), 1) < len_ref[r]
-        scores = dot_nt(spread, keys) + jnp.where(live, 0.0, NEG_FILL)
+        both = [page_ref[r * pages + page].reshape(2 * page_rows, KV_WIDTH) for page in range(count)]
+        both = jnp.concatenate(both, axis=0)
+        size = 2 * count * page_rows
+        place = iota((1, size), 1)
+        live = jnp.logical_and(place % 2 == 0, first + place // 2 < len_ref[r])
+        scores = dot_nt(spread, both) + jnp.where(live, 0.0, NEG_FILL)
         fresh_scores = dot_nt(spread, fresh_rows(r, 0)) + fresh_bias
         largest = jnp.maximum(
             jnp.max(scores, axis=1, keepdims=True), jnp.max(fresh_scores, axis=1, keepdims=True)
@@ -183,7 +177,8 @@
         fresh_weights = jnp.exp(fresh_scores - largest)
         total = jnp.sum(weights, axis=1, keepdims=True)
         total = total + jnp.sum(fresh_weights, axis=1, keepdims=True)
-        acc = dot_nn(weights.astype(BF16), values)
+        moved = [pltpu.roll(tile_of(weights, j), 1, 1) for j in range(size // LANES)]
+        acc = dot_nn(jnp.concatenate(moved, axis=1).astype(BF16), both)
         acc = acc + dot_nn(fresh_weights.astype(BF16), fresh_rows(r, 1))
         acc = jnp.where(own, acc * (1.0 / total), 0.0)
         acc = jnp.sum(acc.reshape(steps * GROUP, KEY_VALUE_HEADS, KV_WIDTH), axis=1)
@@ -208,7 +203,7 @@
                 for page in range(high):
                     for r in both:
                         copy(r, page).wait()
-                made = [attend_pages(r, slot, high) for slot, r in enumerate(both)]
+                made = [attend_pages(r, high) for r in both]
                 for r, (acc, side) in zip(both, made):
                     put(r, acc, side)
 
@@ -221,8 +216,6 @@
         return carry
 
     lax.fori_loop(0, requests // 2, one_pair, 0)
-    for k, out_ref in enumerate(out_refs):
-        out_ref[...] = share_ref[lax.rem(seq_ref[0] + k, devices)]
 
 
 def attend(queries, new_key_value, cache, page_table, cache_len, seq_index, devices):
@@ -233,44 +226,43 @@
     share = (requests * steps * GROUP // devices, KV_WIDTH + LANES)
     smem, hbm = pl.BlockSpec(memory_space=pltpu.SMEM), pl.BlockSpec(memory_space=pl.ANY)
     return pl.pallas_call(
-        functools.partial(attend_kernel, classes, devices),
-        in_specs=[smem] * 3 + [hbm] * 3,
-        out_shape=(jax.ShapeDtypeStruct(share, BF16),) * devices,
+        functools.partial(attend_kernel, classes),
+        in_specs=[smem] + [hbm] * 5,
+        out_shape=jax.ShapeDtypeStruct((devices,) + share, BF16),
         scratch_shapes=[
-            pltpu.VMEM((devices,) + share, BF16),
             pltpu.VMEM((requests * pages, page_rows, 2, KV_WIDTH), BF16),
-            pltpu.VMEM((2, pages, KV_WIDTH // LANES, 2 * page_rows, LANES), F32),
+            pltpu.SMEM(page_table.shape, jnp.int32),
+            pltpu.SMEM(cache_len.shape, jnp.int32),
             pltpu.VMEM(queries.shape, BF16),
             pltpu.VMEM(new_key_value.shape, BF16),
             pltpu.VMEM((steps * GROUP, requests, KV_WIDTH), F32),
             pltpu.VMEM((steps, 2 * requests, KV_WIDTH), F32),
             pltpu.SMEM((requests,), jnp.int32),
             pltpu.SemaphoreType.DMA((requests * pages,)),
-            pltpu.SemaphoreType.DMA((2,)),
+            pltpu.SemaphoreType.DMA((4,)),
         ],
         compiler_params=pltpu.CompilerParams(vmem_limit_bytes=ATTEND_VMEM),
         name="attend",
-    )(page_table, cache_len, seq_index, queries, new_key_value, cache)
-
-
-def join_kernel(*refs):
-    x_refs, out_ref = refs[:-1], refs[-1]
-    rows = x_refs[0].shape[0]
+    )(seq_index, page_table, cache_len, queries, new_key_value, cache)
+
+
+def join_kernel(x_ref, out_ref):
+    blocks, rows, _ = x_ref.shape
     tokens = rows // GROUP
     levels = []
-    for x_ref in x_refs:
-        side = x_ref[:, KV_WIDTH : KV_WIDTH + LANES].astype(F32)
+    for b in range(blocks):
+        side = x_ref[b, :, KV_WIDTH : KV_WIDTH + LANES].astype(F32)
         levels.append(side + pltpu.roll(side, LANES - 8, 1) + pltpu.roll(side, LANES - 16, 1))
     largest = functools.reduce(jnp.maximum, levels)
     weights = [jnp.exp(level - largest) for level in levels]
     inverse = 1.0 / functools.reduce(jnp.add, weights)
     low = iota((rows, LANES), 1) < HEAD_SIZE
     acc = [jnp.zeros((rows, LANES), F32) for _ in range(KV_WIDTH // LANES)]
-    for x_ref, weight in zip(x_refs, weights):
-        share = weight * inverse
+    for b in range(blocks):
+        share = weights[b] * inverse
         for j in range(KV_WIDTH // LANES):
             factor = jnp.where(low, share[:, 2 * j : 2 * j + 1], share[:, 2 * j + 1 : 2 * j + 2])
-            acc[j] = acc[j] + factor * x_ref[:, j * LANES : (j + 1) * LANES].astype(F32)
+            acc[j] = acc[j] + factor * x_ref[b, :, j * LANES : (j + 1) * LANES].astype(F32)
 
     def piece(head, half):
         k, g = head // GROUP, head % GROUP
@@ -286,13 +278,13 @@
 
 
 def join(parts):
-    rows = parts[0].shape[0]
+    rows = parts.shape[1]
     return pl.pallas_call(
         join_kernel,
         out_shape=jax.ShapeDtypeStruct((rows // GROUP, QUERY_HEADS * HEAD_SIZE), BF16),
         compiler_params=params(),
         name="join",
-    )(*parts)
+    )(parts)
 
 
 def side_place(features, count):
@@ -304,11 +296,15 @@
     attn_refs, (hidden_ref, out_ref, wide_ref) = refs[:-3], refs[-3:]
     steps, requests, features = residual_ref.shape
     tokens = steps * requests
-    attn = jnp.concatenate([ref[...].astype(F32) for ref in attn_refs], axis=0).astype(BF16)
+    blocks = [ref[i].astype(F32) for ref in attn_refs for i in range(2)]
+    attn = jnp.concatenate(blocks, axis=0).astype(BF16)
     row, column = iota((tokens, tokens), 0), iota((tokens, tokens), 1)
-    devices, share = len(attn_refs), attn_refs[0].shape[0]
-    token = seq_ref[0] + devices - column // share
-    token = jnp.where(token >= devices, token - devices, token) * share + column % share
+    devices, share = len(blocks), attn_refs[0].shape[1]
+    source = seq_ref[0] + devices - column // (2 * share) * 2
+    source = jnp.where(source >= devices, source - devices, source)
+    other = column // share % 2
+    source = source + other * (1 - source % 2 * 2)
+    token = source * share + column % share
     reorder = jnp.logical_and(row % requests == token // steps, row // requests == token % steps)
     attn = dot_nn(reorder.astype(F32).astype(BF16), attn).astype(BF16)
     residual = residual_ref[...].astype(F32).reshape(tokens, features)
@@ -506,14 +502,16 @@
     scaled = total(0, share) * jnp.concatenate(columns, axis=0)[0:share]
     made = scaled / (1.0 + jnp.exp(-scaled)) * swap_halves(scaled)
     low = iota((half, LANES), 1) < PIECE_WIDTH
-    out_ref[...] = jnp.where(low, made[0:half], swap_halves(made[half:share])).astype(BF16)
+    made = jnp.where(low, made[0:half], swap_halves(made[half:share])).astype(BF16)
+    for b in range(out_ref.shape[0]):
+        out_ref[b] = made
 
 
 def inner(parts):
     return pl.pallas_call(
         inner_kernel,
         out_shape=(
-            jax.ShapeDtypeStruct(((parts[0].shape[0] - 16) // 2, LANES), BF16),
+            jax.ShapeDtypeStruct((len(parts), (parts[0].shape[0] - 16) // 2, LANES), BF16),
             jax.ShapeDtypeStruct((8, LANES), F32),
         ),
         compiler_params=params(),
@@ -521,14 +519,12 @@
     )(*parts)
 
 
-def down_kernel(features, local, devices, first_ref, seq_ref, range_ref, pick_ref, w_ref, logit_ref, *refs):
-    part_refs, out_refs, (x_ref, row_ref, made_ref) = refs[:devices], refs[devices:-3], refs[-3:]
+def down_kernel(features, local, first_ref, range_ref, pick_ref, w_ref, logit_ref, x_ref, *refs):
+    out_refs, (row_ref, made_ref) = refs[:-2], refs[-2:]
     total, rows = pick_ref.shape
     width = w_ref.shape[2]
     window = total // 2 + 16
-    for k, part_ref in enumerate(part_refs):
-        x_ref[lax.rem(seq_ref[0] + devices - k, devices)] = part_ref[...]
-    half = x_ref.shape[1]
+    devices, half, _ = x_ref.shape
     share = 2 * half
     low = iota((half, LANES), 1) < PIECE_WIDTH
     for b in range(0, devices, 2):
@@ -582,23 +578,22 @@
         out_ref[:, tile : tile + LANES] = jnp.where(lane == 1, pair[at, 1:2], side)
 
 
-def down(first, seq_index, ranges, pick, made, logits, weights, exp_count):
+def down(first, ranges, pick, made, logits, weights, exp_count):
     local, features, width = weights.shape
     total, rows = pick.shape
     wide = side_place(features, 2)[0] + LANES
     smem, vmem = pl.BlockSpec(memory_space=pltpu.SMEM), pl.BlockSpec(memory_space=pltpu.VMEM)
     return pl.pallas_call(
-        functools.partial(down_kernel, features, local, len(made)),
-        in_specs=[smem] * 2 + [vmem] * (4 + len(made)),
+        functools.partial(down_kernel, features, local),
+        in_specs=[smem] + [vmem] * 5,
         out_shape=(jax.ShapeDtypeStruct((total // exp_count, wide), F32),) * exp_count,
         scratch_shapes=[
-            pltpu.VMEM((len(made),) + made[0].shape, BF16),
             pltpu.VMEM((rows, width), BF16),
             pltpu.VMEM((rows, wide), F32),
         ],
         compiler_params=params(),
         name="down",
-    )(first, seq_index, ranges, pick, weights, logits, *made)
+    )(first, ranges, pick, weights, logits, made)
 
 
 def finish_kernel(hidden_ref, *refs):
@@ -640,6 +635,10 @@
 def send(x, axis, distance):
     count = lax.axis_size(axis)
     return lax.ppermute(x, axis, [(i, (i + distance) % count) for i in range(count)])
+
+
+def swap(x, axis):
+    return lax.all_to_all(x, axis, split_axis=0, concat_axis=0, tiled=True)
 
 
 def exchange(parts, axis, direction):
@@ -677,11 +676,14 @@
     shares = attend(
         queries, new_key_value, pool, page_table, cache_len, seq_index, seq_count
     )
-    attn = join(exchange(shares, "seq", 1))
-    w_gate_up, attn = lax.optimization_barrier((w_gate_up, attn))
-    gathered = gather(attn, "seq")
+    w_gate_up, shares = lax.optimization_barrier((w_gate_up, shares))
     gate_up_weights = w_gate_up.transpose(0, 2, 1, 3)
-    gate_up_weights, gathered = lax.optimization_barrier((gate_up_weights, gathered))
+    shares = swap(shares, "seq")
+    gate_up_weights, shares = lax.optimization_barrier((gate_up_weights, shares))
+    attn = join(shares)
+    beside = lax.ppermute(attn, "seq", [(i, i ^ 1) for i in range(seq_count)])
+    pair = jnp.stack([attn, beside])
+    gathered = [pair] + [send(pair, "seq", k) for k in range(2, seq_count, 2)]
     hidden, outgoing = hidden_state(seq_index, gathered, residual, w_out, norm_gain, routes)
     incoming = gather(outgoing, "exp")
     pieces = seq_count // PIECES
@@ -693,8 +695,7 @@
         )
         made, logits = inner(exchange(partial, "seq", 1))
         logits = logits[None] if pieces == 1 else lax.all_gather(logits, "seq")[::PIECES]
-        made = gather(made, "seq")
-        return down(first, seq_index, ranges, pick, made, logits, w_down, exp_count), most
+        return down(first, ranges, pick, swap(made, "seq"), logits, w_down, exp_count), most
 
     made, most = one_round(0)
     pairs = w_gate_up.shape[0] * exp_count * steps * CAP

time: 93.1 us -> 87.4 us (0.939)
  starting transfers between devices: 50 us -> 33.8 us
  waiting for transfers between devices: 18.5 us -> 28.1 us
  local copies, waits for them, and re-layouts: 3.46 us -> 4.88 us
  Pallas kernels: 20 us -> 19 us
    ppermute x34 -> x16, starting transfers between devices: 50 us -> 22.7 us  [send(): lax.ppermute(x, axis, [(i, (i + distance) % count) for i in range(count)])]
    all_to_all x0 -> x2, waiting for transfers between devices: none -> 12.7 us  [swap(): return lax.all_to_all(x, axis, split_axis=0, concat_axis=0, tiled=True)]
    all_to_all x0 -> x2, starting transfers between devices: none -> 10.8 us  [swap(): return lax.all_to_all(x, axis, split_axis=0, concat_axis=0, tiled=True)]
    ppermute x34 -> x16, waiting for transfers between devices: 18.5 us -> 12 us  [send(): lax.ppermute(x, axis, [(i, (i + distance) % count) for i in range(count)])]
    ppermute x0 -> x1, waiting for transfers between devices: none -> 3.35 us  [local(): beside = lax.ppermute(attn, 'seq', [(i, i ^ 1) for i in range(seq_count)])]
    optimization_barrier x1, local copies, waits for them, and re-layouts: 2.7 us -> 4.84 us  [local(): w_gate_up, shares = lax.optimization_barrier((w_gate_up, shares))]
    pallas_call x3, Pallas kernels: 14.1 us -> 13 us  [the longest x1 9.83 us: attend(): pl.pallas_call(functools.partial(attend_kernel, classes), in_specs=[smem]...]
  transfers between devices with their start and end apart: 34 -> 19, of which waited for: 13 -> 11; matrix products, arithmetic and copies ran while one was open for 3% -> 6% of each run, Pallas kernels for 0% -> 0%
where the time goes in v5:
time: 87.4 us; the launch traced here: 86.6 us
  starting transfers between devices  33.8 us (39%)
  waiting for transfers between devices  28.1 us (32%)
  Pallas kernels  19 us (22%)
  local copies, waits for them, and re-layouts  4.88 us (6%)
    ppermute x16, starting transfers between devices, send(): lax.ppermute(x, axis, [(i, (i + distance) % count) for i in range(count)])  22.7 us
    all_to_all x2, waiting for transfers between devices, swap(): return lax.all_to_all(x, axis, split_axis=0, concat_axis=0, tiled=True)  12.7 us
    ppermute x16, waiting for transfers between devices, send(): lax.ppermute(x, axis, [(i, (i + distance) % count) for i in range(count)])  12 us
    all_to_all x2, starting transfers between devices, swap(): return lax.all_to_all(x, axis, split_axis=0, concat_axis=0, tiled=True)  10.8 us
    pallas_call x1, Pallas kernels, attend(): pl.pallas_call(functools.partial(attend_kernel, classes), in_specs=[smem]...  9.83 us
    optimization_barrier x1, local copies, waits for them, and re-layouts, local(): w_gate_up, shares = lax.optimization_barrier((w_gate_up, shares))  4.84 us
    pallas_call x1, Pallas kernels, gate_up(): pl.pallas_call(functools.partial(gate_up_kernel, features, local, turn, s...  4.27 us
    ppermute x1, waiting for transfers between devices, local(): beside = lax.ppermute(attn, 'seq', [(i, i ^ 1) for i in range(seq_count)])  3.35 us
  transfers between devices with their start and end apart: 19, of which 11 were waited for; matrix products, arithmetic and copies ran while one was open for 6% of the time, Pallas kernels for 0%

profile of v5, /device:TPU:0, one launch (start us, length us, event | category | flops | bytes accessed | tf_op | source)
XLA Modules:
  0.0 86.6 jit_solution(12233988446404783086)
XLA Ops:
  0.0 9.8 %attend.1 = bf16[8,12,640]{2,1,0:T(8,128)(2,1)} custom-call(s32[1]{0:T(128)} %bitcast.2.seq_ref, s32[8,8]{1,0:T(8,128)} %table_hbm.1, s32[8]{0:T(128)} %len_hbm.1, bf16[4,8,1536]{2,1,0:T(8,128)(2,1)} %q_hbm.1, bf16[4,8,2,512]{3,2,1,0:T(2,128)(2,1)} %fresh_hbm.1, bf16[64,64,2,512]{3,2,1,0:T(2,128)(2,1)} %bitcast.22), custom_call_target="tpu_custom_call" | custom-call | tf_op jit(solution)/shard_map/attend/pallas_call | solution.py:228
  9.8 3.4 %all-to-all-start.1 = ((bf16[8,12,640]{2,1,0:T(8,128)(2,1)}), bf16[8,12,640]{2,1,0:T(8,128)(2,1)S(1)}, u32[]{:S(2)}, u32[]{:S(2)}) async-start(bf16[8,12,640]{2,1,0:T(8,128)(2,1)} %attend.1), calls=%async_computation.1 | async-start | bytes 327680 | tf_op jit(solution)/shard_map/all_to_all | solution.py:641
  13.3 4.8 %copy.16 = bf16[10,192,2,512]{3,1,2,0:T(8,128)(2,1)} copy(bf16[10,192,2,512]{3,2,1,0:T(2,128)(2,1)} %param.24) | data formatting | bytes 7864320 | tf_op jit(solution)/shard_map/optimization_barrier | solution.py:679
  18.1 2.8 %all-to-all-done.1.x_ref = bf16[8,12,640]{2,1,0:T(8,128)(2,1)S(1)} async-done(((bf16[8,12,640]{2,1,0:T(8,128)(2,1)}), bf16[8,12,640]{2,1,0:T(8,128)(2,1)S(1)}, u32[]{:S(2)}, u32[]{:S(2)}) %all-to-all-start.1) | async-done | bytes 122912 | tf_op jit(solution)/shard_map/all_to_all | solution.py:641
  20.9 0.5 join.1
  21.8 3.4 %collective-permute-done.7 = bf16[4,1536]{1,0:T(4,128)(2,1)S(1)} collective-permute-done((bf16[4,1536]{1,0:T(4,128)(2,1)S(1)}, bf16[4,1536]{1,0:T(4,128)(2,1)S(1)}, u32[]{:S(2)}, u32[]{:S(2)}) %collective-permute-start.7) | collective-permute-done | bytes 12320 | tf_op jit(solution)/shard_map/ppermute | solution.py:684
  25.2 1.5 %collective-permute-start.9 = (bf16[2,4,1536]{2,1,0:T(4,128)(2,1)S(1)}, bf16[2,4,1536]{2,1,0:T(4,128)(2,1)S(1)}, u32[]{:S(2)}, u32[]{:S(2)}) collective-permute-start(bf16[2,4,1536]{2,1,0:T(4,128)(2,1)S(1)} %pad_maximum_fusion.refs_0_), channel_id=1, source_target_pairs={{0,16},{4,20},{8,24},{12,28},{16,0},{20,4},{24,8},{28,12},{1,17},{... | collective-permute-start | bytes 73736 | tf_op jit(solution)/shard_map/ppermute | solution.py:637
  26.7 2.3 %collective-permute-start.10 = (bf16[2,4,1536]{2,1,0:T(4,128)(2,1)S(1)}, bf16[2,4,1536]{2,1,0:T(4,128)(2,1)S(1)}, u32[]{:S(2)}, u32[]{:S(2)}) collective-permute-start(bf16[2,4,1536]{2,1,0:T(4,128)(2,1)S(1)} %pad_maximum_fusion.refs_0_), channel_id=1, source_target_pairs={{0,24},{4,28},{8,0},{12,4},{16,8},{20,12},{24,16},{28,20},{1,25},{... | collective-permute-start | bytes 73736 | tf_op jit(solution)/shard_map/ppermute | solution.py:637
  29.0 1.8 %collective-permute-done.8.refs_1_ = bf16[2,4,1536]{2,1,0:T(4,128)(2,1)S(1)} collective-permute-done((bf16[2,4,1536]{2,1,0:T(4,128)(2,1)S(1)}, bf16[2,4,1536]{2,1,0:T(4,128)(2,1)S(1)}, u32[]{:S(2)}, u32[]{:S(2)}) %collective-permute-start.8) | collective-permute-done | bytes 24608 | tf_op jit(solution)/shard_map/ppermute | solution.py:637
  30.8 0.6 collective-permute-done.10.refs_3_
  31.4 0.5 hidden.1
  32.0 2.4 %collective-permute-start.12 = (bf16[32,256]{1,0:T(8,128)(2,1)S(1)}, bf16[32,256]{1,0:T(8,128)(2,1)S(1)}, u32[]{:S(2)}, u32[]{:S(2)}) collective-permute-start(bf16[32,256]{1,0:T(8,128)(2,1)S(1)} %get-tuple-element.102.refs_0_), channel_id=1, source_target_pairs={{0,2},{1,3},{2,0},{3,1},{4,6},{5,7},{6,4},{7,5},{8,10},{9,11},{10,... | collective-permute-start | bytes 49160 | tf_op jit(solution)/shard_map/ppermute | solution.py:637
  34.4 1.4 %collective-permute-start.13 = (bf16[32,256]{1,0:T(8,128)(2,1)S(1)}, bf16[32,256]{1,0:T(8,128)(2,1)S(1)}, u32[]{:S(2)}, u32[]{:S(2)}) collective-permute-start(bf16[32,256]{1,0:T(8,128)(2,1)S(1)} %get-tuple-element.102.refs_0_), channel_id=1, source_target_pairs={{0,3},{1,0},{2,1},{3,2},{4,7},{5,4},{6,5},{7,6},{8,11},{9,8},{10,9... | collective-permute-start | bytes 49160 | tf_op jit(solution)/shard_map/ppermute | solution.py:637
  36.1 1.1 %collective-permute-done.13.refs_3_ = bf16[32,256]{1,0:T(8,128)(2,1)S(1)} collective-permute-done((bf16[32,256]{1,0:T(8,128)(2,1)S(1)}, bf16[32,256]{1,0:T(8,128)(2,1)S(1)}, u32[]{:S(2)}, u32[]{:S(2)}) %collective-permute-start.13) | collective-permute-done | bytes 16416 | tf_op jit(solution)/shard_map/ppermute | solution.py:637
  37.2 4.3 %gate_up.3 = (bf16[368,128]{1,0:T(8,128)(2,1)S(1)}, bf16[368,128]{1,0:T(8,128)(2,1)S(1)}, bf16[368,128]{1,0:T(8,128)(2,1)S(1)}, bf16[368,128]{1,0:T(8,128)(2,1)S...) custom-call(s32[1]{0:T(128)} %bitcast.9.where_ref, ...), custom_call_target="tpu_custom_call" | custom-call | tf_op jit(solution)/shard_map/gate_up/pallas_call | solution.py:462
  41.5 0.7 collective-permute-start.14
  42.2 1.8 %collective-permute-start.15 = (bf16[368,128]{1,0:T(8,128)(2,1)S(1)}, bf16[368,128]{1,0:T(8,128)(2,1)S(1)}, u32[]{:S(2)}, u32[]{:S(2)}) collective-permute-start(bf16[368,128]{1,0:T(8,128)(2,1)S(1)} %get-tuple-element.109), channel_id=1, source_target_pairs={{0,8},{4,12},{8,16},{12,20},{16,24},{20,28},{24,0},{28,4},{1,9},{5... | collective-permute-start | bytes 282632 | tf_op jit(solution)/shard_map/ppermute | solution.py:637
  43.9 2.9 %collective-permute-start.16 = (bf16[368,128]{1,0:T(8,128)(2,1)S(1)}, bf16[368,128]{1,0:T(8,128)(2,1)S(1)}, u32[]{:S(2)}, u32[]{:S(2)}) collective-permute-start(bf16[368,128]{1,0:T(8,128)(2,1)S(1)} %get-tuple-element.110), channel_id=1, source_target_pairs={{0,12},{4,16},{8,20},{12,24},{16,28},{20,0},{24,4},{28,8},{1,13},{... | collective-permute-start | bytes 282632 | tf_op jit(solution)/shard_map/ppermute | solution.py:637
  46.9 2.0 %collective-permute-start.17 = (bf16[368,128]{1,0:T(8,128)(2,1)S(1)}, bf16[368,128]{1,0:T(8,128)(2,1)S(1)}, u32[]{:S(2)}, u32[]{:S(2)}) collective-permute-start(bf16[368,128]{1,0:T(8,128)(2,1)S(1)} %get-tuple-element.111), channel_id=1, source_target_pairs={{0,16},{4,20},{8,24},{12,28},{16,0},{20,4},{24,8},{28,12},{1,17},{... | collective-permute-start | bytes 282632 | tf_op jit(solution)/shard_map/ppermute | solution.py:637
  48.9 0.9 %collective-permute-start.18 = (bf16[368,128]{1,0:T(8,128)(2,1)S(1)}, bf16[368,128]{1,0:T(8,128)(2,1)S(1)}, u32[]{:S(2)}, u32[]{:S(2)}) collective-permute-start(bf16[368,128]{1,0:T(8,128)(2,1)S(1)} %get-tuple-element.112), channel_id=1, source_target_pairs={{0,20},{4,24},{8,28},{12,0},{16,4},{20,8},{24,12},{28,16},{1,21},{... | collective-permute-start | bytes 282632 | tf_op jit(solution)/shard_map/ppermute | solution.py:637
  49.8 1.7 %collective-permute-start.19 = (bf16[368,128]{1,0:T(8,128)(2,1)S(1)}, bf16[368,128]{1,0:T(8,128)(2,1)S(1)}, u32[]{:S(2)}, u32[]{:S(2)}) collective-permute-start(bf16[368,128]{1,0:T(8,128)(2,1)S(1)} %get-tuple-element.113), channel_id=1, source_target_pairs={{0,24},{4,28},{8,0},{12,4},{16,8},{20,12},{24,16},{28,20},{1,25},{... | collective-permute-start | bytes 282632 | tf_op jit(solution)/shard_map/ppermute | solution.py:637
  51.5 2.7 %collective-permute-start.20 = (bf16[368,128]{1,0:T(8,128)(2,1)S(1)}, bf16[368,128]{1,0:T(8,128)(2,1)S(1)}, u32[]{:S(2)}, u32[]{:S(2)}) collective-permute-start(bf16[368,128]{1,0:T(8,128)(2,1)S(1)} %get-tuple-element.114), channel_id=1, source_target_pairs={{0,28},{4,0},{8,4},{12,8},{16,12},{20,16},{24,20},{28,24},{1,29},{... | collective-permute-start | bytes 282632 | tf_op jit(solution)/shard_map/ppermute | solution.py:637
  54.2 3.3 %collective-permute-done.16.refs_3_ = bf16[368,128]{1,0:T(8,128)(2,1)S(1)} collective-permute-done((bf16[368,128]{1,0:T(8,128)(2,1)S(1)}, bf16[368,128]{1,0:T(8,128)(2,1)S(1)}, u32[]{:S(2)}, u32[]{:S(2)}) %collective-permute-start.16) | collective-permute-done | bytes 94240 | tf_op jit(solution)/shard_map/ppermute | solution.py:637
  57.5 1.7 %collective-permute-done.19.refs_6_ = bf16[368,128]{1,0:T(8,128)(2,1)S(1)} collective-permute-done((bf16[368,128]{1,0:T(8,128)(2,1)S(1)}, bf16[368,128]{1,0:T(8,128)(2,1)S(1)}, u32[]{:S(2)}, u32[]{:S(2)}) %collective-permute-start.19) | collective-permute-done | bytes 94240 | tf_op jit(solution)/shard_map/ppermute | solution.py:637
  59.2 1.1 %inner.3 = (bf16[8,176,128]{2,1,0:T(8,128)(2,1)}, f32[8,128]{1,0:T(8,128)S(1)}) custom-call(bf16[368,128]{1,0:T(8,128)(2,1)S(1)} %get-tuple-element.107.refs_0_, bf16[368,128]{1,0:T(8,128)(2,1)S(1)} %collective-permute-done.14.refs_1_, bf16[368,128]{1,0:T(8,128)(2,1)S(1)} %collective-permute-done.15.refs_2_, ...), custom_call_target="tpu_custom_call" | custom-call | tf_op jit(solution)/shard_map/inner/pallas_call | solution.py:511
  60.3 7.4 %all-to-all-start.2 = ((bf16[8,176,128]{2,1,0:T(8,128)(2,1)}), bf16[8,176,128]{2,1,0:T(8,128)(2,1)S(1)}, u32[]{:S(2)}, u32[]{:S(2)}) async-start(bf16[8,176,128]{2,1,0:T(8,128)(2,1)} %get-tuple-element.116), calls=%async_computation.2 | async-start | bytes 720896 | tf_op jit(solution)/shard_map/all_to_all | solution.py:641
  68.3 9.9 %all-to-all-done.2.x_ref = bf16[8,176,128]{2,1,0:T(8,128)(2,1)S(1)} async-done(((bf16[8,176,128]{2,1,0:T(8,128)(2,1)}), bf16[8,176,128]{2,1,0:T(8,128)(2,1)S(1)}, u32[]{:S(2)}, u32[]{:S(2)}) %all-to-all-start.2) | async-done | bytes 360480 | tf_op jit(solution)/shard_map/all_to_all | solution.py:641
  78.3 2.1 %down.3 = (f32[32,256]{1,0:T(8,128)S(1)}, f32[32,256]{1,0:T(8,128)S(1)}, f32[32,256]{1,0:T(8,128)S(1)}, f32[32,256]{1,0:T(8,128)S(1)}) custom-call(s32[16]{0:T(128)S(1)} %get-tuple-element.104.first_ref, f32[16,128]{1,0:T(8,128)S(1)} %get-tuple-element.105.range_ref, bf16[128,352]{1,0:T(8,128)(2,1)S(1)} %get-tuple-element.106.pick_ref, ...), custom_call_target="tpu_custom_call" | custom-call | tf_op jit(solution)/shard_map/down/pallas_call | solution.py:586
  80.4 2.0 %collective-permute-start.22 = (f32[32,256]{1,0:T(8,128)S(1)}, f32[32,256]{1,0:T(8,128)S(1)}, u32[]{:S(2)}, u32[]{:S(2)}) collective-permute-start(f32[32,256]{1,0:T(8,128)S(1)} %get-tuple-element.123), channel_id=1, source_target_pairs={{0,2},{1,3},{2,0},{3,1},{4,6},{5,7},{6,4},{7,5},{8,10},{9,11},{10,... | collective-permute-start | bytes 98312 | tf_op jit(solution)/shard_map/ppermute | solution.py:637
  82.6 2.2 %collective-permute-done.22.refs_2_ = f32[32,256]{1,0:T(8,128)S(1)} collective-permute-done((f32[32,256]{1,0:T(8,128)S(1)}, f32[32,256]{1,0:T(8,128)S(1)}, u32[]{:S(2)}, u32[]{:S(2)}) %collective-permute-start.22) | collective-permute-done | bytes 32800 | tf_op jit(solution)/shard_map/ppermute | solution.py:637
  84.8 1.0 %collective-permute-done.23.refs_3_ = f32[32,256]{1,0:T(8,128)S(1)} collective-permute-done((f32[32,256]{1,0:T(8,128)S(1)}, f32[32,256]{1,0:T(8,128)S(1)}, u32[]{:S(2)}, u32[]{:S(2)}) %collective-permute-start.23) | collective-permute-done | bytes 32800 | tf_op jit(solution)/shard_map/ppermute | solution.py:637
  85.8 0.8 finish.1
  (28 shorter events, 1.1 us)
Async XLA Ops:
  9.8 11.1 %all-to-all-start.1 = ((bf16[8,12,640]{2,1,0:T(8,128)(2,1)}), bf16[8,12,640]{2,1,0:T(8,128)(2,1)S(1)}, u32[]{:S(2)}, u32[]{:S(2)}) async-start(bf16[8,12,640]{2,1,0:T(8,128)(2,1)} %attend.1), calls=%async_computation.1 | async-start | bytes 327680 | tf_op jit(solution)/shard_map/all_to_all | solution.py:641
  13.2 18.1 %copy-start = (bf16[1536,192]{0,1:T(8,128)(2,1)S(1)}, bf16[1536,192]{0,1:T(8,128)(2,1)}, u32[]{:S(2)}) copy-start(bf16[1536,192]{0,1:T(8,128)(2,1)} %param.21) | copy-start | bytes 1769476
  13.3 18.1 %copy-start.1 = (bf16[4,8,192]{2,1,0:T(8,128)(2,1)S(1)}, bf16[4,8,192]{2,1,0:T(8,128)(2,1)}, u32[]{:S(2)}) copy-start(bf16[4,8,192]{2,1,0:T(8,128)(2,1)} %residual_ref.1) | copy-start | bytes 36868
  13.3 18.1 %copy-start.2 = (s32[4,8,8]{2,1,0:T(8,128)S(1)}, s32[4,8,8]{2,1,0:T(8,128)}, u32[]{:S(2)}) copy-start(s32[4,8,8]{2,1,0:T(8,128)} %routes_ref.1) | copy-start | bytes 3076
  13.3 18.1 %copy-start.3 = (f32[192]{0:T(256)S(1)}, f32[192]{0:T(256)}, u32[]{:S(2)}) copy-start(f32[192]{0:T(256)} %param.22) | copy-start | bytes 2308
  13.3 23.9 %copy-start.5 = (bf16[192,40]{0,1:T(8,128)(2,1)S(1)}, bf16[192,40]{0,1:T(8,128)(2,1)}, u32[]{:S(2)}) copy-start(bf16[192,40]{0,1:T(8,128)(2,1)} %param.23) | copy-start | bytes 46084
  18.1 60.1 %copy-start.4 = (bf16[10,192,512]{2,1,0:T(8,128)(2,1)S(1)}, bf16[10,192,512]{2,1,0:T(8,128)(2,1)}, u32[]{:S(2)}) copy-start(bf16[10,192,512]{2,1,0:T(8,128)(2,1)} %w_ref.1) | copy-start | bytes 5898244
  21.4 3.7 %collective-permute-start.7 = (bf16[4,1536]{1,0:T(4,128)(2,1)S(1)}, bf16[4,1536]{1,0:T(4,128)(2,1)S(1)}, u32[]{:S(2)}, u32[]{:S(2)}) collective-permute-start(bf16[4,1536]{1,0:T(4,128)(2,1)S(1)} %join.1), channel_id=1, source_target_pairs={{0,4},{4,0},{8,12},{12,8},{16,20},{20,16},{24,28},{28,24},{1,5},{5... | collective-permute-start | bytes 36872 | tf_op jit(solution)/shard_map/ppermute | solution.py:684
  25.1 5.7 %collective-permute-start.8 = (bf16[2,4,1536]{2,1,0:T(4,128)(2,1)S(1)}, bf16[2,4,1536]{2,1,0:T(4,128)(2,1)S(1)}, u32[]{:S(2)}, u32[]{:S(2)}) collective-permute-start(bf16[2,4,1536]{2,1,0:T(4,128)(2,1)S(1)} %pad_maximum_fusion.refs_0_), channel_id=1, source_target_pairs={{0,8},{4,12},{8,16},{12,20},{16,24},{20,28},{24,0},{28,4},{1,9},{5... | collective-permute-start | bytes 73736 | tf_op jit(solution)/shard_map/ppermute | solution.py:637
  25.2 5.6 %collective-permute-start.9 = (bf16[2,4,1536]{2,1,0:T(4,128)(2,1)S(1)}, bf16[2,4,1536]{2,1,0:T(4,128)(2,1)S(1)}, u32[]{:S(2)}, u32[]{:S(2)}) collective-permute-start(bf16[2,4,1536]{2,1,0:T(4,128)(2,1)S(1)} %pad_maximum_fusion.refs_0_), channel_id=1, source_target_pairs={{0,16},{4,20},{8,24},{12,28},{16,0},{20,4},{24,8},{28,12},{1,17},{... | collective-permute-start | bytes 73736 | tf_op jit(solution)/shard_map/ppermute | solution.py:637
  26.7 4.7 %collective-permute-start.10 = (bf16[2,4,1536]{2,1,0:T(4,128)(2,1)S(1)}, bf16[2,4,1536]{2,1,0:T(4,128)(2,1)S(1)}, u32[]{:S(2)}, u32[]{:S(2)}) collective-permute-start(bf16[2,4,1536]{2,1,0:T(4,128)(2,1)S(1)} %pad_maximum_fusion.refs_0_), channel_id=1, source_target_pairs={{0,24},{4,28},{8,0},{12,4},{16,8},{20,12},{24,16},{28,20},{1,25},{... | collective-permute-start | bytes 73736 | tf_op jit(solution)/shard_map/ppermute | solution.py:637
  31.9 3.9 %collective-permute-start.11 = (bf16[32,256]{1,0:T(8,128)(2,1)S(1)}, bf16[32,256]{1,0:T(8,128)(2,1)S(1)}, u32[]{:S(2)}, u32[]{:S(2)}) collective-permute-start(bf16[32,256]{1,0:T(8,128)(2,1)S(1)} %get-tuple-element.102.refs_0_), channel_id=1, source_target_pairs={{0,1},{1,2},{2,3},{3,0},{4,5},{5,6},{6,7},{7,4},{8,9},{9,10},{10,1... | collective-permute-start | bytes 49160 | tf_op jit(solution)/shard_map/ppermute | solution.py:637
  32.0 4.1 %collective-permute-start.12 = (bf16[32,256]{1,0:T(8,128)(2,1)S(1)}, bf16[32,256]{1,0:T(8,128)(2,1)S(1)}, u32[]{:S(2)}, u32[]{:S(2)}) collective-permute-start(bf16[32,256]{1,0:T(8,128)(2,1)S(1)} %get-tuple-element.102.refs_0_), channel_id=1, source_target_pairs={{0,2},{1,3},{2,0},{3,1},{4,6},{5,7},{6,4},{7,5},{8,10},{9,11},{10,... | collective-permute-start | bytes 49160 | tf_op jit(solution)/shard_map/ppermute | solution.py:637
  34.4 2.8 %collective-permute-start.13 = (bf16[32,256]{1,0:T(8,128)(2,1)S(1)}, bf16[32,256]{1,0:T(8,128)(2,1)S(1)}, u32[]{:S(2)}, u32[]{:S(2)}) collective-permute-start(bf16[32,256]{1,0:T(8,128)(2,1)S(1)} %get-tuple-element.102.refs_0_), channel_id=1, source_target_pairs={{0,3},{1,0},{2,1},{3,2},{4,7},{5,4},{6,5},{7,6},{8,11},{9,8},{10,9... | collective-permute-start | bytes 49160 | tf_op jit(solution)/shard_map/ppermute | solution.py:637
  41.5 8.3 %collective-permute-start.14 = (bf16[368,128]{1,0:T(8,128)(2,1)S(1)}, bf16[368,128]{1,0:T(8,128)(2,1)S(1)}, u32[]{:S(2)}, u32[]{:S(2)}) collective-permute-start(bf16[368,128]{1,0:T(8,128)(2,1)S(1)} %get-tuple-element.108), channel_id=1, source_target_pairs={{0,4},{4,8},{8,12},{12,16},{16,20},{20,24},{24,28},{28,0},{1,5},{5... | collective-permute-start | bytes 282632 | tf_op jit(solution)/shard_map/ppermute | solution.py:637
  42.2 9.3 %collective-permute-start.15 = (bf16[368,128]{1,0:T(8,128)(2,1)S(1)}, bf16[368,128]{1,0:T(8,128)(2,1)S(1)}, u32[]{:S(2)}, u32[]{:S(2)}) collective-permute-start(bf16[368,128]{1,0:T(8,128)(2,1)S(1)} %get-tuple-element.109), channel_id=1, source_target_pairs={{0,8},{4,12},{8,16},{12,20},{16,24},{20,28},{24,0},{28,4},{1,9},{5... | collective-permute-start | bytes 282632 | tf_op jit(solution)/shard_map/ppermute | solution.py:637
  43.9 13.6 %collective-permute-start.16 = (bf16[368,128]{1,0:T(8,128)(2,1)S(1)}, bf16[368,128]{1,0:T(8,128)(2,1)S(1)}, u32[]{:S(2)}, u32[]{:S(2)}) collective-permute-start(bf16[368,128]{1,0:T(8,128)(2,1)S(1)} %get-tuple-element.110), channel_id=1, source_target_pairs={{0,12},{4,16},{8,20},{12,24},{16,28},{20,0},{24,4},{28,8},{1,13},{... | collective-permute-start | bytes 282632 | tf_op jit(solution)/shard_map/ppermute | solution.py:637
  46.9 10.7 %collective-permute-start.17 = (bf16[368,128]{1,0:T(8,128)(2,1)S(1)}, bf16[368,128]{1,0:T(8,128)(2,1)S(1)}, u32[]{:S(2)}, u32[]{:S(2)}) collective-permute-start(bf16[368,128]{1,0:T(8,128)(2,1)S(1)} %get-tuple-element.111), channel_id=1, source_target_pairs={{0,16},{4,20},{8,24},{12,28},{16,0},{20,4},{24,8},{28,12},{1,17},{... | collective-permute-start | bytes 282632 | tf_op jit(solution)/shard_map/ppermute | solution.py:637
  48.9 8.6 %collective-permute-start.18 = (bf16[368,128]{1,0:T(8,128)(2,1)S(1)}, bf16[368,128]{1,0:T(8,128)(2,1)S(1)}, u32[]{:S(2)}, u32[]{:S(2)}) collective-permute-start(bf16[368,128]{1,0:T(8,128)(2,1)S(1)} %get-tuple-element.112), channel_id=1, source_target_pairs={{0,20},{4,24},{8,28},{12,0},{16,4},{20,8},{24,12},{28,16},{1,21},{... | collective-permute-start | bytes 282632 | tf_op jit(solution)/shard_map/ppermute | solution.py:637
  49.8 9.4 %collective-permute-start.19 = (bf16[368,128]{1,0:T(8,128)(2,1)S(1)}, bf16[368,128]{1,0:T(8,128)(2,1)S(1)}, u32[]{:S(2)}, u32[]{:S(2)}) collective-permute-start(bf16[368,128]{1,0:T(8,128)(2,1)S(1)} %get-tuple-element.113), channel_id=1, source_target_pairs={{0,24},{4,28},{8,0},{12,4},{16,8},{20,12},{24,16},{28,20},{1,25},{... | collective-permute-start | bytes 282632 | tf_op jit(solution)/shard_map/ppermute | solution.py:637
  51.5 7.7 %collective-permute-start.20 = (bf16[368,128]{1,0:T(8,128)(2,1)S(1)}, bf16[368,128]{1,0:T(8,128)(2,1)S(1)}, u32[]{:S(2)}, u32[]{:S(2)}) collective-permute-start(bf16[368,128]{1,0:T(8,128)(2,1)S(1)} %get-tuple-element.114), channel_id=1, source_target_pairs={{0,28},{4,0},{8,4},{12,8},{16,12},{20,16},{24,20},{28,24},{1,29},{... | collective-permute-start | bytes 282632 | tf_op jit(solution)/shard_map/ppermute | solution.py:637
  60.3 18.0 %all-to-all-start.2 = ((bf16[8,176,128]{2,1,0:T(8,128)(2,1)}), bf16[8,176,128]{2,1,0:T(8,128)(2,1)S(1)}, u32[]{:S(2)}, u32[]{:S(2)}) async-start(bf16[8,176,128]{2,1,0:T(8,128)(2,1)} %get-tuple-element.116), calls=%async_computation.2 | async-start | bytes 720896 | tf_op jit(solution)/shard_map/all_to_all | solution.py:641
  80.4 2.2 %collective-permute-start.21 = (f32[32,256]{1,0:T(8,128)S(1)}, f32[32,256]{1,0:T(8,128)S(1)}, u32[]{:S(2)}, u32[]{:S(2)}) collective-permute-start(f32[32,256]{1,0:T(8,128)S(1)} %get-tuple-element.122), channel_id=1, source_target_pairs={{0,3},{1,0},{2,1},{3,2},{4,7},{5,4},{6,5},{7,6},{8,11},{9,8},{10,9... | collective-permute-start | bytes 98312 | tf_op jit(solution)/shard_map/ppermute | solution.py:637
  80.4 4.3 %collective-permute-start.22 = (f32[32,256]{1,0:T(8,128)S(1)}, f32[32,256]{1,0:T(8,128)S(1)}, u32[]{:S(2)}, u32[]{:S(2)}) collective-permute-start(f32[32,256]{1,0:T(8,128)S(1)} %get-tuple-element.123), channel_id=1, source_target_pairs={{0,2},{1,3},{2,0},{3,1},{4,6},{5,7},{6,4},{7,5},{8,10},{9,11},{10,... | collective-permute-start | bytes 98312 | tf_op jit(solution)/shard_map/ppermute | solution.py:637
  82.5 3.3 %collective-permute-start.23 = (f32[32,256]{1,0:T(8,128)S(1)}, f32[32,256]{1,0:T(8,128)S(1)}, u32[]{:S(2)}, u32[]{:S(2)}) collective-permute-start(f32[32,256]{1,0:T(8,128)S(1)} %get-tuple-element.124), channel_id=1, source_target_pairs={{0,1},{1,2},{2,3},{3,0},{4,5},{5,6},{6,7},{7,4},{8,9},{9,10},{10,1... | collective-permute-start | bytes 98312 | tf_op jit(solution)/shard_map/ppermute | solution.py:637

commit v6 on v5

--- a/solution.py
+++ b/solution.py
@@ -246,45 +246,86 @@
     )(seq_index, page_table, cache_len, queries, new_key_value, cache)
 
 
-def join_kernel(x_ref, out_ref):
-    blocks, rows, _ = x_ref.shape
-    tokens = rows // GROUP
-    levels = []
-    for b in range(blocks):
-        side = x_ref[b, :, KV_WIDTH : KV_WIDTH + LANES].astype(F32)
-        levels.append(side + pltpu.roll(side, LANES - 8, 1) + pltpu.roll(side, LANES - 16, 1))
+def levels_of(side):
+    side = side.astype(F32)
+    return side + pltpu.roll(side, LANES - 8, 1) + pltpu.roll(side, LANES - 16, 1)
+
+
+def blend(shares, rows):
+    levels = [levels_of(share[:, KV_WIDTH : KV_WIDTH + LANES]) for share in shares]
     largest = functools.reduce(jnp.maximum, levels)
     weights = [jnp.exp(level - largest) for level in levels]
-    inverse = 1.0 / functools.reduce(jnp.add, weights)
+    total = functools.reduce(jnp.add, weights)
+    inverse = 1.0 / total
     low = iota((rows, LANES), 1) < HEAD_SIZE
     acc = [jnp.zeros((rows, LANES), F32) for _ in range(KV_WIDTH // LANES)]
-    for b in range(blocks):
-        share = weights[b] * inverse
+    for weight, share in zip(weights, shares):
+        part = weight * inverse
         for j in range(KV_WIDTH // LANES):
-            factor = jnp.where(low, share[:, 2 * j : 2 * j + 1], share[:, 2 * j + 1 : 2 * j + 2])
-            acc[j] = acc[j] + factor * x_ref[b, :, j * LANES : (j + 1) * LANES].astype(F32)
-
-    def piece(head, half):
-        k, g = head // GROUP, head % GROUP
-        tile = jnp.concatenate(
-            [acc[k // 2][t * GROUP + g : t * GROUP + g + 1] for t in range(tokens)], axis=0
-        )
-        return tile if k % 2 == half else swap_halves(tile)
-
+            factor = jnp.where(low, part[:, 2 * j : 2 * j + 1], part[:, 2 * j + 1 : 2 * j + 2])
+            acc[j] = acc[j] + factor * tile_of(share, j).astype(F32)
+    return acc, largest, total
+
+
+def join_pair_kernel(seq_ref, own_ref, other_ref, *out_refs):
+    pairs = len(out_refs)
+    rows = own_ref.shape[1]
+    lane = iota((rows, LANES), 1)
+    for k, out_ref in enumerate(out_refs):
+        pair = lax.rem(seq_ref[0] // 2 + k, pairs)
+        for i in range(2):
+            at = 2 * pair + i
+            acc, largest, total = blend([own_ref[at], other_ref[at]], rows)
+            level = jnp.where(lane < KEY_VALUE_HEADS, largest + jnp.log(total), 0.0)
+            high = round16(level)
+            middle = round16(level - high)
+            rest = level - high - middle
+            side = high + pltpu.roll(middle, 8, 1) + pltpu.roll(rest, 16, 1)
+            for j, tile in enumerate(acc):
+                out_ref[i, :, j * LANES : (j + 1) * LANES] = tile.astype(BF16)
+            out_ref[i, :, KV_WIDTH : KV_WIDTH + LANES] = side.astype(BF16)
+
+
+def join_pair(seq_index, own, other):
+    devices, rows, width = own.shape
+    smem, vmem = pl.BlockSpec(memory_space=pltpu.SMEM), pl.BlockSpec(memory_space=pltpu.VMEM)
+    return pl.pallas_call(
+        join_pair_kernel,
+        in_specs=[smem, vmem, vmem],
+        out_shape=(jax.ShapeDtypeStruct((2, rows, width), BF16),) * (devices // 2),
+        compiler_params=params(),
+        name="join_pair",
+    )(seq_index, own, other)
+
+
+def join_kernel(*refs):
+    x_refs, out_ref = refs[:-1], refs[-1]
+    _, rows, _ = x_refs[0].shape
+    tokens = rows // GROUP
     low_tokens = iota((tokens, LANES), 1) < HEAD_SIZE
-    for m in range(QUERY_HEADS // 2):
-        tile = jnp.where(low_tokens, piece(2 * m, 0), piece(2 * m + 1, 1)).astype(BF16)
-        out_ref[:, m * LANES : (m + 1) * LANES] = tile
+    for i in range(2):
+        acc, _, _ = blend([x_ref[i] for x_ref in x_refs], rows)
+
+        def piece(head, half):
+            k, g = head // GROUP, head % GROUP
+            tile = jnp.concatenate(
+                [acc[k // 2][t * GROUP + g : t * GROUP + g + 1] for t in range(tokens)], axis=0
+            )
+            return tile if k % 2 == half else swap_halves(tile)
+
+        for m in range(QUERY_HEADS // 2):
+            tile = jnp.where(low_tokens, piece(2 * m, 0), piece(2 * m + 1, 1)).astype(BF16)
+            out_ref[i, :, m * LANES : (m + 1) * LANES] = tile
 
 
 def join(parts):
-    rows = parts.shape[1]
+    rows = parts[0].shape[1]
     return pl.pallas_call(
         join_kernel,
-        out_shape=jax.ShapeDtypeStruct((rows // GROUP, QUERY_HEADS * HEAD_SIZE), BF16),
+        out_shape=jax.ShapeDtypeStruct((2, rows // GROUP, QUERY_HEADS * HEAD_SIZE), BF16),
         compiler_params=params(),
         name="join",
-    )(parts)
+    )(*parts)
 
 
 def side_place(features, count):
@@ -300,11 +341,9 @@
     attn = jnp.concatenate(blocks, axis=0).astype(BF16)
     row, column = iota((tokens, tokens), 0), iota((tokens, tokens), 1)
     devices, share = len(blocks), attn_refs[0].shape[1]
-    source = seq_ref[0] + devices - column // (2 * share) * 2
+    source = seq_ref[0] // 2 * 2 + devices - column // (2 * share) * 2
     source = jnp.where(source >= devices, source - devices, source)
-    other = column // share % 2
-    source = source + other * (1 - source % 2 * 2)
-    token = source * share + column % share
+    token = source * share + column % (2 * share)
     reorder = jnp.logical_and(row % requests == token // steps, row // requests == token % steps)
     attn = dot_nn(reorder.astype(F32).astype(BF16), attn).astype(BF16)
     residual = residual_ref[...].astype(F32).reshape(tokens, features)
@@ -352,7 +391,7 @@
 ):
     part_refs, refs = refs[:sources], refs[sources:]
     out_refs, refs = refs[:devices], refs[devices:]
-    pick_ref, range_ref, first_ref, most_ref, x_ref, row_ref, acc_ref, share_ref = refs
+    pick_ref, range_ref, first_ref, most_ref, x_ref, pair_ref, acc_ref, share_ref = refs
     total = x_ref.shape[0]
     for e, part_ref in enumerate(part_refs):
         x_ref[e * (total // sources) : (e + 1) * (total // sources)] = part_ref[...]
@@ -392,18 +431,28 @@
     ranges = jnp.concatenate([ranges[0:8], ranges[8:16]] + [jnp.zeros((LANES - 16, LANES), F32)], axis=0)
     ranges = ranges.T
     range_ref[...] = ranges[0:16]
-    row_ref[...] = dot_tn(pick, x_ref[...]).astype(BF16)
+    picked = dot_tn(pick, x_ref[...]).astype(BF16)
+    doubled = pair_ref.shape[2]
+    feature, place = iota((x_ref.shape[1], doubled), 0), iota((x_ref.shape[1], doubled), 1)
+    double = jnp.logical_and(place == 2 * feature, feature < features)
+    evens = dot_nn(picked, double.astype(F32).astype(BF16))
+    pair_ref[0] = evens.astype(BF16)
+    for j in range(doubled // LANES):
+        odds = pltpu.roll(tile_of(evens, j), 1, 1)
+        pair_ref[1, :, j * LANES : (j + 1) * LANES] = odds.astype(BF16)
     acc_ref[...] = jnp.zeros_like(acc_ref)
     for j in range(local):
         start_row = jnp.sum(first[:, j : j + 1]).astype(jnp.int32)
         first_ref[j] = start_row
         start = window_start(start_row, rows, window)
-        part = row_ref[pl.ds(start, window), 0:features]
+        part = jnp.concatenate(
+            [pair_ref[half, pl.ds(start, window), 0 : 2 * features] for half in range(2)], axis=0
+        )
+        made = dot_nn(part, w_ref[j].reshape(2 * features, width))
         fresh = start + iota((window, width), 0) >= start_row
         for half in range(2):
             into = (pl.ds(start, window), slice(half * width, (half + 1) * width))
-            made = dot_nn(part, w_ref[j, half])
-            acc_ref[into] = jnp.where(fresh, made, acc_ref[into])
+            acc_ref[into] = jnp.where(fresh, made[half * window : (half + 1) * window], acc_ref[into])
     logits = dot_nt(router_ref[...], x_ref[:, 0:features])
     high = round16(logits)
     both = jnp.concatenate([high, logits - high], axis=0).astype(BF16)
@@ -454,7 +503,7 @@
 
 
 def gate_up(exp_index, seq_index, tokens, weights, w_router, rows, devices, turn):
-    local, _, features, width = weights.shape
+    local, features, _, width = weights.shape
     sources, wide = len(tokens), tokens[0].shape[1]
     total = sources * tokens[0].shape[0]
     share = (rows * PIECES // devices + 16, LANES)
@@ -472,7 +521,7 @@
         ),
         scratch_shapes=[
             pltpu.VMEM((total, wide), BF16),
-            pltpu.VMEM((rows, wide), BF16),
+            pltpu.VMEM((2, rows, padded(2 * features)), BF16),
             pltpu.VMEM((rows, 2 * width), F32),
             pltpu.VMEM((devices,) + share, BF16),
         ],
@@ -503,15 +552,14 @@
     made = scaled / (1.0 + jnp.exp(-scaled)) * swap_halves(scaled)
     low = iota((half, LANES), 1) < PIECE_WIDTH
     made = jnp.where(low, made[0:half], swap_halves(made[half:share])).astype(BF16)
-    for b in range(out_ref.shape[0]):
-        out_ref[b] = made
+    out_ref[...] = made
 
 
 def inner(parts):
     return pl.pallas_call(
         inner_kernel,
         out_shape=(
-            jax.ShapeDtypeStruct((len(parts), (parts[0].shape[0] - 16) // 2, LANES), BF16),
+            jax.ShapeDtypeStruct(((parts[0].shape[0] - 16) // 2, LANES), BF16),
             jax.ShapeDtypeStruct((8, LANES), F32),
         ),
         compiler_params=params(),
@@ -519,12 +567,16 @@
     )(*parts)
 
 
-def down_kernel(features, local, first_ref, range_ref, pick_ref, w_ref, logit_ref, x_ref, *refs):
-    out_refs, (row_ref, made_ref) = refs[:-2], refs[-2:]
+def down_kernel(features, local, pairs, first_ref, seq_ref, range_ref, pick_ref, w_ref, logit_ref, *refs):
+    pair_refs, out_refs, (x_ref, row_ref, made_ref) = refs[:pairs], refs[pairs:-3], refs[-3:]
     total, rows = pick_ref.shape
     width = w_ref.shape[2]
     window = total // 2 + 16
     devices, half, _ = x_ref.shape
+    for k, pair_ref in enumerate(pair_refs):
+        source = lax.rem(seq_ref[0] + devices - 2 * k, devices)
+        x_ref[source] = pair_ref[0]
+        x_ref[source + 1 - lax.rem(source, 2) * 2] = pair_ref[1]
     share = 2 * half
     low = iota((half, LANES), 1) < PIECE_WIDTH
     for b in range(0, devices, 2):
@@ -578,22 +630,23 @@
         out_ref[:, tile : tile + LANES] = jnp.where(lane == 1, pair[at, 1:2], side)
 
 
-def down(first, ranges, pick, made, logits, weights, exp_count):
+def down(first, seq_index, ranges, pick, made, logits, weights, exp_count):
     local, features, width = weights.shape
     total, rows = pick.shape
     wide = side_place(features, 2)[0] + LANES
     smem, vmem = pl.BlockSpec(memory_space=pltpu.SMEM), pl.BlockSpec(memory_space=pltpu.VMEM)
     return pl.pallas_call(
-        functools.partial(down_kernel, features, local),
-        in_specs=[smem] + [vmem] * 5,
+        functools.partial(down_kernel, features, local, len(made)),
+        in_specs=[smem] * 2 + [vmem] * (4 + len(made)),
         out_shape=(jax.ShapeDtypeStruct((total // exp_count, wide), F32),) * exp_count,
         scratch_shapes=[
+            pltpu.VMEM((2 * len(made),) + made[0].shape[1:], BF16),
             pltpu.VMEM((rows, width), BF16),
             pltpu.VMEM((rows, wide), F32),
         ],
         compiler_params=params(),
         name="down",
-    )(first, ranges, pick, weights, logits, made)
+    )(first, seq_index, ranges, pick, weights, logits, *made)
 
 
 def finish_kernel(hidden_ref, *refs):
@@ -637,8 +690,8 @@
     return lax.ppermute(x, axis, [(i, (i + distance) % count) for i in range(count)])
 
 
-def swap(x, axis):
-    return lax.all_to_all(x, axis, split_axis=0, concat_axis=0, tiled=True)
+def neighbour(x, axis):
+    return lax.ppermute(x, axis, [(i, i ^ 1) for i in range(lax.axis_size(axis))])
 
 
 def exchange(parts, axis, direction):
@@ -676,14 +729,9 @@
     shares = attend(
         queries, new_key_value, pool, page_table, cache_len, seq_index, seq_count
     )
-    w_gate_up, shares = lax.optimization_barrier((w_gate_up, shares))
-    gate_up_weights = w_gate_up.transpose(0, 2, 1, 3)
-    shares = swap(shares, "seq")
-    gate_up_weights, shares = lax.optimization_barrier((gate_up_weights, shares))
-    attn = join(shares)
-    beside = lax.ppermute(attn, "seq", [(i, i ^ 1) for i in range(seq_count)])
-    pair = jnp.stack([attn, beside])
-    gathered = [pair] + [send(pair, "seq", k) for k in range(2, seq_count, 2)]
+    shares = join_pair(seq_index, shares, neighbour(shares, "seq"))
+    attn = join(exchange(shares, "seq", 2))
+    gathered = exchange([attn] * (seq_count // 2), "seq", 2)
     hidden, outgoing = hidden_state(seq_index, gathered, residual, w_out, norm_gain, routes)
     incoming = gather(outgoing, "exp")
     pieces = seq_count // PIECES
@@ -691,11 +739,13 @@
 
     def one_round(turn):
         *partial, pick, ranges, first, most = gate_up(
-            exp_index, seq_index, incoming, gate_up_weights, w_router, rows, seq_count, turn
+            exp_index, seq_index, incoming, w_gate_up, w_router, rows, seq_count, turn
         )
         made, logits = inner(exchange(partial, "seq", 1))
         logits = logits[None] if pieces == 1 else lax.all_gather(logits, "seq")[::PIECES]
-        return down(first, ranges, pick, swap(made, "seq"), logits, w_down, exp_count), most
+        made = jnp.stack([made, neighbour(made, "seq")])
+        made = exchange([made] * (seq_count // 2), "seq", 2)
+        return down(first, seq_index, ranges, pick, made, logits, w_down, exp_count), most
 
     made, most = one_round(0)
     pairs = w_gate_up.shape[0] * exp_count * steps * CAP

time: 87.4 us -> 85.9 us (0.983)
  local copies, waits for them, and re-layouts: 4.88 us -> 0.94 us
  Pallas kernels: 19 us -> 21.4 us
    all_to_all x2 -> x0, waiting for transfers between devices: 12.7 us -> none  [swap(): return lax.all_to_all(x, axis, split_axis=0, concat_axis=0, tiled=True)]
    all_to_all x2 -> x0, starting transfers between devices: 10.8 us -> none  [swap(): return lax.all_to_all(x, axis, split_axis=0, concat_axis=0, tiled=True)]
    ppermute x16 -> x22, waiting for transfers between devices: 12 us -> 21.1 us  [send(): lax.ppermute(x, axis, [(i, (i + distance) % count) for i in range(count)])]
    ppermute x16 -> x22, starting transfers between devices: 22.7 us -> 28.7 us  [send(): lax.ppermute(x, axis, [(i, (i + distance) % count) for i in range(count)])]
    optimization_barrier x1 -> x0, local copies, waits for them, and re-layouts: 4.84 us -> none  [local(): w_gate_up, shares = lax.optimization_barrier((w_gate_up, shares))]
    ppermute x1 -> x2, starting transfers between devices: 0.35 us -> 5.09 us  [neighbour(): lax.ppermute(x, axis, [(i, i ^ 1) for i in range(lax.axis_size(axis))])]
    ppermute x1 -> x2, waiting for transfers between devices: 3.35 us -> 7.76 us  [neighbour(): lax.ppermute(x, axis, [(i, i ^ 1) for i in range(lax.axis_size(axis))])]
    pallas_call x1, Pallas kernels: 9.83 us -> 10.8 us  [attend(): pl.pallas_call(functools.partial(attend_kernel, classes), in_specs=[smem]...]
  transfers between devices with their start and end apart: 19 -> 24, of which waited for: 11 -> 16; matrix products, arithmetic and copies ran while one was open for 6% -> 0% of each run, Pallas kernels for 0% -> 0%
where the time goes in v6:
time: 85.9 us
  starting transfers between devices  33.8 us (39%)
  waiting for transfers between devices  28.8 us (34%)
  Pallas kernels  21.4 us (25%)
  local copies, waits for them, and re-layouts  0.94 us (1%)
    ppermute x22, starting transfers between devices, send(): lax.ppermute(x, axis, [(i, (i + distance) % count) for i in range(count)])  28.7 us
    ppermute x22, waiting for transfers between devices, send(): lax.ppermute(x, axis, [(i, (i + distance) % count) for i in range(count)])  21.1 us
    pallas_call x1, Pallas kernels, attend(): pl.pallas_call(functools.partial(attend_kernel, classes), in_specs=[smem]...  10.8 us
    ppermute x2, waiting for transfers between devices, neighbour(): lax.ppermute(x, axis, [(i, i ^ 1) for i in range(lax.axis_size(axis))])  7.76 us
    pallas_call x1, Pallas kernels, gate_up(): pl.pallas_call(functools.partial(gate_up_kernel, features, local, turn, s...  5.16 us
    ppermute x2, starting transfers between devices, neighbour(): lax.ppermute(x, axis, [(i, i ^ 1) for i in range(lax.axis_size(axis))])  5.09 us
    pallas_call x1, Pallas kernels, down(): pl.pallas_call(functools.partial(down_kernel, features, local, len(made))...  2.15 us
  transfers between devices with their start and end apart: 24, of which 16 were waited for; matrix products, arithmetic and copies ran while one was open for 0% of the time, Pallas kernels for 0%

profile of v6, /device:TPU:0, one launch (start us, length us, event | category | flops | bytes accessed | tf_op | source)
XLA Modules:
  0.0 85.9 jit_solution(4918910308133465607)
XLA Ops:
  0.0 10.8 %attend.1.own_ref = bf16[8,12,640]{2,1,0:T(8,128)(2,1)} custom-call(s32[1]{0:T(128)} %bitcast.4.seq_ref, s32[8,8]{1,0:T(8,128)} %table_hbm.1, s32[8]{0:T(128)} %len_hbm.1, bf16[4,8,1536]{2,1,0:T(8,128)(2,1)} %q_hbm.1, bf16[4,8,2,512]{3,2,1,0:T(2,128)(2,1)} %fresh_hbm.1, bf16[64,64,2,512]{3,2,1,0:T(2,128)(2,1)} %bitcast.20), custom_call_target="tpu_custom_call" | custom-call | tf_op jit(solution)/shard_map/attend/pallas_call | solution.py:228
  10.8 1.1 %collective-permute-start.11 = (bf16[8,12,640]{2,1,0:T(8,128)(2,1)}, bf16[8,12,640]{2,1,0:T(8,128)(2,1)S(1)}, u32[]{:S(2)}, u32[]{:S(2)}) collective-permute-start(bf16[8,12,640]{2,1,0:T(8,128)(2,1)} %attend.1.own_ref), channel_id=1, source_target_pairs={{0,4},{4,0},{8,12},{12,8},{16,20},{20,16},{24,28},{28,24},{1,5},{5... | collective-permute-start | bytes 368648 | tf_op jit(solution)/shard_map/ppermute | solution.py:694
  11.9 5.7 %collective-permute-done.11.other_ref = bf16[8,12,640]{2,1,0:T(8,128)(2,1)S(1)} collective-permute-done((bf16[8,12,640]{2,1,0:T(8,128)(2,1)}, bf16[8,12,640]{2,1,0:T(8,128)(2,1)S(1)}, u32[]{:S(2)}, u32[]{:S(2)}) %collective-permute-start.11) | collective-permute-done | bytes 122912 | tf_op jit(solution)/shard_map/ppermute | solution.py:694
  17.7 0.9 %copy-done = bf16[8,12,640]{2,1,0:T(8,128)(2,1)S(1)} copy-done((bf16[8,12,640]{2,1,0:T(8,128)(2,1)S(1)}, bf16[8,12,640]{2,1,0:T(8,128)(2,1)}, u32[]{:S(2)}) %copy-start) | copy-done | bytes 122904
  18.6 1.2 %join_pair.1 = (bf16[2,12,640]{2,1,0:T(8,128)(2,1)S(1)}, bf16[2,12,640]{2,1,0:T(8,128)(2,1)S(1)}, bf16[2,12,640]{2,1,0:T(8,128)(2,1)S(1)}, bf16[2,12,640]{2,1,0:T(8,128)(2,1)S(1)}) custom-call(s32[1]{0:T(128)} %bitcast.4.seq_ref, bf16[8,12,640]{2,1,0:T(8,128)(2,1)S(1)} %copy-done, bf16[8,12,640]{2,1,0:T(8,128)(2,1)S(1)} %collective-permute-done.11.other_ref), custom_call_target="tpu_custom_call" | custom-call | tf_op jit(solution)/shard_map/join_pair/pallas_call | solution.py:292
  19.9 3.7 %collective-permute-start.14 = (bf16[2,12,640]{2,1,0:T(8,128)(2,1)S(1)}, bf16[2,12,640]{2,1,0:T(8,128)(2,1)S(1)}, u32[]{:S(2)}, u32[]{:S(2)}) collective-permute-start(bf16[2,12,640]{2,1,0:T(8,128)(2,1)S(1)} %get-tuple-element.100), channel_id=1, source_target_pairs={{0,24},{4,28},{8,0},{12,4},{16,8},{20,12},{24,16},{28,20},{1,25},{... | collective-permute-start | bytes 92168 | tf_op jit(solution)/shard_map/ppermute | solution.py:690
  23.6 2.0 %collective-permute-done.12.refs_1_ = bf16[2,12,640]{2,1,0:T(8,128)(2,1)S(1)} collective-permute-done((bf16[2,12,640]{2,1,0:T(8,128)(2,1)S(1)}, bf16[2,12,640]{2,1,0:T(8,128)(2,1)S(1)}, u32[]{:S(2)}, u32[]{:S(2)}) %collective-permute-start.12) | collective-permute-done | bytes 30752 | tf_op jit(solution)/shard_map/ppermute | solution.py:690
  26.7 2.0 %collective-permute-start.15 = (bf16[2,4,1536]{2,1,0:T(4,128)(2,1)S(1)}, bf16[2,4,1536]{2,1,0:T(4,128)(2,1)S(1)}, u32[]{:S(2)}, u32[]{:S(2)}) collective-permute-start(bf16[2,4,1536]{2,1,0:T(4,128)(2,1)S(1)} %join.1.refs_0_), channel_id=1, source_target_pairs={{0,8},{4,12},{8,16},{12,20},{16,24},{20,28},{24,0},{28,4},{1,9},{5... | collective-permute-start | bytes 73736 | tf_op jit(solution)/shard_map/ppermute | solution.py:690
  28.8 1.8 %collective-permute-start.16 = (bf16[2,4,1536]{2,1,0:T(4,128)(2,1)S(1)}, bf16[2,4,1536]{2,1,0:T(4,128)(2,1)S(1)}, u32[]{:S(2)}, u32[]{:S(2)}) collective-permute-start(bf16[2,4,1536]{2,1,0:T(4,128)(2,1)S(1)} %join.1.refs_0_), channel_id=1, source_target_pairs={{0,16},{4,20},{8,24},{12,28},{16,0},{20,4},{24,8},{28,12},{1,17},{... | collective-permute-start | bytes 73736 | tf_op jit(solution)/shard_map/ppermute | solution.py:690
  31.2 1.2 %collective-permute-done.15.refs_1_ = bf16[2,4,1536]{2,1,0:T(4,128)(2,1)S(1)} collective-permute-done((bf16[2,4,1536]{2,1,0:T(4,128)(2,1)S(1)}, bf16[2,4,1536]{2,1,0:T(4,128)(2,1)S(1)}, u32[]{:S(2)}, u32[]{:S(2)}) %collective-permute-start.15) | collective-permute-done | bytes 24608 | tf_op jit(solution)/shard_map/ppermute | solution.py:690
  32.4 1.1 %collective-permute-done.16.refs_2_ = bf16[2,4,1536]{2,1,0:T(4,128)(2,1)S(1)} collective-permute-done((bf16[2,4,1536]{2,1,0:T(4,128)(2,1)S(1)}, bf16[2,4,1536]{2,1,0:T(4,128)(2,1)S(1)}, u32[]{:S(2)}, u32[]{:S(2)}) %collective-permute-start.16) | collective-permute-done | bytes 24608 | tf_op jit(solution)/shard_map/ppermute | solution.py:690
  33.5 0.9 %collective-permute-done.17.refs_3_ = bf16[2,4,1536]{2,1,0:T(4,128)(2,1)S(1)} collective-permute-done((bf16[2,4,1536]{2,1,0:T(4,128)(2,1)S(1)}, bf16[2,4,1536]{2,1,0:T(4,128)(2,1)S(1)}, u32[]{:S(2)}, u32[]{:S(2)}) %collective-permute-start.17) | collective-permute-done | bytes 24608 | tf_op jit(solution)/shard_map/ppermute | solution.py:690
  34.9 0.8 collective-permute-start.19
  35.8 1.4 %collective-permute-start.20 = (bf16[32,256]{1,0:T(8,128)(2,1)S(1)}, bf16[32,256]{1,0:T(8,128)(2,1)S(1)}, u32[]{:S(2)}, u32[]{:S(2)}) collective-permute-start(bf16[32,256]{1,0:T(8,128)(2,1)S(1)} %get-tuple-element.102.refs_0_), channel_id=1, source_target_pairs={{0,3},{1,0},{2,1},{3,2},{4,7},{5,4},{6,5},{7,6},{8,11},{9,8},{10,9... | collective-permute-start | bytes 49160 | tf_op jit(solution)/shard_map/ppermute | solution.py:690
  37.2 0.9 %collective-permute-done.18.refs_1_ = bf16[32,256]{1,0:T(8,128)(2,1)S(1)} collective-permute-done((bf16[32,256]{1,0:T(8,128)(2,1)S(1)}, bf16[32,256]{1,0:T(8,128)(2,1)S(1)}, u32[]{:S(2)}, u32[]{:S(2)}) %collective-permute-start.18) | collective-permute-done | bytes 16416 | tf_op jit(solution)/shard_map/ppermute | solution.py:690
  38.8 5.2 %gate_up.3 = (bf16[368,128]{1,0:T(8,128)(2,1)S(1)}, bf16[368,128]{1,0:T(8,128)(2,1)S(1)}, bf16[368,128]{1,0:T(8,128)(2,1)S(1)}, bf16[368,128]{1,0:T(8,128)(2,1)S...) custom-call(s32[1]{0:T(128)} %bitcast.8.where_ref, ...), custom_call_target="tpu_custom_call" | custom-call | tf_op jit(solution)/shard_map/gate_up/pallas_call | solution.py:511
  43.9 1.3 %collective-permute-start.21 = (bf16[368,128]{1,0:T(8,128)(2,1)S(1)}, bf16[368,128]{1,0:T(8,128)(2,1)S(1)}, u32[]{:S(2)}, u32[]{:S(2)}) collective-permute-start(bf16[368,128]{1,0:T(8,128)(2,1)S(1)} %get-tuple-element.108), channel_id=1, source_target_pairs={{0,4},{4,8},{8,12},{12,16},{16,20},{20,24},{24,28},{28,0},{1,5},{5... | collective-permute-start | bytes 282632 | tf_op jit(solution)/shard_map/ppermute | solution.py:690
  45.8 2.7 %collective-permute-start.23 = (bf16[368,128]{1,0:T(8,128)(2,1)S(1)}, bf16[368,128]{1,0:T(8,128)(2,1)S(1)}, u32[]{:S(2)}, u32[]{:S(2)}) collective-permute-start(bf16[368,128]{1,0:T(8,128)(2,1)S(1)} %get-tuple-element.110), channel_id=1, source_target_pairs={{0,12},{4,16},{8,20},{12,24},{16,28},{20,0},{24,4},{28,8},{1,13},{... | collective-permute-start | bytes 282632 | tf_op jit(solution)/shard_map/ppermute | solution.py:690
  48.4 1.4 %collective-permute-start.24 = (bf16[368,128]{1,0:T(8,128)(2,1)S(1)}, bf16[368,128]{1,0:T(8,128)(2,1)S(1)}, u32[]{:S(2)}, u32[]{:S(2)}) collective-permute-start(bf16[368,128]{1,0:T(8,128)(2,1)S(1)} %get-tuple-element.111), channel_id=1, source_target_pairs={{0,16},{4,20},{8,24},{12,28},{16,0},{20,4},{24,8},{28,12},{1,17},{... | collective-permute-start | bytes 282632 | tf_op jit(solution)/shard_map/ppermute | solution.py:690
  49.9 2.2 %collective-permute-start.25 = (bf16[368,128]{1,0:T(8,128)(2,1)S(1)}, bf16[368,128]{1,0:T(8,128)(2,1)S(1)}, u32[]{:S(2)}, u32[]{:S(2)}) collective-permute-start(bf16[368,128]{1,0:T(8,128)(2,1)S(1)} %get-tuple-element.112), channel_id=1, source_target_pairs={{0,20},{4,24},{8,28},{12,0},{16,4},{20,8},{24,12},{28,16},{1,21},{... | collective-permute-start | bytes 282632 | tf_op jit(solution)/shard_map/ppermute | solution.py:690
  52.1 1.0 %collective-permute-start.26 = (bf16[368,128]{1,0:T(8,128)(2,1)S(1)}, bf16[368,128]{1,0:T(8,128)(2,1)S(1)}, u32[]{:S(2)}, u32[]{:S(2)}) collective-permute-start(bf16[368,128]{1,0:T(8,128)(2,1)S(1)} %get-tuple-element.113), channel_id=1, source_target_pairs={{0,24},{4,28},{8,0},{12,4},{16,8},{20,12},{24,16},{28,20},{1,25},{... | collective-permute-start | bytes 282632 | tf_op jit(solution)/shard_map/ppermute | solution.py:690
  53.1 1.9 %collective-permute-start.27 = (bf16[368,128]{1,0:T(8,128)(2,1)S(1)}, bf16[368,128]{1,0:T(8,128)(2,1)S(1)}, u32[]{:S(2)}, u32[]{:S(2)}) collective-permute-start(bf16[368,128]{1,0:T(8,128)(2,1)S(1)} %get-tuple-element.114), channel_id=1, source_target_pairs={{0,28},{4,0},{8,4},{12,8},{16,12},{20,16},{24,20},{28,24},{1,29},{... | collective-permute-start | bytes 282632 | tf_op jit(solution)/shard_map/ppermute | solution.py:690
  55.0 5.4 %collective-permute-done.23.refs_3_ = bf16[368,128]{1,0:T(8,128)(2,1)S(1)} collective-permute-done((bf16[368,128]{1,0:T(8,128)(2,1)S(1)}, bf16[368,128]{1,0:T(8,128)(2,1)S(1)}, u32[]{:S(2)}, u32[]{:S(2)}) %collective-permute-start.23) | collective-permute-done | bytes 94240 | tf_op jit(solution)/shard_map/ppermute | solution.py:690
  61.1 4.0 %collective-permute-start.28 = (bf16[176,128]{1,0:T(8,128)(2,1)S(1)}, bf16[176,128]{1,0:T(8,128)(2,1)S(1)}, u32[]{:S(2)}, u32[]{:S(2)}) collective-permute-start(bf16[176,128]{1,0:T(8,128)(2,1)S(1)} %get-tuple-element.116), channel_id=1, source_target_pairs={{0,4},{4,0},{8,12},{12,8},{16,20},{20,16},{24,28},{28,24},{1,5},{5... | collective-permute-start | bytes 135176 | tf_op jit(solution)/shard_map/ppermute | solution.py:694
  65.1 2.0 %collective-permute-done.28 = bf16[176,128]{1,0:T(8,128)(2,1)S(1)} collective-permute-done((bf16[176,128]{1,0:T(8,128)(2,1)S(1)}, bf16[176,128]{1,0:T(8,128)(2,1)S(1)}, u32[]{:S(2)}, u32[]{:S(2)}) %collective-permute-start.28) | collective-permute-done | bytes 45088 | tf_op jit(solution)/shard_map/ppermute | solution.py:694
  67.1 4.1 %collective-permute-start.29 = (bf16[2,176,128]{2,1,0:T(8,128)(2,1)S(1)}, bf16[2,176,128]{2,1,0:T(8,128)(2,1)S(1)}, u32[]{:S(2)}, u32[]{:S(2)}) collective-permute-start(bf16[2,176,128]{2,1,0:T(8,128)(2,1)S(1)} %pad_maximum_fusion.1.refs_0_), channel_id=1, source_target_pairs={{0,8},{4,12},{8,16},{12,20},{16,24},{20,28},{24,0},{28,4},{1,9},{5... | collective-permute-start | bytes 270344 | tf_op jit(solution)/shard_map/ppermute | solution.py:690
  71.2 0.8 collective-permute-start.30
  72.0 1.6 %collective-permute-start.31 = (bf16[2,176,128]{2,1,0:T(8,128)(2,1)S(1)}, bf16[2,176,128]{2,1,0:T(8,128)(2,1)S(1)}, u32[]{:S(2)}, u32[]{:S(2)}) collective-permute-start(bf16[2,176,128]{2,1,0:T(8,128)(2,1)S(1)} %pad_maximum_fusion.1.refs_0_), channel_id=1, source_target_pairs={{0,24},{4,28},{8,0},{12,4},{16,8},{20,12},{24,16},{28,20},{1,25},{... | collective-permute-start | bytes 270344 | tf_op jit(solution)/shard_map/ppermute | solution.py:690
  74.8 3.7 %collective-permute-done.30.refs_2_ = bf16[2,176,128]{2,1,0:T(8,128)(2,1)S(1)} collective-permute-done((bf16[2,176,128]{2,1,0:T(8,128)(2,1)S(1)}, bf16[2,176,128]{2,1,0:T(8,128)(2,1)S(1)}, u32[]{:S(2)}, u32[]{:S(2)}) %collective-permute-start.30) | collective-permute-done | bytes 90144 | tf_op jit(solution)/shard_map/ppermute | solution.py:690
  78.4 2.1 %down.3 = (f32[32,256]{1,0:T(8,128)S(1)}, f32[32,256]{1,0:T(8,128)S(1)}, f32[32,256]{1,0:T(8,128)S(1)}, f32[32,256]{1,0:T(8,128)S(1)}) custom-call(s32[16]{0:T(128)S(1)} %get-tuple-element.104.first_ref, s32[1]{0:T(128)} %bitcast.4.seq_ref, f32[16,128]{1,0:T(8,128)S(1)} %get-tuple-element.105.range_ref, bf16[128,352]{1,0:T(8,128)(2,1)S(1)} %get-tuple-element.106.pick_ref, ...), custom_call_target="tpu_custom_call" | custom-call | tf_op jit(solution)/shard_map/down/pallas_call | solution.py:638
  81.5 1.1 %collective-permute-done.32.refs_1_ = f32[32,256]{1,0:T(8,128)S(1)} collective-permute-done((f32[32,256]{1,0:T(8,128)S(1)}, f32[32,256]{1,0:T(8,128)S(1)}, u32[]{:S(2)}, u32[]{:S(2)}) %collective-permute-start.32) | collective-permute-done | bytes 32800 | tf_op jit(solution)/shard_map/ppermute | solution.py:690
  82.6 2.6 %collective-permute-done.33.refs_2_ = f32[32,256]{1,0:T(8,128)S(1)} collective-permute-done((f32[32,256]{1,0:T(8,128)S(1)}, f32[32,256]{1,0:T(8,128)S(1)}, u32[]{:S(2)}, u32[]{:S(2)}) %collective-permute-start.33) | collective-permute-done | bytes 32800 | tf_op jit(solution)/shard_map/ppermute | solution.py:690
  (40 shorter events, 6.6 us)
Async XLA Ops:
  0.0 34.4 %copy-start.1 = (bf16[1536,192]{0,1:T(8,128)(2,1)S(1)}, bf16[1536,192]{0,1:T(8,128)(2,1)}, u32[]{:S(2)}) copy-start(bf16[1536,192]{0,1:T(8,128)(2,1)} %param.21) | copy-start | bytes 1769476
  0.0 34.4 %copy-start.2 = (bf16[4,8,192]{2,1,0:T(8,128)(2,1)S(1)}, bf16[4,8,192]{2,1,0:T(8,128)(2,1)}, u32[]{:S(2)}) copy-start(bf16[4,8,192]{2,1,0:T(8,128)(2,1)} %residual_ref.1) | copy-start | bytes 36868
  0.0 34.4 %copy-start.3 = (s32[4,8,8]{2,1,0:T(8,128)S(1)}, s32[4,8,8]{2,1,0:T(8,128)}, u32[]{:S(2)}) copy-start(s32[4,8,8]{2,1,0:T(8,128)} %routes_ref.1) | copy-start | bytes 3076
  0.0 34.4 %copy-start.4 = (f32[192]{0:T(256)S(1)}, f32[192]{0:T(256)}, u32[]{:S(2)}) copy-start(f32[192]{0:T(256)} %param.22) | copy-start | bytes 2308
  0.0 38.8 %copy-start.6 = (bf16[192,40]{0,1:T(8,128)(2,1)S(1)}, bf16[192,40]{0,1:T(8,128)(2,1)}, u32[]{:S(2)}) copy-start(bf16[192,40]{0,1:T(8,128)(2,1)} %param.23) | copy-start | bytes 46084
  0.0 78.4 %copy-start.5 = (bf16[10,192,512]{2,1,0:T(8,128)(2,1)S(1)}, bf16[10,192,512]{2,1,0:T(8,128)(2,1)}, u32[]{:S(2)}) copy-start(bf16[10,192,512]{2,1,0:T(8,128)(2,1)} %w_ref.3) | copy-start | bytes 5898244
  10.8 6.8 %collective-permute-start.11 = (bf16[8,12,640]{2,1,0:T(8,128)(2,1)}, bf16[8,12,640]{2,1,0:T(8,128)(2,1)S(1)}, u32[]{:S(2)}, u32[]{:S(2)}) collective-permute-start(bf16[8,12,640]{2,1,0:T(8,128)(2,1)} %attend.1.own_ref), channel_id=1, source_target_pairs={{0,4},{4,0},{8,12},{12,8},{16,20},{20,16},{24,28},{28,24},{1,5},{5... | collective-permute-start | bytes 368648 | tf_op jit(solution)/shard_map/ppermute | solution.py:694
  17.6 0.9 %copy-start = (bf16[8,12,640]{2,1,0:T(8,128)(2,1)S(1)}, bf16[8,12,640]{2,1,0:T(8,128)(2,1)}, u32[]{:S(2)}) copy-start(bf16[8,12,640]{2,1,0:T(8,128)(2,1)} %attend.1.own_ref) | copy-start | bytes 368644
  19.7 5.9 %collective-permute-start.12 = (bf16[2,12,640]{2,1,0:T(8,128)(2,1)S(1)}, bf16[2,12,640]{2,1,0:T(8,128)(2,1)S(1)}, u32[]{:S(2)}, u32[]{:S(2)}) collective-permute-start(bf16[2,12,640]{2,1,0:T(8,128)(2,1)S(1)} %get-tuple-element.98), channel_id=1, source_target_pairs={{0,8},{4,12},{8,16},{12,20},{16,24},{20,28},{24,0},{28,4},{1,9},{5... | collective-permute-start | bytes 92168 | tf_op jit(solution)/shard_map/ppermute | solution.py:690
  19.8 5.8 %collective-permute-start.13 = (bf16[2,12,640]{2,1,0:T(8,128)(2,1)S(1)}, bf16[2,12,640]{2,1,0:T(8,128)(2,1)S(1)}, u32[]{:S(2)}, u32[]{:S(2)}) collective-permute-start(bf16[2,12,640]{2,1,0:T(8,128)(2,1)S(1)} %get-tuple-element.99), channel_id=1, source_target_pairs={{0,16},{4,20},{8,24},{12,28},{16,0},{20,4},{24,8},{28,12},{1,17},{... | collective-permute-start | bytes 92168 | tf_op jit(solution)/shard_map/ppermute | solution.py:690
  19.9 6.3 %collective-permute-start.14 = (bf16[2,12,640]{2,1,0:T(8,128)(2,1)S(1)}, bf16[2,12,640]{2,1,0:T(8,128)(2,1)S(1)}, u32[]{:S(2)}, u32[]{:S(2)}) collective-permute-start(bf16[2,12,640]{2,1,0:T(8,128)(2,1)S(1)} %get-tuple-element.100), channel_id=1, source_target_pairs={{0,24},{4,28},{8,0},{12,4},{16,8},{20,12},{24,16},{28,20},{1,25},{... | collective-permute-start | bytes 92168 | tf_op jit(solution)/shard_map/ppermute | solution.py:690
  26.7 5.6 %collective-permute-start.15 = (bf16[2,4,1536]{2,1,0:T(4,128)(2,1)S(1)}, bf16[2,4,1536]{2,1,0:T(4,128)(2,1)S(1)}, u32[]{:S(2)}, u32[]{:S(2)}) collective-permute-start(bf16[2,4,1536]{2,1,0:T(4,128)(2,1)S(1)} %join.1.refs_0_), channel_id=1, source_target_pairs={{0,8},{4,12},{8,16},{12,20},{16,24},{20,28},{24,0},{28,4},{1,9},{5... | collective-permute-start | bytes 73736 | tf_op jit(solution)/shard_map/ppermute | solution.py:690
  28.8 4.7 %collective-permute-start.16 = (bf16[2,4,1536]{2,1,0:T(4,128)(2,1)S(1)}, bf16[2,4,1536]{2,1,0:T(4,128)(2,1)S(1)}, u32[]{:S(2)}, u32[]{:S(2)}) collective-permute-start(bf16[2,4,1536]{2,1,0:T(4,128)(2,1)S(1)} %join.1.refs_0_), channel_id=1, source_target_pairs={{0,16},{4,20},{8,24},{12,28},{16,0},{20,4},{24,8},{28,12},{1,17},{... | collective-permute-start | bytes 73736 | tf_op jit(solution)/shard_map/ppermute | solution.py:690
  30.6 3.8 %collective-permute-start.17 = (bf16[2,4,1536]{2,1,0:T(4,128)(2,1)S(1)}, bf16[2,4,1536]{2,1,0:T(4,128)(2,1)S(1)}, u32[]{:S(2)}, u32[]{:S(2)}) collective-permute-start(bf16[2,4,1536]{2,1,0:T(4,128)(2,1)S(1)} %join.1.refs_0_), channel_id=1, source_target_pairs={{0,24},{4,28},{8,0},{12,4},{16,8},{20,12},{24,16},{28,20},{1,25},{... | collective-permute-start | bytes 73736 | tf_op jit(solution)/shard_map/ppermute | solution.py:690
  34.9 3.2 %collective-permute-start.18 = (bf16[32,256]{1,0:T(8,128)(2,1)S(1)}, bf16[32,256]{1,0:T(8,128)(2,1)S(1)}, u32[]{:S(2)}, u32[]{:S(2)}) collective-permute-start(bf16[32,256]{1,0:T(8,128)(2,1)S(1)} %get-tuple-element.102.refs_0_), channel_id=1, source_target_pairs={{0,1},{1,2},{2,3},{3,0},{4,5},{5,6},{6,7},{7,4},{8,9},{9,10},{10,1... | collective-permute-start | bytes 49160 | tf_op jit(solution)/shard_map/ppermute | solution.py:690
  34.9 3.8 %collective-permute-start.19 = (bf16[32,256]{1,0:T(8,128)(2,1)S(1)}, bf16[32,256]{1,0:T(8,128)(2,1)S(1)}, u32[]{:S(2)}, u32[]{:S(2)}) collective-permute-start(bf16[32,256]{1,0:T(8,128)(2,1)S(1)} %get-tuple-element.102.refs_0_), channel_id=1, source_target_pairs={{0,2},{1,3},{2,0},{3,1},{4,6},{5,7},{6,4},{7,5},{8,10},{9,11},{10,... | collective-permute-start | bytes 49160 | tf_op jit(solution)/shard_map/ppermute | solution.py:690
  35.8 3.0 %collective-permute-start.20 = (bf16[32,256]{1,0:T(8,128)(2,1)S(1)}, bf16[32,256]{1,0:T(8,128)(2,1)S(1)}, u32[]{:S(2)}, u32[]{:S(2)}) collective-permute-start(bf16[32,256]{1,0:T(8,128)(2,1)S(1)} %get-tuple-element.102.refs_0_), channel_id=1, source_target_pairs={{0,3},{1,0},{2,1},{3,2},{4,7},{5,4},{6,5},{7,6},{8,11},{9,8},{10,9... | collective-permute-start | bytes 49160 | tf_op jit(solution)/shard_map/ppermute | solution.py:690
  43.9 8.2 %collective-permute-start.21 = (bf16[368,128]{1,0:T(8,128)(2,1)S(1)}, bf16[368,128]{1,0:T(8,128)(2,1)S(1)}, u32[]{:S(2)}, u32[]{:S(2)}) collective-permute-start(bf16[368,128]{1,0:T(8,128)(2,1)S(1)} %get-tuple-element.108), channel_id=1, source_target_pairs={{0,4},{4,8},{8,12},{12,16},{16,20},{20,24},{24,28},{28,0},{1,5},{5... | collective-permute-start | bytes 282632 | tf_op jit(solution)/shard_map/ppermute | solution.py:690
  45.2 7.9 %collective-permute-start.22 = (bf16[368,128]{1,0:T(8,128)(2,1)S(1)}, bf16[368,128]{1,0:T(8,128)(2,1)S(1)}, u32[]{:S(2)}, u32[]{:S(2)}) collective-permute-start(bf16[368,128]{1,0:T(8,128)(2,1)S(1)} %get-tuple-element.109), channel_id=1, source_target_pairs={{0,8},{4,12},{8,16},{12,20},{16,24},{20,28},{24,0},{28,4},{1,9},{5... | collective-permute-start | bytes 282632 | tf_op jit(solution)/shard_map/ppermute | solution.py:690
  45.8 14.6 %collective-permute-start.23 = (bf16[368,128]{1,0:T(8,128)(2,1)S(1)}, bf16[368,128]{1,0:T(8,128)(2,1)S(1)}, u32[]{:S(2)}, u32[]{:S(2)}) collective-permute-start(bf16[368,128]{1,0:T(8,128)(2,1)S(1)} %get-tuple-element.110), channel_id=1, source_target_pairs={{0,12},{4,16},{8,20},{12,24},{16,28},{20,0},{24,4},{28,8},{1,13},{... | collective-permute-start | bytes 282632 | tf_op jit(solution)/shard_map/ppermute | solution.py:690
  48.4 12.3 %collective-permute-start.24 = (bf16[368,128]{1,0:T(8,128)(2,1)S(1)}, bf16[368,128]{1,0:T(8,128)(2,1)S(1)}, u32[]{:S(2)}, u32[]{:S(2)}) collective-permute-start(bf16[368,128]{1,0:T(8,128)(2,1)S(1)} %get-tuple-element.111), channel_id=1, source_target_pairs={{0,16},{4,20},{8,24},{12,28},{16,0},{20,4},{24,8},{28,12},{1,17},{... | collective-permute-start | bytes 282632 | tf_op jit(solution)/shard_map/ppermute | solution.py:690
  49.9 10.9 %collective-permute-start.25 = (bf16[368,128]{1,0:T(8,128)(2,1)S(1)}, bf16[368,128]{1,0:T(8,128)(2,1)S(1)}, u32[]{:S(2)}, u32[]{:S(2)}) collective-permute-start(bf16[368,128]{1,0:T(8,128)(2,1)S(1)} %get-tuple-element.112), channel_id=1, source_target_pairs={{0,20},{4,24},{8,28},{12,0},{16,4},{20,8},{24,12},{28,16},{1,21},{... | collective-permute-start | bytes 282632 | tf_op jit(solution)/shard_map/ppermute | solution.py:690
  52.1 8.6 %collective-permute-start.26 = (bf16[368,128]{1,0:T(8,128)(2,1)S(1)}, bf16[368,128]{1,0:T(8,128)(2,1)S(1)}, u32[]{:S(2)}, u32[]{:S(2)}) collective-permute-start(bf16[368,128]{1,0:T(8,128)(2,1)S(1)} %get-tuple-element.113), channel_id=1, source_target_pairs={{0,24},{4,28},{8,0},{12,4},{16,8},{20,12},{24,16},{28,20},{1,25},{... | collective-permute-start | bytes 282632 | tf_op jit(solution)/shard_map/ppermute | solution.py:690
  53.1 7.7 %collective-permute-start.27 = (bf16[368,128]{1,0:T(8,128)(2,1)S(1)}, bf16[368,128]{1,0:T(8,128)(2,1)S(1)}, u32[]{:S(2)}, u32[]{:S(2)}) collective-permute-start(bf16[368,128]{1,0:T(8,128)(2,1)S(1)} %get-tuple-element.114), channel_id=1, source_target_pairs={{0,28},{4,0},{8,4},{12,8},{16,12},{20,16},{24,20},{28,24},{1,29},{... | collective-permute-start | bytes 282632 | tf_op jit(solution)/shard_map/ppermute | solution.py:690
  61.1 6.0 %collective-permute-start.28 = (bf16[176,128]{1,0:T(8,128)(2,1)S(1)}, bf16[176,128]{1,0:T(8,128)(2,1)S(1)}, u32[]{:S(2)}, u32[]{:S(2)}) collective-permute-start(bf16[176,128]{1,0:T(8,128)(2,1)S(1)} %get-tuple-element.116), channel_id=1, source_target_pairs={{0,4},{4,0},{8,12},{12,8},{16,20},{20,16},{24,28},{28,24},{1,5},{5... | collective-permute-start | bytes 135176 | tf_op jit(solution)/shard_map/ppermute | solution.py:694
  67.1 7.7 %collective-permute-start.29 = (bf16[2,176,128]{2,1,0:T(8,128)(2,1)S(1)}, bf16[2,176,128]{2,1,0:T(8,128)(2,1)S(1)}, u32[]{:S(2)}, u32[]{:S(2)}) collective-permute-start(bf16[2,176,128]{2,1,0:T(8,128)(2,1)S(1)} %pad_maximum_fusion.1.refs_0_), channel_id=1, source_target_pairs={{0,8},{4,12},{8,16},{12,20},{16,24},{20,28},{24,0},{28,4},{1,9},{5... | collective-permute-start | bytes 270344 | tf_op jit(solution)/shard_map/ppermute | solution.py:690
  71.2 7.2 %collective-permute-start.30 = (bf16[2,176,128]{2,1,0:T(8,128)(2,1)S(1)}, bf16[2,176,128]{2,1,0:T(8,128)(2,1)S(1)}, u32[]{:S(2)}, u32[]{:S(2)}) collective-permute-start(bf16[2,176,128]{2,1,0:T(8,128)(2,1)S(1)} %pad_maximum_fusion.1.refs_0_), channel_id=1, source_target_pairs={{0,16},{4,20},{8,24},{12,28},{16,0},{20,4},{24,8},{28,12},{1,17},{... | collective-permute-start | bytes 270344 | tf_op jit(solution)/shard_map/ppermute | solution.py:690
  72.0 6.4 %collective-permute-start.31 = (bf16[2,176,128]{2,1,0:T(8,128)(2,1)S(1)}, bf16[2,176,128]{2,1,0:T(8,128)(2,1)S(1)}, u32[]{:S(2)}, u32[]{:S(2)}) collective-permute-start(bf16[2,176,128]{2,1,0:T(8,128)(2,1)S(1)} %pad_maximum_fusion.1.refs_0_), channel_id=1, source_target_pairs={{0,24},{4,28},{8,0},{12,4},{16,8},{20,12},{24,16},{28,20},{1,25},{... | collective-permute-start | bytes 270344 | tf_op jit(solution)/shard_map/ppermute | solution.py:690
  80.8 1.7 %collective-permute-start.32 = (f32[32,256]{1,0:T(8,128)S(1)}, f32[32,256]{1,0:T(8,128)S(1)}, u32[]{:S(2)}, u32[]{:S(2)}) collective-permute-start(f32[32,256]{1,0:T(8,128)S(1)} %get-tuple-element.122), channel_id=1, source_target_pairs={{0,3},{1,0},{2,1},{3,2},{4,7},{5,4},{6,5},{7,6},{8,11},{9,8},{10,9... | collective-permute-start | bytes 98312 | tf_op jit(solution)/shard_map/ppermute | solution.py:690
  80.9 4.2 %collective-permute-start.33 = (f32[32,256]{1,0:T(8,128)S(1)}, f32[32,256]{1,0:T(8,128)S(1)}, u32[]{:S(2)}, u32[]{:S(2)}) collective-permute-start(f32[32,256]{1,0:T(8,128)S(1)} %get-tuple-element.123), channel_id=1, source_target_pairs={{0,2},{1,3},{2,0},{3,1},{4,6},{5,7},{6,4},{7,5},{8,10},{9,11},{10,... | collective-permute-start | bytes 98312 | tf_op jit(solution)/shard_map/ppermute | solution.py:690
  81.5 3.7 %collective-permute-start.34 = (f32[32,256]{1,0:T(8,128)S(1)}, f32[32,256]{1,0:T(8,128)S(1)}, u32[]{:S(2)}, u32[]{:S(2)}) collective-permute-start(f32[32,256]{1,0:T(8,128)S(1)} %get-tuple-element.124), channel_id=1, source_target_pairs={{0,1},{1,2},{2,3},{3,0},{4,5},{5,6},{6,7},{7,4},{8,9},{9,10},{10,1... | collective-permute-start | bytes 98312 | tf_op jit(solution)/shard_map/ppermute | solution.py:690

commit v7 on v5

--- a/solution.py
+++ b/solution.py
@@ -67,7 +67,7 @@
 
 def attend_kernel(
     classes, seq_ref, table_hbm, len_hbm, q_hbm, fresh_hbm, cache_ref, share_ref,
-    page_ref, table_ref, len_ref, q_ref, fresh_ref, query_ref, new_ref, order_ref, sems, small_sems,
+    page_ref, split_ref, table_ref, len_ref, q_ref, fresh_ref, query_ref, new_ref, sems, small_sems,
 ):
     steps, requests, _ = q_ref.shape
     page_rows = cache_ref.shape[1]
@@ -85,15 +85,6 @@
     for one in small[:2]:
         one.wait()
 
-    held = [jnp.clip(len_ref[r] - first, 0, span) for r in range(requests)]
-    for r in range(requests):
-        ahead = jnp.int32(0)
-        for other in range(requests):
-            if other != r:
-                longer = held[other] >= held[r] if other < r else held[other] > held[r]
-                ahead = ahead + longer.astype(jnp.int32)
-        order_ref[ahead] = r
-
     share = share_ref.shape[1]
     per_request = steps * GROUP // share
 
@@ -112,19 +103,17 @@
 
     bounds = list(zip((0,) + classes[:-1], classes))
 
-    def start(pair, carry):
-        both = order_ref[2 * pair], order_ref[2 * pair + 1]
+    def start(r, carry):
         for low, high in bounds:
 
-            @pl.when(needed(both[0], low))
+            @pl.when(needed(r, low))
             def _():
                 for page in range(low, high):
-                    for r in both:
-                        copy(r, page).start()
+                    copy(r, page).start()
 
         return carry
 
-    lax.fori_loop(0, requests // 2, start, 0)
+    lax.fori_loop(0, requests, start, 0)
     for one in small[2:]:
         one.wait()
 
@@ -163,12 +152,20 @@
             axis=0,
         )
         spread = jnp.where(own, spread, 0.0).astype(BF16)
-        both = [page_ref[r * pages + page].reshape(2 * page_rows, KV_WIDTH) for page in range(count)]
-        both = jnp.concatenate(both, axis=0)
-        size = 2 * count * page_rows
-        place = iota((1, size), 1)
-        live = jnp.logical_and(place % 2 == 0, first + place // 2 < len_ref[r])
-        scores = dot_nt(spread, both) + jnp.where(live, 0.0, NEG_FILL)
+        halves = ([], [])
+        for page in range(count):
+            copy(r, page).wait()
+            block = page_ref[r * pages + page].reshape(2 * page_rows, KV_WIDTH).astype(F32)
+            for j in range(KV_WIDTH // LANES):
+                split_ref[page, j] = tile_of(block, j)
+            for which in range(2):
+                tiles = [
+                    split_ref[page, j, pl.ds(which, page_rows, 2), :] for j in range(KV_WIDTH // LANES)
+                ]
+                halves[which].append(jnp.concatenate(tiles, axis=1).astype(BF16))
+        keys, values = jnp.concatenate(halves[0], axis=0), jnp.concatenate(halves[1], axis=0)
+        live = first + iota((1, count * page_rows), 1) < len_ref[r]
+        scores = dot_nt(spread, keys) + jnp.where(live, 0.0, NEG_FILL)
         fresh_scores = dot_nt(spread, fresh_rows(r, 0)) + fresh_bias
         largest = jnp.maximum(
             jnp.max(scores, axis=1, keepdims=True), jnp.max(fresh_scores, axis=1, keepdims=True)
@@ -177,12 +174,11 @@
         fresh_weights = jnp.exp(fresh_scores - largest)
         total = jnp.sum(weights, axis=1, keepdims=True)
         total = total + jnp.sum(fresh_weights, axis=1, keepdims=True)
-        moved = [pltpu.roll(tile_of(weights, j), 1, 1) for j in range(size // LANES)]
-        acc = dot_nn(jnp.concatenate(moved, axis=1).astype(BF16), both)
+        acc = dot_nn(weights.astype(BF16), values)
         acc = acc + dot_nn(fresh_weights.astype(BF16), fresh_rows(r, 1))
         acc = jnp.where(own, acc * (1.0 / total), 0.0)
         acc = jnp.sum(acc.reshape(steps * GROUP, KEY_VALUE_HEADS, KV_WIDTH), axis=1)
-        level = jnp.where(needed(r, 0), largest + jnp.log(total), NEG_FILL)
+        level = largest + jnp.log(total)
         high = round16(level)
         middle = round16(level - high)
         side = jnp.where(lane == head, high, 0.0)
@@ -191,38 +187,31 @@
         side = jnp.sum(side.reshape(steps * GROUP, KEY_VALUE_HEADS, LANES), axis=1)
         return acc.astype(BF16), side.astype(BF16)
 
-    def one_pair(pair, carry):
-        both = order_ref[2 * pair], order_ref[2 * pair + 1]
+    def one_request(r, carry):
         for low, high in bounds:
-            enough = needed(both[0], low)
+            enough = needed(r, low)
             if high < pages:
-                enough = jnp.logical_and(enough, jnp.logical_not(needed(both[0], high)))
+                enough = jnp.logical_and(enough, jnp.logical_not(needed(r, high)))
 
             @pl.when(enough)
             def _():
-                for page in range(high):
-                    for r in both:
-                        copy(r, page).wait()
-                made = [attend_pages(r, high) for r in both]
-                for r, (acc, side) in zip(both, made):
-                    put(r, acc, side)
-
-        @pl.when(jnp.logical_not(needed(both[0], 0)))
+                put(r, *attend_pages(r, high))
+
+        @pl.when(jnp.logical_not(needed(r, 0)))
         def _():
             empty = jnp.where(iota((steps * GROUP, LANES), 1) < KEY_VALUE_HEADS, NEG_FILL, 0.0)
-            for r in both:
-                put(r, jnp.zeros((steps * GROUP, KV_WIDTH), BF16), empty.astype(BF16))
+            put(r, jnp.zeros((steps * GROUP, KV_WIDTH), BF16), empty.astype(BF16))
 
         return carry
 
-    lax.fori_loop(0, requests // 2, one_pair, 0)
+    lax.fori_loop(0, requests, one_request, 0)
 
 
 def attend(queries, new_key_value, cache, page_table, cache_len, seq_index, devices):
     steps, requests, _ = queries.shape
     pages = page_table.shape[1]
     page_rows = cache.shape[1]
-    classes = tuple(c for c in (2, 4) if c < pages) + (pages,)
+    classes = tuple(c for c in (2, 4, 6) if c < pages) + (pages,)
     share = (requests * steps * GROUP // devices, KV_WIDTH + LANES)
     smem, hbm = pl.BlockSpec(memory_space=pltpu.SMEM), pl.BlockSpec(memory_space=pl.ANY)
     return pl.pallas_call(
@@ -231,13 +220,13 @@
         out_shape=jax.ShapeDtypeStruct((devices,) + share, BF16),
         scratch_shapes=[
             pltpu.VMEM((requests * pages, page_rows, 2, KV_WIDTH), BF16),
+            pltpu.VMEM((pages, KV_WIDTH // LANES, 2 * page_rows, LANES), F32),
             pltpu.SMEM(page_table.shape, jnp.int32),
             pltpu.SMEM(cache_len.shape, jnp.int32),
             pltpu.VMEM(queries.shape, BF16),
             pltpu.VMEM(new_key_value.shape, BF16),
             pltpu.VMEM((steps * GROUP, requests, KV_WIDTH), F32),
             pltpu.VMEM((steps, 2 * requests, KV_WIDTH), F32),
-            pltpu.SMEM((requests,), jnp.int32),
             pltpu.SemaphoreType.DMA((requests * pages,)),
             pltpu.SemaphoreType.DMA((4,)),
         ],
@@ -503,15 +492,14 @@
     made = scaled / (1.0 + jnp.exp(-scaled)) * swap_halves(scaled)
     low = iota((half, LANES), 1) < PIECE_WIDTH
     made = jnp.where(low, made[0:half], swap_halves(made[half:share])).astype(BF16)
-    for b in range(out_ref.shape[0]):
-        out_ref[b] = made
+    out_ref[...] = made
 
 
 def inner(parts):
     return pl.pallas_call(
         inner_kernel,
         out_shape=(
-            jax.ShapeDtypeStruct((len(parts), (parts[0].shape[0] - 16) // 2, LANES), BF16),
+            jax.ShapeDtypeStruct(((parts[0].shape[0] - 16) // 2, LANES), BF16),
             jax.ShapeDtypeStruct((8, LANES), F32),
         ),
         compiler_params=params(),
@@ -519,12 +507,16 @@
     )(*parts)
 
 
-def down_kernel(features, local, first_ref, range_ref, pick_ref, w_ref, logit_ref, x_ref, *refs):
-    out_refs, (row_ref, made_ref) = refs[:-2], refs[-2:]
+def down_kernel(features, local, pairs, first_ref, seq_ref, range_ref, pick_ref, w_ref, logit_ref, *refs):
+    pair_refs, out_refs, (x_ref, row_ref, made_ref) = refs[:pairs], refs[pairs:-3], refs[-3:]
     total, rows = pick_ref.shape
     width = w_ref.shape[2]
     window = total // 2 + 16
     devices, half, _ = x_ref.shape
+    for k, pair_ref in enumerate(pair_refs):
+        source = lax.rem(seq_ref[0] + devices - 2 * k, devices)
+        x_ref[source] = pair_ref[0]
+        x_ref[source + 1 - lax.rem(source, 2) * 2] = pair_ref[1]
     share = 2 * half
     low = iota((half, LANES), 1) < PIECE_WIDTH
     for b in range(0, devices, 2):
@@ -578,22 +570,23 @@
         out_ref[:, tile : tile + LANES] = jnp.where(lane == 1, pair[at, 1:2], side)
 
 
-def down(first, ranges, pick, made, logits, weights, exp_count):
+def down(first, seq_index, ranges, pick, made, logits, weights, exp_count):
     local, features, width = weights.shape
     total, rows = pick.shape
     wide = side_place(features, 2)[0] + LANES
     smem, vmem = pl.BlockSpec(memory_space=pltpu.SMEM), pl.BlockSpec(memory_space=pltpu.VMEM)
     return pl.pallas_call(
-        functools.partial(down_kernel, features, local),
-        in_specs=[smem] + [vmem] * 5,
+        functools.partial(down_kernel, features, local, len(made)),
+        in_specs=[smem] * 2 + [vmem] * (4 + len(made)),
         out_shape=(jax.ShapeDtypeStruct((total // exp_count, wide), F32),) * exp_count,
         scratch_shapes=[
+            pltpu.VMEM((2 * len(made),) + made[0].shape[1:], BF16),
             pltpu.VMEM((rows, width), BF16),
             pltpu.VMEM((rows, wide), F32),
         ],
         compiler_params=params(),
         name="down",
-    )(first, ranges, pick, weights, logits, made)
+    )(first, seq_index, ranges, pick, weights, logits, *made)
 
 
 def finish_kernel(hidden_ref, *refs):
@@ -643,6 +636,13 @@
 
 def exchange(parts, axis, direction):
     return [parts[0]] + [send(part, axis, direction * k) for k, part in enumerate(parts) if k]
+
+
+def pair_gather(block, axis):
+    count = lax.axis_size(axis)
+    beside = lax.ppermute(block, axis, [(i, i ^ 1) for i in range(count)])
+    pair = jnp.stack([block, beside])
+    return [pair] + [send(pair, axis, k) for k in range(2, count, 2)]
 
 
 def gather(block, axis):
@@ -681,9 +681,7 @@
     shares = swap(shares, "seq")
     gate_up_weights, shares = lax.optimization_barrier((gate_up_weights, shares))
     attn = join(shares)
-    beside = lax.ppermute(attn, "seq", [(i, i ^ 1) for i in range(seq_count)])
-    pair = jnp.stack([attn, beside])
-    gathered = [pair] + [send(pair, "seq", k) for k in range(2, seq_count, 2)]
+    gathered = pair_gather(attn, "seq")
     hidden, outgoing = hidden_state(seq_index, gathered, residual, w_out, norm_gain, routes)
     incoming = gather(outgoing, "exp")
     pieces = seq_count // PIECES
@@ -695,7 +693,8 @@
         )
         made, logits = inner(exchange(partial, "seq", 1))
         logits = logits[None] if pieces == 1 else lax.all_gather(logits, "seq")[::PIECES]
-        return down(first, ranges, pick, swap(made, "seq"), logits, w_down, exp_count), most
+        made = pair_gather(made, "seq")
+        return down(first, seq_index, ranges, pick, made, logits, w_down, exp_count), most
 
     made, most = one_round(0)
     pairs = w_gate_up.shape[0] * exp_count * steps * CAP

time: 87.4 us -> 86.5 us (0.990)
  waiting for transfers between devices: 28.1 us -> 25.2 us
  Pallas kernels: 19 us -> 20.1 us
    all_to_all x2 -> x1, waiting for transfers between devices: 12.7 us -> 3.4 us  [swap(): return lax.all_to_all(x, axis, split_axis=0, concat_axis=0, tiled=True)]
    all_to_all x2 -> x1, starting transfers between devices: 10.8 us -> 3.39 us  [swap(): return lax.all_to_all(x, axis, split_axis=0, concat_axis=0, tiled=True)]
    ppermute x16 -> x19, starting transfers between devices: 22.7 us -> 27.7 us  [send(): lax.ppermute(x, axis, [(i, (i + distance) % count) for i in range(count)])]
    ppermute x16 -> x19, waiting for transfers between devices: 12 us -> 16.4 us  [send(): lax.ppermute(x, axis, [(i, (i + distance) % count) for i in range(count)])]
    ppermute x1 -> x2, starting transfers between devices: 0.35 us -> 2.81 us  [pair_gather(): beside = lax.ppermute(block, axis, [(i, i ^ 1) for i in range(count)])]
    ppermute x1 -> x2, waiting for transfers between devices: 3.35 us -> 5.45 us  [pair_gather(): beside = lax.ppermute(block, axis, [(i, i ^ 1) for i in range(count)])]
    pallas_call x1, Pallas kernels: 9.83 us -> 11.7 us  [attend(): pl.pallas_call(functools.partial(attend_kernel, classes), in_specs=[smem]...]
  transfers between devices with their start and end apart: 19 -> 22, of which waited for: 11 -> 15; matrix products, arithmetic and copies ran while one was open for 6% -> 6% of each run, Pallas kernels for 0% -> 0%
where the time goes in v7:
time: 86.5 us; the launch traced here: 85.2 us
  starting transfers between devices  33.9 us (39%)
  waiting for transfers between devices  25.2 us (29%)
  Pallas kernels  20.1 us (23%)
  local copies, waits for them, and re-layouts  4.88 us (6%)
    ppermute x19, starting transfers between devices, send(): lax.ppermute(x, axis, [(i, (i + distance) % count) for i in range(count)])  27.7 us
    ppermute x19, waiting for transfers between devices, send(): lax.ppermute(x, axis, [(i, (i + distance) % count) for i in range(count)])  16.4 us
    pallas_call x1, Pallas kernels, attend(): pl.pallas_call(functools.partial(attend_kernel, classes), in_specs=[smem]...  11.7 us
    ppermute x2, waiting for transfers between devices, pair_gather(): beside = lax.ppermute(block, axis, [(i, i ^ 1) for i in range(count)])  5.45 us
    optimization_barrier x1, local copies, waits for them, and re-layouts, local(): w_gate_up, shares = lax.optimization_barrier((w_gate_up, shares))  4.84 us
    pallas_call x1, Pallas kernels, gate_up(): pl.pallas_call(functools.partial(gate_up_kernel, features, local, turn, s...  4.25 us
    all_to_all x1, waiting for transfers between devices, swap(): return lax.all_to_all(x, axis, split_axis=0, concat_axis=0, tiled=True)  3.4 us
    all_to_all x1, starting transfers between devices, swap(): return lax.all_to_all(x, axis, split_axis=0, concat_axis=0, tiled=True)  3.39 us
  transfers between devices with their start and end apart: 22, of which 15 were waited for; matrix products, arithmetic and copies ran while one was open for 6% of the time, Pallas kernels for 0%

profile of v7, /device:TPU:0, one launch (start us, length us, event | category | flops | bytes accessed | tf_op | source)
XLA Modules:
  0.0 85.2 jit_solution(10214197103801064897)
XLA Ops:
  0.0 11.7 %attend.1 = bf16[8,12,640]{2,1,0:T(8,128)(2,1)} custom-call(s32[1]{0:T(128)} %bitcast.4.seq_ref, s32[8,8]{1,0:T(8,128)} %table_hbm.1, s32[8]{0:T(128)} %len_hbm.1, bf16[4,8,1536]{2,1,0:T(8,128)(2,1)} %q_hbm.1, bf16[4,8,2,512]{3,2,1,0:T(2,128)(2,1)} %fresh_hbm.1, bf16[64,64,2,512]{3,2,1,0:T(2,128)(2,1)} %bitcast.28), custom_call_target="tpu_custom_call" | custom-call | tf_op jit(solution)/shard_map/attend/pallas_call | solution.py:217
  11.7 3.4 %all-to-all-start = ((bf16[8,12,640]{2,1,0:T(8,128)(2,1)}), bf16[8,12,640]{2,1,0:T(8,128)(2,1)S(1)}, u32[]{:S(2)}, u32[]{:S(2)}) async-start(bf16[8,12,640]{2,1,0:T(8,128)(2,1)} %attend.1), calls=%async_computation | async-start | bytes 327680 | tf_op jit(solution)/shard_map/all_to_all | solution.py:634
  15.2 4.8 %copy.16 = bf16[10,192,2,512]{3,1,2,0:T(8,128)(2,1)} copy(bf16[10,192,2,512]{3,2,1,0:T(2,128)(2,1)} %param.24) | data formatting | bytes 7864320 | tf_op jit(solution)/shard_map/optimization_barrier | solution.py:679
  20.0 3.4 %all-to-all-done.x_ref = bf16[8,12,640]{2,1,0:T(8,128)(2,1)S(1)} async-done(((bf16[8,12,640]{2,1,0:T(8,128)(2,1)}), bf16[8,12,640]{2,1,0:T(8,128)(2,1)S(1)}, u32[]{:S(2)}, u32[]{:S(2)}) %all-to-all-start) | async-done | bytes 122912 | tf_op jit(solution)/shard_map/all_to_all | solution.py:634
  24.2 3.4 %collective-permute-done.11 = bf16[4,1536]{1,0:T(4,128)(2,1)S(1)} collective-permute-done((bf16[4,1536]{1,0:T(4,128)(2,1)S(1)}, bf16[4,1536]{1,0:T(4,128)(2,1)S(1)}, u32[]{:S(2)}, u32[]{:S(2)}) %collective-permute-start.11) | collective-permute-done | bytes 12320 | tf_op jit(solution)/shard_map/ppermute | solution.py:643
  27.7 1.1 %collective-permute-start.13 = (bf16[2,4,1536]{2,1,0:T(4,128)(2,1)S(1)}, bf16[2,4,1536]{2,1,0:T(4,128)(2,1)S(1)}, u32[]{:S(2)}, u32[]{:S(2)}) collective-permute-start(bf16[2,4,1536]{2,1,0:T(4,128)(2,1)S(1)} %pad_maximum_fusion.2.refs_0_), channel_id=1, source_target_pairs={{0,16},{4,20},{8,24},{12,28},{16,0},{20,4},{24,8},{28,12},{1,17},{... | collective-permute-start | bytes 73736 | tf_op jit(solution)/shard_map/ppermute | solution.py:630
  28.7 2.8 %collective-permute-start.14 = (bf16[2,4,1536]{2,1,0:T(4,128)(2,1)S(1)}, bf16[2,4,1536]{2,1,0:T(4,128)(2,1)S(1)}, u32[]{:S(2)}, u32[]{:S(2)}) collective-permute-start(bf16[2,4,1536]{2,1,0:T(4,128)(2,1)S(1)} %pad_maximum_fusion.2.refs_0_), channel_id=1, source_target_pairs={{0,24},{4,28},{8,0},{12,4},{16,8},{20,12},{24,16},{28,20},{1,25},{... | collective-permute-start | bytes 73736 | tf_op jit(solution)/shard_map/ppermute | solution.py:630
  31.5 1.8 %collective-permute-done.12.refs_1_ = bf16[2,4,1536]{2,1,0:T(4,128)(2,1)S(1)} collective-permute-done((bf16[2,4,1536]{2,1,0:T(4,128)(2,1)S(1)}, bf16[2,4,1536]{2,1,0:T(4,128)(2,1)S(1)}, u32[]{:S(2)}, u32[]{:S(2)}) %collective-permute-start.12) | collective-permute-done | bytes 24608 | tf_op jit(solution)/shard_map/ppermute | solution.py:630
  34.4 1.8 %collective-permute-start.16 = (bf16[32,256]{1,0:T(8,128)(2,1)S(1)}, bf16[32,256]{1,0:T(8,128)(2,1)S(1)}, u32[]{:S(2)}, u32[]{:S(2)}) collective-permute-start(bf16[32,256]{1,0:T(8,128)(2,1)S(1)} %get-tuple-element.102.refs_0_), channel_id=1, source_target_pairs={{0,2},{1,3},{2,0},{3,1},{4,6},{5,7},{6,4},{7,5},{8,10},{9,11},{10,... | collective-permute-start | bytes 49160 | tf_op jit(solution)/shard_map/ppermute | solution.py:630
  36.3 1.4 %collective-permute-start.17 = (bf16[32,256]{1,0:T(8,128)(2,1)S(1)}, bf16[32,256]{1,0:T(8,128)(2,1)S(1)}, u32[]{:S(2)}, u32[]{:S(2)}) collective-permute-start(bf16[32,256]{1,0:T(8,128)(2,1)S(1)} %get-tuple-element.102.refs_0_), channel_id=1, source_target_pairs={{0,3},{1,0},{2,1},{3,2},{4,7},{5,4},{6,5},{7,6},{8,11},{9,8},{10,9... | collective-permute-start | bytes 49160 | tf_op jit(solution)/shard_map/ppermute | solution.py:630
  38.2 0.9 %collective-permute-done.17.refs_3_ = bf16[32,256]{1,0:T(8,128)(2,1)S(1)} collective-permute-done((bf16[32,256]{1,0:T(8,128)(2,1)S(1)}, bf16[32,256]{1,0:T(8,128)(2,1)S(1)}, u32[]{:S(2)}, u32[]{:S(2)}) %collective-permute-start.17) | collective-permute-done | bytes 16416 | tf_op jit(solution)/shard_map/ppermute | solution.py:630
  39.1 4.3 %gate_up.3 = (bf16[368,128]{1,0:T(8,128)(2,1)S(1)}, bf16[368,128]{1,0:T(8,128)(2,1)S(1)}, bf16[368,128]{1,0:T(8,128)(2,1)S(1)}, bf16[368,128]{1,0:T(8,128)(2,1)S...) custom-call(s32[1]{0:T(128)} %bitcast.11.where_ref, ...), custom_call_target="tpu_custom_call" | custom-call | tf_op jit(solution)/shard_map/gate_up/pallas_call | solution.py:451
  43.4 0.8 collective-permute-start.18
  44.2 2.0 %collective-permute-start.19 = (bf16[368,128]{1,0:T(8,128)(2,1)S(1)}, bf16[368,128]{1,0:T(8,128)(2,1)S(1)}, u32[]{:S(2)}, u32[]{:S(2)}) collective-permute-start(bf16[368,128]{1,0:T(8,128)(2,1)S(1)} %get-tuple-element.109), channel_id=1, source_target_pairs={{0,8},{4,12},{8,16},{12,20},{16,24},{20,28},{24,0},{28,4},{1,9},{5... | collective-permute-start | bytes 282632 | tf_op jit(solution)/shard_map/ppermute | solution.py:630
  46.3 2.5 %collective-permute-start.20 = (bf16[368,128]{1,0:T(8,128)(2,1)S(1)}, bf16[368,128]{1,0:T(8,128)(2,1)S(1)}, u32[]{:S(2)}, u32[]{:S(2)}) collective-permute-start(bf16[368,128]{1,0:T(8,128)(2,1)S(1)} %get-tuple-element.110), channel_id=1, source_target_pairs={{0,12},{4,16},{8,20},{12,24},{16,28},{20,0},{24,4},{28,8},{1,13},{... | collective-permute-start | bytes 282632 | tf_op jit(solution)/shard_map/ppermute | solution.py:630
  48.7 2.0 %collective-permute-start.21 = (bf16[368,128]{1,0:T(8,128)(2,1)S(1)}, bf16[368,128]{1,0:T(8,128)(2,1)S(1)}, u32[]{:S(2)}, u32[]{:S(2)}) collective-permute-start(bf16[368,128]{1,0:T(8,128)(2,1)S(1)} %get-tuple-element.111), channel_id=1, source_target_pairs={{0,16},{4,20},{8,24},{12,28},{16,0},{20,4},{24,8},{28,12},{1,17},{... | collective-permute-start | bytes 282632 | tf_op jit(solution)/shard_map/ppermute | solution.py:630
  50.7 1.1 %collective-permute-start.22 = (bf16[368,128]{1,0:T(8,128)(2,1)S(1)}, bf16[368,128]{1,0:T(8,128)(2,1)S(1)}, u32[]{:S(2)}, u32[]{:S(2)}) collective-permute-start(bf16[368,128]{1,0:T(8,128)(2,1)S(1)} %get-tuple-element.112), channel_id=1, source_target_pairs={{0,20},{4,24},{8,28},{12,0},{16,4},{20,8},{24,12},{28,16},{1,21},{... | collective-permute-start | bytes 282632 | tf_op jit(solution)/shard_map/ppermute | solution.py:630
  51.9 1.3 %collective-permute-start.23 = (bf16[368,128]{1,0:T(8,128)(2,1)S(1)}, bf16[368,128]{1,0:T(8,128)(2,1)S(1)}, u32[]{:S(2)}, u32[]{:S(2)}) collective-permute-start(bf16[368,128]{1,0:T(8,128)(2,1)S(1)} %get-tuple-element.113), channel_id=1, source_target_pairs={{0,24},{4,28},{8,0},{12,4},{16,8},{20,12},{24,16},{28,20},{1,25},{... | collective-permute-start | bytes 282632 | tf_op jit(solution)/shard_map/ppermute | solution.py:630
  53.2 3.0 %collective-permute-start.24 = (bf16[368,128]{1,0:T(8,128)(2,1)S(1)}, bf16[368,128]{1,0:T(8,128)(2,1)S(1)}, u32[]{:S(2)}, u32[]{:S(2)}) collective-permute-start(bf16[368,128]{1,0:T(8,128)(2,1)S(1)} %get-tuple-element.114), channel_id=1, source_target_pairs={{0,28},{4,0},{8,4},{12,8},{16,12},{20,16},{24,20},{28,24},{1,29},{... | collective-permute-start | bytes 282632 | tf_op jit(solution)/shard_map/ppermute | solution.py:630
  56.2 3.3 %collective-permute-done.20.refs_3_ = bf16[368,128]{1,0:T(8,128)(2,1)S(1)} collective-permute-done((bf16[368,128]{1,0:T(8,128)(2,1)S(1)}, bf16[368,128]{1,0:T(8,128)(2,1)S(1)}, u32[]{:S(2)}, u32[]{:S(2)}) %collective-permute-start.20) | collective-permute-done | bytes 94240 | tf_op jit(solution)/shard_map/ppermute | solution.py:630
  59.5 1.9 %collective-permute-done.23.refs_6_ = bf16[368,128]{1,0:T(8,128)(2,1)S(1)} collective-permute-done((bf16[368,128]{1,0:T(8,128)(2,1)S(1)}, bf16[368,128]{1,0:T(8,128)(2,1)S(1)}, u32[]{:S(2)}, u32[]{:S(2)}) %collective-permute-start.23) | collective-permute-done | bytes 94240 | tf_op jit(solution)/shard_map/ppermute | solution.py:630
  61.7 2.5 %collective-permute-start.25 = (bf16[176,128]{1,0:T(8,128)(2,1)S(1)}, bf16[176,128]{1,0:T(8,128)(2,1)S(1)}, u32[]{:S(2)}, u32[]{:S(2)}) collective-permute-start(bf16[176,128]{1,0:T(8,128)(2,1)S(1)} %get-tuple-element.116), channel_id=1, source_target_pairs={{0,4},{4,0},{8,12},{12,8},{16,20},{20,16},{24,28},{28,24},{1,5},{5... | collective-permute-start | bytes 135176 | tf_op jit(solution)/shard_map/ppermute | solution.py:643
  64.2 2.0 %collective-permute-done.25 = bf16[176,128]{1,0:T(8,128)(2,1)S(1)} collective-permute-done((bf16[176,128]{1,0:T(8,128)(2,1)S(1)}, bf16[176,128]{1,0:T(8,128)(2,1)S(1)}, u32[]{:S(2)}, u32[]{:S(2)}) %collective-permute-start.25) | collective-permute-done | bytes 45088 | tf_op jit(solution)/shard_map/ppermute | solution.py:643
  66.3 3.3 %collective-permute-start.26 = (bf16[2,176,128]{2,1,0:T(8,128)(2,1)S(1)}, bf16[2,176,128]{2,1,0:T(8,128)(2,1)S(1)}, u32[]{:S(2)}, u32[]{:S(2)}) collective-permute-start(bf16[2,176,128]{2,1,0:T(8,128)(2,1)S(1)} %pad_maximum_fusion.1.refs_0_), channel_id=1, source_target_pairs={{0,8},{4,12},{8,16},{12,20},{16,24},{20,28},{24,0},{28,4},{1,9},{5... | collective-permute-start | bytes 270344 | tf_op jit(solution)/shard_map/ppermute | solution.py:630
  69.6 1.2 %collective-permute-start.27 = (bf16[2,176,128]{2,1,0:T(8,128)(2,1)S(1)}, bf16[2,176,128]{2,1,0:T(8,128)(2,1)S(1)}, u32[]{:S(2)}, u32[]{:S(2)}) collective-permute-start(bf16[2,176,128]{2,1,0:T(8,128)(2,1)S(1)} %pad_maximum_fusion.1.refs_0_), channel_id=1, source_target_pairs={{0,16},{4,20},{8,24},{12,28},{16,0},{20,4},{24,8},{28,12},{1,17},{... | collective-permute-start | bytes 270344 | tf_op jit(solution)/shard_map/ppermute | solution.py:630
  70.8 1.2 %collective-permute-start.28 = (bf16[2,176,128]{2,1,0:T(8,128)(2,1)S(1)}, bf16[2,176,128]{2,1,0:T(8,128)(2,1)S(1)}, u32[]{:S(2)}, u32[]{:S(2)}) collective-permute-start(bf16[2,176,128]{2,1,0:T(8,128)(2,1)S(1)} %pad_maximum_fusion.1.refs_0_), channel_id=1, source_target_pairs={{0,24},{4,28},{8,0},{12,4},{16,8},{20,12},{24,16},{28,20},{1,25},{... | collective-permute-start | bytes 270344 | tf_op jit(solution)/shard_map/ppermute | solution.py:630
  72.7 1.0 %collective-permute-done.26.refs_1_ = bf16[2,176,128]{2,1,0:T(8,128)(2,1)S(1)} collective-permute-done((bf16[2,176,128]{2,1,0:T(8,128)(2,1)S(1)}, bf16[2,176,128]{2,1,0:T(8,128)(2,1)S(1)}, u32[]{:S(2)}, u32[]{:S(2)}) %collective-permute-start.26) | collective-permute-done | bytes 90144 | tf_op jit(solution)/shard_map/ppermute | solution.py:630
  73.8 3.0 %collective-permute-done.27.refs_2_ = bf16[2,176,128]{2,1,0:T(8,128)(2,1)S(1)} collective-permute-done((bf16[2,176,128]{2,1,0:T(8,128)(2,1)S(1)}, bf16[2,176,128]{2,1,0:T(8,128)(2,1)S(1)}, u32[]{:S(2)}, u32[]{:S(2)}) %collective-permute-start.27) | collective-permute-done | bytes 90144 | tf_op jit(solution)/shard_map/ppermute | solution.py:630
  76.9 2.1 %down.3 = (f32[32,256]{1,0:T(8,128)S(1)}, f32[32,256]{1,0:T(8,128)S(1)}, f32[32,256]{1,0:T(8,128)S(1)}, f32[32,256]{1,0:T(8,128)S(1)}) custom-call(s32[16]{0:T(128)S(1)} %get-tuple-element.104.first_ref, s32[1]{0:T(128)} %bitcast.4.seq_ref, f32[16,128]{1,0:T(8,128)S(1)} %get-tuple-element.105.range_ref, bf16[128,352]{1,0:T(8,128)(2,1)S(1)} %get-tuple-element.106.pick_ref, ...), custom_call_target="tpu_custom_call" | custom-call | tf_op jit(solution)/shard_map/down/pallas_call | solution.py:578
  79.2 0.9 %collective-permute-start.29 = (f32[32,256]{1,0:T(8,128)S(1)}, f32[32,256]{1,0:T(8,128)S(1)}, u32[]{:S(2)}, u32[]{:S(2)}) collective-permute-start(f32[32,256]{1,0:T(8,128)S(1)} %get-tuple-element.122), channel_id=1, source_target_pairs={{0,3},{1,0},{2,1},{3,2},{4,7},{5,4},{6,5},{7,6},{8,11},{9,8},{10,9... | collective-permute-start | bytes 98312 | tf_op jit(solution)/shard_map/ppermute | solution.py:630
  80.2 0.9 %collective-permute-start.30 = (f32[32,256]{1,0:T(8,128)S(1)}, f32[32,256]{1,0:T(8,128)S(1)}, u32[]{:S(2)}, u32[]{:S(2)}) collective-permute-start(f32[32,256]{1,0:T(8,128)S(1)} %get-tuple-element.123), channel_id=1, source_target_pairs={{0,2},{1,3},{2,0},{3,1},{4,6},{5,7},{6,4},{7,5},{8,10},{9,11},{10,... | collective-permute-start | bytes 98312 | tf_op jit(solution)/shard_map/ppermute | solution.py:630
  81.8 2.4 %collective-permute-done.30.refs_2_ = f32[32,256]{1,0:T(8,128)S(1)} collective-permute-done((f32[32,256]{1,0:T(8,128)S(1)}, f32[32,256]{1,0:T(8,128)S(1)}, u32[]{:S(2)}, u32[]{:S(2)}) %collective-permute-start.30) | collective-permute-done | bytes 32800 | tf_op jit(solution)/shard_map/ppermute | solution.py:630
  (35 shorter events, 5.0 us)
Async XLA Ops:
  11.7 11.7 %all-to-all-start = ((bf16[8,12,640]{2,1,0:T(8,128)(2,1)}), bf16[8,12,640]{2,1,0:T(8,128)(2,1)S(1)}, u32[]{:S(2)}, u32[]{:S(2)}) async-start(bf16[8,12,640]{2,1,0:T(8,128)(2,1)} %attend.1), calls=%async_computation | async-start | bytes 327680 | tf_op jit(solution)/shard_map/all_to_all | solution.py:634
  15.1 18.7 %copy-start = (bf16[1536,192]{0,1:T(8,128)(2,1)S(1)}, bf16[1536,192]{0,1:T(8,128)(2,1)}, u32[]{:S(2)}) copy-start(bf16[1536,192]{0,1:T(8,128)(2,1)} %param.21) | copy-start | bytes 1769476
  15.1 18.7 %copy-start.1 = (bf16[4,8,192]{2,1,0:T(8,128)(2,1)S(1)}, bf16[4,8,192]{2,1,0:T(8,128)(2,1)}, u32[]{:S(2)}) copy-start(bf16[4,8,192]{2,1,0:T(8,128)(2,1)} %residual_ref.1) | copy-start | bytes 36868
  15.1 18.7 %copy-start.2 = (s32[4,8,8]{2,1,0:T(8,128)S(1)}, s32[4,8,8]{2,1,0:T(8,128)}, u32[]{:S(2)}) copy-start(s32[4,8,8]{2,1,0:T(8,128)} %routes_ref.1) | copy-start | bytes 3076
  15.1 18.7 %copy-start.3 = (f32[192]{0:T(256)S(1)}, f32[192]{0:T(256)}, u32[]{:S(2)}) copy-start(f32[192]{0:T(256)} %param.22) | copy-start | bytes 2308
  15.2 24.0 %copy-start.5 = (bf16[192,40]{0,1:T(8,128)(2,1)S(1)}, bf16[192,40]{0,1:T(8,128)(2,1)}, u32[]{:S(2)}) copy-start(bf16[192,40]{0,1:T(8,128)(2,1)} %param.23) | copy-start | bytes 46084
  20.0 56.9 %copy-start.4 = (bf16[10,192,512]{2,1,0:T(8,128)(2,1)S(1)}, bf16[10,192,512]{2,1,0:T(8,128)(2,1)}, u32[]{:S(2)}) copy-start(bf16[10,192,512]{2,1,0:T(8,128)(2,1)} %w_ref.1) | copy-start | bytes 5898244
  23.9 3.7 %collective-permute-start.11 = (bf16[4,1536]{1,0:T(4,128)(2,1)S(1)}, bf16[4,1536]{1,0:T(4,128)(2,1)S(1)}, u32[]{:S(2)}, u32[]{:S(2)}) collective-permute-start(bf16[4,1536]{1,0:T(4,128)(2,1)S(1)} %join.1), channel_id=1, source_target_pairs={{0,4},{4,0},{8,12},{12,8},{16,20},{20,16},{24,28},{28,24},{1,5},{5... | collective-permute-start | bytes 36872 | tf_op jit(solution)/shard_map/ppermute | solution.py:643
  27.6 5.7 %collective-permute-start.12 = (bf16[2,4,1536]{2,1,0:T(4,128)(2,1)S(1)}, bf16[2,4,1536]{2,1,0:T(4,128)(2,1)S(1)}, u32[]{:S(2)}, u32[]{:S(2)}) collective-permute-start(bf16[2,4,1536]{2,1,0:T(4,128)(2,1)S(1)} %pad_maximum_fusion.2.refs_0_), channel_id=1, source_target_pairs={{0,8},{4,12},{8,16},{12,20},{16,24},{20,28},{24,0},{28,4},{1,9},{5... | collective-permute-start | bytes 73736 | tf_op jit(solution)/shard_map/ppermute | solution.py:630
  27.7 5.6 %collective-permute-start.13 = (bf16[2,4,1536]{2,1,0:T(4,128)(2,1)S(1)}, bf16[2,4,1536]{2,1,0:T(4,128)(2,1)S(1)}, u32[]{:S(2)}, u32[]{:S(2)}) collective-permute-start(bf16[2,4,1536]{2,1,0:T(4,128)(2,1)S(1)} %pad_maximum_fusion.2.refs_0_), channel_id=1, source_target_pairs={{0,16},{4,20},{8,24},{12,28},{16,0},{20,4},{24,8},{28,12},{1,17},{... | collective-permute-start | bytes 73736 | tf_op jit(solution)/shard_map/ppermute | solution.py:630
  28.7 5.1 %collective-permute-start.14 = (bf16[2,4,1536]{2,1,0:T(4,128)(2,1)S(1)}, bf16[2,4,1536]{2,1,0:T(4,128)(2,1)S(1)}, u32[]{:S(2)}, u32[]{:S(2)}) collective-permute-start(bf16[2,4,1536]{2,1,0:T(4,128)(2,1)S(1)} %pad_maximum_fusion.2.refs_0_), channel_id=1, source_target_pairs={{0,24},{4,28},{8,0},{12,4},{16,8},{20,12},{24,16},{28,20},{1,25},{... | collective-permute-start | bytes 73736 | tf_op jit(solution)/shard_map/ppermute | solution.py:630
  34.4 3.3 %collective-permute-start.15 = (bf16[32,256]{1,0:T(8,128)(2,1)S(1)}, bf16[32,256]{1,0:T(8,128)(2,1)S(1)}, u32[]{:S(2)}, u32[]{:S(2)}) collective-permute-start(bf16[32,256]{1,0:T(8,128)(2,1)S(1)} %get-tuple-element.102.refs_0_), channel_id=1, source_target_pairs={{0,1},{1,2},{2,3},{3,0},{4,5},{5,6},{6,7},{7,4},{8,9},{9,10},{10,1... | collective-permute-start | bytes 49160 | tf_op jit(solution)/shard_map/ppermute | solution.py:630
  34.4 3.8 %collective-permute-start.16 = (bf16[32,256]{1,0:T(8,128)(2,1)S(1)}, bf16[32,256]{1,0:T(8,128)(2,1)S(1)}, u32[]{:S(2)}, u32[]{:S(2)}) collective-permute-start(bf16[32,256]{1,0:T(8,128)(2,1)S(1)} %get-tuple-element.102.refs_0_), channel_id=1, source_target_pairs={{0,2},{1,3},{2,0},{3,1},{4,6},{5,7},{6,4},{7,5},{8,10},{9,11},{10,... | collective-permute-start | bytes 49160 | tf_op jit(solution)/shard_map/ppermute | solution.py:630
  36.3 2.8 %collective-permute-start.17 = (bf16[32,256]{1,0:T(8,128)(2,1)S(1)}, bf16[32,256]{1,0:T(8,128)(2,1)S(1)}, u32[]{:S(2)}, u32[]{:S(2)}) collective-permute-start(bf16[32,256]{1,0:T(8,128)(2,1)S(1)} %get-tuple-element.102.refs_0_), channel_id=1, source_target_pairs={{0,3},{1,0},{2,1},{3,2},{4,7},{5,4},{6,5},{7,6},{8,11},{9,8},{10,9... | collective-permute-start | bytes 49160 | tf_op jit(solution)/shard_map/ppermute | solution.py:630
  43.4 8.5 %collective-permute-start.18 = (bf16[368,128]{1,0:T(8,128)(2,1)S(1)}, bf16[368,128]{1,0:T(8,128)(2,1)S(1)}, u32[]{:S(2)}, u32[]{:S(2)}) collective-permute-start(bf16[368,128]{1,0:T(8,128)(2,1)S(1)} %get-tuple-element.108), channel_id=1, source_target_pairs={{0,4},{4,8},{8,12},{12,16},{16,20},{20,24},{24,28},{28,0},{1,5},{5... | collective-permute-start | bytes 282632 | tf_op jit(solution)/shard_map/ppermute | solution.py:630
  44.2 9.0 %collective-permute-start.19 = (bf16[368,128]{1,0:T(8,128)(2,1)S(1)}, bf16[368,128]{1,0:T(8,128)(2,1)S(1)}, u32[]{:S(2)}, u32[]{:S(2)}) collective-permute-start(bf16[368,128]{1,0:T(8,128)(2,1)S(1)} %get-tuple-element.109), channel_id=1, source_target_pairs={{0,8},{4,12},{8,16},{12,20},{16,24},{20,28},{24,0},{28,4},{1,9},{5... | collective-permute-start | bytes 282632 | tf_op jit(solution)/shard_map/ppermute | solution.py:630
  46.3 13.2 %collective-permute-start.20 = (bf16[368,128]{1,0:T(8,128)(2,1)S(1)}, bf16[368,128]{1,0:T(8,128)(2,1)S(1)}, u32[]{:S(2)}, u32[]{:S(2)}) collective-permute-start(bf16[368,128]{1,0:T(8,128)(2,1)S(1)} %get-tuple-element.110), channel_id=1, source_target_pairs={{0,12},{4,16},{8,20},{12,24},{16,28},{20,0},{24,4},{28,8},{1,13},{... | collective-permute-start | bytes 282632 | tf_op jit(solution)/shard_map/ppermute | solution.py:630
  48.7 10.7 %collective-permute-start.21 = (bf16[368,128]{1,0:T(8,128)(2,1)S(1)}, bf16[368,128]{1,0:T(8,128)(2,1)S(1)}, u32[]{:S(2)}, u32[]{:S(2)}) collective-permute-start(bf16[368,128]{1,0:T(8,128)(2,1)S(1)} %get-tuple-element.111), channel_id=1, source_target_pairs={{0,16},{4,20},{8,24},{12,28},{16,0},{20,4},{24,8},{28,12},{1,17},{... | collective-permute-start | bytes 282632 | tf_op jit(solution)/shard_map/ppermute | solution.py:630
  50.7 8.7 %collective-permute-start.22 = (bf16[368,128]{1,0:T(8,128)(2,1)S(1)}, bf16[368,128]{1,0:T(8,128)(2,1)S(1)}, u32[]{:S(2)}, u32[]{:S(2)}) collective-permute-start(bf16[368,128]{1,0:T(8,128)(2,1)S(1)} %get-tuple-element.112), channel_id=1, source_target_pairs={{0,20},{4,24},{8,28},{12,0},{16,4},{20,8},{24,12},{28,16},{1,21},{... | collective-permute-start | bytes 282632 | tf_op jit(solution)/shard_map/ppermute | solution.py:630
  51.9 9.5 %collective-permute-start.23 = (bf16[368,128]{1,0:T(8,128)(2,1)S(1)}, bf16[368,128]{1,0:T(8,128)(2,1)S(1)}, u32[]{:S(2)}, u32[]{:S(2)}) collective-permute-start(bf16[368,128]{1,0:T(8,128)(2,1)S(1)} %get-tuple-element.113), channel_id=1, source_target_pairs={{0,24},{4,28},{8,0},{12,4},{16,8},{20,12},{24,16},{28,20},{1,25},{... | collective-permute-start | bytes 282632 | tf_op jit(solution)/shard_map/ppermute | solution.py:630
  53.2 8.2 %collective-permute-start.24 = (bf16[368,128]{1,0:T(8,128)(2,1)S(1)}, bf16[368,128]{1,0:T(8,128)(2,1)S(1)}, u32[]{:S(2)}, u32[]{:S(2)}) collective-permute-start(bf16[368,128]{1,0:T(8,128)(2,1)S(1)} %get-tuple-element.114), channel_id=1, source_target_pairs={{0,28},{4,0},{8,4},{12,8},{16,12},{20,16},{24,20},{28,24},{1,29},{... | collective-permute-start | bytes 282632 | tf_op jit(solution)/shard_map/ppermute | solution.py:630
  61.7 4.6 %collective-permute-start.25 = (bf16[176,128]{1,0:T(8,128)(2,1)S(1)}, bf16[176,128]{1,0:T(8,128)(2,1)S(1)}, u32[]{:S(2)}, u32[]{:S(2)}) collective-permute-start(bf16[176,128]{1,0:T(8,128)(2,1)S(1)} %get-tuple-element.116), channel_id=1, source_target_pairs={{0,4},{4,0},{8,12},{12,8},{16,20},{20,16},{24,28},{28,24},{1,5},{5... | collective-permute-start | bytes 135176 | tf_op jit(solution)/shard_map/ppermute | solution.py:643
  66.3 7.5 %collective-permute-start.26 = (bf16[2,176,128]{2,1,0:T(8,128)(2,1)S(1)}, bf16[2,176,128]{2,1,0:T(8,128)(2,1)S(1)}, u32[]{:S(2)}, u32[]{:S(2)}) collective-permute-start(bf16[2,176,128]{2,1,0:T(8,128)(2,1)S(1)} %pad_maximum_fusion.1.refs_0_), channel_id=1, source_target_pairs={{0,8},{4,12},{8,16},{12,20},{16,24},{20,28},{24,0},{28,4},{1,9},{5... | collective-permute-start | bytes 270344 | tf_op jit(solution)/shard_map/ppermute | solution.py:630
  69.6 7.2 %collective-permute-start.27 = (bf16[2,176,128]{2,1,0:T(8,128)(2,1)S(1)}, bf16[2,176,128]{2,1,0:T(8,128)(2,1)S(1)}, u32[]{:S(2)}, u32[]{:S(2)}) collective-permute-start(bf16[2,176,128]{2,1,0:T(8,128)(2,1)S(1)} %pad_maximum_fusion.1.refs_0_), channel_id=1, source_target_pairs={{0,16},{4,20},{8,24},{12,28},{16,0},{20,4},{24,8},{28,12},{1,17},{... | collective-permute-start | bytes 270344 | tf_op jit(solution)/shard_map/ppermute | solution.py:630
  70.8 6.1 %collective-permute-start.28 = (bf16[2,176,128]{2,1,0:T(8,128)(2,1)S(1)}, bf16[2,176,128]{2,1,0:T(8,128)(2,1)S(1)}, u32[]{:S(2)}, u32[]{:S(2)}) collective-permute-start(bf16[2,176,128]{2,1,0:T(8,128)(2,1)S(1)} %pad_maximum_fusion.1.refs_0_), channel_id=1, source_target_pairs={{0,24},{4,28},{8,0},{12,4},{16,8},{20,12},{24,16},{28,20},{1,25},{... | collective-permute-start | bytes 270344 | tf_op jit(solution)/shard_map/ppermute | solution.py:630
  79.2 2.5 %collective-permute-start.29 = (f32[32,256]{1,0:T(8,128)S(1)}, f32[32,256]{1,0:T(8,128)S(1)}, u32[]{:S(2)}, u32[]{:S(2)}) collective-permute-start(f32[32,256]{1,0:T(8,128)S(1)} %get-tuple-element.122), channel_id=1, source_target_pairs={{0,3},{1,0},{2,1},{3,2},{4,7},{5,4},{6,5},{7,6},{8,11},{9,8},{10,9... | collective-permute-start | bytes 98312 | tf_op jit(solution)/shard_map/ppermute | solution.py:630
  80.2 4.0 %collective-permute-start.30 = (f32[32,256]{1,0:T(8,128)S(1)}, f32[32,256]{1,0:T(8,128)S(1)}, u32[]{:S(2)}, u32[]{:S(2)}) collective-permute-start(f32[32,256]{1,0:T(8,128)S(1)} %get-tuple-element.123), channel_id=1, source_target_pairs={{0,2},{1,3},{2,0},{3,1},{4,6},{5,7},{6,4},{7,5},{8,10},{9,11},{10,... | collective-permute-start | bytes 98312 | tf_op jit(solution)/shard_map/ppermute | solution.py:630
  81.0 3.4 %collective-permute-start.31 = (f32[32,256]{1,0:T(8,128)S(1)}, f32[32,256]{1,0:T(8,128)S(1)}, u32[]{:S(2)}, u32[]{:S(2)}) collective-permute-start(f32[32,256]{1,0:T(8,128)S(1)} %get-tuple-element.124), channel_id=1, source_target_pairs={{0,1},{1,2},{2,3},{3,0},{4,5},{5,6},{6,7},{7,4},{8,9},{9,10},{10,1... | collective-permute-start | bytes 98312 | tf_op jit(solution)/shard_map/ppermute | solution.py:630

commit v8 on v5

--- a/solution.py
+++ b/solution.py
@@ -222,7 +222,7 @@
     steps, requests, _ = queries.shape
     pages = page_table.shape[1]
     page_rows = cache.shape[1]
-    classes = tuple(c for c in (2, 4) if c < pages) + (pages,)
+    classes = tuple(c for c in (2, 4, 6) if c < pages) + (pages,)
     share = (requests * steps * GROUP // devices, KV_WIDTH + LANES)
     smem, hbm = pl.BlockSpec(memory_space=pltpu.SMEM), pl.BlockSpec(memory_space=pl.ANY)
     return pl.pallas_call(
@@ -503,15 +503,14 @@
     made = scaled / (1.0 + jnp.exp(-scaled)) * swap_halves(scaled)
     low = iota((half, LANES), 1) < PIECE_WIDTH
     made = jnp.where(low, made[0:half], swap_halves(made[half:share])).astype(BF16)
-    for b in range(out_ref.shape[0]):
-        out_ref[b] = made
+    out_ref[...] = made
 
 
 def inner(parts):
     return pl.pallas_call(
         inner_kernel,
         out_shape=(
-            jax.ShapeDtypeStruct((len(parts), (parts[0].shape[0] - 16) // 2, LANES), BF16),
+            jax.ShapeDtypeStruct(((parts[0].shape[0] - 16) // 2, LANES), BF16),
             jax.ShapeDtypeStruct((8, LANES), F32),
         ),
         compiler_params=params(),
@@ -519,12 +518,17 @@
     )(*parts)
 
 
-def down_kernel(features, local, first_ref, range_ref, pick_ref, w_ref, logit_ref, x_ref, *refs):
-    out_refs, (row_ref, made_ref) = refs[:-2], refs[-2:]
+def down_kernel(features, local, first_ref, seq_ref, range_ref, pick_ref, w_ref, logit_ref, *refs):
+    (own_ref, beside_ref, behind_ref, other_ref), refs = refs[:4], refs[4:]
+    out_refs, (x_ref, row_ref, made_ref) = refs[:-3], refs[-3:]
     total, rows = pick_ref.shape
     width = w_ref.shape[2]
     window = total // 2 + 16
     devices, half, _ = x_ref.shape
+    for k in range(devices // 2):
+        source = lax.rem(seq_ref[0] + devices - 2 * k, devices)
+        x_ref[source] = behind_ref[k - 1] if k else own_ref[...]
+        x_ref[source + 1 - lax.rem(source, 2) * 2] = other_ref[k - 1] if k else beside_ref[...]
     share = 2 * half
     low = iota((half, LANES), 1) < PIECE_WIDTH
     for b in range(0, devices, 2):
@@ -578,22 +582,23 @@
         out_ref[:, tile : tile + LANES] = jnp.where(lane == 1, pair[at, 1:2], side)
 
 
-def down(first, ranges, pick, made, logits, weights, exp_count):
+def down(first, seq_index, ranges, pick, made, logits, weights, exp_count):
     local, features, width = weights.shape
     total, rows = pick.shape
     wide = side_place(features, 2)[0] + LANES
     smem, vmem = pl.BlockSpec(memory_space=pltpu.SMEM), pl.BlockSpec(memory_space=pltpu.VMEM)
     return pl.pallas_call(
         functools.partial(down_kernel, features, local),
-        in_specs=[smem] + [vmem] * 5,
+        in_specs=[smem] * 2 + [vmem] * (4 + len(made)),
         out_shape=(jax.ShapeDtypeStruct((total // exp_count, wide), F32),) * exp_count,
         scratch_shapes=[
+            pltpu.VMEM((2 * made[2].shape[0] + 2,) + made[0].shape, BF16),
             pltpu.VMEM((rows, width), BF16),
             pltpu.VMEM((rows, wide), F32),
         ],
         compiler_params=params(),
         name="down",
-    )(first, ranges, pick, weights, logits, made)
+    )(first, seq_index, ranges, pick, weights, logits, *made)
 
 
 def finish_kernel(hidden_ref, *refs):
@@ -643,6 +648,15 @@
 
 def exchange(parts, axis, direction):
     return [parts[0]] + [send(part, axis, direction * k) for k, part in enumerate(parts) if k]
+
+
+def neighbour(x, axis):
+    return lax.ppermute(x, axis, [(i, i ^ 1) for i in range(lax.axis_size(axis))])
+
+
+def pair_gather(block, axis):
+    pair = jnp.stack([block, neighbour(block, axis)])
+    return [pair] + [send(pair, axis, k) for k in range(2, lax.axis_size(axis), 2)]
 
 
 def gather(block, axis):
@@ -681,9 +695,7 @@
     shares = swap(shares, "seq")
     gate_up_weights, shares = lax.optimization_barrier((gate_up_weights, shares))
     attn = join(shares)
-    beside = lax.ppermute(attn, "seq", [(i, i ^ 1) for i in range(seq_count)])
-    pair = jnp.stack([attn, beside])
-    gathered = [pair] + [send(pair, "seq", k) for k in range(2, seq_count, 2)]
+    gathered = pair_gather(attn, "seq")
     hidden, outgoing = hidden_state(seq_index, gathered, residual, w_out, norm_gain, routes)
     incoming = gather(outgoing, "exp")
     pieces = seq_count // PIECES
@@ -695,7 +707,9 @@
         )
         made, logits = inner(exchange(partial, "seq", 1))
         logits = logits[None] if pieces == 1 else lax.all_gather(logits, "seq")[::PIECES]
-        return down(first, ranges, pick, swap(made, "seq"), logits, w_down, exp_count), most
+        behind = jnp.stack([send(made, "seq", k) for k in range(2, seq_count, 2)])
+        made = [made, neighbour(made, "seq"), behind, neighbour(behind, "seq")]
+        return down(first, seq_index, ranges, pick, made, logits, w_down, exp_count), most
 
     made, most = one_round(0)
     pairs = w_gate_up.shape[0] * exp_count * steps * CAP

time: 87.4 us -> 86.5 us (0.990)
  waiting for transfers between devices: 28.1 us -> 24.2 us
  starting transfers between devices: 33.8 us -> 37.6 us
    all_to_all x2 -> x1, waiting for transfers between devices: 12.7 us -> 2.62 us  [swap(): return lax.all_to_all(x, axis, split_axis=0, concat_axis=0, tiled=True)]
    all_to_all x2 -> x1, starting transfers between devices: 10.8 us -> 3.39 us  [swap(): return lax.all_to_all(x, axis, split_axis=0, concat_axis=0, tiled=True)]
    ppermute x16 -> x19, starting transfers between devices: 22.7 us -> 30 us  [send(): lax.ppermute(x, axis, [(i, (i + distance) % count) for i in range(count)])]
    ppermute x1 -> x3, starting transfers between devices: 0.35 us -> 4.22 us  [neighbour(): lax.ppermute(x, axis, [(i, i ^ 1) for i in range(lax.axis_size(axis))])]
    ppermute x16 -> x19, waiting for transfers between devices: 12 us -> 15.4 us  [send(): lax.ppermute(x, axis, [(i, (i + distance) % count) for i in range(count)])]
    ppermute x1 -> x3, waiting for transfers between devices: 3.35 us -> 6.15 us  [neighbour(): lax.ppermute(x, axis, [(i, i ^ 1) for i in range(lax.axis_size(axis))])]
  transfers between devices with their start and end apart: 19 -> 23, of which waited for: 11 -> 15; matrix products, arithmetic and copies ran while one was open for 6% -> 6% of each run, Pallas kernels for 0% -> 0%
where the time goes in v8:
time: 86.5 us; the launch traced here: 85.9 us
  starting transfers between devices  37.6 us (43%)
  waiting for transfers between devices  24.2 us (28%)
  Pallas kernels  18.2 us (21%)
  local copies, waits for them, and re-layouts  4.87 us (6%)
    ppermute x19, starting transfers between devices, send(): lax.ppermute(x, axis, [(i, (i + distance) % count) for i in range(count)])  30 us
    ppermute x19, waiting for transfers between devices, send(): lax.ppermute(x, axis, [(i, (i + distance) % count) for i in range(count)])  15.4 us
    pallas_call x1, Pallas kernels, attend(): pl.pallas_call(functools.partial(attend_kernel, classes), in_specs=[smem]...  9.85 us
    ppermute x3, waiting for transfers between devices, neighbour(): lax.ppermute(x, axis, [(i, i ^ 1) for i in range(lax.axis_size(axis))])  6.15 us
    optimization_barrier x1, local copies, waits for them, and re-layouts, local(): w_gate_up, shares = lax.optimization_barrier((w_gate_up, shares))  4.83 us
    pallas_call x1, Pallas kernels, gate_up(): pl.pallas_call(functools.partial(gate_up_kernel, features, local, turn, s...  4.25 us
    ppermute x3, starting transfers between devices, neighbour(): lax.ppermute(x, axis, [(i, i ^ 1) for i in range(lax.axis_size(axis))])  4.22 us
    all_to_all x1, starting transfers between devices, swap(): return lax.all_to_all(x, axis, split_axis=0, concat_axis=0, tiled=True)  3.39 us
  transfers between devices with their start and end apart: 23, of which 15 were waited for; matrix products, arithmetic and copies ran while one was open for 6% of the time, Pallas kernels for 0%

profile of v8, /device:TPU:0, one launch (start us, length us, event | category | flops | bytes accessed | tf_op | source)
XLA Modules:
  0.0 85.9 jit_solution(936200511005333524)
XLA Ops:
  0.0 9.9 %attend.1 = bf16[8,12,640]{2,1,0:T(8,128)(2,1)} custom-call(s32[1]{0:T(128)} %bitcast.5.seq_ref, s32[8,8]{1,0:T(8,128)} %table_hbm.1, s32[8]{0:T(128)} %len_hbm.1, bf16[4,8,1536]{2,1,0:T(8,128)(2,1)} %q_hbm.1, bf16[4,8,2,512]{3,2,1,0:T(2,128)(2,1)} %fresh_hbm.1, bf16[64,64,2,512]{3,2,1,0:T(2,128)(2,1)} %bitcast.28), custom_call_target="tpu_custom_call" | custom-call | tf_op jit(solution)/shard_map/attend/pallas_call | solution.py:228
  9.9 3.4 %all-to-all-start = ((bf16[8,12,640]{2,1,0:T(8,128)(2,1)}), bf16[8,12,640]{2,1,0:T(8,128)(2,1)S(1)}, u32[]{:S(2)}, u32[]{:S(2)}) async-start(bf16[8,12,640]{2,1,0:T(8,128)(2,1)} %attend.1), calls=%async_computation | async-start | bytes 327680 | tf_op jit(solution)/shard_map/all_to_all | solution.py:646
  13.3 4.8 %copy.16 = bf16[10,192,2,512]{3,1,2,0:T(8,128)(2,1)} copy(bf16[10,192,2,512]{3,2,1,0:T(2,128)(2,1)} %param.24) | data formatting | bytes 7864320 | tf_op jit(solution)/shard_map/optimization_barrier | solution.py:693
  18.2 2.6 %all-to-all-done.x_ref = bf16[8,12,640]{2,1,0:T(8,128)(2,1)S(1)} async-done(((bf16[8,12,640]{2,1,0:T(8,128)(2,1)}), bf16[8,12,640]{2,1,0:T(8,128)(2,1)S(1)}, u32[]{:S(2)}, u32[]{:S(2)}) %all-to-all-start) | async-done | bytes 122912 | tf_op jit(solution)/shard_map/all_to_all | solution.py:646
  21.2 1.0 %collective-permute-start.12 = (bf16[4,1536]{1,0:T(4,128)(2,1)S(1)}, bf16[4,1536]{1,0:T(4,128)(2,1)S(1)}, u32[]{:S(2)}, u32[]{:S(2)}) collective-permute-start(bf16[4,1536]{1,0:T(4,128)(2,1)S(1)} %join.1), channel_id=1, source_target_pairs={{0,4},{4,0},{8,12},{12,8},{16,20},{20,16},{24,28},{28,24},{1,5},{5... | collective-permute-start | bytes 36872 | tf_op jit(solution)/shard_map/ppermute | solution.py:654
  22.2 2.7 %collective-permute-done.12 = bf16[4,1536]{1,0:T(4,128)(2,1)S(1)} collective-permute-done((bf16[4,1536]{1,0:T(4,128)(2,1)S(1)}, bf16[4,1536]{1,0:T(4,128)(2,1)S(1)}, u32[]{:S(2)}, u32[]{:S(2)}) %collective-permute-start.12) | collective-permute-done | bytes 12320 | tf_op jit(solution)/shard_map/ppermute | solution.py:654
  25.3 1.4 %collective-permute-start.14 = (bf16[2,4,1536]{2,1,0:T(4,128)(2,1)S(1)}, bf16[2,4,1536]{2,1,0:T(4,128)(2,1)S(1)}, u32[]{:S(2)}, u32[]{:S(2)}) collective-permute-start(bf16[2,4,1536]{2,1,0:T(4,128)(2,1)S(1)} %pad_maximum_fusion.2.refs_0_), channel_id=1, source_target_pairs={{0,16},{4,20},{8,24},{12,28},{16,0},{20,4},{24,8},{28,12},{1,17},{... | collective-permute-start | bytes 73736 | tf_op jit(solution)/shard_map/ppermute | solution.py:642
  26.7 2.1 %collective-permute-start.15 = (bf16[2,4,1536]{2,1,0:T(4,128)(2,1)S(1)}, bf16[2,4,1536]{2,1,0:T(4,128)(2,1)S(1)}, u32[]{:S(2)}, u32[]{:S(2)}) collective-permute-start(bf16[2,4,1536]{2,1,0:T(4,128)(2,1)S(1)} %pad_maximum_fusion.2.refs_0_), channel_id=1, source_target_pairs={{0,24},{4,28},{8,0},{12,4},{16,8},{20,12},{24,16},{28,20},{1,25},{... | collective-permute-start | bytes 73736 | tf_op jit(solution)/shard_map/ppermute | solution.py:642
  28.9 1.8 %collective-permute-done.13.refs_1_ = bf16[2,4,1536]{2,1,0:T(4,128)(2,1)S(1)} collective-permute-done((bf16[2,4,1536]{2,1,0:T(4,128)(2,1)S(1)}, bf16[2,4,1536]{2,1,0:T(4,128)(2,1)S(1)}, u32[]{:S(2)}, u32[]{:S(2)}) %collective-permute-start.13) | collective-permute-done | bytes 24608 | tf_op jit(solution)/shard_map/ppermute | solution.py:642
  30.7 0.6 collective-permute-done.15.refs_3_
  31.8 3.2 %collective-permute-start.17 = (bf16[32,256]{1,0:T(8,128)(2,1)S(1)}, bf16[32,256]{1,0:T(8,128)(2,1)S(1)}, u32[]{:S(2)}, u32[]{:S(2)}) collective-permute-start(bf16[32,256]{1,0:T(8,128)(2,1)S(1)} %get-tuple-element.102.refs_0_), channel_id=1, source_target_pairs={{0,2},{1,3},{2,0},{3,1},{4,6},{5,7},{6,4},{7,5},{8,10},{9,11},{10,... | collective-permute-start | bytes 49160 | tf_op jit(solution)/shard_map/ppermute | solution.py:642
  35.0 1.4 %collective-permute-start.18 = (bf16[32,256]{1,0:T(8,128)(2,1)S(1)}, bf16[32,256]{1,0:T(8,128)(2,1)S(1)}, u32[]{:S(2)}, u32[]{:S(2)}) collective-permute-start(bf16[32,256]{1,0:T(8,128)(2,1)S(1)} %get-tuple-element.102.refs_0_), channel_id=1, source_target_pairs={{0,3},{1,0},{2,1},{3,2},{4,7},{5,4},{6,5},{7,6},{8,11},{9,8},{10,9... | collective-permute-start | bytes 49160 | tf_op jit(solution)/shard_map/ppermute | solution.py:642
  36.7 1.1 %collective-permute-done.18.refs_3_ = bf16[32,256]{1,0:T(8,128)(2,1)S(1)} collective-permute-done((bf16[32,256]{1,0:T(8,128)(2,1)S(1)}, bf16[32,256]{1,0:T(8,128)(2,1)S(1)}, u32[]{:S(2)}, u32[]{:S(2)}) %collective-permute-start.18) | collective-permute-done | bytes 16416 | tf_op jit(solution)/shard_map/ppermute | solution.py:642
  37.8 4.2 %gate_up.3 = (bf16[368,128]{1,0:T(8,128)(2,1)S(1)}, bf16[368,128]{1,0:T(8,128)(2,1)S(1)}, bf16[368,128]{1,0:T(8,128)(2,1)S(1)}, bf16[368,128]{1,0:T(8,128)(2,1)S...) custom-call(s32[1]{0:T(128)} %bitcast.12.where_ref, ...), custom_call_target="tpu_custom_call" | custom-call | tf_op jit(solution)/shard_map/gate_up/pallas_call | solution.py:462
  42.5 1.8 %collective-permute-start.20 = (bf16[368,128]{1,0:T(8,128)(2,1)S(1)}, bf16[368,128]{1,0:T(8,128)(2,1)S(1)}, u32[]{:S(2)}, u32[]{:S(2)}) collective-permute-start(bf16[368,128]{1,0:T(8,128)(2,1)S(1)} %get-tuple-element.109), channel_id=1, source_target_pairs={{0,8},{4,12},{8,16},{12,20},{16,24},{20,28},{24,0},{28,4},{1,9},{5... | collective-permute-start | bytes 282632 | tf_op jit(solution)/shard_map/ppermute | solution.py:642
  44.3 3.1 %collective-permute-start.21 = (bf16[368,128]{1,0:T(8,128)(2,1)S(1)}, bf16[368,128]{1,0:T(8,128)(2,1)S(1)}, u32[]{:S(2)}, u32[]{:S(2)}) collective-permute-start(bf16[368,128]{1,0:T(8,128)(2,1)S(1)} %get-tuple-element.110), channel_id=1, source_target_pairs={{0,12},{4,16},{8,20},{12,24},{16,28},{20,0},{24,4},{28,8},{1,13},{... | collective-permute-start | bytes 282632 | tf_op jit(solution)/shard_map/ppermute | solution.py:642
  47.4 2.0 %collective-permute-start.22 = (bf16[368,128]{1,0:T(8,128)(2,1)S(1)}, bf16[368,128]{1,0:T(8,128)(2,1)S(1)}, u32[]{:S(2)}, u32[]{:S(2)}) collective-permute-start(bf16[368,128]{1,0:T(8,128)(2,1)S(1)} %get-tuple-element.111), channel_id=1, source_target_pairs={{0,16},{4,20},{8,24},{12,28},{16,0},{20,4},{24,8},{28,12},{1,17},{... | collective-permute-start | bytes 282632 | tf_op jit(solution)/shard_map/ppermute | solution.py:642
  49.5 0.5 collective-permute-start.23
  50.2 1.6 %collective-permute-start.24 = (bf16[368,128]{1,0:T(8,128)(2,1)S(1)}, bf16[368,128]{1,0:T(8,128)(2,1)S(1)}, u32[]{:S(2)}, u32[]{:S(2)}) collective-permute-start(bf16[368,128]{1,0:T(8,128)(2,1)S(1)} %get-tuple-element.113), channel_id=1, source_target_pairs={{0,24},{4,28},{8,0},{12,4},{16,8},{20,12},{24,16},{28,20},{1,25},{... | collective-permute-start | bytes 282632 | tf_op jit(solution)/shard_map/ppermute | solution.py:642
  51.9 3.0 %collective-permute-start.25 = (bf16[368,128]{1,0:T(8,128)(2,1)S(1)}, bf16[368,128]{1,0:T(8,128)(2,1)S(1)}, u32[]{:S(2)}, u32[]{:S(2)}) collective-permute-start(bf16[368,128]{1,0:T(8,128)(2,1)S(1)} %get-tuple-element.114), channel_id=1, source_target_pairs={{0,28},{4,0},{8,4},{12,8},{16,12},{20,16},{24,20},{28,24},{1,29},{... | collective-permute-start | bytes 282632 | tf_op jit(solution)/shard_map/ppermute | solution.py:642
  54.9 3.3 %collective-permute-done.21.refs_3_ = bf16[368,128]{1,0:T(8,128)(2,1)S(1)} collective-permute-done((bf16[368,128]{1,0:T(8,128)(2,1)S(1)}, bf16[368,128]{1,0:T(8,128)(2,1)S(1)}, u32[]{:S(2)}, u32[]{:S(2)}) %collective-permute-start.21) | collective-permute-done | bytes 94240 | tf_op jit(solution)/shard_map/ppermute | solution.py:642
  58.7 5.4 %collective-permute-start.29 = (bf16[176,128]{1,0:T(8,128)(2,1)S(1)}, bf16[176,128]{1,0:T(8,128)(2,1)S(1)}, u32[]{:S(2)}, u32[]{:S(2)}) collective-permute-start(bf16[176,128]{1,0:T(8,128)(2,1)S(1)} %get-tuple-element.116.refs_0_), channel_id=1, source_target_pairs={{0,24},{4,28},{8,0},{12,4},{16,8},{20,12},{24,16},{28,20},{1,25},{... | collective-permute-start | bytes 135176 | tf_op jit(solution)/shard_map/ppermute | solution.py:642
  64.5 1.2 %collective-permute-start.27 = (bf16[176,128]{1,0:T(8,128)(2,1)S(1)}, bf16[176,128]{1,0:T(8,128)(2,1)S(1)}, u32[]{:S(2)}, u32[]{:S(2)}) collective-permute-start(bf16[176,128]{1,0:T(8,128)(2,1)S(1)} %get-tuple-element.116.refs_0_), channel_id=1, source_target_pairs={{0,8},{4,12},{8,16},{12,20},{16,24},{20,28},{24,0},{28,4},{1,9},{5... | collective-permute-start | bytes 135176 | tf_op jit(solution)/shard_map/ppermute | solution.py:642
  66.1 3.2 %collective-permute-done.28 = bf16[176,128]{1,0:T(8,128)(2,1)S(1)} collective-permute-done((bf16[176,128]{1,0:T(8,128)(2,1)S(1)}, bf16[176,128]{1,0:T(8,128)(2,1)S(1)}, u32[]{:S(2)}, u32[]{:S(2)}) %collective-permute-start.28) | collective-permute-done | bytes 45088 | tf_op jit(solution)/shard_map/ppermute | solution.py:642
  69.3 1.1 %collective-permute-done.27 = bf16[176,128]{1,0:T(8,128)(2,1)S(1)} collective-permute-done((bf16[176,128]{1,0:T(8,128)(2,1)S(1)}, bf16[176,128]{1,0:T(8,128)(2,1)S(1)}, u32[]{:S(2)}, u32[]{:S(2)}) %collective-permute-start.27) | collective-permute-done | bytes 45088 | tf_op jit(solution)/shard_map/ppermute | solution.py:642
  70.4 3.2 %collective-permute-start.30 = (bf16[3,176,128]{2,1,0:T(8,128)(2,1)S(1)}, bf16[3,176,128]{2,1,0:T(8,128)(2,1)S(1)}, u32[]{:S(2)}, u32[]{:S(2)}) collective-permute-start(bf16[3,176,128]{2,1,0:T(8,128)(2,1)S(1)} %pad_maximum_fusion.1.refs_2_), channel_id=1, source_target_pairs={{0,4},{4,0},{8,12},{12,8},{16,20},{20,16},{24,28},{28,24},{1,5},{5... | collective-permute-start | bytes 405512 | tf_op jit(solution)/shard_map/ppermute | solution.py:654
  74.2 3.4 %collective-permute-done.26.refs_1_ = bf16[176,128]{1,0:T(8,128)(2,1)S(1)} collective-permute-done((bf16[176,128]{1,0:T(8,128)(2,1)S(1)}, bf16[176,128]{1,0:T(8,128)(2,1)S(1)}, u32[]{:S(2)}, u32[]{:S(2)}) %collective-permute-start.26) | collective-permute-done | bytes 45088 | tf_op jit(solution)/shard_map/ppermute | solution.py:654
  77.6 2.1 %down.3 = (f32[32,256]{1,0:T(8,128)S(1)}, f32[32,256]{1,0:T(8,128)S(1)}, f32[32,256]{1,0:T(8,128)S(1)}, f32[32,256]{1,0:T(8,128)S(1)}) custom-call(s32[16]{0:T(128)S(1)} %get-tuple-element.104.first_ref, s32[1]{0:T(128)} %bitcast.5.seq_ref, f32[16,128]{1,0:T(8,128)S(1)} %get-tuple-element.105.range_ref, bf16[128,352]{1,0:T(8,128)(2,1)S(1)} %get-tuple-element.106.pick_ref, ...), custom_call_target="tpu_custom_call" | custom-call | tf_op jit(solution)/shard_map/down/pallas_call | solution.py:590
  80.1 1.8 %collective-permute-start.32 = (f32[32,256]{1,0:T(8,128)S(1)}, f32[32,256]{1,0:T(8,128)S(1)}, u32[]{:S(2)}, u32[]{:S(2)}) collective-permute-start(f32[32,256]{1,0:T(8,128)S(1)} %get-tuple-element.123), channel_id=1, source_target_pairs={{0,2},{1,3},{2,0},{3,1},{4,6},{5,7},{6,4},{7,5},{8,10},{9,11},{10,... | collective-permute-start | bytes 98312 | tf_op jit(solution)/shard_map/ppermute | solution.py:642
  82.0 2.2 %collective-permute-done.32.refs_2_ = f32[32,256]{1,0:T(8,128)S(1)} collective-permute-done((f32[32,256]{1,0:T(8,128)S(1)}, f32[32,256]{1,0:T(8,128)S(1)}, u32[]{:S(2)}, u32[]{:S(2)}) %collective-permute-start.32) | collective-permute-done | bytes 32800 | tf_op jit(solution)/shard_map/ppermute | solution.py:642
  84.2 0.9 %collective-permute-done.33.refs_3_ = f32[32,256]{1,0:T(8,128)S(1)} collective-permute-done((f32[32,256]{1,0:T(8,128)S(1)}, f32[32,256]{1,0:T(8,128)S(1)}, u32[]{:S(2)}, u32[]{:S(2)}) %collective-permute-start.33) | collective-permute-done | bytes 32800 | tf_op jit(solution)/shard_map/ppermute | solution.py:642
  85.1 0.8 finish.1
  (37 shorter events, 4.3 us)
Async XLA Ops:
  9.9 10.9 %all-to-all-start = ((bf16[8,12,640]{2,1,0:T(8,128)(2,1)}), bf16[8,12,640]{2,1,0:T(8,128)(2,1)S(1)}, u32[]{:S(2)}, u32[]{:S(2)}) async-start(bf16[8,12,640]{2,1,0:T(8,128)(2,1)} %attend.1), calls=%async_computation | async-start | bytes 327680 | tf_op jit(solution)/shard_map/all_to_all | solution.py:646
  13.3 18.0 %copy-start = (bf16[1536,192]{0,1:T(8,128)(2,1)S(1)}, bf16[1536,192]{0,1:T(8,128)(2,1)}, u32[]{:S(2)}) copy-start(bf16[1536,192]{0,1:T(8,128)(2,1)} %param.21) | copy-start | bytes 1769476
  13.3 17.9 %copy-start.1 = (bf16[4,8,192]{2,1,0:T(8,128)(2,1)S(1)}, bf16[4,8,192]{2,1,0:T(8,128)(2,1)}, u32[]{:S(2)}) copy-start(bf16[4,8,192]{2,1,0:T(8,128)(2,1)} %residual_ref.1) | copy-start | bytes 36868
  13.3 17.9 %copy-start.2 = (s32[4,8,8]{2,1,0:T(8,128)S(1)}, s32[4,8,8]{2,1,0:T(8,128)}, u32[]{:S(2)}) copy-start(s32[4,8,8]{2,1,0:T(8,128)} %routes_ref.1) | copy-start | bytes 3076
  13.3 17.9 %copy-start.3 = (f32[192]{0:T(256)S(1)}, f32[192]{0:T(256)}, u32[]{:S(2)}) copy-start(f32[192]{0:T(256)} %param.22) | copy-start | bytes 2308
  13.3 24.5 %copy-start.5 = (bf16[192,40]{0,1:T(8,128)(2,1)S(1)}, bf16[192,40]{0,1:T(8,128)(2,1)}, u32[]{:S(2)}) copy-start(bf16[192,40]{0,1:T(8,128)(2,1)} %param.23) | copy-start | bytes 46084
  18.2 59.5 %copy-start.4 = (bf16[10,192,512]{2,1,0:T(8,128)(2,1)S(1)}, bf16[10,192,512]{2,1,0:T(8,128)(2,1)}, u32[]{:S(2)}) copy-start(bf16[10,192,512]{2,1,0:T(8,128)(2,1)} %w_ref.1) | copy-start | bytes 5898244
  21.2 3.7 %collective-permute-start.12 = (bf16[4,1536]{1,0:T(4,128)(2,1)S(1)}, bf16[4,1536]{1,0:T(4,128)(2,1)S(1)}, u32[]{:S(2)}, u32[]{:S(2)}) collective-permute-start(bf16[4,1536]{1,0:T(4,128)(2,1)S(1)} %join.1), channel_id=1, source_target_pairs={{0,4},{4,0},{8,12},{12,8},{16,20},{20,16},{24,28},{28,24},{1,5},{5... | collective-permute-start | bytes 36872 | tf_op jit(solution)/shard_map/ppermute | solution.py:654
  25.0 5.7 %collective-permute-start.13 = (bf16[2,4,1536]{2,1,0:T(4,128)(2,1)S(1)}, bf16[2,4,1536]{2,1,0:T(4,128)(2,1)S(1)}, u32[]{:S(2)}, u32[]{:S(2)}) collective-permute-start(bf16[2,4,1536]{2,1,0:T(4,128)(2,1)S(1)} %pad_maximum_fusion.2.refs_0_), channel_id=1, source_target_pairs={{0,8},{4,12},{8,16},{12,20},{16,24},{20,28},{24,0},{28,4},{1,9},{5... | collective-permute-start | bytes 73736 | tf_op jit(solution)/shard_map/ppermute | solution.py:642
  25.3 5.3 %collective-permute-start.14 = (bf16[2,4,1536]{2,1,0:T(4,128)(2,1)S(1)}, bf16[2,4,1536]{2,1,0:T(4,128)(2,1)S(1)}, u32[]{:S(2)}, u32[]{:S(2)}) collective-permute-start(bf16[2,4,1536]{2,1,0:T(4,128)(2,1)S(1)} %pad_maximum_fusion.2.refs_0_), channel_id=1, source_target_pairs={{0,16},{4,20},{8,24},{12,28},{16,0},{20,4},{24,8},{28,12},{1,17},{... | collective-permute-start | bytes 73736 | tf_op jit(solution)/shard_map/ppermute | solution.py:642
  26.7 4.5 %collective-permute-start.15 = (bf16[2,4,1536]{2,1,0:T(4,128)(2,1)S(1)}, bf16[2,4,1536]{2,1,0:T(4,128)(2,1)S(1)}, u32[]{:S(2)}, u32[]{:S(2)}) collective-permute-start(bf16[2,4,1536]{2,1,0:T(4,128)(2,1)S(1)} %pad_maximum_fusion.2.refs_0_), channel_id=1, source_target_pairs={{0,24},{4,28},{8,0},{12,4},{16,8},{20,12},{24,16},{28,20},{1,25},{... | collective-permute-start | bytes 73736 | tf_op jit(solution)/shard_map/ppermute | solution.py:642
  31.7 4.7 %collective-permute-start.16 = (bf16[32,256]{1,0:T(8,128)(2,1)S(1)}, bf16[32,256]{1,0:T(8,128)(2,1)S(1)}, u32[]{:S(2)}, u32[]{:S(2)}) collective-permute-start(bf16[32,256]{1,0:T(8,128)(2,1)S(1)} %get-tuple-element.102.refs_0_), channel_id=1, source_target_pairs={{0,1},{1,2},{2,3},{3,0},{4,5},{5,6},{6,7},{7,4},{8,9},{9,10},{10,1... | collective-permute-start | bytes 49160 | tf_op jit(solution)/shard_map/ppermute | solution.py:642
  31.8 4.9 %collective-permute-start.17 = (bf16[32,256]{1,0:T(8,128)(2,1)S(1)}, bf16[32,256]{1,0:T(8,128)(2,1)S(1)}, u32[]{:S(2)}, u32[]{:S(2)}) collective-permute-start(bf16[32,256]{1,0:T(8,128)(2,1)S(1)} %get-tuple-element.102.refs_0_), channel_id=1, source_target_pairs={{0,2},{1,3},{2,0},{3,1},{4,6},{5,7},{6,4},{7,5},{8,10},{9,11},{10,... | collective-permute-start | bytes 49160 | tf_op jit(solution)/shard_map/ppermute | solution.py:642
  35.0 2.8 %collective-permute-start.18 = (bf16[32,256]{1,0:T(8,128)(2,1)S(1)}, bf16[32,256]{1,0:T(8,128)(2,1)S(1)}, u32[]{:S(2)}, u32[]{:S(2)}) collective-permute-start(bf16[32,256]{1,0:T(8,128)(2,1)S(1)} %get-tuple-element.102.refs_0_), channel_id=1, source_target_pairs={{0,3},{1,0},{2,1},{3,2},{4,7},{5,4},{6,5},{7,6},{8,11},{9,8},{10,9... | collective-permute-start | bytes 49160 | tf_op jit(solution)/shard_map/ppermute | solution.py:642
  42.1 8.1 %collective-permute-start.19 = (bf16[368,128]{1,0:T(8,128)(2,1)S(1)}, bf16[368,128]{1,0:T(8,128)(2,1)S(1)}, u32[]{:S(2)}, u32[]{:S(2)}) collective-permute-start(bf16[368,128]{1,0:T(8,128)(2,1)S(1)} %get-tuple-element.108), channel_id=1, source_target_pairs={{0,4},{4,8},{8,12},{12,16},{16,20},{20,24},{24,28},{28,0},{1,5},{5... | collective-permute-start | bytes 282632 | tf_op jit(solution)/shard_map/ppermute | solution.py:642
  42.5 9.3 %collective-permute-start.20 = (bf16[368,128]{1,0:T(8,128)(2,1)S(1)}, bf16[368,128]{1,0:T(8,128)(2,1)S(1)}, u32[]{:S(2)}, u32[]{:S(2)}) collective-permute-start(bf16[368,128]{1,0:T(8,128)(2,1)S(1)} %get-tuple-element.109), channel_id=1, source_target_pairs={{0,8},{4,12},{8,16},{12,20},{16,24},{20,28},{24,0},{28,4},{1,9},{5... | collective-permute-start | bytes 282632 | tf_op jit(solution)/shard_map/ppermute | solution.py:642
  44.3 13.8 %collective-permute-start.21 = (bf16[368,128]{1,0:T(8,128)(2,1)S(1)}, bf16[368,128]{1,0:T(8,128)(2,1)S(1)}, u32[]{:S(2)}, u32[]{:S(2)}) collective-permute-start(bf16[368,128]{1,0:T(8,128)(2,1)S(1)} %get-tuple-element.110), channel_id=1, source_target_pairs={{0,12},{4,16},{8,20},{12,24},{16,28},{20,0},{24,4},{28,8},{1,13},{... | collective-permute-start | bytes 282632 | tf_op jit(solution)/shard_map/ppermute | solution.py:642
  47.4 10.7 %collective-permute-start.22 = (bf16[368,128]{1,0:T(8,128)(2,1)S(1)}, bf16[368,128]{1,0:T(8,128)(2,1)S(1)}, u32[]{:S(2)}, u32[]{:S(2)}) collective-permute-start(bf16[368,128]{1,0:T(8,128)(2,1)S(1)} %get-tuple-element.111), channel_id=1, source_target_pairs={{0,16},{4,20},{8,24},{12,28},{16,0},{20,4},{24,8},{28,12},{1,17},{... | collective-permute-start | bytes 282632 | tf_op jit(solution)/shard_map/ppermute | solution.py:642
  49.5 8.7 %collective-permute-start.23 = (bf16[368,128]{1,0:T(8,128)(2,1)S(1)}, bf16[368,128]{1,0:T(8,128)(2,1)S(1)}, u32[]{:S(2)}, u32[]{:S(2)}) collective-permute-start(bf16[368,128]{1,0:T(8,128)(2,1)S(1)} %get-tuple-element.112), channel_id=1, source_target_pairs={{0,20},{4,24},{8,28},{12,0},{16,4},{20,8},{24,12},{28,16},{1,21},{... | collective-permute-start | bytes 282632 | tf_op jit(solution)/shard_map/ppermute | solution.py:642
  50.2 7.9 %collective-permute-start.24 = (bf16[368,128]{1,0:T(8,128)(2,1)S(1)}, bf16[368,128]{1,0:T(8,128)(2,1)S(1)}, u32[]{:S(2)}, u32[]{:S(2)}) collective-permute-start(bf16[368,128]{1,0:T(8,128)(2,1)S(1)} %get-tuple-element.113), channel_id=1, source_target_pairs={{0,24},{4,28},{8,0},{12,4},{16,8},{20,12},{24,16},{28,20},{1,25},{... | collective-permute-start | bytes 282632 | tf_op jit(solution)/shard_map/ppermute | solution.py:642
  51.9 6.5 %collective-permute-start.25 = (bf16[368,128]{1,0:T(8,128)(2,1)S(1)}, bf16[368,128]{1,0:T(8,128)(2,1)S(1)}, u32[]{:S(2)}, u32[]{:S(2)}) collective-permute-start(bf16[368,128]{1,0:T(8,128)(2,1)S(1)} %get-tuple-element.114), channel_id=1, source_target_pairs={{0,28},{4,0},{8,4},{12,8},{16,12},{20,16},{24,20},{28,24},{1,29},{... | collective-permute-start | bytes 282632 | tf_op jit(solution)/shard_map/ppermute | solution.py:642
  58.7 7.4 %collective-permute-start.29 = (bf16[176,128]{1,0:T(8,128)(2,1)S(1)}, bf16[176,128]{1,0:T(8,128)(2,1)S(1)}, u32[]{:S(2)}, u32[]{:S(2)}) collective-permute-start(bf16[176,128]{1,0:T(8,128)(2,1)S(1)} %get-tuple-element.116.refs_0_), channel_id=1, source_target_pairs={{0,24},{4,28},{8,0},{12,4},{16,8},{20,12},{24,16},{28,20},{1,25},{... | collective-permute-start | bytes 135176 | tf_op jit(solution)/shard_map/ppermute | solution.py:642
  64.1 5.1 %collective-permute-start.28 = (bf16[176,128]{1,0:T(8,128)(2,1)S(1)}, bf16[176,128]{1,0:T(8,128)(2,1)S(1)}, u32[]{:S(2)}, u32[]{:S(2)}) collective-permute-start(bf16[176,128]{1,0:T(8,128)(2,1)S(1)} %get-tuple-element.116.refs_0_), channel_id=1, source_target_pairs={{0,16},{4,20},{8,24},{12,28},{16,0},{20,4},{24,8},{28,12},{1,17},{... | collective-permute-start | bytes 135176 | tf_op jit(solution)/shard_map/ppermute | solution.py:642
  64.5 5.8 %collective-permute-start.27 = (bf16[176,128]{1,0:T(8,128)(2,1)S(1)}, bf16[176,128]{1,0:T(8,128)(2,1)S(1)}, u32[]{:S(2)}, u32[]{:S(2)}) collective-permute-start(bf16[176,128]{1,0:T(8,128)(2,1)S(1)} %get-tuple-element.116.refs_0_), channel_id=1, source_target_pairs={{0,8},{4,12},{8,16},{12,20},{16,24},{20,28},{24,0},{28,4},{1,9},{5... | collective-permute-start | bytes 135176 | tf_op jit(solution)/shard_map/ppermute | solution.py:642
  70.4 7.2 %collective-permute-start.30 = (bf16[3,176,128]{2,1,0:T(8,128)(2,1)S(1)}, bf16[3,176,128]{2,1,0:T(8,128)(2,1)S(1)}, u32[]{:S(2)}, u32[]{:S(2)}) collective-permute-start(bf16[3,176,128]{2,1,0:T(8,128)(2,1)S(1)} %pad_maximum_fusion.1.refs_2_), channel_id=1, source_target_pairs={{0,4},{4,0},{8,12},{12,8},{16,20},{20,16},{24,28},{28,24},{1,5},{5... | collective-permute-start | bytes 405512 | tf_op jit(solution)/shard_map/ppermute | solution.py:654
  73.6 4.0 %collective-permute-start.26 = (bf16[176,128]{1,0:T(8,128)(2,1)S(1)}, bf16[176,128]{1,0:T(8,128)(2,1)S(1)}, u32[]{:S(2)}, u32[]{:S(2)}) collective-permute-start(bf16[176,128]{1,0:T(8,128)(2,1)S(1)} %get-tuple-element.116.refs_0_), channel_id=1, source_target_pairs={{0,4},{4,0},{8,12},{12,8},{16,20},{20,16},{24,28},{28,24},{1,5},{5... | collective-permute-start | bytes 135176 | tf_op jit(solution)/shard_map/ppermute | solution.py:654
  80.0 2.0 %collective-permute-start.31 = (f32[32,256]{1,0:T(8,128)S(1)}, f32[32,256]{1,0:T(8,128)S(1)}, u32[]{:S(2)}, u32[]{:S(2)}) collective-permute-start(f32[32,256]{1,0:T(8,128)S(1)} %get-tuple-element.122), channel_id=1, source_target_pairs={{0,3},{1,0},{2,1},{3,2},{4,7},{5,4},{6,5},{7,6},{8,11},{9,8},{10,9... | collective-permute-start | bytes 98312 | tf_op jit(solution)/shard_map/ppermute | solution.py:642
  80.1 4.2 %collective-permute-start.32 = (f32[32,256]{1,0:T(8,128)S(1)}, f32[32,256]{1,0:T(8,128)S(1)}, u32[]{:S(2)}, u32[]{:S(2)}) collective-permute-start(f32[32,256]{1,0:T(8,128)S(1)} %get-tuple-element.123), channel_id=1, source_target_pairs={{0,2},{1,3},{2,0},{3,1},{4,6},{5,7},{6,4},{7,5},{8,10},{9,11},{10,... | collective-permute-start | bytes 98312 | tf_op jit(solution)/shard_map/ppermute | solution.py:642
  81.8 3.3 %collective-permute-start.33 = (f32[32,256]{1,0:T(8,128)S(1)}, f32[32,256]{1,0:T(8,128)S(1)}, u32[]{:S(2)}, u32[]{:S(2)}) collective-permute-start(f32[32,256]{1,0:T(8,128)S(1)} %get-tuple-element.124), channel_id=1, source_target_pairs={{0,1},{1,2},{2,3},{3,0},{4,5},{5,6},{6,7},{7,4},{8,9},{9,10},{10,1... | collective-permute-start | bytes 98312 | tf_op jit(solution)/shard_map/ppermute | solution.py:642

commit v9 on v8

--- a/solution.py
+++ b/solution.py
@@ -146,8 +146,8 @@
     own = iota((rows, KV_WIDTH), 1) // HEAD_SIZE == iota((rows, KV_WIDTH), 0) % KEY_VALUE_HEADS
     lane = iota((rows, LANES), 1)
     head = iota((rows, LANES), 0) % KEY_VALUE_HEADS
-    row_step = iota((rows, 16), 0) // (GROUP * KEY_VALUE_HEADS)
-    kept = jnp.logical_and(iota((rows, 16), 1) <= row_step, seq_ref[0] == 0)
+    lane_step = iota((16, LANES), 1) // (GROUP * KEY_VALUE_HEADS)
+    kept = jnp.logical_and(iota((16, LANES), 0) <= lane_step, seq_ref[0] == 0)
     fresh_bias = jnp.where(kept, 0.0, NEG_FILL)
 
     def fresh_rows(r, which):
@@ -162,27 +162,30 @@
             ],
             axis=0,
         )
-        spread = jnp.where(own, spread, 0.0).astype(BF16)
+        spread = jnp.where(own, spread, 0.0)
+        spread = jnp.concatenate([spread, jnp.zeros((LANES - rows, KV_WIDTH), F32)], axis=0).astype(BF16)
         both = [page_ref[r * pages + page].reshape(2 * page_rows, KV_WIDTH) for page in range(count)]
         both = jnp.concatenate(both, axis=0)
         size = 2 * count * page_rows
-        place = iota((1, size), 1)
-        live = jnp.logical_and(place % 2 == 0, first + place // 2 < len_ref[r])
-        scores = dot_nt(spread, both) + jnp.where(live, 0.0, NEG_FILL)
-        fresh_scores = dot_nt(spread, fresh_rows(r, 0)) + fresh_bias
+        place = iota((size, LANES), 0)
+        live = jnp.logical_and(place % 2 == 0, place < 2 * (len_ref[r] - first))
+        scores = jnp.where(live, dot_nt(both, spread), NEG_FILL)
+        fresh_scores = dot_nt(fresh_rows(r, 0), spread) + fresh_bias
         largest = jnp.maximum(
-            jnp.max(scores, axis=1, keepdims=True), jnp.max(fresh_scores, axis=1, keepdims=True)
+            jnp.max(scores, axis=0, keepdims=True), jnp.max(fresh_scores, axis=0, keepdims=True)
         )
         weights = jnp.exp(scores - largest)
         fresh_weights = jnp.exp(fresh_scores - largest)
-        total = jnp.sum(weights, axis=1, keepdims=True)
-        total = total + jnp.sum(fresh_weights, axis=1, keepdims=True)
-        moved = [pltpu.roll(tile_of(weights, j), 1, 1) for j in range(size // LANES)]
-        acc = dot_nn(jnp.concatenate(moved, axis=1).astype(BF16), both)
-        acc = acc + dot_nn(fresh_weights.astype(BF16), fresh_rows(r, 1))
-        acc = jnp.where(own, acc * (1.0 / total), 0.0)
+        total = jnp.sum(weights, axis=0, keepdims=True)
+        total = total + jnp.sum(fresh_weights, axis=0, keepdims=True)
+        inverse = 1.0 / total
+        moved = pltpu.roll(weights * inverse, 1, 0).astype(BF16)
+        acc = dot_tn(moved, both)
+        acc = acc + dot_tn((fresh_weights * inverse).astype(BF16), fresh_rows(r, 1))
+        acc = jnp.where(own, acc[0:rows], 0.0)
         acc = jnp.sum(acc.reshape(steps * GROUP, KEY_VALUE_HEADS, KV_WIDTH), axis=1)
         level = jnp.where(needed(r, 0), largest + jnp.log(total), NEG_FILL)
+        level = jnp.broadcast_to(level, (LANES, LANES)).T[0:rows]
         high = round16(level)
         middle = round16(level - high)
         side = jnp.where(lane == head, high, 0.0)

time: 86.5 us -> 88.4 us (1.022)
  waiting for transfers between devices: 24.2 us -> 27.1 us
  Pallas kernels: 18.2 us -> 19.7 us
  starting transfers between devices: 37.6 us -> 36.2 us
    ppermute x19, waiting for transfers between devices: 15.4 us -> 17.3 us  [send(): lax.ppermute(x, axis, [(i, (i + distance) % count) for i in range(count)])]
    pallas_call x1, Pallas kernels: 9.85 us -> 11.3 us  [attend(): pl.pallas_call(functools.partial(attend_kernel, classes), in_specs=[smem]...]
    ppermute x3, starting transfers between devices: 4.22 us -> 3.25 us  [neighbour(): lax.ppermute(x, axis, [(i, i ^ 1) for i in range(lax.axis_size(axis))])]
    ppermute x3, waiting for transfers between devices: 6.15 us -> 7.08 us  [neighbour(): lax.ppermute(x, axis, [(i, i ^ 1) for i in range(lax.axis_size(axis))])]
  transfers between devices with their start and end apart: 23 -> 23, of which waited for: 15 -> 14; matrix products, arithmetic and copies ran while one was open for 6% -> 5% of each run, Pallas kernels for 0% -> 0%
where the time goes in v9:
time: 88.4 us; the launch traced here: 88.5 us
  starting transfers between devices  36.2 us (41%)
  waiting for transfers between devices  27.1 us (31%)
  Pallas kernels  19.7 us (22%)
  local copies, waits for them, and re-layouts  4.87 us (6%)
    ppermute x19, starting transfers between devices, send(): lax.ppermute(x, axis, [(i, (i + distance) % count) for i in range(count)])  29.5 us
    ppermute x19, waiting for transfers between devices, send(): lax.ppermute(x, axis, [(i, (i + distance) % count) for i in range(count)])  17.3 us
    pallas_call x1, Pallas kernels, attend(): pl.pallas_call(functools.partial(attend_kernel, classes), in_specs=[smem]...  11.3 us
    ppermute x3, waiting for transfers between devices, neighbour(): lax.ppermute(x, axis, [(i, i ^ 1) for i in range(lax.axis_size(axis))])  7.08 us
    optimization_barrier x1, local copies, waits for them, and re-layouts, local(): w_gate_up, shares = lax.optimization_barrier((w_gate_up, shares))  4.83 us
    pallas_call x1, Pallas kernels, gate_up(): pl.pallas_call(functools.partial(gate_up_kernel, features, local, turn, s...  4.25 us
    all_to_all x1, starting transfers between devices, swap(): return lax.all_to_all(x, axis, split_axis=0, concat_axis=0, tiled=True)  3.39 us
    ppermute x3, starting transfers between devices, neighbour(): lax.ppermute(x, axis, [(i, i ^ 1) for i in range(lax.axis_size(axis))])  3.25 us
  transfers between devices with their start and end apart: 23, of which 14 were waited for; matrix products, arithmetic and copies ran while one was open for 5% of the time, Pallas kernels for 0%

profile of v9, /device:TPU:0, one launch (start us, length us, event | category | flops | bytes accessed | tf_op | source)
XLA Modules:
  0.0 88.5 jit_solution(10287801048593365900)
XLA Ops:
  0.0 11.3 %attend.1 = bf16[8,12,640]{2,1,0:T(8,128)(2,1)} custom-call(s32[1]{0:T(128)} %bitcast.5.seq_ref, s32[8,8]{1,0:T(8,128)} %table_hbm.1, s32[8]{0:T(128)} %len_hbm.1, bf16[4,8,1536]{2,1,0:T(8,128)(2,1)} %q_hbm.1, bf16[4,8,2,512]{3,2,1,0:T(2,128)(2,1)} %fresh_hbm.1, bf16[64,64,2,512]{3,2,1,0:T(2,128)(2,1)} %bitcast.28), custom_call_target="tpu_custom_call" | custom-call | tf_op jit(solution)/shard_map/attend/pallas_call | solution.py:231
  11.3 3.4 %all-to-all-start = ((bf16[8,12,640]{2,1,0:T(8,128)(2,1)}), bf16[8,12,640]{2,1,0:T(8,128)(2,1)S(1)}, u32[]{:S(2)}, u32[]{:S(2)}) async-start(bf16[8,12,640]{2,1,0:T(8,128)(2,1)} %attend.1), calls=%async_computation | async-start | bytes 327680 | tf_op jit(solution)/shard_map/all_to_all | solution.py:649
  14.7 4.8 %copy.16 = bf16[10,192,2,512]{3,1,2,0:T(8,128)(2,1)} copy(bf16[10,192,2,512]{3,2,1,0:T(2,128)(2,1)} %param.24) | data formatting | bytes 7864320 | tf_op jit(solution)/shard_map/optimization_barrier | solution.py:696
  19.6 2.7 %all-to-all-done.x_ref = bf16[8,12,640]{2,1,0:T(8,128)(2,1)S(1)} async-done(((bf16[8,12,640]{2,1,0:T(8,128)(2,1)}), bf16[8,12,640]{2,1,0:T(8,128)(2,1)S(1)}, u32[]{:S(2)}, u32[]{:S(2)}) %all-to-all-start) | async-done | bytes 122912 | tf_op jit(solution)/shard_map/all_to_all | solution.py:649
  22.8 3.7 %collective-permute-done.12 = bf16[4,1536]{1,0:T(4,128)(2,1)S(1)} collective-permute-done((bf16[4,1536]{1,0:T(4,128)(2,1)S(1)}, bf16[4,1536]{1,0:T(4,128)(2,1)S(1)}, u32[]{:S(2)}, u32[]{:S(2)}) %collective-permute-start.12) | collective-permute-done | bytes 12320 | tf_op jit(solution)/shard_map/ppermute | solution.py:657
  26.5 1.6 %collective-permute-start.14 = (bf16[2,4,1536]{2,1,0:T(4,128)(2,1)S(1)}, bf16[2,4,1536]{2,1,0:T(4,128)(2,1)S(1)}, u32[]{:S(2)}, u32[]{:S(2)}) collective-permute-start(bf16[2,4,1536]{2,1,0:T(4,128)(2,1)S(1)} %pad_maximum_fusion.2.refs_0_), channel_id=1, source_target_pairs={{0,16},{4,20},{8,24},{12,28},{16,0},{20,4},{24,8},{28,12},{1,17},{... | collective-permute-start | bytes 73736 | tf_op jit(solution)/shard_map/ppermute | solution.py:645
  28.1 2.2 %collective-permute-start.15 = (bf16[2,4,1536]{2,1,0:T(4,128)(2,1)S(1)}, bf16[2,4,1536]{2,1,0:T(4,128)(2,1)S(1)}, u32[]{:S(2)}, u32[]{:S(2)}) collective-permute-start(bf16[2,4,1536]{2,1,0:T(4,128)(2,1)S(1)} %pad_maximum_fusion.2.refs_0_), channel_id=1, source_target_pairs={{0,24},{4,28},{8,0},{12,4},{16,8},{20,12},{24,16},{28,20},{1,25},{... | collective-permute-start | bytes 73736 | tf_op jit(solution)/shard_map/ppermute | solution.py:645
  30.4 1.8 %collective-permute-done.13.refs_1_ = bf16[2,4,1536]{2,1,0:T(4,128)(2,1)S(1)} collective-permute-done((bf16[2,4,1536]{2,1,0:T(4,128)(2,1)S(1)}, bf16[2,4,1536]{2,1,0:T(4,128)(2,1)S(1)}, u32[]{:S(2)}, u32[]{:S(2)}) %collective-permute-start.13) | collective-permute-done | bytes 24608 | tf_op jit(solution)/shard_map/ppermute | solution.py:645
  32.2 0.9 %collective-permute-done.15.refs_3_ = bf16[2,4,1536]{2,1,0:T(4,128)(2,1)S(1)} collective-permute-done((bf16[2,4,1536]{2,1,0:T(4,128)(2,1)S(1)}, bf16[2,4,1536]{2,1,0:T(4,128)(2,1)S(1)}, u32[]{:S(2)}, u32[]{:S(2)}) %collective-permute-start.15) | collective-permute-done | bytes 24608 | tf_op jit(solution)/shard_map/ppermute | solution.py:645
  33.8 4.1 %collective-permute-start.17 = (bf16[32,256]{1,0:T(8,128)(2,1)S(1)}, bf16[32,256]{1,0:T(8,128)(2,1)S(1)}, u32[]{:S(2)}, u32[]{:S(2)}) collective-permute-start(bf16[32,256]{1,0:T(8,128)(2,1)S(1)} %get-tuple-element.102.refs_0_), channel_id=1, source_target_pairs={{0,2},{1,3},{2,0},{3,1},{4,6},{5,7},{6,4},{7,5},{8,10},{9,11},{10,... | collective-permute-start | bytes 49160 | tf_op jit(solution)/shard_map/ppermute | solution.py:645
  37.8 1.4 %collective-permute-start.18 = (bf16[32,256]{1,0:T(8,128)(2,1)S(1)}, bf16[32,256]{1,0:T(8,128)(2,1)S(1)}, u32[]{:S(2)}, u32[]{:S(2)}) collective-permute-start(bf16[32,256]{1,0:T(8,128)(2,1)S(1)} %get-tuple-element.102.refs_0_), channel_id=1, source_target_pairs={{0,3},{1,0},{2,1},{3,2},{4,7},{5,4},{6,5},{7,6},{8,11},{9,8},{10,9... | collective-permute-start | bytes 49160 | tf_op jit(solution)/shard_map/ppermute | solution.py:645
  39.5 1.1 %collective-permute-done.18.refs_3_ = bf16[32,256]{1,0:T(8,128)(2,1)S(1)} collective-permute-done((bf16[32,256]{1,0:T(8,128)(2,1)S(1)}, bf16[32,256]{1,0:T(8,128)(2,1)S(1)}, u32[]{:S(2)}, u32[]{:S(2)}) %collective-permute-start.18) | collective-permute-done | bytes 16416 | tf_op jit(solution)/shard_map/ppermute | solution.py:645
  40.7 4.2 %gate_up.3 = (bf16[368,128]{1,0:T(8,128)(2,1)S(1)}, bf16[368,128]{1,0:T(8,128)(2,1)S(1)}, bf16[368,128]{1,0:T(8,128)(2,1)S(1)}, bf16[368,128]{1,0:T(8,128)(2,1)S...) custom-call(s32[1]{0:T(128)} %bitcast.12.where_ref, ...), custom_call_target="tpu_custom_call" | custom-call | tf_op jit(solution)/shard_map/gate_up/pallas_call | solution.py:465
  44.9 0.9 collective-permute-start.19
  45.8 1.4 %collective-permute-start.20 = (bf16[368,128]{1,0:T(8,128)(2,1)S(1)}, bf16[368,128]{1,0:T(8,128)(2,1)S(1)}, u32[]{:S(2)}, u32[]{:S(2)}) collective-permute-start(bf16[368,128]{1,0:T(8,128)(2,1)S(1)} %get-tuple-element.109), channel_id=1, source_target_pairs={{0,8},{4,12},{8,16},{12,20},{16,24},{20,28},{24,0},{28,4},{1,9},{5... | collective-permute-start | bytes 282632 | tf_op jit(solution)/shard_map/ppermute | solution.py:645
  47.1 3.1 %collective-permute-start.21 = (bf16[368,128]{1,0:T(8,128)(2,1)S(1)}, bf16[368,128]{1,0:T(8,128)(2,1)S(1)}, u32[]{:S(2)}, u32[]{:S(2)}) collective-permute-start(bf16[368,128]{1,0:T(8,128)(2,1)S(1)} %get-tuple-element.110), channel_id=1, source_target_pairs={{0,12},{4,16},{8,20},{12,24},{16,28},{20,0},{24,4},{28,8},{1,13},{... | collective-permute-start | bytes 282632 | tf_op jit(solution)/shard_map/ppermute | solution.py:645
  50.2 2.1 %collective-permute-start.22 = (bf16[368,128]{1,0:T(8,128)(2,1)S(1)}, bf16[368,128]{1,0:T(8,128)(2,1)S(1)}, u32[]{:S(2)}, u32[]{:S(2)}) collective-permute-start(bf16[368,128]{1,0:T(8,128)(2,1)S(1)} %get-tuple-element.111), channel_id=1, source_target_pairs={{0,16},{4,20},{8,24},{12,28},{16,0},{20,4},{24,8},{28,12},{1,17},{... | collective-permute-start | bytes 282632 | tf_op jit(solution)/shard_map/ppermute | solution.py:645
  52.3 1.1 %collective-permute-start.23 = (bf16[368,128]{1,0:T(8,128)(2,1)S(1)}, bf16[368,128]{1,0:T(8,128)(2,1)S(1)}, u32[]{:S(2)}, u32[]{:S(2)}) collective-permute-start(bf16[368,128]{1,0:T(8,128)(2,1)S(1)} %get-tuple-element.112), channel_id=1, source_target_pairs={{0,20},{4,24},{8,28},{12,0},{16,4},{20,8},{24,12},{28,16},{1,21},{... | collective-permute-start | bytes 282632 | tf_op jit(solution)/shard_map/ppermute | solution.py:645
  53.4 1.3 %collective-permute-start.24 = (bf16[368,128]{1,0:T(8,128)(2,1)S(1)}, bf16[368,128]{1,0:T(8,128)(2,1)S(1)}, u32[]{:S(2)}, u32[]{:S(2)}) collective-permute-start(bf16[368,128]{1,0:T(8,128)(2,1)S(1)} %get-tuple-element.113), channel_id=1, source_target_pairs={{0,24},{4,28},{8,0},{12,4},{16,8},{20,12},{24,16},{28,20},{1,25},{... | collective-permute-start | bytes 282632 | tf_op jit(solution)/shard_map/ppermute | solution.py:645
  54.7 2.9 %collective-permute-start.25 = (bf16[368,128]{1,0:T(8,128)(2,1)S(1)}, bf16[368,128]{1,0:T(8,128)(2,1)S(1)}, u32[]{:S(2)}, u32[]{:S(2)}) collective-permute-start(bf16[368,128]{1,0:T(8,128)(2,1)S(1)} %get-tuple-element.114), channel_id=1, source_target_pairs={{0,28},{4,0},{8,4},{12,8},{16,12},{20,16},{24,20},{28,24},{1,29},{... | collective-permute-start | bytes 282632 | tf_op jit(solution)/shard_map/ppermute | solution.py:645
  57.6 3.3 %collective-permute-done.21.refs_3_ = bf16[368,128]{1,0:T(8,128)(2,1)S(1)} collective-permute-done((bf16[368,128]{1,0:T(8,128)(2,1)S(1)}, bf16[368,128]{1,0:T(8,128)(2,1)S(1)}, u32[]{:S(2)}, u32[]{:S(2)}) %collective-permute-start.21) | collective-permute-done | bytes 94240 | tf_op jit(solution)/shard_map/ppermute | solution.py:645
  61.0 1.9 %collective-permute-done.24.refs_6_ = bf16[368,128]{1,0:T(8,128)(2,1)S(1)} collective-permute-done((bf16[368,128]{1,0:T(8,128)(2,1)S(1)}, bf16[368,128]{1,0:T(8,128)(2,1)S(1)}, u32[]{:S(2)}, u32[]{:S(2)}) %collective-permute-start.24) | collective-permute-done | bytes 94240 | tf_op jit(solution)/shard_map/ppermute | solution.py:645
  63.2 3.7 %collective-permute-start.29 = (bf16[176,128]{1,0:T(8,128)(2,1)S(1)}, bf16[176,128]{1,0:T(8,128)(2,1)S(1)}, u32[]{:S(2)}, u32[]{:S(2)}) collective-permute-start(bf16[176,128]{1,0:T(8,128)(2,1)S(1)} %get-tuple-element.116.refs_0_), channel_id=1, source_target_pairs={{0,24},{4,28},{8,0},{12,4},{16,8},{20,12},{24,16},{28,20},{1,25},{... | collective-permute-start | bytes 135176 | tf_op jit(solution)/shard_map/ppermute | solution.py:645
  67.3 1.2 %collective-permute-start.27 = (bf16[176,128]{1,0:T(8,128)(2,1)S(1)}, bf16[176,128]{1,0:T(8,128)(2,1)S(1)}, u32[]{:S(2)}, u32[]{:S(2)}) collective-permute-start(bf16[176,128]{1,0:T(8,128)(2,1)S(1)} %get-tuple-element.116.refs_0_), channel_id=1, source_target_pairs={{0,8},{4,12},{8,16},{12,20},{16,24},{20,28},{24,0},{28,4},{1,9},{5... | collective-permute-start | bytes 135176 | tf_op jit(solution)/shard_map/ppermute | solution.py:645
  68.8 3.3 %collective-permute-done.28 = bf16[176,128]{1,0:T(8,128)(2,1)S(1)} collective-permute-done((bf16[176,128]{1,0:T(8,128)(2,1)S(1)}, bf16[176,128]{1,0:T(8,128)(2,1)S(1)}, u32[]{:S(2)}, u32[]{:S(2)}) %collective-permute-start.28) | collective-permute-done | bytes 45088 | tf_op jit(solution)/shard_map/ppermute | solution.py:645
  72.1 1.1 %collective-permute-done.27 = bf16[176,128]{1,0:T(8,128)(2,1)S(1)} collective-permute-done((bf16[176,128]{1,0:T(8,128)(2,1)S(1)}, bf16[176,128]{1,0:T(8,128)(2,1)S(1)}, u32[]{:S(2)}, u32[]{:S(2)}) %collective-permute-start.27) | collective-permute-done | bytes 45088 | tf_op jit(solution)/shard_map/ppermute | solution.py:645
  73.2 3.1 %collective-permute-start.30 = (bf16[3,176,128]{2,1,0:T(8,128)(2,1)S(1)}, bf16[3,176,128]{2,1,0:T(8,128)(2,1)S(1)}, u32[]{:S(2)}, u32[]{:S(2)}) collective-permute-start(bf16[3,176,128]{2,1,0:T(8,128)(2,1)S(1)} %pad_maximum_fusion.1.refs_2_), channel_id=1, source_target_pairs={{0,4},{4,0},{8,12},{12,8},{16,20},{20,16},{24,28},{28,24},{1,5},{5... | collective-permute-start | bytes 405512 | tf_op jit(solution)/shard_map/ppermute | solution.py:657
  77.0 3.4 %collective-permute-done.26.refs_1_ = bf16[176,128]{1,0:T(8,128)(2,1)S(1)} collective-permute-done((bf16[176,128]{1,0:T(8,128)(2,1)S(1)}, bf16[176,128]{1,0:T(8,128)(2,1)S(1)}, u32[]{:S(2)}, u32[]{:S(2)}) %collective-permute-start.26) | collective-permute-done | bytes 45088 | tf_op jit(solution)/shard_map/ppermute | solution.py:657
  80.4 2.1 %down.3 = (f32[32,256]{1,0:T(8,128)S(1)}, f32[32,256]{1,0:T(8,128)S(1)}, f32[32,256]{1,0:T(8,128)S(1)}, f32[32,256]{1,0:T(8,128)S(1)}) custom-call(s32[16]{0:T(128)S(1)} %get-tuple-element.104.first_ref, s32[1]{0:T(128)} %bitcast.5.seq_ref, f32[16,128]{1,0:T(8,128)S(1)} %get-tuple-element.105.range_ref, bf16[128,352]{1,0:T(8,128)(2,1)S(1)} %get-tuple-element.106.pick_ref, ...), custom_call_target="tpu_custom_call" | custom-call | tf_op jit(solution)/shard_map/down/pallas_call | solution.py:593
  82.6 1.8 %collective-permute-start.32 = (f32[32,256]{1,0:T(8,128)S(1)}, f32[32,256]{1,0:T(8,128)S(1)}, u32[]{:S(2)}, u32[]{:S(2)}) collective-permute-start(f32[32,256]{1,0:T(8,128)S(1)} %get-tuple-element.123), channel_id=1, source_target_pairs={{0,2},{1,3},{2,0},{3,1},{4,6},{5,7},{6,4},{7,5},{8,10},{9,11},{10,... | collective-permute-start | bytes 98312 | tf_op jit(solution)/shard_map/ppermute | solution.py:645
  84.6 2.2 %collective-permute-done.32.refs_2_ = f32[32,256]{1,0:T(8,128)S(1)} collective-permute-done((f32[32,256]{1,0:T(8,128)S(1)}, f32[32,256]{1,0:T(8,128)S(1)}, u32[]{:S(2)}, u32[]{:S(2)}) %collective-permute-start.32) | collective-permute-done | bytes 32800 | tf_op jit(solution)/shard_map/ppermute | solution.py:645
  86.8 1.0 %collective-permute-done.33.refs_3_ = f32[32,256]{1,0:T(8,128)S(1)} collective-permute-done((f32[32,256]{1,0:T(8,128)S(1)}, f32[32,256]{1,0:T(8,128)S(1)}, u32[]{:S(2)}, u32[]{:S(2)}) %collective-permute-start.33) | collective-permute-done | bytes 32800 | tf_op jit(solution)/shard_map/ppermute | solution.py:645
  (37 shorter events, 3.8 us)
Async XLA Ops:
  11.3 11.0 %all-to-all-start = ((bf16[8,12,640]{2,1,0:T(8,128)(2,1)}), bf16[8,12,640]{2,1,0:T(8,128)(2,1)S(1)}, u32[]{:S(2)}, u32[]{:S(2)}) async-start(bf16[8,12,640]{2,1,0:T(8,128)(2,1)} %attend.1), calls=%async_computation | async-start | bytes 327680 | tf_op jit(solution)/shard_map/all_to_all | solution.py:649
  14.7 18.4 %copy-start = (bf16[1536,192]{0,1:T(8,128)(2,1)S(1)}, bf16[1536,192]{0,1:T(8,128)(2,1)}, u32[]{:S(2)}) copy-start(bf16[1536,192]{0,1:T(8,128)(2,1)} %param.21) | copy-start | bytes 1769476
  14.7 18.4 %copy-start.1 = (bf16[4,8,192]{2,1,0:T(8,128)(2,1)S(1)}, bf16[4,8,192]{2,1,0:T(8,128)(2,1)}, u32[]{:S(2)}) copy-start(bf16[4,8,192]{2,1,0:T(8,128)(2,1)} %residual_ref.1) | copy-start | bytes 36868
  14.7 18.4 %copy-start.2 = (s32[4,8,8]{2,1,0:T(8,128)S(1)}, s32[4,8,8]{2,1,0:T(8,128)}, u32[]{:S(2)}) copy-start(s32[4,8,8]{2,1,0:T(8,128)} %routes_ref.1) | copy-start | bytes 3076
  14.7 18.4 %copy-start.3 = (f32[192]{0:T(256)S(1)}, f32[192]{0:T(256)}, u32[]{:S(2)}) copy-start(f32[192]{0:T(256)} %param.22) | copy-start | bytes 2308
  14.7 25.9 %copy-start.5 = (bf16[192,40]{0,1:T(8,128)(2,1)S(1)}, bf16[192,40]{0,1:T(8,128)(2,1)}, u32[]{:S(2)}) copy-start(bf16[192,40]{0,1:T(8,128)(2,1)} %param.23) | copy-start | bytes 46084
  19.6 60.8 %copy-start.4 = (bf16[10,192,512]{2,1,0:T(8,128)(2,1)S(1)}, bf16[10,192,512]{2,1,0:T(8,128)(2,1)}, u32[]{:S(2)}) copy-start(bf16[10,192,512]{2,1,0:T(8,128)(2,1)} %w_ref.1) | copy-start | bytes 5898244
  22.8 3.7 %collective-permute-start.12 = (bf16[4,1536]{1,0:T(4,128)(2,1)S(1)}, bf16[4,1536]{1,0:T(4,128)(2,1)S(1)}, u32[]{:S(2)}, u32[]{:S(2)}) collective-permute-start(bf16[4,1536]{1,0:T(4,128)(2,1)S(1)} %join.1), channel_id=1, source_target_pairs={{0,4},{4,0},{8,12},{12,8},{16,20},{20,16},{24,28},{28,24},{1,5},{5... | collective-permute-start | bytes 36872 | tf_op jit(solution)/shard_map/ppermute | solution.py:657
  26.5 5.7 %collective-permute-start.13 = (bf16[2,4,1536]{2,1,0:T(4,128)(2,1)S(1)}, bf16[2,4,1536]{2,1,0:T(4,128)(2,1)S(1)}, u32[]{:S(2)}, u32[]{:S(2)}) collective-permute-start(bf16[2,4,1536]{2,1,0:T(4,128)(2,1)S(1)} %pad_maximum_fusion.2.refs_0_), channel_id=1, source_target_pairs={{0,8},{4,12},{8,16},{12,20},{16,24},{20,28},{24,0},{28,4},{1,9},{5... | collective-permute-start | bytes 73736 | tf_op jit(solution)/shard_map/ppermute | solution.py:645
  26.5 5.6 %collective-permute-start.14 = (bf16[2,4,1536]{2,1,0:T(4,128)(2,1)S(1)}, bf16[2,4,1536]{2,1,0:T(4,128)(2,1)S(1)}, u32[]{:S(2)}, u32[]{:S(2)}) collective-permute-start(bf16[2,4,1536]{2,1,0:T(4,128)(2,1)S(1)} %pad_maximum_fusion.2.refs_0_), channel_id=1, source_target_pairs={{0,16},{4,20},{8,24},{12,28},{16,0},{20,4},{24,8},{28,12},{1,17},{... | collective-permute-start | bytes 73736 | tf_op jit(solution)/shard_map/ppermute | solution.py:645
  28.1 5.0 %collective-permute-start.15 = (bf16[2,4,1536]{2,1,0:T(4,128)(2,1)S(1)}, bf16[2,4,1536]{2,1,0:T(4,128)(2,1)S(1)}, u32[]{:S(2)}, u32[]{:S(2)}) collective-permute-start(bf16[2,4,1536]{2,1,0:T(4,128)(2,1)S(1)} %pad_maximum_fusion.2.refs_0_), channel_id=1, source_target_pairs={{0,24},{4,28},{8,0},{12,4},{16,8},{20,12},{24,16},{28,20},{1,25},{... | collective-permute-start | bytes 73736 | tf_op jit(solution)/shard_map/ppermute | solution.py:645
  33.6 5.6 %collective-permute-start.16 = (bf16[32,256]{1,0:T(8,128)(2,1)S(1)}, bf16[32,256]{1,0:T(8,128)(2,1)S(1)}, u32[]{:S(2)}, u32[]{:S(2)}) collective-permute-start(bf16[32,256]{1,0:T(8,128)(2,1)S(1)} %get-tuple-element.102.refs_0_), channel_id=1, source_target_pairs={{0,1},{1,2},{2,3},{3,0},{4,5},{5,6},{6,7},{7,4},{8,9},{9,10},{10,1... | collective-permute-start | bytes 49160 | tf_op jit(solution)/shard_map/ppermute | solution.py:645
  33.8 5.8 %collective-permute-start.17 = (bf16[32,256]{1,0:T(8,128)(2,1)S(1)}, bf16[32,256]{1,0:T(8,128)(2,1)S(1)}, u32[]{:S(2)}, u32[]{:S(2)}) collective-permute-start(bf16[32,256]{1,0:T(8,128)(2,1)S(1)} %get-tuple-element.102.refs_0_), channel_id=1, source_target_pairs={{0,2},{1,3},{2,0},{3,1},{4,6},{5,7},{6,4},{7,5},{8,10},{9,11},{10,... | collective-permute-start | bytes 49160 | tf_op jit(solution)/shard_map/ppermute | solution.py:645
  37.8 2.8 %collective-permute-start.18 = (bf16[32,256]{1,0:T(8,128)(2,1)S(1)}, bf16[32,256]{1,0:T(8,128)(2,1)S(1)}, u32[]{:S(2)}, u32[]{:S(2)}) collective-permute-start(bf16[32,256]{1,0:T(8,128)(2,1)S(1)} %get-tuple-element.102.refs_0_), channel_id=1, source_target_pairs={{0,3},{1,0},{2,1},{3,2},{4,7},{5,4},{6,5},{7,6},{8,11},{9,8},{10,9... | collective-permute-start | bytes 49160 | tf_op jit(solution)/shard_map/ppermute | solution.py:645
  44.9 8.5 %collective-permute-start.19 = (bf16[368,128]{1,0:T(8,128)(2,1)S(1)}, bf16[368,128]{1,0:T(8,128)(2,1)S(1)}, u32[]{:S(2)}, u32[]{:S(2)}) collective-permute-start(bf16[368,128]{1,0:T(8,128)(2,1)S(1)} %get-tuple-element.108), channel_id=1, source_target_pairs={{0,4},{4,8},{8,12},{12,16},{16,20},{20,24},{24,28},{28,0},{1,5},{5... | collective-permute-start | bytes 282632 | tf_op jit(solution)/shard_map/ppermute | solution.py:645
  45.8 8.9 %collective-permute-start.20 = (bf16[368,128]{1,0:T(8,128)(2,1)S(1)}, bf16[368,128]{1,0:T(8,128)(2,1)S(1)}, u32[]{:S(2)}, u32[]{:S(2)}) collective-permute-start(bf16[368,128]{1,0:T(8,128)(2,1)S(1)} %get-tuple-element.109), channel_id=1, source_target_pairs={{0,8},{4,12},{8,16},{12,20},{16,24},{20,28},{24,0},{28,4},{1,9},{5... | collective-permute-start | bytes 282632 | tf_op jit(solution)/shard_map/ppermute | solution.py:645
  47.1 13.8 %collective-permute-start.21 = (bf16[368,128]{1,0:T(8,128)(2,1)S(1)}, bf16[368,128]{1,0:T(8,128)(2,1)S(1)}, u32[]{:S(2)}, u32[]{:S(2)}) collective-permute-start(bf16[368,128]{1,0:T(8,128)(2,1)S(1)} %get-tuple-element.110), channel_id=1, source_target_pairs={{0,12},{4,16},{8,20},{12,24},{16,28},{20,0},{24,4},{28,8},{1,13},{... | collective-permute-start | bytes 282632 | tf_op jit(solution)/shard_map/ppermute | solution.py:645
  50.2 10.7 %collective-permute-start.22 = (bf16[368,128]{1,0:T(8,128)(2,1)S(1)}, bf16[368,128]{1,0:T(8,128)(2,1)S(1)}, u32[]{:S(2)}, u32[]{:S(2)}) collective-permute-start(bf16[368,128]{1,0:T(8,128)(2,1)S(1)} %get-tuple-element.111), channel_id=1, source_target_pairs={{0,16},{4,20},{8,24},{12,28},{16,0},{20,4},{24,8},{28,12},{1,17},{... | collective-permute-start | bytes 282632 | tf_op jit(solution)/shard_map/ppermute | solution.py:645
  52.3 8.7 %collective-permute-start.23 = (bf16[368,128]{1,0:T(8,128)(2,1)S(1)}, bf16[368,128]{1,0:T(8,128)(2,1)S(1)}, u32[]{:S(2)}, u32[]{:S(2)}) collective-permute-start(bf16[368,128]{1,0:T(8,128)(2,1)S(1)} %get-tuple-element.112), channel_id=1, source_target_pairs={{0,20},{4,24},{8,28},{12,0},{16,4},{20,8},{24,12},{28,16},{1,21},{... | collective-permute-start | bytes 282632 | tf_op jit(solution)/shard_map/ppermute | solution.py:645
  53.4 9.5 %collective-permute-start.24 = (bf16[368,128]{1,0:T(8,128)(2,1)S(1)}, bf16[368,128]{1,0:T(8,128)(2,1)S(1)}, u32[]{:S(2)}, u32[]{:S(2)}) collective-permute-start(bf16[368,128]{1,0:T(8,128)(2,1)S(1)} %get-tuple-element.113), channel_id=1, source_target_pairs={{0,24},{4,28},{8,0},{12,4},{16,8},{20,12},{24,16},{28,20},{1,25},{... | collective-permute-start | bytes 282632 | tf_op jit(solution)/shard_map/ppermute | solution.py:645
  54.7 8.2 %collective-permute-start.25 = (bf16[368,128]{1,0:T(8,128)(2,1)S(1)}, bf16[368,128]{1,0:T(8,128)(2,1)S(1)}, u32[]{:S(2)}, u32[]{:S(2)}) collective-permute-start(bf16[368,128]{1,0:T(8,128)(2,1)S(1)} %get-tuple-element.114), channel_id=1, source_target_pairs={{0,28},{4,0},{8,4},{12,8},{16,12},{20,16},{24,20},{28,24},{1,29},{... | collective-permute-start | bytes 282632 | tf_op jit(solution)/shard_map/ppermute | solution.py:645
  63.2 5.6 %collective-permute-start.29 = (bf16[176,128]{1,0:T(8,128)(2,1)S(1)}, bf16[176,128]{1,0:T(8,128)(2,1)S(1)}, u32[]{:S(2)}, u32[]{:S(2)}) collective-permute-start(bf16[176,128]{1,0:T(8,128)(2,1)S(1)} %get-tuple-element.116.refs_0_), channel_id=1, source_target_pairs={{0,24},{4,28},{8,0},{12,4},{16,8},{20,12},{24,16},{28,20},{1,25},{... | collective-permute-start | bytes 135176 | tf_op jit(solution)/shard_map/ppermute | solution.py:645
  66.9 5.2 %collective-permute-start.28 = (bf16[176,128]{1,0:T(8,128)(2,1)S(1)}, bf16[176,128]{1,0:T(8,128)(2,1)S(1)}, u32[]{:S(2)}, u32[]{:S(2)}) collective-permute-start(bf16[176,128]{1,0:T(8,128)(2,1)S(1)} %get-tuple-element.116.refs_0_), channel_id=1, source_target_pairs={{0,16},{4,20},{8,24},{12,28},{16,0},{20,4},{24,8},{28,12},{1,17},{... | collective-permute-start | bytes 135176 | tf_op jit(solution)/shard_map/ppermute | solution.py:645
  67.3 5.8 %collective-permute-start.27 = (bf16[176,128]{1,0:T(8,128)(2,1)S(1)}, bf16[176,128]{1,0:T(8,128)(2,1)S(1)}, u32[]{:S(2)}, u32[]{:S(2)}) collective-permute-start(bf16[176,128]{1,0:T(8,128)(2,1)S(1)} %get-tuple-element.116.refs_0_), channel_id=1, source_target_pairs={{0,8},{4,12},{8,16},{12,20},{16,24},{20,28},{24,0},{28,4},{1,9},{5... | collective-permute-start | bytes 135176 | tf_op jit(solution)/shard_map/ppermute | solution.py:645
  73.2 7.2 %collective-permute-start.30 = (bf16[3,176,128]{2,1,0:T(8,128)(2,1)S(1)}, bf16[3,176,128]{2,1,0:T(8,128)(2,1)S(1)}, u32[]{:S(2)}, u32[]{:S(2)}) collective-permute-start(bf16[3,176,128]{2,1,0:T(8,128)(2,1)S(1)} %pad_maximum_fusion.1.refs_2_), channel_id=1, source_target_pairs={{0,4},{4,0},{8,12},{12,8},{16,20},{20,16},{24,28},{28,24},{1,5},{5... | collective-permute-start | bytes 405512 | tf_op jit(solution)/shard_map/ppermute | solution.py:657
  76.4 4.0 %collective-permute-start.26 = (bf16[176,128]{1,0:T(8,128)(2,1)S(1)}, bf16[176,128]{1,0:T(8,128)(2,1)S(1)}, u32[]{:S(2)}, u32[]{:S(2)}) collective-permute-start(bf16[176,128]{1,0:T(8,128)(2,1)S(1)} %get-tuple-element.116.refs_0_), channel_id=1, source_target_pairs={{0,4},{4,0},{8,12},{12,8},{16,20},{20,16},{24,28},{28,24},{1,5},{5... | collective-permute-start | bytes 135176 | tf_op jit(solution)/shard_map/ppermute | solution.py:657
  82.6 2.0 %collective-permute-start.31 = (f32[32,256]{1,0:T(8,128)S(1)}, f32[32,256]{1,0:T(8,128)S(1)}, u32[]{:S(2)}, u32[]{:S(2)}) collective-permute-start(f32[32,256]{1,0:T(8,128)S(1)} %get-tuple-element.122), channel_id=1, source_target_pairs={{0,3},{1,0},{2,1},{3,2},{4,7},{5,4},{6,5},{7,6},{8,11},{9,8},{10,9... | collective-permute-start | bytes 98312 | tf_op jit(solution)/shard_map/ppermute | solution.py:645
  82.6 4.2 %collective-permute-start.32 = (f32[32,256]{1,0:T(8,128)S(1)}, f32[32,256]{1,0:T(8,128)S(1)}, u32[]{:S(2)}, u32[]{:S(2)}) collective-permute-start(f32[32,256]{1,0:T(8,128)S(1)} %get-tuple-element.123), channel_id=1, source_target_pairs={{0,2},{1,3},{2,0},{3,1},{4,6},{5,7},{6,4},{7,5},{8,10},{9,11},{10,... | collective-permute-start | bytes 98312 | tf_op jit(solution)/shard_map/ppermute | solution.py:645
  84.4 3.3 %collective-permute-start.33 = (f32[32,256]{1,0:T(8,128)S(1)}, f32[32,256]{1,0:T(8,128)S(1)}, u32[]{:S(2)}, u32[]{:S(2)}) collective-permute-start(f32[32,256]{1,0:T(8,128)S(1)} %get-tuple-element.124), channel_id=1, source_target_pairs={{0,1},{1,2},{2,3},{3,0},{4,5},{5,6},{6,7},{7,4},{8,9},{9,10},{10,1... | collective-permute-start | bytes 98312 | tf_op jit(solution)/shard_map/ppermute | solution.py:645

commit v10 on v8

--- a/solution.py
+++ b/solution.py
@@ -518,17 +518,16 @@
     )(*parts)
 
 
-def down_kernel(features, local, first_ref, seq_ref, range_ref, pick_ref, w_ref, logit_ref, *refs):
-    (own_ref, beside_ref, behind_ref, other_ref), refs = refs[:4], refs[4:]
-    out_refs, (x_ref, row_ref, made_ref) = refs[:-3], refs[-3:]
+def down_kernel(features, local, pairs, first_ref, seq_ref, range_ref, pick_ref, w_ref, logit_ref, *refs):
+    pair_refs, out_refs, (x_ref, row_ref, made_ref) = refs[:pairs], refs[pairs:-3], refs[-3:]
     total, rows = pick_ref.shape
     width = w_ref.shape[2]
     window = total // 2 + 16
     devices, half, _ = x_ref.shape
-    for k in range(devices // 2):
+    for k, pair_ref in enumerate(pair_refs):
         source = lax.rem(seq_ref[0] + devices - 2 * k, devices)
-        x_ref[source] = behind_ref[k - 1] if k else own_ref[...]
-        x_ref[source + 1 - lax.rem(source, 2) * 2] = other_ref[k - 1] if k else beside_ref[...]
+        x_ref[source] = pair_ref[0]
+        x_ref[source + 1 - lax.rem(source, 2) * 2] = pair_ref[1]
     share = 2 * half
     low = iota((half, LANES), 1) < PIECE_WIDTH
     for b in range(0, devices, 2):
@@ -588,11 +587,11 @@
     wide = side_place(features, 2)[0] + LANES
     smem, vmem = pl.BlockSpec(memory_space=pltpu.SMEM), pl.BlockSpec(memory_space=pltpu.VMEM)
     return pl.pallas_call(
-        functools.partial(down_kernel, features, local),
+        functools.partial(down_kernel, features, local, len(made)),
         in_specs=[smem] * 2 + [vmem] * (4 + len(made)),
         out_shape=(jax.ShapeDtypeStruct((total // exp_count, wide), F32),) * exp_count,
         scratch_shapes=[
-            pltpu.VMEM((2 * made[2].shape[0] + 2,) + made[0].shape, BF16),
+            pltpu.VMEM((2 * len(made),) + made[0].shape[1:], BF16),
             pltpu.VMEM((rows, width), BF16),
             pltpu.VMEM((rows, wide), F32),
         ],
@@ -650,13 +649,11 @@
     return [parts[0]] + [send(part, axis, direction * k) for k, part in enumerate(parts) if k]
 
 
-def neighbour(x, axis):
-    return lax.ppermute(x, axis, [(i, i ^ 1) for i in range(lax.axis_size(axis))])
-
-
 def pair_gather(block, axis):
-    pair = jnp.stack([block, neighbour(block, axis)])
-    return [pair] + [send(pair, axis, k) for k in range(2, lax.axis_size(axis), 2)]
+    count = lax.axis_size(axis)
+    beside = lax.ppermute(block, axis, [(i, i ^ 1) for i in range(count)])
+    pair = jnp.stack([block, beside])
+    return [pair] + [send(pair, axis, k) for k in range(2, count, 2)]
 
 
 def gather(block, axis):
@@ -707,8 +704,7 @@
         )
         made, logits = inner(exchange(partial, "seq", 1))
         logits = logits[None] if pieces == 1 else lax.all_gather(logits, "seq")[::PIECES]
-        behind = jnp.stack([send(made, "seq", k) for k in range(2, seq_count, 2)])
-        made = [made, neighbour(made, "seq"), behind, neighbour(behind, "seq")]
+        made = pair_gather(made, "seq")
         return down(first, seq_index, ranges, pick, made, logits, w_down, exp_count), most
 
     made, most = one_round(0)

time: 86.5 us -> 84.6 us (0.978)
  starting transfers between devices: 37.6 us -> 35.7 us
    ppermute x19, starting transfers between devices: 30 us -> 28.4 us  [send(): lax.ppermute(x, axis, [(i, (i + distance) % count) for i in range(count)])]
    all_to_all x1, waiting for transfers between devices: 2.62 us -> 3.61 us  [swap(): return lax.all_to_all(x, axis, split_axis=0, concat_axis=0, tiled=True)]
    ppermute x3 -> x2, waiting for transfers between devices: 6.15 us -> 5.63 us  [pair_gather(): beside = lax.ppermute(block, axis, [(i, i ^ 1) for i in range(count)])]
    ppermute x3 -> x2, starting transfers between devices: 4.22 us -> 3.93 us  [pair_gather(): beside = lax.ppermute(block, axis, [(i, i ^ 1) for i in range(count)])]
  transfers between devices with their start and end apart: 23 -> 22, of which waited for: 15 -> 16; matrix products, arithmetic and copies ran while one was open for 6% -> 6% of each run, Pallas kernels for 0% -> 0%
where the time goes in v10:
time: 84.6 us; the launch traced here: 84.1 us
  starting transfers between devices  35.7 us (42%)
  waiting for transfers between devices  24 us (28%)
  Pallas kernels  18.5 us (22%)
  local copies, waits for them, and re-layouts  4.88 us (6%)
    ppermute x19, starting transfers between devices, send(): lax.ppermute(x, axis, [(i, (i + distance) % count) for i in range(count)])  28.4 us
    ppermute x19, waiting for transfers between devices, send(): lax.ppermute(x, axis, [(i, (i + distance) % count) for i in range(count)])  14.8 us
    pallas_call x1, Pallas kernels, attend(): pl.pallas_call(functools.partial(attend_kernel, classes), in_specs=[smem]...  10.1 us
    ppermute x2, waiting for transfers between devices, pair_gather(): beside = lax.ppermute(block, axis, [(i, i ^ 1) for i in range(count)])  5.63 us
    optimization_barrier x1, local copies, waits for them, and re-layouts, local(): w_gate_up, shares = lax.optimization_barrier((w_gate_up, shares))  4.84 us
    pallas_call x1, Pallas kernels, gate_up(): pl.pallas_call(functools.partial(gate_up_kernel, features, local, turn, s...  4.26 us
    ppermute x2, starting transfers between devices, pair_gather(): beside = lax.ppermute(block, axis, [(i, i ^ 1) for i in range(count)])  3.93 us
    all_to_all x1, waiting for transfers between devices, swap(): return lax.all_to_all(x, axis, split_axis=0, concat_axis=0, tiled=True)  3.61 us
  transfers between devices with their start and end apart: 22, of which 16 were waited for; matrix products, arithmetic and copies ran while one was open for 6% of the time, Pallas kernels for 0%

profile of v10, /device:TPU:0, one launch (start us, length us, event | category | flops | bytes accessed | tf_op | source)
XLA Modules:
  0.0 84.1 jit_solution(5988303869765626698)
XLA Ops:
  0.0 10.1 %attend.1 = bf16[8,12,640]{2,1,0:T(8,128)(2,1)} custom-call(s32[1]{0:T(128)} %bitcast.4.seq_ref, s32[8,8]{1,0:T(8,128)} %table_hbm.1, s32[8]{0:T(128)} %len_hbm.1, bf16[4,8,1536]{2,1,0:T(8,128)(2,1)} %q_hbm.1, bf16[4,8,2,512]{3,2,1,0:T(2,128)(2,1)} %fresh_hbm.1, bf16[64,64,2,512]{3,2,1,0:T(2,128)(2,1)} %bitcast.28), custom_call_target="tpu_custom_call" | custom-call | tf_op jit(solution)/shard_map/attend/pallas_call | solution.py:228
  10.1 3.4 %all-to-all-start = ((bf16[8,12,640]{2,1,0:T(8,128)(2,1)}), bf16[8,12,640]{2,1,0:T(8,128)(2,1)S(1)}, u32[]{:S(2)}, u32[]{:S(2)}) async-start(bf16[8,12,640]{2,1,0:T(8,128)(2,1)} %attend.1), calls=%async_computation | async-start | bytes 327680 | tf_op jit(solution)/shard_map/all_to_all | solution.py:645
  13.5 4.8 %copy.16 = bf16[10,192,2,512]{3,1,2,0:T(8,128)(2,1)} copy(bf16[10,192,2,512]{3,2,1,0:T(2,128)(2,1)} %param.24) | data formatting | bytes 7864320 | tf_op jit(solution)/shard_map/optimization_barrier | solution.py:690
  18.4 3.6 %all-to-all-done.x_ref = bf16[8,12,640]{2,1,0:T(8,128)(2,1)S(1)} async-done(((bf16[8,12,640]{2,1,0:T(8,128)(2,1)}), bf16[8,12,640]{2,1,0:T(8,128)(2,1)S(1)}, u32[]{:S(2)}, u32[]{:S(2)}) %all-to-all-start) | async-done | bytes 122912 | tf_op jit(solution)/shard_map/all_to_all | solution.py:645
  22.5 3.6 %collective-permute-done.11 = bf16[4,1536]{1,0:T(4,128)(2,1)S(1)} collective-permute-done((bf16[4,1536]{1,0:T(4,128)(2,1)S(1)}, bf16[4,1536]{1,0:T(4,128)(2,1)S(1)}, u32[]{:S(2)}, u32[]{:S(2)}) %collective-permute-start.11) | collective-permute-done | bytes 12320 | tf_op jit(solution)/shard_map/ppermute | solution.py:654
  26.3 1.1 %collective-permute-start.13 = (bf16[2,4,1536]{2,1,0:T(4,128)(2,1)S(1)}, bf16[2,4,1536]{2,1,0:T(4,128)(2,1)S(1)}, u32[]{:S(2)}, u32[]{:S(2)}) collective-permute-start(bf16[2,4,1536]{2,1,0:T(4,128)(2,1)S(1)} %pad_maximum_fusion.2.refs_0_), channel_id=1, source_target_pairs={{0,16},{4,20},{8,24},{12,28},{16,0},{20,4},{24,8},{28,12},{1,17},{... | collective-permute-start | bytes 73736 | tf_op jit(solution)/shard_map/ppermute | solution.py:641
  27.4 2.6 %collective-permute-start.14 = (bf16[2,4,1536]{2,1,0:T(4,128)(2,1)S(1)}, bf16[2,4,1536]{2,1,0:T(4,128)(2,1)S(1)}, u32[]{:S(2)}, u32[]{:S(2)}) collective-permute-start(bf16[2,4,1536]{2,1,0:T(4,128)(2,1)S(1)} %pad_maximum_fusion.2.refs_0_), channel_id=1, source_target_pairs={{0,24},{4,28},{8,0},{12,4},{16,8},{20,12},{24,16},{28,20},{1,25},{... | collective-permute-start | bytes 73736 | tf_op jit(solution)/shard_map/ppermute | solution.py:641
  30.0 1.8 %collective-permute-done.12.refs_1_ = bf16[2,4,1536]{2,1,0:T(4,128)(2,1)S(1)} collective-permute-done((bf16[2,4,1536]{2,1,0:T(4,128)(2,1)S(1)}, bf16[2,4,1536]{2,1,0:T(4,128)(2,1)S(1)}, u32[]{:S(2)}, u32[]{:S(2)}) %collective-permute-start.12) | collective-permute-done | bytes 24608 | tf_op jit(solution)/shard_map/ppermute | solution.py:641
  31.8 0.6 collective-permute-done.14.refs_3_
  33.0 2.2 %collective-permute-start.16 = (bf16[32,256]{1,0:T(8,128)(2,1)S(1)}, bf16[32,256]{1,0:T(8,128)(2,1)S(1)}, u32[]{:S(2)}, u32[]{:S(2)}) collective-permute-start(bf16[32,256]{1,0:T(8,128)(2,1)S(1)} %get-tuple-element.102.refs_0_), channel_id=1, source_target_pairs={{0,2},{1,3},{2,0},{3,1},{4,6},{5,7},{6,4},{7,5},{8,10},{9,11},{10,... | collective-permute-start | bytes 49160 | tf_op jit(solution)/shard_map/ppermute | solution.py:641
  35.2 1.4 %collective-permute-start.17 = (bf16[32,256]{1,0:T(8,128)(2,1)S(1)}, bf16[32,256]{1,0:T(8,128)(2,1)S(1)}, u32[]{:S(2)}, u32[]{:S(2)}) collective-permute-start(bf16[32,256]{1,0:T(8,128)(2,1)S(1)} %get-tuple-element.102.refs_0_), channel_id=1, source_target_pairs={{0,3},{1,0},{2,1},{3,2},{4,7},{5,4},{6,5},{7,6},{8,11},{9,8},{10,9... | collective-permute-start | bytes 49160 | tf_op jit(solution)/shard_map/ppermute | solution.py:641
  36.9 1.1 %collective-permute-done.17.refs_3_ = bf16[32,256]{1,0:T(8,128)(2,1)S(1)} collective-permute-done((bf16[32,256]{1,0:T(8,128)(2,1)S(1)}, bf16[32,256]{1,0:T(8,128)(2,1)S(1)}, u32[]{:S(2)}, u32[]{:S(2)}) %collective-permute-start.17) | collective-permute-done | bytes 16416 | tf_op jit(solution)/shard_map/ppermute | solution.py:641
  38.0 4.3 %gate_up.3 = (bf16[368,128]{1,0:T(8,128)(2,1)S(1)}, bf16[368,128]{1,0:T(8,128)(2,1)S(1)}, bf16[368,128]{1,0:T(8,128)(2,1)S(1)}, bf16[368,128]{1,0:T(8,128)(2,1)S...) custom-call(s32[1]{0:T(128)} %bitcast.11.where_ref, ...), custom_call_target="tpu_custom_call" | custom-call | tf_op jit(solution)/shard_map/gate_up/pallas_call | solution.py:462
  42.9 1.8 %collective-permute-start.19 = (bf16[368,128]{1,0:T(8,128)(2,1)S(1)}, bf16[368,128]{1,0:T(8,128)(2,1)S(1)}, u32[]{:S(2)}, u32[]{:S(2)}) collective-permute-start(bf16[368,128]{1,0:T(8,128)(2,1)S(1)} %get-tuple-element.109), channel_id=1, source_target_pairs={{0,8},{4,12},{8,16},{12,20},{16,24},{20,28},{24,0},{28,4},{1,9},{5... | collective-permute-start | bytes 282632 | tf_op jit(solution)/shard_map/ppermute | solution.py:641
  44.7 3.0 %collective-permute-start.20 = (bf16[368,128]{1,0:T(8,128)(2,1)S(1)}, bf16[368,128]{1,0:T(8,128)(2,1)S(1)}, u32[]{:S(2)}, u32[]{:S(2)}) collective-permute-start(bf16[368,128]{1,0:T(8,128)(2,1)S(1)} %get-tuple-element.110), channel_id=1, source_target_pairs={{0,12},{4,16},{8,20},{12,24},{16,28},{20,0},{24,4},{28,8},{1,13},{... | collective-permute-start | bytes 282632 | tf_op jit(solution)/shard_map/ppermute | solution.py:641
  47.6 2.0 %collective-permute-start.21 = (bf16[368,128]{1,0:T(8,128)(2,1)S(1)}, bf16[368,128]{1,0:T(8,128)(2,1)S(1)}, u32[]{:S(2)}, u32[]{:S(2)}) collective-permute-start(bf16[368,128]{1,0:T(8,128)(2,1)S(1)} %get-tuple-element.111), channel_id=1, source_target_pairs={{0,16},{4,20},{8,24},{12,28},{16,0},{20,4},{24,8},{28,12},{1,17},{... | collective-permute-start | bytes 282632 | tf_op jit(solution)/shard_map/ppermute | solution.py:641
  49.7 0.7 collective-permute-start.22
  50.4 1.7 %collective-permute-start.23 = (bf16[368,128]{1,0:T(8,128)(2,1)S(1)}, bf16[368,128]{1,0:T(8,128)(2,1)S(1)}, u32[]{:S(2)}, u32[]{:S(2)}) collective-permute-start(bf16[368,128]{1,0:T(8,128)(2,1)S(1)} %get-tuple-element.113), channel_id=1, source_target_pairs={{0,24},{4,28},{8,0},{12,4},{16,8},{20,12},{24,16},{28,20},{1,25},{... | collective-permute-start | bytes 282632 | tf_op jit(solution)/shard_map/ppermute | solution.py:641
  52.1 3.0 %collective-permute-start.24 = (bf16[368,128]{1,0:T(8,128)(2,1)S(1)}, bf16[368,128]{1,0:T(8,128)(2,1)S(1)}, u32[]{:S(2)}, u32[]{:S(2)}) collective-permute-start(bf16[368,128]{1,0:T(8,128)(2,1)S(1)} %get-tuple-element.114), channel_id=1, source_target_pairs={{0,28},{4,0},{8,4},{12,8},{16,12},{20,16},{24,20},{28,24},{1,29},{... | collective-permute-start | bytes 282632 | tf_op jit(solution)/shard_map/ppermute | solution.py:641
  55.1 3.3 %collective-permute-done.20.refs_3_ = bf16[368,128]{1,0:T(8,128)(2,1)S(1)} collective-permute-done((bf16[368,128]{1,0:T(8,128)(2,1)S(1)}, bf16[368,128]{1,0:T(8,128)(2,1)S(1)}, u32[]{:S(2)}, u32[]{:S(2)}) %collective-permute-start.20) | collective-permute-done | bytes 94240 | tf_op jit(solution)/shard_map/ppermute | solution.py:641
  58.9 3.8 %collective-permute-start.25 = (bf16[176,128]{1,0:T(8,128)(2,1)S(1)}, bf16[176,128]{1,0:T(8,128)(2,1)S(1)}, u32[]{:S(2)}, u32[]{:S(2)}) collective-permute-start(bf16[176,128]{1,0:T(8,128)(2,1)S(1)} %get-tuple-element.116), channel_id=1, source_target_pairs={{0,4},{4,0},{8,12},{12,8},{16,20},{20,16},{24,28},{28,24},{1,5},{5... | collective-permute-start | bytes 135176 | tf_op jit(solution)/shard_map/ppermute | solution.py:654
  62.8 2.0 %collective-permute-done.25 = bf16[176,128]{1,0:T(8,128)(2,1)S(1)} collective-permute-done((bf16[176,128]{1,0:T(8,128)(2,1)S(1)}, bf16[176,128]{1,0:T(8,128)(2,1)S(1)}, u32[]{:S(2)}, u32[]{:S(2)}) %collective-permute-start.25) | collective-permute-done | bytes 45088 | tf_op jit(solution)/shard_map/ppermute | solution.py:654
  64.8 3.7 %collective-permute-start.26 = (bf16[2,176,128]{2,1,0:T(8,128)(2,1)S(1)}, bf16[2,176,128]{2,1,0:T(8,128)(2,1)S(1)}, u32[]{:S(2)}, u32[]{:S(2)}) collective-permute-start(bf16[2,176,128]{2,1,0:T(8,128)(2,1)S(1)} %pad_maximum_fusion.1.refs_0_), channel_id=1, source_target_pairs={{0,8},{4,12},{8,16},{12,20},{16,24},{20,28},{24,0},{28,4},{1,9},{5... | collective-permute-start | bytes 270344 | tf_op jit(solution)/shard_map/ppermute | solution.py:641
  68.5 1.3 %collective-permute-start.27 = (bf16[2,176,128]{2,1,0:T(8,128)(2,1)S(1)}, bf16[2,176,128]{2,1,0:T(8,128)(2,1)S(1)}, u32[]{:S(2)}, u32[]{:S(2)}) collective-permute-start(bf16[2,176,128]{2,1,0:T(8,128)(2,1)S(1)} %pad_maximum_fusion.1.refs_0_), channel_id=1, source_target_pairs={{0,16},{4,20},{8,24},{12,28},{16,0},{20,4},{24,8},{28,12},{1,17},{... | collective-permute-start | bytes 270344 | tf_op jit(solution)/shard_map/ppermute | solution.py:641
  69.8 1.2 %collective-permute-start.28 = (bf16[2,176,128]{2,1,0:T(8,128)(2,1)S(1)}, bf16[2,176,128]{2,1,0:T(8,128)(2,1)S(1)}, u32[]{:S(2)}, u32[]{:S(2)}) collective-permute-start(bf16[2,176,128]{2,1,0:T(8,128)(2,1)S(1)} %pad_maximum_fusion.1.refs_0_), channel_id=1, source_target_pairs={{0,24},{4,28},{8,0},{12,4},{16,8},{20,12},{24,16},{28,20},{1,25},{... | collective-permute-start | bytes 270344 | tf_op jit(solution)/shard_map/ppermute | solution.py:641
  71.7 1.0 %collective-permute-done.26.refs_1_ = bf16[2,176,128]{2,1,0:T(8,128)(2,1)S(1)} collective-permute-done((bf16[2,176,128]{2,1,0:T(8,128)(2,1)S(1)}, bf16[2,176,128]{2,1,0:T(8,128)(2,1)S(1)}, u32[]{:S(2)}, u32[]{:S(2)}) %collective-permute-start.26) | collective-permute-done | bytes 90144 | tf_op jit(solution)/shard_map/ppermute | solution.py:641
  72.7 3.0 %collective-permute-done.27.refs_2_ = bf16[2,176,128]{2,1,0:T(8,128)(2,1)S(1)} collective-permute-done((bf16[2,176,128]{2,1,0:T(8,128)(2,1)S(1)}, bf16[2,176,128]{2,1,0:T(8,128)(2,1)S(1)}, u32[]{:S(2)}, u32[]{:S(2)}) %collective-permute-start.27) | collective-permute-done | bytes 90144 | tf_op jit(solution)/shard_map/ppermute | solution.py:641
  75.8 2.1 %down.3 = (f32[32,256]{1,0:T(8,128)S(1)}, f32[32,256]{1,0:T(8,128)S(1)}, f32[32,256]{1,0:T(8,128)S(1)}, f32[32,256]{1,0:T(8,128)S(1)}) custom-call(s32[16]{0:T(128)S(1)} %get-tuple-element.104.first_ref, s32[1]{0:T(128)} %bitcast.4.seq_ref, f32[16,128]{1,0:T(8,128)S(1)} %get-tuple-element.105.range_ref, bf16[128,352]{1,0:T(8,128)(2,1)S(1)} %get-tuple-element.106.pick_ref, ...), custom_call_target="tpu_custom_call" | custom-call | tf_op jit(solution)/shard_map/down/pallas_call | solution.py:589
  78.2 0.9 %collective-permute-start.29 = (f32[32,256]{1,0:T(8,128)S(1)}, f32[32,256]{1,0:T(8,128)S(1)}, u32[]{:S(2)}, u32[]{:S(2)}) collective-permute-start(f32[32,256]{1,0:T(8,128)S(1)} %get-tuple-element.122), channel_id=1, source_target_pairs={{0,3},{1,0},{2,1},{3,2},{4,7},{5,4},{6,5},{7,6},{8,11},{9,8},{10,9... | collective-permute-start | bytes 98312 | tf_op jit(solution)/shard_map/ppermute | solution.py:641
  79.1 0.9 %collective-permute-start.30 = (f32[32,256]{1,0:T(8,128)S(1)}, f32[32,256]{1,0:T(8,128)S(1)}, u32[]{:S(2)}, u32[]{:S(2)}) collective-permute-start(f32[32,256]{1,0:T(8,128)S(1)} %get-tuple-element.123), channel_id=1, source_target_pairs={{0,2},{1,3},{2,0},{3,1},{4,6},{5,7},{6,4},{7,5},{8,10},{9,11},{10,... | collective-permute-start | bytes 98312 | tf_op jit(solution)/shard_map/ppermute | solution.py:641
  80.7 2.4 %collective-permute-done.30.refs_2_ = f32[32,256]{1,0:T(8,128)S(1)} collective-permute-done((f32[32,256]{1,0:T(8,128)S(1)}, f32[32,256]{1,0:T(8,128)S(1)}, u32[]{:S(2)}, u32[]{:S(2)}) %collective-permute-start.30) | collective-permute-done | bytes 32800 | tf_op jit(solution)/shard_map/ppermute | solution.py:641
  83.3 0.8 finish.1
  (35 shorter events, 4.2 us)
Async XLA Ops:
  10.1 11.9 %all-to-all-start = ((bf16[8,12,640]{2,1,0:T(8,128)(2,1)}), bf16[8,12,640]{2,1,0:T(8,128)(2,1)S(1)}, u32[]{:S(2)}, u32[]{:S(2)}) async-start(bf16[8,12,640]{2,1,0:T(8,128)(2,1)} %attend.1), calls=%async_computation | async-start | bytes 327680 | tf_op jit(solution)/shard_map/all_to_all | solution.py:645
  13.5 19.0 %copy-start = (bf16[1536,192]{0,1:T(8,128)(2,1)S(1)}, bf16[1536,192]{0,1:T(8,128)(2,1)}, u32[]{:S(2)}) copy-start(bf16[1536,192]{0,1:T(8,128)(2,1)} %param.21) | copy-start | bytes 1769476
  13.5 18.9 %copy-start.1 = (bf16[4,8,192]{2,1,0:T(8,128)(2,1)S(1)}, bf16[4,8,192]{2,1,0:T(8,128)(2,1)}, u32[]{:S(2)}) copy-start(bf16[4,8,192]{2,1,0:T(8,128)(2,1)} %residual_ref.1) | copy-start | bytes 36868
  13.5 18.9 %copy-start.2 = (s32[4,8,8]{2,1,0:T(8,128)S(1)}, s32[4,8,8]{2,1,0:T(8,128)}, u32[]{:S(2)}) copy-start(s32[4,8,8]{2,1,0:T(8,128)} %routes_ref.1) | copy-start | bytes 3076
  13.5 18.9 %copy-start.3 = (f32[192]{0:T(256)S(1)}, f32[192]{0:T(256)}, u32[]{:S(2)}) copy-start(f32[192]{0:T(256)} %param.22) | copy-start | bytes 2308
  13.5 24.5 %copy-start.5 = (bf16[192,40]{0,1:T(8,128)(2,1)S(1)}, bf16[192,40]{0,1:T(8,128)(2,1)}, u32[]{:S(2)}) copy-start(bf16[192,40]{0,1:T(8,128)(2,1)} %param.23) | copy-start | bytes 46084
  18.4 57.4 %copy-start.4 = (bf16[10,192,512]{2,1,0:T(8,128)(2,1)S(1)}, bf16[10,192,512]{2,1,0:T(8,128)(2,1)}, u32[]{:S(2)}) copy-start(bf16[10,192,512]{2,1,0:T(8,128)(2,1)} %w_ref.1) | copy-start | bytes 5898244
  22.4 3.7 %collective-permute-start.11 = (bf16[4,1536]{1,0:T(4,128)(2,1)S(1)}, bf16[4,1536]{1,0:T(4,128)(2,1)S(1)}, u32[]{:S(2)}, u32[]{:S(2)}) collective-permute-start(bf16[4,1536]{1,0:T(4,128)(2,1)S(1)} %join.1), channel_id=1, source_target_pairs={{0,4},{4,0},{8,12},{12,8},{16,20},{20,16},{24,28},{28,24},{1,5},{5... | collective-permute-start | bytes 36872 | tf_op jit(solution)/shard_map/ppermute | solution.py:654
  26.2 5.7 %collective-permute-start.12 = (bf16[2,4,1536]{2,1,0:T(4,128)(2,1)S(1)}, bf16[2,4,1536]{2,1,0:T(4,128)(2,1)S(1)}, u32[]{:S(2)}, u32[]{:S(2)}) collective-permute-start(bf16[2,4,1536]{2,1,0:T(4,128)(2,1)S(1)} %pad_maximum_fusion.2.refs_0_), channel_id=1, source_target_pairs={{0,8},{4,12},{8,16},{12,20},{16,24},{20,28},{24,0},{28,4},{1,9},{5... | collective-permute-start | bytes 73736 | tf_op jit(solution)/shard_map/ppermute | solution.py:641
  26.3 5.5 %collective-permute-start.13 = (bf16[2,4,1536]{2,1,0:T(4,128)(2,1)S(1)}, bf16[2,4,1536]{2,1,0:T(4,128)(2,1)S(1)}, u32[]{:S(2)}, u32[]{:S(2)}) collective-permute-start(bf16[2,4,1536]{2,1,0:T(4,128)(2,1)S(1)} %pad_maximum_fusion.2.refs_0_), channel_id=1, source_target_pairs={{0,16},{4,20},{8,24},{12,28},{16,0},{20,4},{24,8},{28,12},{1,17},{... | collective-permute-start | bytes 73736 | tf_op jit(solution)/shard_map/ppermute | solution.py:641
  27.4 5.0 %collective-permute-start.14 = (bf16[2,4,1536]{2,1,0:T(4,128)(2,1)S(1)}, bf16[2,4,1536]{2,1,0:T(4,128)(2,1)S(1)}, u32[]{:S(2)}, u32[]{:S(2)}) collective-permute-start(bf16[2,4,1536]{2,1,0:T(4,128)(2,1)S(1)} %pad_maximum_fusion.2.refs_0_), channel_id=1, source_target_pairs={{0,24},{4,28},{8,0},{12,4},{16,8},{20,12},{24,16},{28,20},{1,25},{... | collective-permute-start | bytes 73736 | tf_op jit(solution)/shard_map/ppermute | solution.py:641
  32.9 3.7 %collective-permute-start.15 = (bf16[32,256]{1,0:T(8,128)(2,1)S(1)}, bf16[32,256]{1,0:T(8,128)(2,1)S(1)}, u32[]{:S(2)}, u32[]{:S(2)}) collective-permute-start(bf16[32,256]{1,0:T(8,128)(2,1)S(1)} %get-tuple-element.102.refs_0_), channel_id=1, source_target_pairs={{0,1},{1,2},{2,3},{3,0},{4,5},{5,6},{6,7},{7,4},{8,9},{9,10},{10,1... | collective-permute-start | bytes 49160 | tf_op jit(solution)/shard_map/ppermute | solution.py:641
  33.0 3.9 %collective-permute-start.16 = (bf16[32,256]{1,0:T(8,128)(2,1)S(1)}, bf16[32,256]{1,0:T(8,128)(2,1)S(1)}, u32[]{:S(2)}, u32[]{:S(2)}) collective-permute-start(bf16[32,256]{1,0:T(8,128)(2,1)S(1)} %get-tuple-element.102.refs_0_), channel_id=1, source_target_pairs={{0,2},{1,3},{2,0},{3,1},{4,6},{5,7},{6,4},{7,5},{8,10},{9,11},{10,... | collective-permute-start | bytes 49160 | tf_op jit(solution)/shard_map/ppermute | solution.py:641
  35.2 2.8 %collective-permute-start.17 = (bf16[32,256]{1,0:T(8,128)(2,1)S(1)}, bf16[32,256]{1,0:T(8,128)(2,1)S(1)}, u32[]{:S(2)}, u32[]{:S(2)}) collective-permute-start(bf16[32,256]{1,0:T(8,128)(2,1)S(1)} %get-tuple-element.102.refs_0_), channel_id=1, source_target_pairs={{0,3},{1,0},{2,1},{3,2},{4,7},{5,4},{6,5},{7,6},{8,11},{9,8},{10,9... | collective-permute-start | bytes 49160 | tf_op jit(solution)/shard_map/ppermute | solution.py:641
  42.3 8.1 %collective-permute-start.18 = (bf16[368,128]{1,0:T(8,128)(2,1)S(1)}, bf16[368,128]{1,0:T(8,128)(2,1)S(1)}, u32[]{:S(2)}, u32[]{:S(2)}) collective-permute-start(bf16[368,128]{1,0:T(8,128)(2,1)S(1)} %get-tuple-element.108), channel_id=1, source_target_pairs={{0,4},{4,8},{8,12},{12,16},{16,20},{20,24},{24,28},{28,0},{1,5},{5... | collective-permute-start | bytes 282632 | tf_op jit(solution)/shard_map/ppermute | solution.py:641
  42.9 9.2 %collective-permute-start.19 = (bf16[368,128]{1,0:T(8,128)(2,1)S(1)}, bf16[368,128]{1,0:T(8,128)(2,1)S(1)}, u32[]{:S(2)}, u32[]{:S(2)}) collective-permute-start(bf16[368,128]{1,0:T(8,128)(2,1)S(1)} %get-tuple-element.109), channel_id=1, source_target_pairs={{0,8},{4,12},{8,16},{12,20},{16,24},{20,28},{24,0},{28,4},{1,9},{5... | collective-permute-start | bytes 282632 | tf_op jit(solution)/shard_map/ppermute | solution.py:641
  44.7 13.6 %collective-permute-start.20 = (bf16[368,128]{1,0:T(8,128)(2,1)S(1)}, bf16[368,128]{1,0:T(8,128)(2,1)S(1)}, u32[]{:S(2)}, u32[]{:S(2)}) collective-permute-start(bf16[368,128]{1,0:T(8,128)(2,1)S(1)} %get-tuple-element.110), channel_id=1, source_target_pairs={{0,12},{4,16},{8,20},{12,24},{16,28},{20,0},{24,4},{28,8},{1,13},{... | collective-permute-start | bytes 282632 | tf_op jit(solution)/shard_map/ppermute | solution.py:641
  47.6 10.7 %collective-permute-start.21 = (bf16[368,128]{1,0:T(8,128)(2,1)S(1)}, bf16[368,128]{1,0:T(8,128)(2,1)S(1)}, u32[]{:S(2)}, u32[]{:S(2)}) collective-permute-start(bf16[368,128]{1,0:T(8,128)(2,1)S(1)} %get-tuple-element.111), channel_id=1, source_target_pairs={{0,16},{4,20},{8,24},{12,28},{16,0},{20,4},{24,8},{28,12},{1,17},{... | collective-permute-start | bytes 282632 | tf_op jit(solution)/shard_map/ppermute | solution.py:641
  49.7 8.7 %collective-permute-start.22 = (bf16[368,128]{1,0:T(8,128)(2,1)S(1)}, bf16[368,128]{1,0:T(8,128)(2,1)S(1)}, u32[]{:S(2)}, u32[]{:S(2)}) collective-permute-start(bf16[368,128]{1,0:T(8,128)(2,1)S(1)} %get-tuple-element.112), channel_id=1, source_target_pairs={{0,20},{4,24},{8,28},{12,0},{16,4},{20,8},{24,12},{28,16},{1,21},{... | collective-permute-start | bytes 282632 | tf_op jit(solution)/shard_map/ppermute | solution.py:641
  50.4 8.0 %collective-permute-start.23 = (bf16[368,128]{1,0:T(8,128)(2,1)S(1)}, bf16[368,128]{1,0:T(8,128)(2,1)S(1)}, u32[]{:S(2)}, u32[]{:S(2)}) collective-permute-start(bf16[368,128]{1,0:T(8,128)(2,1)S(1)} %get-tuple-element.113), channel_id=1, source_target_pairs={{0,24},{4,28},{8,0},{12,4},{16,8},{20,12},{24,16},{28,20},{1,25},{... | collective-permute-start | bytes 282632 | tf_op jit(solution)/shard_map/ppermute | solution.py:641
  52.1 6.5 %collective-permute-start.24 = (bf16[368,128]{1,0:T(8,128)(2,1)S(1)}, bf16[368,128]{1,0:T(8,128)(2,1)S(1)}, u32[]{:S(2)}, u32[]{:S(2)}) collective-permute-start(bf16[368,128]{1,0:T(8,128)(2,1)S(1)} %get-tuple-element.114), channel_id=1, source_target_pairs={{0,28},{4,0},{8,4},{12,8},{16,12},{20,16},{24,20},{28,24},{1,29},{... | collective-permute-start | bytes 282632 | tf_op jit(solution)/shard_map/ppermute | solution.py:641
  58.9 5.9 %collective-permute-start.25 = (bf16[176,128]{1,0:T(8,128)(2,1)S(1)}, bf16[176,128]{1,0:T(8,128)(2,1)S(1)}, u32[]{:S(2)}, u32[]{:S(2)}) collective-permute-start(bf16[176,128]{1,0:T(8,128)(2,1)S(1)} %get-tuple-element.116), channel_id=1, source_target_pairs={{0,4},{4,0},{8,12},{12,8},{16,20},{20,16},{24,28},{28,24},{1,5},{5... | collective-permute-start | bytes 135176 | tf_op jit(solution)/shard_map/ppermute | solution.py:654
  64.8 7.9 %collective-permute-start.26 = (bf16[2,176,128]{2,1,0:T(8,128)(2,1)S(1)}, bf16[2,176,128]{2,1,0:T(8,128)(2,1)S(1)}, u32[]{:S(2)}, u32[]{:S(2)}) collective-permute-start(bf16[2,176,128]{2,1,0:T(8,128)(2,1)S(1)} %pad_maximum_fusion.1.refs_0_), channel_id=1, source_target_pairs={{0,8},{4,12},{8,16},{12,20},{16,24},{20,28},{24,0},{28,4},{1,9},{5... | collective-permute-start | bytes 270344 | tf_op jit(solution)/shard_map/ppermute | solution.py:641
  68.5 7.2 %collective-permute-start.27 = (bf16[2,176,128]{2,1,0:T(8,128)(2,1)S(1)}, bf16[2,176,128]{2,1,0:T(8,128)(2,1)S(1)}, u32[]{:S(2)}, u32[]{:S(2)}) collective-permute-start(bf16[2,176,128]{2,1,0:T(8,128)(2,1)S(1)} %pad_maximum_fusion.1.refs_0_), channel_id=1, source_target_pairs={{0,16},{4,20},{8,24},{12,28},{16,0},{20,4},{24,8},{28,12},{1,17},{... | collective-permute-start | bytes 270344 | tf_op jit(solution)/shard_map/ppermute | solution.py:641
  69.8 6.0 %collective-permute-start.28 = (bf16[2,176,128]{2,1,0:T(8,128)(2,1)S(1)}, bf16[2,176,128]{2,1,0:T(8,128)(2,1)S(1)}, u32[]{:S(2)}, u32[]{:S(2)}) collective-permute-start(bf16[2,176,128]{2,1,0:T(8,128)(2,1)S(1)} %pad_maximum_fusion.1.refs_0_), channel_id=1, source_target_pairs={{0,24},{4,28},{8,0},{12,4},{16,8},{20,12},{24,16},{28,20},{1,25},{... | collective-permute-start | bytes 270344 | tf_op jit(solution)/shard_map/ppermute | solution.py:641
  78.2 2.5 %collective-permute-start.29 = (f32[32,256]{1,0:T(8,128)S(1)}, f32[32,256]{1,0:T(8,128)S(1)}, u32[]{:S(2)}, u32[]{:S(2)}) collective-permute-start(f32[32,256]{1,0:T(8,128)S(1)} %get-tuple-element.122), channel_id=1, source_target_pairs={{0,3},{1,0},{2,1},{3,2},{4,7},{5,4},{6,5},{7,6},{8,11},{9,8},{10,9... | collective-permute-start | bytes 98312 | tf_op jit(solution)/shard_map/ppermute | solution.py:641
  79.1 4.0 %collective-permute-start.30 = (f32[32,256]{1,0:T(8,128)S(1)}, f32[32,256]{1,0:T(8,128)S(1)}, u32[]{:S(2)}, u32[]{:S(2)}) collective-permute-start(f32[32,256]{1,0:T(8,128)S(1)} %get-tuple-element.123), channel_id=1, source_target_pairs={{0,2},{1,3},{2,0},{3,1},{4,6},{5,7},{6,4},{7,5},{8,10},{9,11},{10,... | collective-permute-start | bytes 98312 | tf_op jit(solution)/shard_map/ppermute | solution.py:641
  80.0 3.4 %collective-permute-start.31 = (f32[32,256]{1,0:T(8,128)S(1)}, f32[32,256]{1,0:T(8,128)S(1)}, u32[]{:S(2)}, u32[]{:S(2)}) collective-permute-start(f32[32,256]{1,0:T(8,128)S(1)} %get-tuple-element.124), channel_id=1, source_target_pairs={{0,1},{1,2},{2,3},{3,0},{4,5},{5,6},{6,7},{7,4},{8,9},{9,10},{10,1... | collective-permute-start | bytes 98312 | tf_op jit(solution)/shard_map/ppermute | solution.py:641

commit v11 on v10

--- a/solution.py
+++ b/solution.py
@@ -222,7 +222,7 @@
     steps, requests, _ = queries.shape
     pages = page_table.shape[1]
     page_rows = cache.shape[1]
-    classes = tuple(c for c in (2, 4, 6) if c < pages) + (pages,)
+    classes = tuple(c for c in (1, 2, 4, 6) if c < pages) + (pages,)
     share = (requests * steps * GROUP // devices, KV_WIDTH + LANES)
     smem, hbm = pl.BlockSpec(memory_space=pltpu.SMEM), pl.BlockSpec(memory_space=pl.ANY)
     return pl.pallas_call(

time: 84.6 us -> 84 us (level); the launches traced: 84.1 us -> 84.5 us
  waiting for transfers between devices: 24 us -> 25.7 us
  Pallas kernels: 18.5 us -> 17.6 us
    ppermute x19, waiting for transfers between devices: 14.8 us -> 16.4 us  [send(): lax.ppermute(x, axis, [(i, (i + distance) % count) for i in range(count)])]
    ppermute x2, starting transfers between devices: 3.93 us -> 2.63 us  [pair_gather(): beside = lax.ppermute(block, axis, [(i, i ^ 1) for i in range(count)])]
    ppermute x19, starting transfers between devices: 28.4 us -> 29.3 us  [send(): lax.ppermute(x, axis, [(i, (i + distance) % count) for i in range(count)])]
    pallas_call x1, Pallas kernels: 10.1 us -> 9.2 us  [attend(): pl.pallas_call(functools.partial(attend_kernel, classes), in_specs=[smem]...]
  transfers between devices with their start and end apart: 22 -> 22, of which waited for: 16 -> 15; matrix products, arithmetic and copies ran while one was open for 6% -> 6% of each run, Pallas kernels for 0% -> 0%
where the time goes in v11:
time: 84 us; the launch traced here: 84.5 us
  starting transfers between devices  35.3 us (42%)
  waiting for transfers between devices  25.7 us (31%)
  Pallas kernels  17.6 us (21%)
  local copies, waits for them, and re-layouts  4.88 us (6%)
  between operations  0.84 us (1%)
    ppermute x19, starting transfers between devices, send(): lax.ppermute(x, axis, [(i, (i + distance) % count) for i in range(count)])  29.3 us
    ppermute x19, waiting for transfers between devices, send(): lax.ppermute(x, axis, [(i, (i + distance) % count) for i in range(count)])  16.4 us
    pallas_call x1, Pallas kernels, attend(): pl.pallas_call(functools.partial(attend_kernel, classes), in_specs=[smem]...  9.2 us
    ppermute x2, waiting for transfers between devices, pair_gather(): beside = lax.ppermute(block, axis, [(i, i ^ 1) for i in range(count)])  5.63 us
    optimization_barrier x1, local copies, waits for them, and re-layouts, local(): w_gate_up, shares = lax.optimization_barrier((w_gate_up, shares))  4.84 us
    pallas_call x1, Pallas kernels, gate_up(): pl.pallas_call(functools.partial(gate_up_kernel, features, local, turn, s...  4.26 us
    all_to_all x1, waiting for transfers between devices, swap(): return lax.all_to_all(x, axis, split_axis=0, concat_axis=0, tiled=True)  3.62 us
    all_to_all x1, starting transfers between devices, swap(): return lax.all_to_all(x, axis, split_axis=0, concat_axis=0, tiled=True)  3.39 us
  transfers between devices with their start and end apart: 22, of which 15 were waited for; matrix products, arithmetic and copies ran while one was open for 6% of the time, Pallas kernels for 0%

profile of v11, /device:TPU:0, one launch (start us, length us, event | category | flops | bytes accessed | tf_op | source)
XLA Modules:
  0.0 84.5 jit_solution(10575219680434800986)
XLA Ops:
  0.0 9.2 %attend.1 = bf16[8,12,640]{2,1,0:T(8,128)(2,1)} custom-call(s32[1]{0:T(128)} %bitcast.4.seq_ref, s32[8,8]{1,0:T(8,128)} %table_hbm.1, s32[8]{0:T(128)} %len_hbm.1, bf16[4,8,1536]{2,1,0:T(8,128)(2,1)} %q_hbm.1, bf16[4,8,2,512]{3,2,1,0:T(2,128)(2,1)} %fresh_hbm.1, bf16[64,64,2,512]{3,2,1,0:T(2,128)(2,1)} %bitcast.28), custom_call_target="tpu_custom_call" | custom-call | tf_op jit(solution)/shard_map/attend/pallas_call | solution.py:228
  9.2 3.4 %all-to-all-start = ((bf16[8,12,640]{2,1,0:T(8,128)(2,1)}), bf16[8,12,640]{2,1,0:T(8,128)(2,1)S(1)}, u32[]{:S(2)}, u32[]{:S(2)}) async-start(bf16[8,12,640]{2,1,0:T(8,128)(2,1)} %attend.1), calls=%async_computation | async-start | bytes 327680 | tf_op jit(solution)/shard_map/all_to_all | solution.py:645
  12.7 4.8 %copy.16 = bf16[10,192,2,512]{3,1,2,0:T(8,128)(2,1)} copy(bf16[10,192,2,512]{3,2,1,0:T(2,128)(2,1)} %param.24) | data formatting | bytes 7864320 | tf_op jit(solution)/shard_map/optimization_barrier | solution.py:690
  17.5 3.6 %all-to-all-done.x_ref = bf16[8,12,640]{2,1,0:T(8,128)(2,1)S(1)} async-done(((bf16[8,12,640]{2,1,0:T(8,128)(2,1)}), bf16[8,12,640]{2,1,0:T(8,128)(2,1)S(1)}, u32[]{:S(2)}, u32[]{:S(2)}) %all-to-all-start) | async-done | bytes 122912 | tf_op jit(solution)/shard_map/all_to_all | solution.py:645
  21.7 3.6 %collective-permute-done.11 = bf16[4,1536]{1,0:T(4,128)(2,1)S(1)} collective-permute-done((bf16[4,1536]{1,0:T(4,128)(2,1)S(1)}, bf16[4,1536]{1,0:T(4,128)(2,1)S(1)}, u32[]{:S(2)}, u32[]{:S(2)}) %collective-permute-start.11) | collective-permute-done | bytes 12320 | tf_op jit(solution)/shard_map/ppermute | solution.py:654
  25.5 1.1 %collective-permute-start.13 = (bf16[2,4,1536]{2,1,0:T(4,128)(2,1)S(1)}, bf16[2,4,1536]{2,1,0:T(4,128)(2,1)S(1)}, u32[]{:S(2)}, u32[]{:S(2)}) collective-permute-start(bf16[2,4,1536]{2,1,0:T(4,128)(2,1)S(1)} %pad_maximum_fusion.2.refs_0_), channel_id=1, source_target_pairs={{0,16},{4,20},{8,24},{12,28},{16,0},{20,4},{24,8},{28,12},{1,17},{... | collective-permute-start | bytes 73736 | tf_op jit(solution)/shard_map/ppermute | solution.py:641
  26.6 2.6 %collective-permute-start.14 = (bf16[2,4,1536]{2,1,0:T(4,128)(2,1)S(1)}, bf16[2,4,1536]{2,1,0:T(4,128)(2,1)S(1)}, u32[]{:S(2)}, u32[]{:S(2)}) collective-permute-start(bf16[2,4,1536]{2,1,0:T(4,128)(2,1)S(1)} %pad_maximum_fusion.2.refs_0_), channel_id=1, source_target_pairs={{0,24},{4,28},{8,0},{12,4},{16,8},{20,12},{24,16},{28,20},{1,25},{... | collective-permute-start | bytes 73736 | tf_op jit(solution)/shard_map/ppermute | solution.py:641
  29.2 1.8 %collective-permute-done.12.refs_1_ = bf16[2,4,1536]{2,1,0:T(4,128)(2,1)S(1)} collective-permute-done((bf16[2,4,1536]{2,1,0:T(4,128)(2,1)S(1)}, bf16[2,4,1536]{2,1,0:T(4,128)(2,1)S(1)}, u32[]{:S(2)}, u32[]{:S(2)}) %collective-permute-start.12) | collective-permute-done | bytes 24608 | tf_op jit(solution)/shard_map/ppermute | solution.py:641
  32.2 3.5 %collective-permute-start.16 = (bf16[32,256]{1,0:T(8,128)(2,1)S(1)}, bf16[32,256]{1,0:T(8,128)(2,1)S(1)}, u32[]{:S(2)}, u32[]{:S(2)}) collective-permute-start(bf16[32,256]{1,0:T(8,128)(2,1)S(1)} %get-tuple-element.102.refs_0_), channel_id=1, source_target_pairs={{0,2},{1,3},{2,0},{3,1},{4,6},{5,7},{6,4},{7,5},{8,10},{9,11},{10,... | collective-permute-start | bytes 49160 | tf_op jit(solution)/shard_map/ppermute | solution.py:641
  35.6 1.4 %collective-permute-start.17 = (bf16[32,256]{1,0:T(8,128)(2,1)S(1)}, bf16[32,256]{1,0:T(8,128)(2,1)S(1)}, u32[]{:S(2)}, u32[]{:S(2)}) collective-permute-start(bf16[32,256]{1,0:T(8,128)(2,1)S(1)} %get-tuple-element.102.refs_0_), channel_id=1, source_target_pairs={{0,3},{1,0},{2,1},{3,2},{4,7},{5,4},{6,5},{7,6},{8,11},{9,8},{10,9... | collective-permute-start | bytes 49160 | tf_op jit(solution)/shard_map/ppermute | solution.py:641
  37.4 1.1 %collective-permute-done.17.refs_3_ = bf16[32,256]{1,0:T(8,128)(2,1)S(1)} collective-permute-done((bf16[32,256]{1,0:T(8,128)(2,1)S(1)}, bf16[32,256]{1,0:T(8,128)(2,1)S(1)}, u32[]{:S(2)}, u32[]{:S(2)}) %collective-permute-start.17) | collective-permute-done | bytes 16416 | tf_op jit(solution)/shard_map/ppermute | solution.py:641
  38.5 4.3 %gate_up.3 = (bf16[368,128]{1,0:T(8,128)(2,1)S(1)}, bf16[368,128]{1,0:T(8,128)(2,1)S(1)}, bf16[368,128]{1,0:T(8,128)(2,1)S(1)}, bf16[368,128]{1,0:T(8,128)(2,1)S...) custom-call(s32[1]{0:T(128)} %bitcast.11.where_ref, ...), custom_call_target="tpu_custom_call" | custom-call | tf_op jit(solution)/shard_map/gate_up/pallas_call | solution.py:462
  42.7 0.9 %collective-permute-start.18 = (bf16[368,128]{1,0:T(8,128)(2,1)S(1)}, bf16[368,128]{1,0:T(8,128)(2,1)S(1)}, u32[]{:S(2)}, u32[]{:S(2)}) collective-permute-start(bf16[368,128]{1,0:T(8,128)(2,1)S(1)} %get-tuple-element.108), channel_id=1, source_target_pairs={{0,4},{4,8},{8,12},{12,16},{16,20},{20,24},{24,28},{28,0},{1,5},{5... | collective-permute-start | bytes 282632 | tf_op jit(solution)/shard_map/ppermute | solution.py:641
  43.6 1.4 %collective-permute-start.19 = (bf16[368,128]{1,0:T(8,128)(2,1)S(1)}, bf16[368,128]{1,0:T(8,128)(2,1)S(1)}, u32[]{:S(2)}, u32[]{:S(2)}) collective-permute-start(bf16[368,128]{1,0:T(8,128)(2,1)S(1)} %get-tuple-element.109), channel_id=1, source_target_pairs={{0,8},{4,12},{8,16},{12,20},{16,24},{20,28},{24,0},{28,4},{1,9},{5... | collective-permute-start | bytes 282632 | tf_op jit(solution)/shard_map/ppermute | solution.py:641
  45.0 3.1 %collective-permute-start.20 = (bf16[368,128]{1,0:T(8,128)(2,1)S(1)}, bf16[368,128]{1,0:T(8,128)(2,1)S(1)}, u32[]{:S(2)}, u32[]{:S(2)}) collective-permute-start(bf16[368,128]{1,0:T(8,128)(2,1)S(1)} %get-tuple-element.110), channel_id=1, source_target_pairs={{0,12},{4,16},{8,20},{12,24},{16,28},{20,0},{24,4},{28,8},{1,13},{... | collective-permute-start | bytes 282632 | tf_op jit(solution)/shard_map/ppermute | solution.py:641
  48.1 2.1 %collective-permute-start.21 = (bf16[368,128]{1,0:T(8,128)(2,1)S(1)}, bf16[368,128]{1,0:T(8,128)(2,1)S(1)}, u32[]{:S(2)}, u32[]{:S(2)}) collective-permute-start(bf16[368,128]{1,0:T(8,128)(2,1)S(1)} %get-tuple-element.111), channel_id=1, source_target_pairs={{0,16},{4,20},{8,24},{12,28},{16,0},{20,4},{24,8},{28,12},{1,17},{... | collective-permute-start | bytes 282632 | tf_op jit(solution)/shard_map/ppermute | solution.py:641
  50.1 1.1 %collective-permute-start.22 = (bf16[368,128]{1,0:T(8,128)(2,1)S(1)}, bf16[368,128]{1,0:T(8,128)(2,1)S(1)}, u32[]{:S(2)}, u32[]{:S(2)}) collective-permute-start(bf16[368,128]{1,0:T(8,128)(2,1)S(1)} %get-tuple-element.112), channel_id=1, source_target_pairs={{0,20},{4,24},{8,28},{12,0},{16,4},{20,8},{24,12},{28,16},{1,21},{... | collective-permute-start | bytes 282632 | tf_op jit(solution)/shard_map/ppermute | solution.py:641
  51.2 1.3 %collective-permute-start.23 = (bf16[368,128]{1,0:T(8,128)(2,1)S(1)}, bf16[368,128]{1,0:T(8,128)(2,1)S(1)}, u32[]{:S(2)}, u32[]{:S(2)}) collective-permute-start(bf16[368,128]{1,0:T(8,128)(2,1)S(1)} %get-tuple-element.113), channel_id=1, source_target_pairs={{0,24},{4,28},{8,0},{12,4},{16,8},{20,12},{24,16},{28,20},{1,25},{... | collective-permute-start | bytes 282632 | tf_op jit(solution)/shard_map/ppermute | solution.py:641
  52.5 2.9 %collective-permute-start.24 = (bf16[368,128]{1,0:T(8,128)(2,1)S(1)}, bf16[368,128]{1,0:T(8,128)(2,1)S(1)}, u32[]{:S(2)}, u32[]{:S(2)}) collective-permute-start(bf16[368,128]{1,0:T(8,128)(2,1)S(1)} %get-tuple-element.114), channel_id=1, source_target_pairs={{0,28},{4,0},{8,4},{12,8},{16,12},{20,16},{24,20},{28,24},{1,29},{... | collective-permute-start | bytes 282632 | tf_op jit(solution)/shard_map/ppermute | solution.py:641
  55.5 3.3 %collective-permute-done.20.refs_3_ = bf16[368,128]{1,0:T(8,128)(2,1)S(1)} collective-permute-done((bf16[368,128]{1,0:T(8,128)(2,1)S(1)}, bf16[368,128]{1,0:T(8,128)(2,1)S(1)}, u32[]{:S(2)}, u32[]{:S(2)}) %collective-permute-start.20) | collective-permute-done | bytes 94240 | tf_op jit(solution)/shard_map/ppermute | solution.py:641
  58.8 1.9 %collective-permute-done.23.refs_6_ = bf16[368,128]{1,0:T(8,128)(2,1)S(1)} collective-permute-done((bf16[368,128]{1,0:T(8,128)(2,1)S(1)}, bf16[368,128]{1,0:T(8,128)(2,1)S(1)}, u32[]{:S(2)}, u32[]{:S(2)}) %collective-permute-start.23) | collective-permute-done | bytes 94240 | tf_op jit(solution)/shard_map/ppermute | solution.py:641
  61.0 2.5 %collective-permute-start.25 = (bf16[176,128]{1,0:T(8,128)(2,1)S(1)}, bf16[176,128]{1,0:T(8,128)(2,1)S(1)}, u32[]{:S(2)}, u32[]{:S(2)}) collective-permute-start(bf16[176,128]{1,0:T(8,128)(2,1)S(1)} %get-tuple-element.116), channel_id=1, source_target_pairs={{0,4},{4,0},{8,12},{12,8},{16,20},{20,16},{24,28},{28,24},{1,5},{5... | collective-permute-start | bytes 135176 | tf_op jit(solution)/shard_map/ppermute | solution.py:654
  63.6 2.0 %collective-permute-done.25 = bf16[176,128]{1,0:T(8,128)(2,1)S(1)} collective-permute-done((bf16[176,128]{1,0:T(8,128)(2,1)S(1)}, bf16[176,128]{1,0:T(8,128)(2,1)S(1)}, u32[]{:S(2)}, u32[]{:S(2)}) %collective-permute-start.25) | collective-permute-done | bytes 45088 | tf_op jit(solution)/shard_map/ppermute | solution.py:654
  65.6 3.3 %collective-permute-start.26 = (bf16[2,176,128]{2,1,0:T(8,128)(2,1)S(1)}, bf16[2,176,128]{2,1,0:T(8,128)(2,1)S(1)}, u32[]{:S(2)}, u32[]{:S(2)}) collective-permute-start(bf16[2,176,128]{2,1,0:T(8,128)(2,1)S(1)} %pad_maximum_fusion.1.refs_0_), channel_id=1, source_target_pairs={{0,8},{4,12},{8,16},{12,20},{16,24},{20,28},{24,0},{28,4},{1,9},{5... | collective-permute-start | bytes 270344 | tf_op jit(solution)/shard_map/ppermute | solution.py:641
  68.9 1.3 %collective-permute-start.27 = (bf16[2,176,128]{2,1,0:T(8,128)(2,1)S(1)}, bf16[2,176,128]{2,1,0:T(8,128)(2,1)S(1)}, u32[]{:S(2)}, u32[]{:S(2)}) collective-permute-start(bf16[2,176,128]{2,1,0:T(8,128)(2,1)S(1)} %pad_maximum_fusion.1.refs_0_), channel_id=1, source_target_pairs={{0,16},{4,20},{8,24},{12,28},{16,0},{20,4},{24,8},{28,12},{1,17},{... | collective-permute-start | bytes 270344 | tf_op jit(solution)/shard_map/ppermute | solution.py:641
  70.2 1.2 %collective-permute-start.28 = (bf16[2,176,128]{2,1,0:T(8,128)(2,1)S(1)}, bf16[2,176,128]{2,1,0:T(8,128)(2,1)S(1)}, u32[]{:S(2)}, u32[]{:S(2)}) collective-permute-start(bf16[2,176,128]{2,1,0:T(8,128)(2,1)S(1)} %pad_maximum_fusion.1.refs_0_), channel_id=1, source_target_pairs={{0,24},{4,28},{8,0},{12,4},{16,8},{20,12},{24,16},{28,20},{1,25},{... | collective-permute-start | bytes 270344 | tf_op jit(solution)/shard_map/ppermute | solution.py:641
  72.1 1.0 %collective-permute-done.26.refs_1_ = bf16[2,176,128]{2,1,0:T(8,128)(2,1)S(1)} collective-permute-done((bf16[2,176,128]{2,1,0:T(8,128)(2,1)S(1)}, bf16[2,176,128]{2,1,0:T(8,128)(2,1)S(1)}, u32[]{:S(2)}, u32[]{:S(2)}) %collective-permute-start.26) | collective-permute-done | bytes 90144 | tf_op jit(solution)/shard_map/ppermute | solution.py:641
  73.1 3.0 %collective-permute-done.27.refs_2_ = bf16[2,176,128]{2,1,0:T(8,128)(2,1)S(1)} collective-permute-done((bf16[2,176,128]{2,1,0:T(8,128)(2,1)S(1)}, bf16[2,176,128]{2,1,0:T(8,128)(2,1)S(1)}, u32[]{:S(2)}, u32[]{:S(2)}) %collective-permute-start.27) | collective-permute-done | bytes 90144 | tf_op jit(solution)/shard_map/ppermute | solution.py:641
  76.2 2.1 %down.3 = (f32[32,256]{1,0:T(8,128)S(1)}, f32[32,256]{1,0:T(8,128)S(1)}, f32[32,256]{1,0:T(8,128)S(1)}, f32[32,256]{1,0:T(8,128)S(1)}) custom-call(s32[16]{0:T(128)S(1)} %get-tuple-element.104.first_ref, s32[1]{0:T(128)} %bitcast.4.seq_ref, f32[16,128]{1,0:T(8,128)S(1)} %get-tuple-element.105.range_ref, bf16[128,352]{1,0:T(8,128)(2,1)S(1)} %get-tuple-element.106.pick_ref, ...), custom_call_target="tpu_custom_call" | custom-call | tf_op jit(solution)/shard_map/down/pallas_call | solution.py:589
  78.6 0.9 %collective-permute-start.29 = (f32[32,256]{1,0:T(8,128)S(1)}, f32[32,256]{1,0:T(8,128)S(1)}, u32[]{:S(2)}, u32[]{:S(2)}) collective-permute-start(f32[32,256]{1,0:T(8,128)S(1)} %get-tuple-element.122), channel_id=1, source_target_pairs={{0,3},{1,0},{2,1},{3,2},{4,7},{5,4},{6,5},{7,6},{8,11},{9,8},{10,9... | collective-permute-start | bytes 98312 | tf_op jit(solution)/shard_map/ppermute | solution.py:641
  79.5 0.9 %collective-permute-start.30 = (f32[32,256]{1,0:T(8,128)S(1)}, f32[32,256]{1,0:T(8,128)S(1)}, u32[]{:S(2)}, u32[]{:S(2)}) collective-permute-start(f32[32,256]{1,0:T(8,128)S(1)} %get-tuple-element.123), channel_id=1, source_target_pairs={{0,2},{1,3},{2,0},{3,1},{4,6},{5,7},{6,4},{7,5},{8,10},{9,11},{10,... | collective-permute-start | bytes 98312 | tf_op jit(solution)/shard_map/ppermute | solution.py:641
  81.1 2.3 %collective-permute-done.30.refs_2_ = f32[32,256]{1,0:T(8,128)S(1)} collective-permute-done((f32[32,256]{1,0:T(8,128)S(1)}, f32[32,256]{1,0:T(8,128)S(1)}, u32[]{:S(2)}, u32[]{:S(2)}) %collective-permute-start.30) | collective-permute-done | bytes 32800 | tf_op jit(solution)/shard_map/ppermute | solution.py:641
  (35 shorter events, 4.6 us)
Async XLA Ops:
  9.2 11.9 %all-to-all-start = ((bf16[8,12,640]{2,1,0:T(8,128)(2,1)}), bf16[8,12,640]{2,1,0:T(8,128)(2,1)S(1)}, u32[]{:S(2)}, u32[]{:S(2)}) async-start(bf16[8,12,640]{2,1,0:T(8,128)(2,1)} %attend.1), calls=%async_computation | async-start | bytes 327680 | tf_op jit(solution)/shard_map/all_to_all | solution.py:645
  12.6 19.0 %copy-start = (bf16[1536,192]{0,1:T(8,128)(2,1)S(1)}, bf16[1536,192]{0,1:T(8,128)(2,1)}, u32[]{:S(2)}) copy-start(bf16[1536,192]{0,1:T(8,128)(2,1)} %param.21) | copy-start | bytes 1769476
  12.6 19.0 %copy-start.1 = (bf16[4,8,192]{2,1,0:T(8,128)(2,1)S(1)}, bf16[4,8,192]{2,1,0:T(8,128)(2,1)}, u32[]{:S(2)}) copy-start(bf16[4,8,192]{2,1,0:T(8,128)(2,1)} %residual_ref.1) | copy-start | bytes 36868
  12.6 18.9 %copy-start.2 = (s32[4,8,8]{2,1,0:T(8,128)S(1)}, s32[4,8,8]{2,1,0:T(8,128)}, u32[]{:S(2)}) copy-start(s32[4,8,8]{2,1,0:T(8,128)} %routes_ref.1) | copy-start | bytes 3076
  12.6 18.9 %copy-start.3 = (f32[192]{0:T(256)S(1)}, f32[192]{0:T(256)}, u32[]{:S(2)}) copy-start(f32[192]{0:T(256)} %param.22) | copy-start | bytes 2308
  12.7 25.8 %copy-start.5 = (bf16[192,40]{0,1:T(8,128)(2,1)S(1)}, bf16[192,40]{0,1:T(8,128)(2,1)}, u32[]{:S(2)}) copy-start(bf16[192,40]{0,1:T(8,128)(2,1)} %param.23) | copy-start | bytes 46084
  17.5 58.7 %copy-start.4 = (bf16[10,192,512]{2,1,0:T(8,128)(2,1)S(1)}, bf16[10,192,512]{2,1,0:T(8,128)(2,1)}, u32[]{:S(2)}) copy-start(bf16[10,192,512]{2,1,0:T(8,128)(2,1)} %w_ref.1) | copy-start | bytes 5898244
  21.6 3.7 %collective-permute-start.11 = (bf16[4,1536]{1,0:T(4,128)(2,1)S(1)}, bf16[4,1536]{1,0:T(4,128)(2,1)S(1)}, u32[]{:S(2)}, u32[]{:S(2)}) collective-permute-start(bf16[4,1536]{1,0:T(4,128)(2,1)S(1)} %join.1), channel_id=1, source_target_pairs={{0,4},{4,0},{8,12},{12,8},{16,20},{20,16},{24,28},{28,24},{1,5},{5... | collective-permute-start | bytes 36872 | tf_op jit(solution)/shard_map/ppermute | solution.py:654
  25.3 5.7 %collective-permute-start.12 = (bf16[2,4,1536]{2,1,0:T(4,128)(2,1)S(1)}, bf16[2,4,1536]{2,1,0:T(4,128)(2,1)S(1)}, u32[]{:S(2)}, u32[]{:S(2)}) collective-permute-start(bf16[2,4,1536]{2,1,0:T(4,128)(2,1)S(1)} %pad_maximum_fusion.2.refs_0_), channel_id=1, source_target_pairs={{0,8},{4,12},{8,16},{12,20},{16,24},{20,28},{24,0},{28,4},{1,9},{5... | collective-permute-start | bytes 73736 | tf_op jit(solution)/shard_map/ppermute | solution.py:641
  25.5 5.5 %collective-permute-start.13 = (bf16[2,4,1536]{2,1,0:T(4,128)(2,1)S(1)}, bf16[2,4,1536]{2,1,0:T(4,128)(2,1)S(1)}, u32[]{:S(2)}, u32[]{:S(2)}) collective-permute-start(bf16[2,4,1536]{2,1,0:T(4,128)(2,1)S(1)} %pad_maximum_fusion.2.refs_0_), channel_id=1, source_target_pairs={{0,16},{4,20},{8,24},{12,28},{16,0},{20,4},{24,8},{28,12},{1,17},{... | collective-permute-start | bytes 73736 | tf_op jit(solution)/shard_map/ppermute | solution.py:641
  26.6 5.0 %collective-permute-start.14 = (bf16[2,4,1536]{2,1,0:T(4,128)(2,1)S(1)}, bf16[2,4,1536]{2,1,0:T(4,128)(2,1)S(1)}, u32[]{:S(2)}, u32[]{:S(2)}) collective-permute-start(bf16[2,4,1536]{2,1,0:T(4,128)(2,1)S(1)} %pad_maximum_fusion.2.refs_0_), channel_id=1, source_target_pairs={{0,24},{4,28},{8,0},{12,4},{16,8},{20,12},{24,16},{28,20},{1,25},{... | collective-permute-start | bytes 73736 | tf_op jit(solution)/shard_map/ppermute | solution.py:641
  32.1 4.9 %collective-permute-start.15 = (bf16[32,256]{1,0:T(8,128)(2,1)S(1)}, bf16[32,256]{1,0:T(8,128)(2,1)S(1)}, u32[]{:S(2)}, u32[]{:S(2)}) collective-permute-start(bf16[32,256]{1,0:T(8,128)(2,1)S(1)} %get-tuple-element.102.refs_0_), channel_id=1, source_target_pairs={{0,1},{1,2},{2,3},{3,0},{4,5},{5,6},{6,7},{7,4},{8,9},{9,10},{10,1... | collective-permute-start | bytes 49160 | tf_op jit(solution)/shard_map/ppermute | solution.py:641
  32.2 5.2 %collective-permute-start.16 = (bf16[32,256]{1,0:T(8,128)(2,1)S(1)}, bf16[32,256]{1,0:T(8,128)(2,1)S(1)}, u32[]{:S(2)}, u32[]{:S(2)}) collective-permute-start(bf16[32,256]{1,0:T(8,128)(2,1)S(1)} %get-tuple-element.102.refs_0_), channel_id=1, source_target_pairs={{0,2},{1,3},{2,0},{3,1},{4,6},{5,7},{6,4},{7,5},{8,10},{9,11},{10,... | collective-permute-start | bytes 49160 | tf_op jit(solution)/shard_map/ppermute | solution.py:641
  35.6 2.8 %collective-permute-start.17 = (bf16[32,256]{1,0:T(8,128)(2,1)S(1)}, bf16[32,256]{1,0:T(8,128)(2,1)S(1)}, u32[]{:S(2)}, u32[]{:S(2)}) collective-permute-start(bf16[32,256]{1,0:T(8,128)(2,1)S(1)} %get-tuple-element.102.refs_0_), channel_id=1, source_target_pairs={{0,3},{1,0},{2,1},{3,2},{4,7},{5,4},{6,5},{7,6},{8,11},{9,8},{10,9... | collective-permute-start | bytes 49160 | tf_op jit(solution)/shard_map/ppermute | solution.py:641
  42.7 8.5 %collective-permute-start.18 = (bf16[368,128]{1,0:T(8,128)(2,1)S(1)}, bf16[368,128]{1,0:T(8,128)(2,1)S(1)}, u32[]{:S(2)}, u32[]{:S(2)}) collective-permute-start(bf16[368,128]{1,0:T(8,128)(2,1)S(1)} %get-tuple-element.108), channel_id=1, source_target_pairs={{0,4},{4,8},{8,12},{12,16},{16,20},{20,24},{24,28},{28,0},{1,5},{5... | collective-permute-start | bytes 282632 | tf_op jit(solution)/shard_map/ppermute | solution.py:641
  43.6 8.9 %collective-permute-start.19 = (bf16[368,128]{1,0:T(8,128)(2,1)S(1)}, bf16[368,128]{1,0:T(8,128)(2,1)S(1)}, u32[]{:S(2)}, u32[]{:S(2)}) collective-permute-start(bf16[368,128]{1,0:T(8,128)(2,1)S(1)} %get-tuple-element.109), channel_id=1, source_target_pairs={{0,8},{4,12},{8,16},{12,20},{16,24},{20,28},{24,0},{28,4},{1,9},{5... | collective-permute-start | bytes 282632 | tf_op jit(solution)/shard_map/ppermute | solution.py:641
  45.0 13.8 %collective-permute-start.20 = (bf16[368,128]{1,0:T(8,128)(2,1)S(1)}, bf16[368,128]{1,0:T(8,128)(2,1)S(1)}, u32[]{:S(2)}, u32[]{:S(2)}) collective-permute-start(bf16[368,128]{1,0:T(8,128)(2,1)S(1)} %get-tuple-element.110), channel_id=1, source_target_pairs={{0,12},{4,16},{8,20},{12,24},{16,28},{20,0},{24,4},{28,8},{1,13},{... | collective-permute-start | bytes 282632 | tf_op jit(solution)/shard_map/ppermute | solution.py:641
  48.1 10.7 %collective-permute-start.21 = (bf16[368,128]{1,0:T(8,128)(2,1)S(1)}, bf16[368,128]{1,0:T(8,128)(2,1)S(1)}, u32[]{:S(2)}, u32[]{:S(2)}) collective-permute-start(bf16[368,128]{1,0:T(8,128)(2,1)S(1)} %get-tuple-element.111), channel_id=1, source_target_pairs={{0,16},{4,20},{8,24},{12,28},{16,0},{20,4},{24,8},{28,12},{1,17},{... | collective-permute-start | bytes 282632 | tf_op jit(solution)/shard_map/ppermute | solution.py:641
  50.1 8.7 %collective-permute-start.22 = (bf16[368,128]{1,0:T(8,128)(2,1)S(1)}, bf16[368,128]{1,0:T(8,128)(2,1)S(1)}, u32[]{:S(2)}, u32[]{:S(2)}) collective-permute-start(bf16[368,128]{1,0:T(8,128)(2,1)S(1)} %get-tuple-element.112), channel_id=1, source_target_pairs={{0,20},{4,24},{8,28},{12,0},{16,4},{20,8},{24,12},{28,16},{1,21},{... | collective-permute-start | bytes 282632 | tf_op jit(solution)/shard_map/ppermute | solution.py:641
  51.2 9.5 %collective-permute-start.23 = (bf16[368,128]{1,0:T(8,128)(2,1)S(1)}, bf16[368,128]{1,0:T(8,128)(2,1)S(1)}, u32[]{:S(2)}, u32[]{:S(2)}) collective-permute-start(bf16[368,128]{1,0:T(8,128)(2,1)S(1)} %get-tuple-element.113), channel_id=1, source_target_pairs={{0,24},{4,28},{8,0},{12,4},{16,8},{20,12},{24,16},{28,20},{1,25},{... | collective-permute-start | bytes 282632 | tf_op jit(solution)/shard_map/ppermute | solution.py:641
  52.5 8.2 %collective-permute-start.24 = (bf16[368,128]{1,0:T(8,128)(2,1)S(1)}, bf16[368,128]{1,0:T(8,128)(2,1)S(1)}, u32[]{:S(2)}, u32[]{:S(2)}) collective-permute-start(bf16[368,128]{1,0:T(8,128)(2,1)S(1)} %get-tuple-element.114), channel_id=1, source_target_pairs={{0,28},{4,0},{8,4},{12,8},{16,12},{20,16},{24,20},{28,24},{1,29},{... | collective-permute-start | bytes 282632 | tf_op jit(solution)/shard_map/ppermute | solution.py:641
  61.0 4.6 %collective-permute-start.25 = (bf16[176,128]{1,0:T(8,128)(2,1)S(1)}, bf16[176,128]{1,0:T(8,128)(2,1)S(1)}, u32[]{:S(2)}, u32[]{:S(2)}) collective-permute-start(bf16[176,128]{1,0:T(8,128)(2,1)S(1)} %get-tuple-element.116), channel_id=1, source_target_pairs={{0,4},{4,0},{8,12},{12,8},{16,20},{20,16},{24,28},{28,24},{1,5},{5... | collective-permute-start | bytes 135176 | tf_op jit(solution)/shard_map/ppermute | solution.py:654
  65.6 7.5 %collective-permute-start.26 = (bf16[2,176,128]{2,1,0:T(8,128)(2,1)S(1)}, bf16[2,176,128]{2,1,0:T(8,128)(2,1)S(1)}, u32[]{:S(2)}, u32[]{:S(2)}) collective-permute-start(bf16[2,176,128]{2,1,0:T(8,128)(2,1)S(1)} %pad_maximum_fusion.1.refs_0_), channel_id=1, source_target_pairs={{0,8},{4,12},{8,16},{12,20},{16,24},{20,28},{24,0},{28,4},{1,9},{5... | collective-permute-start | bytes 270344 | tf_op jit(solution)/shard_map/ppermute | solution.py:641
  68.9 7.2 %collective-permute-start.27 = (bf16[2,176,128]{2,1,0:T(8,128)(2,1)S(1)}, bf16[2,176,128]{2,1,0:T(8,128)(2,1)S(1)}, u32[]{:S(2)}, u32[]{:S(2)}) collective-permute-start(bf16[2,176,128]{2,1,0:T(8,128)(2,1)S(1)} %pad_maximum_fusion.1.refs_0_), channel_id=1, source_target_pairs={{0,16},{4,20},{8,24},{12,28},{16,0},{20,4},{24,8},{28,12},{1,17},{... | collective-permute-start | bytes 270344 | tf_op jit(solution)/shard_map/ppermute | solution.py:641
  70.2 6.0 %collective-permute-start.28 = (bf16[2,176,128]{2,1,0:T(8,128)(2,1)S(1)}, bf16[2,176,128]{2,1,0:T(8,128)(2,1)S(1)}, u32[]{:S(2)}, u32[]{:S(2)}) collective-permute-start(bf16[2,176,128]{2,1,0:T(8,128)(2,1)S(1)} %pad_maximum_fusion.1.refs_0_), channel_id=1, source_target_pairs={{0,24},{4,28},{8,0},{12,4},{16,8},{20,12},{24,16},{28,20},{1,25},{... | collective-permute-start | bytes 270344 | tf_op jit(solution)/shard_map/ppermute | solution.py:641
  78.6 2.5 %collective-permute-start.29 = (f32[32,256]{1,0:T(8,128)S(1)}, f32[32,256]{1,0:T(8,128)S(1)}, u32[]{:S(2)}, u32[]{:S(2)}) collective-permute-start(f32[32,256]{1,0:T(8,128)S(1)} %get-tuple-element.122), channel_id=1, source_target_pairs={{0,3},{1,0},{2,1},{3,2},{4,7},{5,4},{6,5},{7,6},{8,11},{9,8},{10,9... | collective-permute-start | bytes 98312 | tf_op jit(solution)/shard_map/ppermute | solution.py:641
  79.5 3.9 %collective-permute-start.30 = (f32[32,256]{1,0:T(8,128)S(1)}, f32[32,256]{1,0:T(8,128)S(1)}, u32[]{:S(2)}, u32[]{:S(2)}) collective-permute-start(f32[32,256]{1,0:T(8,128)S(1)} %get-tuple-element.123), channel_id=1, source_target_pairs={{0,2},{1,3},{2,0},{3,1},{4,6},{5,7},{6,4},{7,5},{8,10},{9,11},{10,... | collective-permute-start | bytes 98312 | tf_op jit(solution)/shard_map/ppermute | solution.py:641
  80.4 3.4 %collective-permute-start.31 = (f32[32,256]{1,0:T(8,128)S(1)}, f32[32,256]{1,0:T(8,128)S(1)}, u32[]{:S(2)}, u32[]{:S(2)}) collective-permute-start(f32[32,256]{1,0:T(8,128)S(1)} %get-tuple-element.124), channel_id=1, source_target_pairs={{0,1},{1,2},{2,3},{3,0},{4,5},{5,6},{6,7},{7,4},{8,9},{9,10},{10,1... | collective-permute-start | bytes 98312 | tf_op jit(solution)/shard_map/ppermute | solution.py:641
